TPU v7x, 32 devices: a whole 2x2x4 slice. The times are simulated.
32 devices in a mesh: segment: 4 (over z), ctx: 8 (over y, x, core).
Axes of the slice: x: 2, y: 2, z: 4, core: 2. Of those that a mesh axis runs over, the one named last changes fastest.
Arguments:
- acts: bfloat16 [4, 1024, 2048], P('segment', 'ctx'), may hold values from -10 to 10
- norm_gains: float32 [4, 3, 2048], P('segment'), may hold values from 0.25 to 1.75
- w_kv: bfloat16 [4, 2048, 1024], P('segment', None, 'ctx'), may hold values from -1 to 36.35534
- dt_in: bfloat16 [4, 2048, 128], P('segment'), may hold values from -0.125 to 0.125
- dt_out: bfloat16 [4, 128, 2048], P('segment'), may hold values from -0.5 to 0.5
- dt_bias: float32 [4, 2048], P('segment'), may hold values from -3 to -1
- decay_rate: float32 [4, 2048], P('segment'), may hold values from 0.002 to 2
- w_bc: bfloat16 [4, 2048, 32], P('segment'), may hold values from -0.03125 to 0.03125
- skip_gain: float32 [4, 2048], P('segment'), may hold values from 0.25 to 1.75
- w_router: bfloat16 [4, 2048, 4], P('segment'), may hold values from -1.109145 to 1.109145
- routes: int32 [4, 1024, 2], P('segment', 'ctx'), may hold values from 0 to 3, all different within a row; in each aligned block of 128 rows (0 to 127, 128 to 255, ..., all dimensions but the last counted through in order) at most 64 rows name the same one
- w_up: bfloat16 [4, 2048, 28672], P('segment', None, 'ctx'), may hold values from -0.125 to 0.125
- w_down: bfloat16 [4, 28672, 2048], P('segment', 'ctx'), may hold values from -0.0625 to 0.0625
Outputs:
- handed: bfloat16 [4, 1024, 2048], P('segment', 'ctx')
Inputs may be any that keep to these rules, and one draw needn't show every extreme that they name: `routes`: in each section, the 128 rows of one context shard name every expert exactly 64 times; a token's 2 experts differ.
All inputs are finite; a program needn't handle non-finite values.
Results may differ from a plain program's by a relative error of at most 0.017.
Values may be sent and summed in bfloat16 or wider, within the bound.
No kernel may reach another device: no remote copies, remote signals or barrier semaphores. Data moves between devices by JAX's collectives and lax.ppermute only.
A program may use at most 128 MiB of HBM per device.

v0:
```python
import jax
import jax.numpy as jnp
from jax import lax
from jax.sharding import PartitionSpec as P

HEADS = 16
KVH = 4
HD = 128
EXPERTS = 4


def entering(array, axis, join, neutral):
    place = lax.axis_index(axis)
    gathered = jax.tree.map(
        lambda a, kind: lax.all_gather(a.astype(kind), axis), array, (jnp.bfloat16, jnp.bfloat16)
    )
    state = jax.tree.map(lambda a, e: jnp.zeros_like(a) + jnp.asarray(e, a.dtype), array, neutral)

    def one(turn, state):
        return join(
            state,
            jax.tree.map(
                lambda a, own: lax.dynamic_index_in_dim(a, turn, 0, False).astype(own.dtype),
                gathered,
                array,
            ),
        )

    return lax.fori_loop(0, place, one, state)


def shifted(value, axis, steps):
    count = lax.axis_size(axis)
    pairs = [(source, (source + steps) % count) for source in range(count)]
    return lax.ppermute(value, axis, pairs)


def rms_norm(values, gain):
    return values * lax.rsqrt(jnp.mean(values * values, -1, keepdims=True) + 1e-06) * gain


def combine_states(earlier, later):
    return (earlier[0] * later[0], later[0][:, None] * earlier[1] + later[1])


def on_device(
    acts,
    norm_gains,
    w_kv,
    dt_in,
    dt_out,
    dt_bias,
    decay_rate,
    w_bc,
    skip_gain,
    w_router,
    routes,
    w_up,
    w_down,
):
    shard_count = lax.axis_size("ctx")
    shard_index = lax.axis_index("ctx")
    start_x = acts[0].astype(jnp.float32)
    rows_here = start_x.shape[0]
    width = start_x.shape[1]
    group = HEADS // KVH
    normed = rms_norm(start_x, norm_gains[0, 0]).astype(jnp.bfloat16)
    kv_rows = jnp.dot(
        normed,
        lax.all_gather(w_kv[0], "ctx", axis=1, tiled=True),
        preferred_element_type=jnp.float32,
    ).astype(jnp.bfloat16)
    keys = kv_rows[:, : KVH * HD].reshape(rows_here, KVH, HD)
    values = kv_rows[:, KVH * HD :].reshape(rows_here, KVH, HD)
    queries = normed.reshape(rows_here, KVH, group, HD)
    query_pos = shard_index * rows_here + jnp.arange(rows_here, dtype=jnp.int32)
    running = jnp.full((rows_here, KVH, group), -1e30, jnp.float32)
    key_piece = lax.all_gather(keys, "ctx", axis=0, tiled=True)
    value_piece = lax.all_gather(values, "ctx", axis=0, tiled=True)
    key_pos = jnp.arange(key_piece.shape[0], dtype=jnp.int32)
    scores = jnp.einsum(
        "tgrd,sgd->tgrs", queries, key_piece, preferred_element_type=jnp.float32
    ) * HD ** (-0.5)
    allowed = (key_pos[None, :] <= query_pos[:, None])[:, None, None, :]
    scores = jnp.where(allowed, scores, -1e30)
    newest = jnp.maximum(running, jnp.max(scores, -1))
    weights = jnp.where(allowed, jnp.exp(scores - newest[..., None]), 0.0)
    total = jnp.sum(weights, -1)
    summed = jnp.einsum(
        "tgrs,sgd->tgrd",
        weights.astype(jnp.bfloat16),
        value_piece,
        preferred_element_type=jnp.float32,
    )
    _, total, summed = (newest, total, summed)
    first = start_x + (summed / total[..., None]).reshape(rows_here, width)
    mixed_in = rms_norm(first, norm_gains[0, 1]).astype(jnp.bfloat16)
    low_rank = jnp.dot(mixed_in, dt_in[0], preferred_element_type=jnp.float32).astype(jnp.bfloat16)
    step_size = jax.nn.softplus(
        jnp.dot(low_rank, dt_out[0], preferred_element_type=jnp.float32) + dt_bias[0]
    )
    log_decay = step_size * decay_rate[0]
    state_width = w_bc.shape[2] // 2
    both = jnp.dot(mixed_in, w_bc[0], preferred_element_type=jnp.float32)
    b_part = both[:, :state_width]
    c_part = both[:, state_width:]
    driven = step_size * mixed_in.astype(jnp.float32)
    block_rows = min(32, rows_here)
    block_count = rows_here // block_rows
    lower_mask = jnp.arange(block_rows)[:, None] >= jnp.arange(block_rows)[None, :]
    lower_float = lower_mask.astype(jnp.float32)

    def block_scan(carry, item):
        state, offset_sum = carry
        rate_block, drive_block, b_block, c_block = item
        running_sum = jnp.dot(lower_float, rate_block, precision=lax.Precision.HIGHEST)
        coupling = jnp.dot(c_block, b_block.T, precision=lax.Precision.HIGHEST)
        distance = jnp.maximum(running_sum[:, None, :] - running_sum[None, :, :], 0.0)
        fading = jnp.where(lower_mask[:, :, None], jnp.exp(-distance), 0.0)
        within = jnp.sum(fading * coupling[:, :, None] * drive_block[None, :, :], 1)
        decay_in = jnp.exp(-running_sum)
        from_state = jnp.dot(c_block, state.T, precision=lax.Precision.HIGHEST) * decay_in
        tail_weight = jnp.exp(running_sum - running_sum[-1][None, :]) * drive_block
        state = decay_in[-1][:, None] * state + jnp.dot(
            tail_weight.T, b_block, precision=lax.Precision.HIGHEST
        )
        shard_decay = jnp.exp(-(offset_sum[None, :] + running_sum))
        return ((state, offset_sum + running_sum[-1]), (within + from_state, shard_decay))

    start_carry = (jnp.zeros((width, state_width), jnp.float32), jnp.zeros((width,), jnp.float32))
    scan_items = (
        log_decay.reshape(block_count, block_rows, width),
        driven.reshape(block_count, block_rows, width),
        b_part.reshape(block_count, block_rows, state_width),
        c_part.reshape(block_count, block_rows, state_width),
    )
    (end_state, end_offset), (block_out, block_decay) = lax.scan(
        block_scan, start_carry, scan_items
    )
    local_out = block_out.reshape(rows_here, width)
    products = block_decay.reshape(rows_here, width)
    end_product = jnp.exp(-end_offset)
    identity = (jnp.ones((width,), jnp.float32), jnp.zeros((width, state_width), jnp.float32))
    incoming = entering((end_product, end_state), "ctx", combine_states, identity)[1]
    carried = jnp.dot(c_part, incoming.T, precision=lax.Precision.HIGHEST) * products
    second = first + local_out + carried + skip_gain[0] * mixed_in.astype(jnp.float32)
    expert_in = rms_norm(second, norm_gains[0, 2]).astype(jnp.bfloat16)
    logits = jnp.dot(expert_in, w_router[0], preferred_element_type=jnp.float32)
    top_count = routes.shape[2]
    expert_ids = jnp.arange(EXPERTS, dtype=jnp.int32)
    picked = (routes[0][:, :, None] == expert_ids[None, None, :]).astype(jnp.float32)
    chosen = jnp.sum(picked * logits[:, None, :], -1)
    gates = jax.nn.softmax(chosen, -1)
    flat_route = routes[0].reshape(-1)
    flat_hits = (flat_route[:, None] == expert_ids[None, :]).astype(jnp.int32)
    earlier_hits = jnp.cumsum(flat_hits, 0) - flat_hits
    slot_rank = jnp.sum(earlier_hits * flat_hits, -1)
    capacity = rows_here * top_count // EXPERTS
    parts = shard_count // EXPERTS
    position = flat_route * capacity + slot_rank
    slot_ids = jnp.arange(EXPERTS * capacity, dtype=jnp.int32)
    placing = (position[None, :] == slot_ids[:, None]).astype(jnp.bfloat16)
    repeated = jnp.repeat(expert_in, top_count, 0)
    packed = (
        jnp.dot(placing, repeated, preferred_element_type=jnp.float32)
        .astype(jnp.bfloat16)
        .reshape(EXPERTS, capacity, width)
    )
    up_local = w_up[0]
    down_local = w_down[0]
    outgoing = jnp.repeat(packed, parts, 0)
    received = lax.all_to_all(outgoing, "ctx", split_axis=0, concat_axis=0, tiled=True)
    flat_rows = received.reshape(-1, width)
    hidden = jax.nn.silu(jnp.dot(flat_rows, up_local, preferred_element_type=jnp.float32)).astype(
        jnp.bfloat16
    )
    part_out = (
        jnp.dot(hidden, down_local, preferred_element_type=jnp.float32)
        .astype(jnp.bfloat16)
        .reshape(received.shape)
    )
    returned = lax.all_to_all(part_out, "ctx", split_axis=0, concat_axis=0, tiled=True)
    expert_out = (
        returned.reshape(EXPERTS, parts, capacity, width)
        .astype(jnp.float32)
        .sum(1)
        .reshape(EXPERTS * capacity, width)
    )
    weighting = (position[:, None] == slot_ids[None, :]).astype(jnp.float32) * gates.reshape(-1)[
        :, None
    ]
    moe_rows = (
        jnp.dot(weighting, expert_out, precision=lax.Precision.HIGHEST)
        .reshape(rows_here, top_count, width)
        .sum(1)
    )
    finished = (second + moe_rows).astype(jnp.bfloat16)
    return shifted(finished[None], "segment", 1)


def solution(mesh):
    in_specs = (
        P("segment", "ctx", None),
        P("segment", None, None),
        P("segment", None, "ctx"),
        P("segment", None, None),
        P("segment", None, None),
        P("segment", None),
        P("segment", None),
        P("segment", None, None),
        P("segment", None),
        P("segment", None, None),
        P("segment", "ctx", None),
        P("segment", None, "ctx"),
        P("segment", "ctx", None),
    )
    out_specs = P("segment", "ctx", None)
    return jax.shard_map(
        on_device, mesh=mesh, in_specs=in_specs, out_specs=out_specs, check_vma=False
    )
```

profile of v0, /device:TPU:0, one launch (start us, length us, event | category | flops | bytes accessed | tf_op | source)
XLA Modules:
  0.0 279.4 jit_solution(7777968642208696614)
XLA Ops:
  6.5 0.7 all-gather.11.cloned.1.call-update
  7.3 1.2 fusion.47
  8.5 0.7 fusion.86
  9.3 40.1 %all-gather.11.cloned.1.call-done = bf16[1,2048,1024]{2,1,0:T(8,128)(2,1)} async-done(((bf16[1,2048,128]{2,1,0:T(8,128)(2,1)}), bf16[1,2048,1024]{2,1,0:T(8,128)(2,1)}) %all-gather.11.cloned.1.call-update) | async-done | bytes 4194320 | tf_op jit(solution)/shard_map/all_gather | solution.py:70
  49.4 3.1 %fusion.41 = bf16[128,1024]{1,0:T(8,128)(2,1)S(1)} fusion(bf16[1,2048,1024]{2,1,0:T(8,128)(2,1)} %all-gather.11.cloned.1.call-done, bf16[1,128,2048]{2,1,0:T(8,128)(2,1)} %param.17, f32[2048]{0:T(1024)S(1)} %bitcast.242, f32[128]{0:T(128)S(1)} %add_rsqrt_fusion.2), kind=kOutput, calls=%fused_computation.56 | convolution fusion | flops 538050560 | bytes 4989440 | tf_op jit(solution)/shard_map/dot_general | solution.py:68
  52.6 0.7 copy.89
  53.3 0.8 copy.68
  54.4 1.2 reduce-window.6
  56.0 0.8 copy.79
  56.8 1.2 copy.61
  58.2 18.7 %all-gather.9.cloned.1.call-done = bf16[1024,4,128]{2,0,1:T(8,128)(2,1)} async-done(((bf16[128,4,128]{2,0,1:T(8,128)(2,1)}), bf16[1024,4,128]{2,0,1:T(8,128)(2,1)}) %all-gather.9.cloned.1.call-update) | async-done | bytes 1048592 | tf_op jit(solution)/shard_map/all_gather | solution.py:78
  76.9 2.8 fusion.23
  79.8 3.2 %copy-done.2 = f32[4,1024,128,4]{2,1,3,0:T(8,128)} copy-done((f32[4,1024,128,4]{2,1,3,0:T(8,128)}, f32[4,1024,128,4]{2,1,3,0:T(8,128)S(1)}, u32[]{:S(2)}) %copy-start.2) | copy-done | bytes 8388632
  83.0 2.0 fusion.24
  85.0 17.4 %all-gather.7.cloned.1.call-done = bf16[1024,4,128]{0,2,1:T(8,128)(2,1)} async-done(((bf16[128,4,128]{0,2,1:T(8,128)(2,1)}), bf16[1024,4,128]{0,2,1:T(8,128)(2,1)}) %all-gather.7.cloned.1.call-update) | async-done | bytes 1048592 | tf_op jit(solution)/shard_map/all_gather | solution.py:79
  102.4 7.3 %multiply_reduce_fusion.2 = (f32[128]{0:T(128)S(1)}, f32[128,4,4,128]{0,3,2,1:T(8,128)}, f32[128,4,4,128]{0,3,2,1:T(8,128)}) fusion(f32[128,4,4,128]{0,3,2,1:T(8,128)S(1)} %bitcast.221, f32[128,4,4]{0,2,1:T(4,128)S(1)} %fusion.24, f32[4,1024,128,4]{2,1,3,0:T(8,128)} %copy-done.2, f32[128,4,4]{0,2,1:T(4,128)S(1)} %broadcast_maximum_fusion, ...), kind=kOutput, calls=%fused_computation.73 | convolution fusion | flops 548405120 | bytes 12730880 | tf_op jit(solution)/shard_map/tgrs,sgd->tgrd/dot_general | solution.py:89
  109.7 1.6 copy.64
  111.3 1.6 multiply_convert_fusion.3
  113.3 3.7 %convert_multiply_fusion.1 = (f32[128,2048]{1,0:T(8,128)}, bf16[128,2048]{1,0:T(8,128)(2,1)S(1)}, f32[128,2048]{1,0:T(8,128)}) fusion(f32[2048]{0:T(1024)S(1)} %bitcast.245, f32[128]{0:T(128)S(1)} %add_rsqrt_fusion.1, f32[128,2048]{1,0:T(8,128)S(1)} %copy.64, bf16[1,128,2048]{2,1,0:T(8,128)(2,1)S(1)} %copy-done.3, f32[2048]{0:T(1024)S(1)} %bitcast.247, ...), kind=kOutput, calls=%fused_computation.55 | convolution fusion | flops 138166272 | bytes 5792256 | tf_op jit(solution)/shard_map/dot_general | solution.py:100
  117.0 30.0 %while.30 = (s32[]{:T(128)}, f32[2048,16]{0,1:T(8,128)S(1)}, f32[2048]{0:T(1024)S(1)}, f32[4,32,2048]{2,1,0:T(8,128)}, f32[4,32,2048]{2,1,0:T(8,128)}, /*index=5...) while((s32[]{:T(128)}, f32[2048,16]{0,1:T(8,128)S(1)}, ...), condition=%wide.region_6.7_spmd.clone, body=%wide.region_4.6_spmd.clone.sunk | while | flops 65805312 | bytes 4443777 | solution.py:137
  117.0 0.2 fusion.119
  117.2 1.3 negate_exponential_fusion.2
  118.5 1.0 dynamic-slice_bitcast_fusion.2
  119.5 2.7 multiply_reduce_fusion.4
  122.2 1.1 fusion.120
  123.4 0.3 convolution_add_fusion.3
  123.7 0.8 bitcast_dynamic-update-slice_fusion.2
  124.7 1.3 negate_exponential_fusion.2
  126.0 1.0 dynamic-slice_bitcast_fusion.2
  127.0 2.7 multiply_reduce_fusion.4
  129.7 1.1 fusion.120
  130.9 0.3 convolution_add_fusion.3
  131.2 0.8 bitcast_dynamic-update-slice_fusion.2
  132.2 1.3 negate_exponential_fusion.2
  133.5 1.0 dynamic-slice_bitcast_fusion.2
  134.5 2.7 multiply_reduce_fusion.4
  137.2 1.1 fusion.120
  138.4 0.3 convolution_add_fusion.3
  138.7 0.8 bitcast_dynamic-update-slice_fusion.2
  139.7 1.3 negate_exponential_fusion.2
  141.0 1.0 dynamic-slice_bitcast_fusion.2
  142.0 2.7 multiply_reduce_fusion.4
  144.7 1.1 fusion.120
  145.9 0.3 convolution_add_fusion.3
  146.2 0.8 bitcast_dynamic-update-slice_fusion.2
  147.0 9.8 %all-gather.2 = bf16[16384,16]{0,1:T(8,128)(2,1)S(1)} all-gather(bf16[2048,16]{0,1:T(8,128)(2,1)S(1)} %convert_element_type.116), channel_id=4, replica_groups=mesh['segment'=4,'ctx'=8] {'ctx'}, dimensions={0}, use_global_device_ids=true | all-gather | bytes 589824 | tf_op jit(solution)/shard_map/all_gather | solution.py:15
  156.9 8.1 %all-gather.1 = bf16[16384]{0:T(1024)(128)(2,1)S(1)} all-gather(bf16[2048]{0:T(1024)(128)(2,1)S(1)} %exponential_convert_fusion), channel_id=3, replica_groups=mesh['segment'=4,'ctx'=8] {'ctx'}, dimensions={0}, use_global_device_ids=true | all-gather | bytes 36864 | tf_op jit(solution)/shard_map/all_gather | solution.py:15
  165.2 1.4 bitcast_add_fusion
  166.6 2.6 multiply_reduce_fusion.1
  169.4 0.6 broadcast_in_dim.83
  170.0 1.2 reshape.253
  171.2 1.7 convolution_convert_fusion
  172.9 0.3 broadcast_in_dim.84
  173.2 30.0 %all_to_all.10 = bf16[8,64,2048]{2,1,0:T(8,128)(2,1)S(1)} all-to-all(bf16[8,64,2048]{2,1,0:T(8,128)(2,1)S(1)} %bitcast.219), channel_id=1, replica_groups=mesh['segment'=4,'ctx'=8] {'ctx'}, dimensions={0} | all-to-all | bytes 4194304 | tf_op jit(solution)/shard_map/all_to_all | solution.py:172
  203.2 11.9 %multiply_convert_fusion = bf16[512,3584]{1,0:T(8,128)(2,1)S(1)} fusion(bf16[512,2048]{1,0:T(8,128)(2,1)S(1)} %bitcast.226, bf16[1,2048,3584]{2,1,0:T(8,128)(2,1)} %param.28), kind=kOutput, calls=%fused_computation.37 | convolution fusion | flops 7525367808 | bytes 20447232 | tf_op jit(solution)/shard_map/dot_general | solution.py:174
  215.1 8.9 %fusion.33 = bf16[512,2048]{1,0:T(8,128)(2,1)} fusion(bf16[512,3584]{1,0:T(8,128)(2,1)S(1)} %multiply_convert_fusion, bf16[1,3584,2048]{2,1,0:T(8,128)(2,1)S(1)} %bitcast.252), kind=kOutput, calls=%fused_computation.46 | convolution fusion | flops 7517241344 | bytes 20447232 | tf_op jit(solution)/shard_map/dot_general | solution.py:178
  224.1 4.3 %all-to-all-start.1 = ((bf16[8,64,2048]{2,1,0:T(8,128)(2,1)}), bf16[8,64,2048]{2,1,0:T(8,128)(2,1)}, u32[]{:S(2)}, u32[]{:S(2)}) async-start(bf16[8,64,2048]{2,1,0:T(8,128)(2,1)} %bitcast.225), calls=%async_computation.1 | async-start | bytes 4194304 | tf_op jit(solution)/shard_map/all_to_all | solution.py:182
  228.7 0.3 fusion.72
  229.1 26.0 %all-to-all-done.1 = bf16[8,64,2048]{2,1,0:T(8,128)(2,1)} async-done(((bf16[8,64,2048]{2,1,0:T(8,128)(2,1)}), bf16[8,64,2048]{2,1,0:T(8,128)(2,1)}, u32[]{:S(2)}, u32[]{:S(2)}) %all-to-all-start.1) | async-done | bytes 2097184 | tf_op jit(solution)/shard_map/all_to_all | solution.py:182
  255.1 2.4 convert_reduce_fusion
  257.4 1.9 convolution_reduce_fusion
  259.5 1.5 collective-permute-start
  261.1 11.0 %collective-permute-done = bf16[1,128,2048]{2,1,0:T(8,128)(2,1)S(1)} collective-permute-done((bf16[1,128,2048]{2,1,0:T(8,128)(2,1)S(1)}, bf16[1,128,2048]{2,1,0:T(8,128)(2,1)S(1)}, u32[]{:S(2)}, u32[]{:S(2)}) %collective-permute-start) | collective-permute-done | bytes 524320 | tf_op jit(solution)/shard_map/ppermute | solution.py:35
  272.1 0.8 copy.114
  (96 shorter events, 3.2 us)
Async XLA Ops:
  6.5 106.7 %copy-start = (bf16[1,128,2048]{2,1,0:T(8,128)(2,1)S(1)}, bf16[1,128,2048]{2,1,0:T(8,128)(2,1)}, u32[]{:S(2)}) copy-start(bf16[1,128,2048]{2,1,0:T(8,128)(2,1)} %param.21) | copy-start | bytes 1572868
  6.5 42.9 %all-gather.11.cloned.1.call-start = ((), (), s32[]{:S(2)}) async-start(), calls=%async_computation.4 | async-start | bytes 4718592 | tf_op jit(solution)/shard_map/all_gather | solution.py:70
  7.3 69.7 %all-gather.9.cloned.1.call-start = ((), (), s32[]{:S(2)}) async-start(), calls=%async_computation.3 | async-start | bytes 1179648 | tf_op jit(solution)/shard_map/all_gather | solution.py:78
  53.3 49.2 %all-gather.7.cloned.1.call-start = ((), (), s32[]{:S(2)}) async-start(), calls=%async_computation.2 | async-start | bytes 1179648 | tf_op jit(solution)/shard_map/all_gather | solution.py:79
  79.7 3.2 %copy-start.2 = (f32[4,1024,128,4]{2,1,3,0:T(8,128)}, f32[4,1024,128,4]{2,1,3,0:T(8,128)S(1)}, u32[]{:S(2)}) copy-start(f32[4,1024,128,4]{2,1,3,0:T(8,128)S(1)} %get-tuple-element.251) | copy-start | bytes 25165828
  85.0 27.9 %copy-start.4 = (bf16[1,2048,32]{1,2,0:T(8,128)(2,1)S(1)}, bf16[1,2048,32]{1,2,0:T(8,128)(2,1)}, u32[]{:S(2)}) copy-start(bf16[1,2048,32]{1,2,0:T(8,128)(2,1)} %param.24) | copy-start | bytes 393220
  85.0 28.3 %copy-start.3 = (bf16[1,128,2048]{2,1,0:T(8,128)(2,1)S(1)}, bf16[1,128,2048]{2,1,0:T(8,128)(2,1)}, u32[]{:S(2)}) copy-start(bf16[1,128,2048]{2,1,0:T(8,128)(2,1)} %param.17) | copy-start | bytes 1572868
  85.0 28.3 %copy-start.6 = (f32[1,2048]{1,0:T(1,128)S(1)}, f32[1,2048]{1,0:T(1,128)}, u32[]{:S(2)}) copy-start(f32[1,2048]{1,0:T(1,128)} %param.23) | copy-start | bytes 24580
  85.0 28.3 %copy-start.7 = (f32[1,2048]{1,0:T(1,128)S(1)}, f32[1,2048]{1,0:T(1,128)}, u32[]{:S(2)}) copy-start(f32[1,2048]{1,0:T(1,128)} %param.22) | copy-start | bytes 24580
  117.0 49.7 %copy-start.8 = (f32[1,2048]{1,0:T(1,128)S(1)}, f32[1,2048]{1,0:T(1,128)}, u32[]{:S(2)}) copy-start(f32[1,2048]{1,0:T(1,128)} %param.25) | copy-start | bytes 24580
  173.2 41.9 %slice-start = ((s8[14680064]{0:T(1024)(128)(4,1)}), s8[4194304]{0:T(1024)(128)(4,1)S(1)}, s32[]{:S(2)}) async-start(s8[14680064]{0:T(1024)(128)(4,1)} %bitcast.251), calls=%async_computation.5 | async-start | bytes 8388608
  203.1 11.9 %slice-start.1 = ((s8[14680064]{0:T(1024)(128)(4,1)}), s8[4194304]{0:T(1024)(128)(4,1)S(1)}, s32[]{:S(2)}) async-start(s8[14680064]{0:T(1024)(128)(4,1)} %bitcast.251), calls=%async_computation.6 | async-start | bytes 8388608
  203.2 11.9 %slice-start.2 = ((s8[14680064]{0:T(1024)(128)(4,1)}), s8[4194304]{0:T(1024)(128)(4,1)S(1)}, s32[]{:S(2)}) async-start(s8[14680064]{0:T(1024)(128)(4,1)} %bitcast.251), calls=%async_computation.7 | async-start | bytes 8388608
  203.2 11.9 %slice-start.3 = ((s8[14680064]{0:T(1024)(128)(4,1)}), s8[2097152]{0:T(1024)(128)(4,1)S(1)}, s32[]{:S(2)}) async-start(s8[14680064]{0:T(1024)(128)(4,1)} %bitcast.251), calls=%async_computation.8 | async-start | bytes 4194304
  215.1 13.6 %copy-start.5 = (bf16[1,2048,4]{1,2,0:T(4,128)(2,1)S(1)}, bf16[1,2048,4]{1,2,0:T(4,128)(2,1)}, u32[]{:S(2)}) copy-start(bf16[1,2048,4]{1,2,0:T(4,128)(2,1)} %param.26) | copy-start | bytes 49156
  215.1 57.8 %copy-start.1 = (bf16[1,128,2048]{2,1,0:T(8,128)(2,1)S(1)}, bf16[1,128,2048]{2,1,0:T(8,128)(2,1)}, u32[]{:S(2)}) copy-start(bf16[1,128,2048]{2,1,0:T(8,128)(2,1)} %param.21) | copy-start | bytes 1572868
  224.1 31.0 %all-to-all-start.1 = ((bf16[8,64,2048]{2,1,0:T(8,128)(2,1)}), bf16[8,64,2048]{2,1,0:T(8,128)(2,1)}, u32[]{:S(2)}, u32[]{:S(2)}) async-start(bf16[8,64,2048]{2,1,0:T(8,128)(2,1)} %bitcast.225), calls=%async_computation.1 | async-start | bytes 4194304 | tf_op jit(solution)/shard_map/all_to_all | solution.py:182
  259.5 12.5 %collective-permute-start = (bf16[1,128,2048]{2,1,0:T(8,128)(2,1)S(1)}, bf16[1,128,2048]{2,1,0:T(8,128)(2,1)S(1)}, u32[]{:S(2)}, u32[]{:S(2)}) collective-permute-start(bf16[1,128,2048]{2,1,0:T(8,128)(2,1)S(1)} %fusion.55), channel_id=1, source_target_pairs={{0,8},{8,16},{16,24},{24,0},{1,9},{9,17},{17,25},{25,1},{2,10},{10... | collective-permute-start | bytes 1572872 | tf_op jit(solution)/shard_map/ppermute | solution.py:35
Sparse Core Ops, SparseCore 0:
  9.2 40.1 all-gather.10
  53.4 23.5 all-gather.8
  78.8 23.5 all-gather.6
where the time goes:
time: 281 us; the launch traced here: 279 us
  waiting for transfers between devices  114 us (41%)
  matrix products  56.2 us (20%)
  blocking collectives  47.9 us (17%)
  other arithmetic  24.3 us (9%)
  local copies, waits for them, and re-layouts  17 us (6%)
  between operations  13.6 us (5%)
  starting transfers between devices  5.96 us (2%)
    all_gather x1, waiting for transfers between devices, on_device(): lax.all_gather(w_kv[0], 'ctx', axis=1, tiled=True)  40.1 us
    all_to_all x1, blocking collectives, on_device(): lax.all_to_all(outgoing, 'ctx', split_axis=0, concat_axis=0, tiled=True)  30 us
    all_to_all x1, waiting for transfers between devices, on_device(): lax.all_to_all(part_out, 'ctx', split_axis=0, concat_axis=0, tiled=True)  26 us
    all_gather x1, waiting for transfers between devices, on_device(): key_piece = lax.all_gather(keys, 'ctx', axis=0, tiled=True)  18.7 us
    all_gather x2, blocking collectives, entering(): lax.all_gather(a.astype(kind), axis)  17.9 us
    all_gather x1, waiting for transfers between devices, on_device(): value_piece = lax.all_gather(values, 'ctx', axis=0, tiled=True)  17.4 us
    dot_general x1, matrix products, on_device(): jnp.dot(flat_rows, up_local, preferred_element_type=jnp.float32)  11.9 us
    ppermute x1, waiting for transfers between devices, shifted(): return lax.ppermute(value, axis, pairs)  11 us
  transfers between devices with their start and end apart: 5, of which 5 were waited for; matrix products, arithmetic and copies ran while one was open for 4% of the time, Pallas kernels for 0%

commit v1 on v0

v1 whole, which is shorter than its diff:
```python
import functools

import jax
import jax.numpy as jnp
from jax import lax
from jax.experimental import pallas as pl
from jax.experimental.pallas import tpu as pltpu
from jax.sharding import PartitionSpec as P

HEADS = 16
KVH = 4
HD = 128
GROUP = HEADS // KVH
EXPERTS = 4
EIGHT = 8
STRIP = 16
LANES = 128
PAIR = 2
CHUNKS = 2
F32 = jnp.float32
BF16 = jnp.bfloat16
VMEM = pl.BlockSpec(memory_space=pltpu.VMEM)
SMEM = pl.BlockSpec(memory_space=pltpu.SMEM)


def params(mib):
    return pltpu.CompilerParams(vmem_limit_bytes=mib * 2**20)


def cost(flops, moved, transcendentals=0):
    return pl.CostEstimate(
        flops=int(flops), bytes_accessed=int(moved), transcendentals=int(transcendentals)
    )


def shape(dims, dtype):
    return jax.ShapeDtypeStruct(tuple(dims), dtype)


def in_hbm(array):
    return pltpu.with_memory_space_constraint(array, pltpu.HBM)


def rms_norm(values, gain):
    return values * lax.rsqrt(jnp.mean(values * values, -1, keepdims=True) + 1e-06) * gain


def strips(rows, body):
    def step(index, carry):
        body(pl.ds(pl.multiple_of(index * STRIP, STRIP), STRIP))
        return carry

    lax.fori_loop(0, rows // STRIP, step, 0, unroll=4)


def split(values):
    high = values.astype(BF16)
    return high, (values - high.astype(F32)).astype(BF16)


def dot(a, b, dims=((1,), (0,))):
    return lax.dot_general(a, b, (dims, ((), ())), preferred_element_type=F32)


def dot_split(a, b, dims=((1,), (0,))):
    a_high, a_low = a
    b_high, b_low = b
    return dot(a_high, b_high, dims) + (dot(a_high, b_low, dims) + dot(a_low, b_high, dims))


def iota(dims, axis):
    return lax.broadcasted_iota(jnp.int32, dims, axis)


def norm_kernel(gains, *refs):
    xs, out = refs[:-1], refs[-1]
    rows = xs[0].shape[0]
    for slot, x in enumerate(xs):

        def body(at, slot=slot, x=x):
            out[slot, at, :] = rms_norm(x[at, :].astype(F32), gains[0]).astype(BF16)

        strips(rows, body)


def project_kernel(place, gains, near, w_own, w_other, *refs):
    xs, (q_out, kv_out, far, weights) = refs[:-4], refs[-4:]
    rows, width = xs[0].shape
    head = place[0] % KVH
    key_at = place[1]
    weights[:, pl.ds(pl.multiple_of(key_at * HD, HD), HD)] = w_own[...]
    weights[:, pl.ds(pl.multiple_of((1 - key_at) * HD, HD), HD)] = w_other[...]
    norm_kernel(gains, *xs, far)
    for half, normed in enumerate((near, far)):
        count = normed.shape[0]
        both = dot(normed[...].reshape(count * rows, width), weights[...]).astype(BF16)
        here = pl.ds(half * count * rows, count * rows)
        kv_out[0, here, :] = both[:, :HD]
        kv_out[1, here, :] = both[:, HD:]
        for slot in range(count):
            for part in range(GROUP):
                cols = pl.ds(pl.multiple_of((head * GROUP + part) * HD, HD), HD)
                q_out[half * count + slot, pl.ds(part * rows, rows), :] = normed[slot, :, cols]


def near_kernel(place, q, kv, largest_out, total_out, summed):
    me = place[0]
    rows = q.shape[1] // GROUP
    count = kv.shape[1]
    lane = iota((rows, count), 1)
    key_shard = me ^ (lane // rows)
    later = lane % rows > iota((rows, count), 0)
    for slot in range(KVH):
        shard = me ^ slot
        hidden = (key_shard > shard) | ((key_shard == shard) & later)
        scores = dot(q[slot], kv[0], ((1,), (1,))) * HD ** (-0.5)
        scores = scores.reshape(GROUP, rows, count)
        scores = jnp.where(hidden[None], -1e30, scores).reshape(GROUP * rows, count)
        largest = jnp.max(scores, -1, keepdims=True)
        weights = jnp.exp(scores - largest)
        total = jnp.sum(weights, -1, keepdims=True)
        summed[slot] = dot(weights.astype(BF16), kv[1])
        largest_out[slot] = jnp.broadcast_to(largest, (GROUP * rows, LANES))
        total_out[slot] = jnp.broadcast_to(total, (GROUP * rows, LANES))


def far_kernel(turn, slots, last, place, q, largest, total, summed, past, *outs):
    rows = q.shape[1] // GROUP
    wide = past.shape[1] // LANES
    mine = place[0] // KVH
    seen = (mine ^ turn) < mine

    def keep(at, top, weight, value):
        if last:
            result = (value / weight).astype(BF16)
            for part in range(GROUP):
                cols = slice(part * HD, (part + 1) * HD)
                outs[at][:, cols] = result[part * rows : (part + 1) * rows]
        else:
            outs[0][slots[at]] = top
            outs[1][slots[at]] = weight
            outs[2][slots[at]] = value

    @pl.when(seen)
    def _():
        for at, slot in enumerate(slots):
            scores = dot(q[slot], past[0], ((1,), (1,))) * HD ** (-0.5)
            top = jnp.broadcast_to(jnp.max(scores, -1, keepdims=True), (GROUP * rows, LANES))
            newest = jnp.maximum(largest[slot], top)
            weights = jnp.exp(scores - jnp.concatenate([newest] * wide, 1))
            fade = jnp.exp(largest[slot] - newest)
            weight = jnp.broadcast_to(jnp.sum(weights, -1, keepdims=True), (GROUP * rows, LANES))
            value = summed[slot] * fade + dot(weights.astype(BF16), past[1])
            keep(at, newest, total[slot] * fade + weight, value)

    @pl.when(jnp.logical_not(seen))
    def _():
        for at, slot in enumerate(slots):
            keep(at, largest[slot], total[slot], summed[slot])


def prepare_kernel(
    place, x, gains, skip, dt_in, dt_out, bias, rate, w_bct, *refs
):
    attended = refs[:KVH]
    base, keep_out, drive_out, chunk_state, chunk_keep, bc_out, coef_out, ends = refs[KVH:-4]
    mixed, pre, tail_high, tail_low = refs[-4:]
    rows, width = x.shape
    state = w_bct.shape[0] // 2
    chunks = rows // EIGHT
    head = place[0] % KVH
    span = GROUP * HD
    for slot in range(KVH):
        cols = pl.ds(pl.multiple_of((head ^ slot) * span, span), span)
        base[:, cols] = x[:, cols].astype(F32) + attended[slot][...].astype(F32)

    def normalize(at):
        first = base[at, :]
        mixed_in = rms_norm(first, gains[1]).astype(BF16)
        mixed[at, :] = mixed_in
        base[at, :] = first + skip[...] * mixed_in.astype(F32)

    strips(rows, normalize)
    low_rank = dot(mixed[...], dt_in[...]).astype(BF16)
    pre[...] = dot(low_rank, dt_out[...])
    bc = dot(mixed[...], w_bct[...], ((1,), (1,)))
    bct = dot(w_bct[...], mixed[...], ((1,), (1,)))
    bc_out[...] = bc
    b_rows = bct[:state]
    coupling = dot_split(split(bc[:, state:]), split(b_rows))
    row, lane = iota((rows, rows), 0), iota((rows, rows), 1)
    coef = jnp.zeros((rows, rows), F32)
    for back in range(EIGHT):
        diagonal = jnp.sum(jnp.where(lane == row - back, coupling, 0.0), 1, keepdims=True)
        coef = coef + jnp.where((lane == back) & (row % EIGHT >= back), diagonal, 0.0)
    coef_out[...] = coef

    edge = iota((EIGHT, width), 0)

    def steps(index, carry):
        at = pl.ds(pl.multiple_of(index * STRIP, STRIP), STRIP)
        raw = pre[at, :] + bias[...]
        step_size = jnp.maximum(raw, 0.0) + jnp.log1p(jnp.exp(-jnp.abs(raw)))
        keep = jnp.exp(-step_size * rate[...])
        drive = step_size * mixed[at, :].astype(F32)
        keep_out[at, :] = keep
        drive_out[at, :] = drive
        tails = []
        for part in range(STRIP // EIGHT):
            kept = keep[part * EIGHT : (part + 1) * EIGHT]
            after = jnp.where(edge < EIGHT - 1, pltpu.roll(kept, EIGHT - 1, 0), 1.0)
            for hop in (1, 2, 4):
                after = after * jnp.where(
                    edge < EIGHT - hop, pltpu.roll(after, EIGHT - hop, 0), 1.0
                )
            chunk_keep[pl.ds(index * (STRIP // EIGHT) + part, 1), :] = after[0:1] * kept[0:1]
            tails.append(after * drive[part * EIGHT : (part + 1) * EIGHT])
        high, low = split(jnp.concatenate(tails, 0))
        tail_high[at, :] = high
        tail_low[at, :] = low
        return carry

    lax.fori_loop(0, rows // STRIP, steps, 0, unroll=2)

    spread = jnp.concatenate([b_rows] * chunks, 0)
    own = iota(spread.shape, 0) // state == iota(spread.shape, 1) // EIGHT
    spread = split(jnp.where(own, spread, 0.0))
    chunk_state[...] = dot_split(spread, (tail_high[...], tail_low[...]))
    products = []
    for tile in range(width // LANES):
        cols = pl.ds(tile * LANES, LANES)
        total = jnp.zeros((state, LANES), F32)
        product = jnp.ones((1, LANES), F32)
        for chunk in range(chunks):
            kept = chunk_keep[chunk : chunk + 1, cols]
            total = total * kept + chunk_state[chunk * state : (chunk + 1) * state, cols]
            product = product * kept
        ends[:, cols] = total.astype(BF16)
        products.append(product)
    ends[:, width:] = jnp.concatenate(products, 0).astype(BF16)


def pair_kernel(place, own, other, ends):
    width = own.shape[1] - LANES
    first = lax.rem(place[0], 2) == 0
    mine = own[...].astype(F32)
    its = other[...].astype(F32)
    earlier = jnp.where(first, mine, its)
    later = jnp.where(first, its, mine)
    fade = later[:, width:]
    for tile in range(width // LANES):
        cols = slice(tile * LANES, (tile + 1) * LANES)
        ends[:, cols] = (earlier[:, cols] * fade[tile : tile + 1] + later[:, cols]).astype(BF16)
    ends[:, width:] = (earlier[:, width:] * fade).astype(BF16)


def within_kernel(coef, base, keep, drive, second, faded):
    rows, width = base.shape
    edge = iota((EIGHT, width), 0)

    def chunk(index, carry):
        at = pl.ds(pl.multiple_of(index * EIGHT, EIGHT), EIGHT)
        kept = keep[at, :]
        factors = coef[at, :]
        moved = drive[at, :]
        total = base[at, :] + factors[:, 0:1] * moved
        for back in range(1, EIGHT):
            moved = kept * pltpu.roll(moved, 1, 0)
            total = total + factors[:, back : back + 1] * moved
        second[at, :] = total
        for hop in (1, 2, 4):
            kept = kept * jnp.where(edge >= hop, pltpu.roll(kept, hop, 0), 1.0)
        faded[at, :] = kept
        return carry

    lax.fori_loop(0, rows // EIGHT, chunk, 0, unroll=2)


def route_kernel(
    place, before, faded, chunk_state, chunk_keep, bc, gains, router_t, routes_t, beside, *refs
):
    ends, (second, weighting), packed = refs[:-10], refs[-10:-8], refs[-8:-4]
    state_high, state_low, carried, expert_in = refs[-4:]
    rows, width = before.shape
    chunks = chunk_keep.shape[0]
    state = chunk_state.shape[0] // chunks
    me = place[0]
    own = place[2]
    fades = [end[:, width:].astype(F32) for end in ends]
    last_fade = beside[:, width:].astype(F32)
    second_core = lax.rem(me, 2) == 1
    for tile in range(width // LANES):
        cols = pl.ds(tile * LANES, LANES)
        total = jnp.zeros((state, LANES), F32)
        for end, fade in zip(ends[::-1], fades[::-1]):
            total = total * fade[tile : tile + 1] + end[:, cols].astype(F32)
        joined = total * last_fade[tile : tile + 1] + beside[:, cols].astype(F32)
        total = jnp.where(second_core, joined, total)
        for chunk in range(chunks):
            at = pl.ds(chunk * state, state)
            high, low = split(total)
            state_high[at, cols] = high
            state_low[at, cols] = low
            total = total * chunk_keep[chunk : chunk + 1, cols] + chunk_state[at, cols]
    wide = chunks * state
    repeat = (iota((state, wide), 1) % state == iota((state, wide), 0)).astype(BF16)
    here = iota((rows, wide), 1) // state == iota((rows, wide), 0) // EIGHT
    spread = [
        jnp.where(here, dot(part, repeat), 0.0).astype(BF16) for part in split(bc[:, state:])
    ]
    carried[...] = dot_split(spread, (state_high[...], state_low[...]))

    def normalize(at):
        values = before[at, :] + carried[at, :] * faded[at, :]
        second[at, :] = values
        expert_in[at, :] = rms_norm(values, gains[2]).astype(BF16)

    strips(rows, normalize)

    expert = iota((EXPERTS, rows), 0)
    uses = (routes_t[0:1, :] == expert) | (routes_t[1:2, :] == expert)
    logits = jnp.where(uses, dot(router_t[...], expert_in[...], ((1,), (1,))), -1e30)
    gates = jnp.where(uses, jnp.exp(logits - jnp.max(logits, 0, keepdims=True)), 0.0)
    gates = gates / jnp.sum(gates, 0, keepdims=True)
    sooner = (iota((rows, rows), 0) < iota((rows, rows), 1)).astype(BF16)
    ranks = dot(jnp.where(uses, 1.0, 0.0).astype(BF16), sooner)
    ranks = jnp.where(uses, ranks, -1.0).astype(jnp.int32)
    capacity = packed[0].shape[0]
    place_row = iota((capacity, rows), 0)
    weights = []
    for slot in range(EXPERTS):
        mine = expert == (own ^ slot)
        rank = jnp.sum(jnp.where(mine, ranks, 0), 0, keepdims=True)
        gate = jnp.sum(jnp.where(mine, gates, 0.0), 0, keepdims=True)
        placing = place_row == rank
        weights.append(jnp.where(placing, gate, 0.0))
        packed[slot][...] = dot(placing.astype(BF16), expert_in[...]).astype(BF16)
    weighting[...] = jnp.concatenate(weights, 0).T


def fetch_kernel(pieces, *refs):
    count = len(pieces)
    sources, outs, sems = refs[:count], refs[-count - 1 : -1], refs[-1]
    copies = []
    for source, out, number in zip(sources, outs, pieces):
        rows = source.shape[0] // number
        for piece in range(number):
            at = pl.ds(piece * rows, rows)
            copies.append(
                pltpu.make_async_copy(source.at[at], out.at[at], sems.at[len(copies)])
            )
    for copy in copies:
        copy.start()
    for copy in copies:
        copy.wait()


def fetch(arrays, pieces, after):
    return pl.pallas_call(
        functools.partial(fetch_kernel, pieces),
        out_shape=tuple(shape(array.shape, array.dtype) for array in arrays),
        in_specs=[pl.BlockSpec(memory_space=pl.ANY)] * (len(arrays) + 1),
        out_specs=(VMEM,) * len(arrays),
        scratch_shapes=[pltpu.SemaphoreType.DMA((sum(pieces),))],
        compiler_params=params(4),
        cost_estimate=cost(0, sum(array.size * 4 for array in arrays)),
        name="fetch",
    )(*[in_hbm(array) for array in arrays], after)


def gather_kernel(after, *refs):
    blocks, out = refs[:-1], refs[-1]
    capacity = blocks[0].shape[0]
    for at, block in enumerate(blocks):
        out[at * capacity : (at + 1) * capacity, :] = block[...]


def up_kernel(w_up, tokens, hidden):
    tile = 256 if hidden.shape[1] % 256 == 0 else LANES
    for low in range(0, hidden.shape[1], tile):
        cols = slice(low, low + tile)
        raised = dot(tokens[...], w_up[:, cols])
        hidden[:, cols] = (raised * jax.nn.sigmoid(raised)).astype(BF16)


def down_kernel(start, w_down, *refs):
    hiddens, outs = refs[:-PAIR], refs[-PAIR:]
    hidden = jnp.concatenate([block[...] for block in hiddens], 0)
    rows, width = outs[0].shape
    tile = 256
    for low in range(0, width, tile):
        result = dot(hidden, w_down[:, start + low : start + low + tile]).astype(BF16)
        for at, out in enumerate(outs):
            out[:, low : low + tile] = result[at * rows : (at + 1) * rows]


def join_kernel(*refs):
    parts, outs = refs[:-EXPERTS], refs[-EXPERTS:]
    capacity = outs[0].shape[0]
    for slot, out in enumerate(outs):
        at = slice(slot * capacity, (slot + 1) * capacity)
        total = parts[0][at, :].astype(F32)
        for part in parts[1:]:
            total = total + part[at, :].astype(F32)
        out[...] = total.astype(BF16)


def finish_kernel(start, second, weighting, *refs):
    blocks, out = refs[:-1], refs[-1]
    rows = jnp.concatenate([block[...] for block in blocks], 0)
    high, low = split(weighting[...])
    cols = slice(start, start + out.shape[1])
    out[...] = (second[:, cols] + (dot(high, rows) + dot(low, rows))).astype(BF16)


def exchange(value, axis, mask, later_only=False):
    count = lax.axis_size(axis)
    pairs = [(at, at ^ mask) for at in range(count) if not later_only or at < at ^ mask]
    return lax.ppermute(value, axis, pairs)


def handed_on(value, axis, steps):
    count = lax.axis_size(axis)
    return lax.ppermute(value, axis, [(at, at + steps) for at in range(count - steps)])


def shifted(value, axis, steps):
    count = lax.axis_size(axis)
    return lax.ppermute(value, axis, [(at, (at + steps) % count) for at in range(count)])


def head_weights(w_kv, shard_count, shard_index):
    if w_kv.shape[1] == HD and shard_count == 2 * KVH:
        return w_kv, exchange(w_kv, "ctx", KVH), shard_index // KVH
    whole = lax.all_gather(w_kv, "ctx", axis=1, tiled=True)
    head = shard_index % KVH
    return (
        lax.dynamic_slice_in_dim(whole, head * HD, HD, 1),
        lax.dynamic_slice_in_dim(whole, (KVH + head) * HD, HD, 1),
        jnp.zeros_like(shard_index),
    )


def on_device(
    acts,
    norm_gains,
    w_kv,
    dt_in,
    dt_out,
    dt_bias,
    decay_rate,
    w_bc,
    skip_gain,
    w_router,
    routes,
    w_up,
    w_down,
):
    shard_count = lax.axis_size("ctx")
    me = lax.axis_index("ctx")
    tokens = acts[0]
    rows, width = tokens.shape
    gains = norm_gains.transpose(1, 0, 2)
    parts = shard_count // EXPERTS
    group_rows = KVH * rows
    state = w_bc.shape[2] // 2
    chunks = rows // EIGHT
    capacity = rows * routes.shape[2] // EXPERTS

    near_tokens = exchange(tokens, "ctx", 2)
    w_own, w_other, key_at = head_weights(w_kv[0], shard_count, me)
    beside = exchange(tokens, "ctx", 1)
    far_tokens = exchange(near_tokens, "ctx", 1)
    place = jnp.stack([me, key_at, me // parts]).astype(jnp.int32)
    near_normed = pl.pallas_call(
        norm_kernel,
        out_shape=shape((2, rows, width), BF16),
        in_specs=[VMEM] * 3,
        out_specs=VMEM,
        compiler_params=params(16),
        cost_estimate=cost(16 * rows * width, 8 * rows * width),
        name="norm",
    )(in_hbm(gains), in_hbm(tokens), beside)
    queries, kv = pl.pallas_call(
        project_kernel,
        out_shape=(
            shape((KVH, GROUP * rows, HD), BF16),
            shape((2, group_rows, HD), BF16),
        ),
        in_specs=[SMEM] + [VMEM] * 6,
        out_specs=(VMEM, VMEM),
        scratch_shapes=[
            pltpu.VMEM((2, rows, width), BF16),
            pltpu.VMEM((width, 2 * HD), BF16),
        ],
        compiler_params=params(24),
        cost_estimate=cost(4 * group_rows * width * HD, 8 * group_rows * width),
        name="project",
    )(place, in_hbm(gains), near_normed, in_hbm(w_own), w_other, near_tokens, far_tokens)
    turns = shard_count // KVH
    pasts = [exchange(kv, "ctx", turn * KVH, later_only=True) for turn in range(1, turns)]
    small = [dt_in[0], dt_out[0], w_bc[0].T, tokens, w_router[0].T]
    in_one, in_two, in_bct, in_tokens, in_router = fetch(small, (2, 2, 1, 2, 1), kv)
    scored = GROUP * rows * group_rows * KVH
    tallies = (shape((KVH, GROUP * rows, LANES), F32),) * 2 + (
        shape((KVH, GROUP * rows, HD), F32),
    )
    tally = pl.pallas_call(
        near_kernel,
        out_shape=tallies,
        in_specs=[SMEM, VMEM, VMEM],
        out_specs=(VMEM,) * 3,
        compiler_params=params(16),
        cost_estimate=cost(4 * scored * HD, 4 * group_rows * GROUP * HD * 4, scored),
        name="near",
    )(place, queries, kv)
    attended = [None] * KVH
    for slots in ((2, 3), (0, 1)):
        state_now = tally
        for turn, past in enumerate(pasts, 1):
            last = turn == turns - 1
            state_now = pl.pallas_call(
                functools.partial(far_kernel, turn, slots, last),
                out_shape=(shape((rows, GROUP * HD), BF16),) * len(slots) if last else tallies,
                in_specs=[SMEM] + [VMEM] * 5,
                out_specs=(VMEM,) * (len(slots) if last else 3),
                compiler_params=params(16),
                cost_estimate=cost(2 * scored * HD, 2 * group_rows * GROUP * HD * 4, scored // 2),
                name="far",
            )(place, queries, *state_now, past)
        for slot, block in zip(slots, state_now):
            attended[slot] = exchange(block, "ctx", slot) if slot else block

    base, keep, drive, chunk_state, chunk_keep, bc, coef, ends = pl.pallas_call(
        prepare_kernel,
        out_shape=(
            shape((rows, width), F32),
            shape((rows, width), F32),
            shape((rows, width), F32),
            shape((chunks * state, width), F32),
            shape((chunks, width), F32),
            shape((rows, 2 * state), F32),
            shape((rows, rows), F32),
            shape((state, width + LANES), BF16),
        ),
        in_specs=[SMEM] + [VMEM] * (8 + KVH),
        out_specs=(VMEM,) * 8,
        scratch_shapes=[
            pltpu.VMEM((rows, width), BF16),
            pltpu.VMEM((rows, width), F32),
            pltpu.VMEM((rows, width), BF16),
            pltpu.VMEM((rows, width), BF16),
        ],
        compiler_params=params(32),
        cost_estimate=cost(10 * rows * width * 256, 30 * rows * width, 3 * rows * width),
        name="prepare",
    )(
        place,
        in_tokens,
        in_hbm(gains),
        in_hbm(skip_gain),
        in_one,
        in_two,
        in_hbm(dt_bias),
        in_hbm(decay_rate),
        in_bct,
        *attended,
    )
    beside_ends = exchange(ends, "ctx", 1)
    chip_ends = pl.pallas_call(
        pair_kernel,
        out_shape=shape(ends.shape, BF16),
        in_specs=[SMEM, VMEM, VMEM],
        out_specs=VMEM,
        compiler_params=params(8),
        cost_estimate=cost(4 * ends.size, 8 * ends.size),
        name="pair",
    )(place, ends, beside_ends)
    earlier_ends = [handed_on(chip_ends, "ctx", steps) for steps in range(2, shard_count, 2)]
    before, faded = pl.pallas_call(
        within_kernel,
        out_shape=(shape((rows, width), F32), shape((rows, width), F32)),
        in_specs=[VMEM] * 4,
        out_specs=(VMEM, VMEM),
        compiler_params=params(16),
        cost_estimate=cost(40 * rows * width, 20 * rows * width),
        name="within",
    )(coef, base, keep, drive)
    second, weighting, *packed = pl.pallas_call(
        route_kernel,
        out_shape=(shape((rows, width), F32), shape((rows, EXPERTS * capacity), F32))
        + (shape((capacity, width), BF16),) * EXPERTS,
        in_specs=[SMEM] + [VMEM] * (9 + len(earlier_ends)),
        out_specs=(VMEM,) * (2 + EXPERTS),
        scratch_shapes=[
            pltpu.VMEM((chunks * state, width), BF16),
            pltpu.VMEM((chunks * state, width), BF16),
            pltpu.VMEM((rows, width), F32),
            pltpu.VMEM((rows, width), BF16),
        ],
        compiler_params=params(24),
        cost_estimate=cost(10 * rows * width * 256, 30 * rows * width),
        name="route",
    )(
        place,
        before,
        faded,
        chunk_state,
        chunk_keep,
        bc,
        in_hbm(gains),
        in_router,
        in_hbm(routes[0].T),
        beside_ends,
        *earlier_ends,
    )

    arrived = [packed[0]] + [
        exchange(packed[slot], "ctx", slot * parts) for slot in range(1, EXPERTS)
    ]
    raising, lowering = fetch([w_up[0], w_down[0]], (16, 16), packed[0])
    units = raising.shape[1]
    expert_rows = EXPERTS * capacity
    arrived = pl.pallas_call(
        gather_kernel,
        out_shape=shape((expert_rows, width), BF16),
        in_specs=[pl.BlockSpec(memory_space=pl.ANY)] + [VMEM] * EXPERTS,
        out_specs=VMEM,
        compiler_params=params(8),
        cost_estimate=cost(0, 4 * expert_rows * width),
        name="gather",
    )(raising, *arrived)
    hiddens = []
    for turn in range(parts):
        hiddens.append(
            pl.pallas_call(
                up_kernel,
                out_shape=shape((expert_rows, units), BF16),
                in_specs=[VMEM, VMEM],
                out_specs=VMEM,
                compiler_params=params(14),
                cost_estimate=cost(2 * expert_rows * width * units, 2 * width * units),
                name="up",
            )(raising, exchange(arrived, "ctx", turn) if turn else arrived)
        )
    chunk_width = width // CHUNKS
    results = []
    for chunk in range(CHUNKS):
        start = chunk * chunk_width
        part_out = []
        for turn in range(0, parts, PAIR):
            part_out += pl.pallas_call(
                functools.partial(down_kernel, start),
                out_shape=(shape((expert_rows, chunk_width), BF16),) * PAIR,
                in_specs=[VMEM] * (1 + PAIR),
                out_specs=(VMEM,) * PAIR,
                compiler_params=params(14),
                cost_estimate=cost(
                    2 * PAIR * expert_rows * chunk_width * units, 2 * chunk_width * units
                ),
                name="down",
            )(lowering, *hiddens[turn : turn + PAIR])
        sums = [part_out[0]] + [
            exchange(part_out[turn], "ctx", turn) for turn in range(1, parts)
        ]
        joined = pl.pallas_call(
            join_kernel,
            out_shape=(shape((capacity, chunk_width), BF16),) * EXPERTS,
            in_specs=[VMEM] * parts,
            out_specs=(VMEM,) * EXPERTS,
            compiler_params=params(8),
            cost_estimate=cost(
                4 * EXPERTS * capacity * chunk_width, 8 * EXPERTS * capacity * chunk_width
            ),
            name="join",
        )(*sums)
        returned = [joined[0]] + [
            exchange(joined[slot], "ctx", slot * parts) for slot in range(1, EXPERTS)
        ]
        finished = pl.pallas_call(
            functools.partial(finish_kernel, start),
            out_shape=shape((rows, chunk_width), BF16),
            in_specs=[VMEM] * (2 + EXPERTS),
            out_specs=VMEM,
            compiler_params=params(8),
            cost_estimate=cost(
                4 * rows * EXPERTS * capacity * chunk_width, 10 * rows * chunk_width
            ),
            name="finish",
        )(second, weighting, *returned)
        results.append(shifted(finished, "segment", 1))
    return jnp.concatenate(results, 1)[None]


def solution(mesh):
    in_specs = (
        P("segment", "ctx", None),
        P("segment", None, None),
        P("segment", None, "ctx"),
        P("segment", None, None),
        P("segment", None, None),
        P("segment", None),
        P("segment", None),
        P("segment", None, None),
        P("segment", None),
        P("segment", None, None),
        P("segment", "ctx", None),
        P("segment", None, "ctx"),
        P("segment", "ctx", None),
    )
    out_specs = P("segment", "ctx", None)
    return jax.shard_map(
        on_device, mesh=mesh, in_specs=in_specs, out_specs=out_specs, check_vma=False
    )
```

time: 281 us -> 118 us (0.42)
  waiting for transfers between devices: 114 us -> 33.5 us
  matrix products: 56.2 us -> 0 us
  blocking collectives: 47.9 us -> 0 us
  Pallas kernels: 0 us -> 47.3 us
  starting transfers between devices: 5.96 us -> 36.2 us
  other arithmetic: 24.3 us -> 0.9 us
  local copies, waits for them, and re-layouts: 17 us -> 0 us
  between operations: 13.6 us -> 0.24 us
    all_gather x3 -> x0, waiting for transfers between devices: 76.2 us -> none  [the longest x1 40.1 us: on_device(): lax.all_gather(w_kv[0], 'ctx', axis=1, tiled=True)]
    dot_general x27 -> x0, matrix products: 56.2 us -> none  [the longest x1 11.9 us: on_device(): jnp.dot(flat_rows, up_local, preferred_element_type=jnp.float32)]
    pallas_call x0 -> x20, Pallas kernels: none -> 47.3 us  [the longest x2 11.1 us: fetch(): pl.pallas_call(functools.partial(fetch_kernel, pieces), out_shape=tuple((...]
    ppermute x1 -> x26, starting transfers between devices: 1.54 us -> 36.2 us  [the longest x21 22.7 us: exchange(): return lax.ppermute(value, axis, pairs)]
    all_to_all x1 -> x0, blocking collectives: 30 us -> none  [on_device(): lax.all_to_all(outgoing, 'ctx', split_axis=0, concat_axis=0, tiled=True)]
    all_to_all x1 -> x0, waiting for transfers between devices: 26 us -> none  [on_device(): lax.all_to_all(part_out, 'ctx', split_axis=0, concat_axis=0, tiled=True)]
    ppermute x1 -> x26, waiting for transfers between devices: 11 us -> 33.5 us  [the longest x21 25 us: exchange(): return lax.ppermute(value, axis, pairs)]
    all_gather x2 -> x0, blocking collectives: 17.9 us -> none  [entering(): lax.all_gather(a.astype(kind), axis)]
  transfers between devices with their start and end apart: 5 -> 26, of which waited for: 5 -> 15; matrix products, arithmetic and copies ran while one was open for 4% -> 0% of each run, Pallas kernels for 0% -> 22%
where the time goes in v1:
time: 118 us
  Pallas kernels  47.3 us (40%)
  starting transfers between devices  36.2 us (31%)
  waiting for transfers between devices  33.5 us (28%)
    ppermute x21, waiting for transfers between devices, exchange(): return lax.ppermute(value, axis, pairs)  25 us
    ppermute x21, starting transfers between devices, exchange(): return lax.ppermute(value, axis, pairs)  22.7 us
    pallas_call x2, Pallas kernels, fetch(): pl.pallas_call(functools.partial(fetch_kernel, pieces), out_shape=tuple((...  11.1 us
    ppermute x3, starting transfers between devices, handed_on(): lax.ppermute(value, axis, [(at, at + steps) for at in range(count - steps)])  10.2 us
    ppermute x2, waiting for transfers between devices, shifted(): lax.ppermute(value, axis, [(at, (at + steps) % count) for at in range(cou...  8.36 us
    pallas_call x2, Pallas kernels, on_device(): pl.pallas_call(up_kernel, out_shape=shape((expert_rows, units), BF16), in...  7.93 us
    pallas_call x2, Pallas kernels, on_device(): pl.pallas_call(functools.partial(down_kernel, start), out_shape=(shape((e...  7.88 us
    pallas_call x1, Pallas kernels, on_device(): pl.pallas_call(prepare_kernel, out_shape=(shape((rows, width), F32), shap...  5.61 us
  transfers between devices with their start and end apart: 26, of which 15 were waited for; matrix products, arithmetic and copies ran while one was open for 0% of the time, Pallas kernels for 22%

profile of v1, /device:TPU:0, one launch (start us, length us, event | category | flops | bytes accessed | tf_op | source)
XLA Modules:
  0.0 118.1 jit_solution(12477416270243875939)
XLA Ops:
  0.0 2.9 %collective-permute-start.2 = (bf16[128,2048]{1,0:T(8,128)(2,1)}, bf16[128,2048]{1,0:T(8,128)(2,1)S(1)}, u32[]{:S(2)}, u32[]{:S(2)}) collective-permute-start(bf16[128,2048]{1,0:T(8,128)(2,1)} %bitcast.23), channel_id=1, source_target_pairs={{0,2},{1,3},{2,0},{3,1},{4,6},{5,7},{6,4},{7,5},{8,10},{9,11},{10,... | collective-permute-start | bytes 1572872 | tf_op jit(solution)/shard_map/ppermute | solution.py:419
  2.9 0.0 collective-permute-start
  2.9 1.5 %collective-permute-start.1 = (bf16[2048,128]{1,0:T(8,128)(2,1)}, bf16[2048,128]{1,0:T(8,128)(2,1)S(1)}, u32[]{:S(2)}, u32[]{:S(2)}) collective-permute-start(bf16[2048,128]{1,0:T(8,128)(2,1)} %bitcast.27), channel_id=1, source_target_pairs={{0,4},{1,5},{2,6},{3,7},{4,0},{5,1},{6,2},{7,3},{8,12},{9,13},{10,... | collective-permute-start | bytes 1572872 | tf_op jit(solution)/shard_map/ppermute | solution.py:419
  4.5 10.6 %collective-permute-done.2.refs_0_ = bf16[128,2048]{1,0:T(8,128)(2,1)S(1)} collective-permute-done((bf16[128,2048]{1,0:T(8,128)(2,1)}, bf16[128,2048]{1,0:T(8,128)(2,1)S(1)}, u32[]{:S(2)}, u32[]{:S(2)}) %collective-permute-start.2) | collective-permute-done | bytes 524320 | tf_op jit(solution)/shard_map/ppermute | solution.py:419
  15.1 0.1 pad_add_fusion.place
  15.1 0.0 collective-permute-done.refs_1_
  15.2 1.7 %norm.1.near = bf16[2,128,2048]{2,1,0:T(8,128)(2,1)S(1)} custom-call(f32[3,1,2048]{2,1,0:T(1,128)} %bitcast.31, bf16[128,2048]{1,0:T(8,128)(2,1)} %bitcast.25, bf16[128,2048]{1,0:T(8,128)(2,1)S(1)} %collective-permute-done.refs_1_), custom_call_target="tpu_custom_call" | custom-call | flops 4194304 | bytes 2097152 | tf_op jit(solution)/shard_map/norm/pallas_call | solution.py:475
  16.9 0.6 collective-permute-done.1.w_other
  17.5 2.7 %project.1 = (bf16[4,512,128]{2,1,0:T(8,128)(2,1)S(1)}, bf16[2,512,128]{2,1,0:T(8,128)(2,1)S(1)}) custom-call(s32[3]{0:T(128)S(1)} %pad_add_fusion.place, f32[3,1,2048]{2,1,0:T(1,128)} %bitcast.32, bf16[2,128,2048]{2,1,0:T(8,128)(2,1)S(1)} %norm.1.near, bf16[2048,128]{1,0:T(8,128)(2,1)} %bitcast.28, bf16[2048,128]{1,0:T(8,128)(2,1)S(1)} %collective-permute-done.1.w_other, ...), custom_call_target="tpu_custom_call" | custom-call | flops 536870912 | bytes 8388608 | tf_op jit(solution)/shard_map/project/pallas_call | solution.py:484
  20.2 3.4 %collective-permute-start.4 = (bf16[2,512,128]{2,1,0:T(8,128)(2,1)S(1)}, bf16[2,512,128]{2,1,0:T(8,128)(2,1)S(1)}, u32[]{:S(2)}, u32[]{:S(2)}) collective-permute-start(bf16[2,512,128]{2,1,0:T(8,128)(2,1)S(1)} %get-tuple-element.49.refs_5_.kv), channel_id=1, source_target_pairs={{0,4},{1,5},{2,6},{3,7},{8,12},{9,13},{10,14},{11,15},{16,20},{17,... | collective-permute-start | bytes 786440 | tf_op jit(solution)/shard_map/ppermute | solution.py:419
  23.6 2.5 %near.1 = (f32[4,512,128]{2,1,0:T(8,128)S(1)}, f32[4,512,128]{2,1,0:T(8,128)S(1)}, f32[4,512,128]{2,1,0:T(8,128)S(1)}) custom-call(s32[3]{0:T(128)S(1)} %pad_add_fusion.place, bf16[4,512,128]{2,1,0:T(8,128)(2,1)S(1)} %get-tuple-element.54.q, bf16[2,512,128]{2,1,0:T(8,128)(2,1)S(1)} %get-tuple-element.49.refs_5_.kv), custom_call_target="tpu_custom_call" | custom-call | flops 536870912 | bytes 4194304 | tf_op jit(solution)/shard_map/near/pallas_call | solution.py:508
  26.1 3.3 %collective-permute-done.4.past = bf16[2,512,128]{2,1,0:T(8,128)(2,1)S(1)} collective-permute-done((bf16[2,512,128]{2,1,0:T(8,128)(2,1)S(1)}, bf16[2,512,128]{2,1,0:T(8,128)(2,1)S(1)}, u32[]{:S(2)}, u32[]{:S(2)}) %collective-permute-start.4) | collective-permute-done | bytes 262176 | tf_op jit(solution)/shard_map/ppermute | solution.py:419
  29.4 0.6 far.3
  30.1 1.6 %collective-permute-start.6 = (bf16[128,512]{1,0:T(8,128)(2,1)S(1)}, bf16[128,512]{1,0:T(8,128)(2,1)S(1)}, u32[]{:S(2)}, u32[]{:S(2)}) collective-permute-start(bf16[128,512]{1,0:T(8,128)(2,1)S(1)} %get-tuple-element.60), channel_id=1, source_target_pairs={{0,2},{1,3},{2,0},{3,1},{4,6},{5,7},{6,4},{7,5},{8,10},{9,11},{10,... | collective-permute-start | bytes 393224 | tf_op jit(solution)/shard_map/ppermute | solution.py:419
  31.7 0.0 collective-permute-start.7
  31.7 0.6 far.2
  32.3 0.7 collective-permute-start.5
  33.0 1.5 %fetch.2 = (bf16[2048,128]{1,0:T(8,128)(2,1)S(1)}, bf16[128,2048]{1,0:T(8,128)(2,1)S(1)}, bf16[32,2048]{1,0:T(8,128)(2,1)S(1)}, bf16[128,2048]{1,0:T(8,128)(2,1)S(1)}, bf16[4,2048]{1,0:T(4,128)(2,1)S(1)}) custom-call(bf16[2048,128]{1,0:T(8,128)(2,1)} %bitcast.29, bf16[128,2048]{1,0:T(8,128)(2,1)} %bitcast.30, bf16[32,2048]{1,0:T(8,128)(2,1)} %bitcast.35, ...), custom_call_target="tpu_custom_call" | custom-call | bytes 3440640 | tf_op jit(solution)/shard_map/fetch/pallas_call | solution.py:359
  34.5 1.1 collective-permute-done.6.refs_2_
  35.6 1.9 %collective-permute-done.7.refs_3_ = bf16[128,512]{1,0:T(8,128)(2,1)S(1)} collective-permute-done((bf16[128,512]{1,0:T(8,128)(2,1)S(1)}, bf16[128,512]{1,0:T(8,128)(2,1)S(1)}, u32[]{:S(2)}, u32[]{:S(2)}) %collective-permute-start.7) | collective-permute-done | bytes 131104 | tf_op jit(solution)/shard_map/ppermute | solution.py:419
  37.4 0.0 collective-permute-done.5.refs_1_
  37.4 5.6 %prepare.1 = (f32[128,2048]{1,0:T(8,128)S(1)}, f32[128,2048]{1,0:T(8,128)S(1)}, f32[128,2048]{1,0:T(8,128)S(1)}, f32[256,2048]{1,0:T(8,128)S(1)}, f32[16,2048]{1...) custom-call(s32[3]{0:T(128)S(1)} %pad_add_fusion.place, ...), custom_call_target="tpu_custom_call" | custom-call | flops 671088640 | bytes 7864320 | tf_op jit(solution)/shard_map/prepare/pallas_call | solution.py:534
  43.1 0.4 collective-permute-start.8
  43.4 1.0 collective-permute-done.8.other.beside
  44.4 0.6 pair.1
  45.0 6.4 %collective-permute-start.11 = (bf16[16,2176]{1,0:T(8,128)(2,1)S(1)}, bf16[16,2176]{1,0:T(8,128)(2,1)S(1)}, u32[]{:S(2)}, u32[]{:S(2)}) collective-permute-start(bf16[16,2176]{1,0:T(8,128)(2,1)S(1)} %pair.1), channel_id=1, source_target_pairs={{0,6},{1,7},{8,14},{9,15},{16,22},{17,23},{24,30},{25,31}} | collective-permute-start | bytes 208904 | tf_op jit(solution)/shard_map/ppermute | solution.py:424
  51.4 1.3 %collective-permute-start.10 = (bf16[16,2176]{1,0:T(8,128)(2,1)S(1)}, bf16[16,2176]{1,0:T(8,128)(2,1)S(1)}, u32[]{:S(2)}, u32[]{:S(2)}) collective-permute-start(bf16[16,2176]{1,0:T(8,128)(2,1)S(1)} %pair.1), channel_id=1, source_target_pairs={{0,4},{1,5},{2,6},{3,7},{8,12},{9,13},{10,14},{11,15},{16,20},{17,... | collective-permute-start | bytes 208904 | tf_op jit(solution)/shard_map/ppermute | solution.py:424
  52.7 2.5 %collective-permute-start.9 = (bf16[16,2176]{1,0:T(8,128)(2,1)S(1)}, bf16[16,2176]{1,0:T(8,128)(2,1)S(1)}, u32[]{:S(2)}, u32[]{:S(2)}) collective-permute-start(bf16[16,2176]{1,0:T(8,128)(2,1)S(1)} %pair.1), channel_id=1, source_target_pairs={{0,2},{1,3},{2,4},{3,5},{4,6},{5,7},{8,10},{9,11},{10,12},{11,13},... | collective-permute-start | bytes 208904 | tf_op jit(solution)/shard_map/ppermute | solution.py:424
  55.2 1.7 %within.1 = (f32[128,2048]{1,0:T(8,128)S(1)}, f32[128,2048]{1,0:T(8,128)S(1)}) custom-call(f32[128,128]{1,0:T(8,128)S(1)} %get-tuple-element.62.coef, f32[128,2048]{1,0:T(8,128)S(1)} %get-tuple-element.63.base, f32[128,2048]{1,0:T(8,128)S(1)} %get-tuple-element.64.keep, f32[128,2048]{1,0:T(8,128)S(1)} %get-tuple-element.65.drive), custom_call_target="tpu_custom_call" | custom-call | flops 10485760 | bytes 5242880 | tf_op jit(solution)/shard_map/within/pallas_call | solution.py:580
  57.0 0.0 collective-permute-done.10.refs_1_
  57.0 0.2 collective-permute-done.9.refs_0_
  57.1 3.3 %route.1 = (f32[128,2048]{1,0:T(8,128)S(1)}, f32[128,256]{1,0:T(8,128)S(1)}, bf16[64,2048]{1,0:T(8,128)(2,1)S(1)}, bf16[64,2048]{1,0:T(8,128)(2,1)S(1)}, bf16[64...) custom-call(s32[3]{0:T(128)S(1)} %pad_add_fusion.place, f32[128,2048]{1,0:T(8,128)S(1)} %get-tuple-element.66.before, ...), custom_call_target="tpu_custom_call" | custom-call | flops 671088640 | bytes 7864320 | tf_op jit(solution)/shard_map/route/pallas_call | solution.py:589
  60.5 2.4 %collective-permute-start.12 = (bf16[64,2048]{1,0:T(8,128)(2,1)S(1)}, bf16[64,2048]{1,0:T(8,128)(2,1)S(1)}, u32[]{:S(2)}, u32[]{:S(2)}) collective-permute-start(bf16[64,2048]{1,0:T(8,128)(2,1)S(1)} %get-tuple-element.78), channel_id=1, source_target_pairs={{0,2},{1,3},{2,0},{3,1},{4,6},{5,7},{6,4},{7,5},{8,10},{9,11},{10,... | collective-permute-start | bytes 786440 | tf_op jit(solution)/shard_map/ppermute | solution.py:419
  62.9 1.5 %collective-permute-start.14 = (bf16[64,2048]{1,0:T(8,128)(2,1)S(1)}, bf16[64,2048]{1,0:T(8,128)(2,1)S(1)}, u32[]{:S(2)}, u32[]{:S(2)}) collective-permute-start(bf16[64,2048]{1,0:T(8,128)(2,1)S(1)} %get-tuple-element.80), channel_id=1, source_target_pairs={{0,6},{1,7},{2,4},{3,5},{4,2},{5,3},{6,0},{7,1},{8,14},{9,15},{10,... | collective-permute-start | bytes 786440 | tf_op jit(solution)/shard_map/ppermute | solution.py:419
  64.5 9.6 %fetch.3 = (bf16[2048,3584]{1,0:T(8,128)(2,1)S(1)}, bf16[3584,2048]{1,0:T(8,128)(2,1)S(1)}) custom-call(bf16[2048,3584]{1,0:T(8,128)(2,1)} %bitcast.21, bf16[3584,2048]{1,0:T(8,128)(2,1)} %bitcast.22, bf16[64,2048]{1,0:T(8,128)(2,1)S(1)} %get-tuple-element.75.refs_2_.refs_0_), custom_call_target="tpu_custom_call" | custom-call | bytes 58720256 | tf_op jit(solution)/shard_map/fetch/pallas_call | solution.py:359
  74.1 1.3 %collective-permute-done.14.refs_3_ = bf16[64,2048]{1,0:T(8,128)(2,1)S(1)} collective-permute-done((bf16[64,2048]{1,0:T(8,128)(2,1)S(1)}, bf16[64,2048]{1,0:T(8,128)(2,1)S(1)}, u32[]{:S(2)}, u32[]{:S(2)}) %collective-permute-start.14) | collective-permute-done | bytes 262176 | tf_op jit(solution)/shard_map/ppermute | solution.py:419
  75.4 0.1 gather.1.tokens
  75.5 0.1 collective-permute-start.15
  75.6 4.0 %up.2.refs_0_ = bf16[256,3584]{1,0:T(8,128)(2,1)S(1)} custom-call(bf16[2048,3584]{1,0:T(8,128)(2,1)S(1)} %get-tuple-element.77.after.w_up, bf16[256,2048]{1,0:T(8,128)(2,1)S(1)} %gather.1.tokens), custom_call_target="tpu_custom_call" | custom-call | flops 3758096384 | bytes 14680064 | tf_op jit(solution)/shard_map/up/pallas_call | solution.py:636
  79.5 4.0 %up.3.refs_1_ = bf16[256,3584]{1,0:T(8,128)(2,1)S(1)} custom-call(bf16[2048,3584]{1,0:T(8,128)(2,1)S(1)} %get-tuple-element.77.after.w_up, bf16[256,2048]{1,0:T(8,128)(2,1)S(1)} %collective-permute-done.15.tokens), custom_call_target="tpu_custom_call" | custom-call | flops 3758096384 | bytes 14680064 | tf_op jit(solution)/shard_map/up/pallas_call | solution.py:636
  83.5 3.9 %down.3 = (bf16[256,1024]{1,0:T(8,128)(2,1)S(1)}, bf16[256,1024]{1,0:T(8,128)(2,1)S(1)}) custom-call(bf16[3584,2048]{1,0:T(8,128)(2,1)S(1)} %get-tuple-element.76.w_down, bf16[256,3584]{1,0:T(8,128)(2,1)S(1)} %up.2.refs_0_, bf16[256,3584]{1,0:T(8,128)(2,1)S(1)} %up.3.refs_1_), custom_call_target="tpu_custom_call" | custom-call | flops 3758096384 | bytes 7340032 | tf_op jit(solution)/shard_map/down/pallas_call | solution.py:652
  87.5 0.6 collective-permute-start.21
  88.0 3.9 %down.2 = (bf16[256,1024]{1,0:T(8,128)(2,1)S(1)}, bf16[256,1024]{1,0:T(8,128)(2,1)S(1)}) custom-call(bf16[3584,2048]{1,0:T(8,128)(2,1)S(1)} %get-tuple-element.76.w_down, bf16[256,3584]{1,0:T(8,128)(2,1)S(1)} %up.2.refs_0_, bf16[256,3584]{1,0:T(8,128)(2,1)S(1)} %up.3.refs_1_), custom_call_target="tpu_custom_call" | custom-call | flops 3758096384 | bytes 7340032 | tf_op jit(solution)/shard_map/down/pallas_call | solution.py:652
  92.0 0.1 collective-permute-start.16
  92.1 0.1 join.3
  92.2 0.8 collective-permute-start.22
  93.0 1.5 %collective-permute-start.23 = (bf16[64,1024]{1,0:T(8,128)(2,1)S(1)}, bf16[64,1024]{1,0:T(8,128)(2,1)S(1)}, u32[]{:S(2)}, u32[]{:S(2)}) collective-permute-start(bf16[64,1024]{1,0:T(8,128)(2,1)S(1)} %get-tuple-element.91), channel_id=1, source_target_pairs={{0,4},{1,5},{2,6},{3,7},{4,0},{5,1},{6,2},{7,3},{8,12},{9,13},{10,... | collective-permute-start | bytes 393224 | tf_op jit(solution)/shard_map/ppermute | solution.py:419
  94.5 1.3 %collective-permute-start.24 = (bf16[64,1024]{1,0:T(8,128)(2,1)S(1)}, bf16[64,1024]{1,0:T(8,128)(2,1)S(1)}, u32[]{:S(2)}, u32[]{:S(2)}) collective-permute-start(bf16[64,1024]{1,0:T(8,128)(2,1)S(1)} %get-tuple-element.92), channel_id=1, source_target_pairs={{0,6},{1,7},{2,4},{3,5},{4,2},{5,3},{6,0},{7,1},{8,14},{9,15},{10,... | collective-permute-start | bytes 393224 | tf_op jit(solution)/shard_map/ppermute | solution.py:419
  95.7 0.1 join.2
  95.9 0.8 collective-permute-start.17
  96.6 1.5 %collective-permute-start.18 = (bf16[64,1024]{1,0:T(8,128)(2,1)S(1)}, bf16[64,1024]{1,0:T(8,128)(2,1)S(1)}, u32[]{:S(2)}, u32[]{:S(2)}) collective-permute-start(bf16[64,1024]{1,0:T(8,128)(2,1)S(1)} %get-tuple-element.85), channel_id=1, source_target_pairs={{0,4},{1,5},{2,6},{3,7},{4,0},{5,1},{6,2},{7,3},{8,12},{9,13},{10,... | collective-permute-start | bytes 393224 | tf_op jit(solution)/shard_map/ppermute | solution.py:419
  98.2 0.4 collective-permute-done.22.refs_1_
  98.5 1.7 %collective-permute-start.19 = (bf16[64,1024]{1,0:T(8,128)(2,1)S(1)}, bf16[64,1024]{1,0:T(8,128)(2,1)S(1)}, u32[]{:S(2)}, u32[]{:S(2)}) collective-permute-start(bf16[64,1024]{1,0:T(8,128)(2,1)S(1)} %get-tuple-element.86), channel_id=1, source_target_pairs={{0,6},{1,7},{2,4},{3,5},{4,2},{5,3},{6,0},{7,1},{8,14},{9,15},{10,... | collective-permute-start | bytes 393224 | tf_op jit(solution)/shard_map/ppermute | solution.py:419
  100.2 1.2 %collective-permute-done.23.refs_2_ = bf16[64,1024]{1,0:T(8,128)(2,1)S(1)} collective-permute-done((bf16[64,1024]{1,0:T(8,128)(2,1)S(1)}, bf16[64,1024]{1,0:T(8,128)(2,1)S(1)}, u32[]{:S(2)}, u32[]{:S(2)}) %collective-permute-start.23) | collective-permute-done | bytes 131104 | tf_op jit(solution)/shard_map/ppermute | solution.py:419
  101.4 0.4 collective-permute-done.24.refs_3_
  101.8 0.3 finish.3
  102.1 1.6 %collective-permute-start.25 = (bf16[128,1024]{1,0:T(8,128)(2,1)S(1)}, bf16[128,1024]{1,0:T(8,128)(2,1)S(1)}, u32[]{:S(2)}, u32[]{:S(2)}) collective-permute-start(bf16[128,1024]{1,0:T(8,128)(2,1)S(1)} %finish.3), channel_id=1, source_target_pairs={{0,8},{8,16},{16,24},{24,0},{1,9},{9,17},{17,25},{25,1},{2,10},{10... | collective-permute-start | bytes 786440 | tf_op jit(solution)/shard_map/ppermute | solution.py:429
  103.7 0.5 collective-permute-done.17.refs_1_
  104.2 2.8 %collective-permute-done.18.refs_2_ = bf16[64,1024]{1,0:T(8,128)(2,1)S(1)} collective-permute-done((bf16[64,1024]{1,0:T(8,128)(2,1)S(1)}, bf16[64,1024]{1,0:T(8,128)(2,1)S(1)}, u32[]{:S(2)}, u32[]{:S(2)}) %collective-permute-start.18) | collective-permute-done | bytes 131104 | tf_op jit(solution)/shard_map/ppermute | solution.py:419
  107.0 0.3 finish.2
  107.3 1.6 %collective-permute-start.20 = (bf16[128,1024]{1,0:T(8,128)(2,1)S(1)}, bf16[128,1024]{1,0:T(8,128)(2,1)S(1)}, u32[]{:S(2)}, u32[]{:S(2)}) collective-permute-start(bf16[128,1024]{1,0:T(8,128)(2,1)S(1)} %finish.2), channel_id=1, source_target_pairs={{0,8},{8,16},{16,24},{24,0},{1,9},{9,17},{17,25},{25,1},{2,10},{10... | collective-permute-start | bytes 786440 | tf_op jit(solution)/shard_map/ppermute | solution.py:429
  108.9 1.8 %collective-permute-done.25 = bf16[128,1024]{1,0:T(8,128)(2,1)S(1)} collective-permute-done((bf16[128,1024]{1,0:T(8,128)(2,1)S(1)}, bf16[128,1024]{1,0:T(8,128)(2,1)S(1)}, u32[]{:S(2)}, u32[]{:S(2)}) %collective-permute-start.25) | collective-permute-done | bytes 262176 | tf_op jit(solution)/shard_map/ppermute | solution.py:429
  110.7 6.6 %collective-permute-done.20 = bf16[128,1024]{1,0:T(8,128)(2,1)S(1)} collective-permute-done((bf16[128,1024]{1,0:T(8,128)(2,1)S(1)}, bf16[128,1024]{1,0:T(8,128)(2,1)S(1)}, u32[]{:S(2)}, u32[]{:S(2)}) %collective-permute-start.20) | collective-permute-done | bytes 262176 | tf_op jit(solution)/shard_map/ppermute | solution.py:429
  117.3 0.8 maximum_bitcast_fusion
  (10 shorter events, 0.0 us)
Async XLA Ops:
  0.0 15.1 %collective-permute-start.2 = (bf16[128,2048]{1,0:T(8,128)(2,1)}, bf16[128,2048]{1,0:T(8,128)(2,1)S(1)}, u32[]{:S(2)}, u32[]{:S(2)}) collective-permute-start(bf16[128,2048]{1,0:T(8,128)(2,1)} %bitcast.23), channel_id=1, source_target_pairs={{0,2},{1,3},{2,0},{3,1},{4,6},{5,7},{6,4},{7,5},{8,10},{9,11},{10,... | collective-permute-start | bytes 1572872 | tf_op jit(solution)/shard_map/ppermute | solution.py:419
  2.9 12.2 %collective-permute-start = (bf16[128,2048]{1,0:T(8,128)(2,1)}, bf16[128,2048]{1,0:T(8,128)(2,1)S(1)}, u32[]{:S(2)}, u32[]{:S(2)}) collective-permute-start(bf16[128,2048]{1,0:T(8,128)(2,1)} %bitcast.24), channel_id=1, source_target_pairs={{0,1},{1,0},{2,3},{3,2},{4,5},{5,4},{6,7},{7,6},{8,9},{9,8},{10,11... | collective-permute-start | bytes 1572872 | tf_op jit(solution)/shard_map/ppermute | solution.py:419
  2.9 14.5 %collective-permute-start.1 = (bf16[2048,128]{1,0:T(8,128)(2,1)}, bf16[2048,128]{1,0:T(8,128)(2,1)S(1)}, u32[]{:S(2)}, u32[]{:S(2)}) collective-permute-start(bf16[2048,128]{1,0:T(8,128)(2,1)} %bitcast.27), channel_id=1, source_target_pairs={{0,4},{1,5},{2,6},{3,7},{4,0},{5,1},{6,2},{7,3},{8,12},{9,13},{10,... | collective-permute-start | bytes 1572872 | tf_op jit(solution)/shard_map/ppermute | solution.py:419
  15.1 2.4 %collective-permute-start.3 = (bf16[128,2048]{1,0:T(8,128)(2,1)S(1)}, bf16[128,2048]{1,0:T(8,128)(2,1)S(1)}, u32[]{:S(2)}, u32[]{:S(2)}) collective-permute-start(bf16[128,2048]{1,0:T(8,128)(2,1)S(1)} %collective-permute-done.2.refs_0_), channel_id=1, source_target_pairs={{0,1},{1,0},{2,3},{3,2},{4,5},{5,4},{6,7},{7,6},{8,9},{9,8},{10,11... | collective-permute-start | bytes 1572872 | tf_op jit(solution)/shard_map/ppermute | solution.py:419
  20.2 9.3 %collective-permute-start.4 = (bf16[2,512,128]{2,1,0:T(8,128)(2,1)S(1)}, bf16[2,512,128]{2,1,0:T(8,128)(2,1)S(1)}, u32[]{:S(2)}, u32[]{:S(2)}) collective-permute-start(bf16[2,512,128]{2,1,0:T(8,128)(2,1)S(1)} %get-tuple-element.49.refs_5_.kv), channel_id=1, source_target_pairs={{0,4},{1,5},{2,6},{3,7},{8,12},{9,13},{10,14},{11,15},{16,20},{17,... | collective-permute-start | bytes 786440 | tf_op jit(solution)/shard_map/ppermute | solution.py:419
  30.1 5.5 %collective-permute-start.6 = (bf16[128,512]{1,0:T(8,128)(2,1)S(1)}, bf16[128,512]{1,0:T(8,128)(2,1)S(1)}, u32[]{:S(2)}, u32[]{:S(2)}) collective-permute-start(bf16[128,512]{1,0:T(8,128)(2,1)S(1)} %get-tuple-element.60), channel_id=1, source_target_pairs={{0,2},{1,3},{2,0},{3,1},{4,6},{5,7},{6,4},{7,5},{8,10},{9,11},{10,... | collective-permute-start | bytes 393224 | tf_op jit(solution)/shard_map/ppermute | solution.py:419
  31.7 5.8 %collective-permute-start.7 = (bf16[128,512]{1,0:T(8,128)(2,1)S(1)}, bf16[128,512]{1,0:T(8,128)(2,1)S(1)}, u32[]{:S(2)}, u32[]{:S(2)}) collective-permute-start(bf16[128,512]{1,0:T(8,128)(2,1)S(1)} %get-tuple-element.61), channel_id=1, source_target_pairs={{0,3},{1,2},{2,1},{3,0},{4,7},{5,6},{6,5},{7,4},{8,11},{9,10},{10,... | collective-permute-start | bytes 393224 | tf_op jit(solution)/shard_map/ppermute | solution.py:419
  32.3 5.1 %collective-permute-start.5 = (bf16[128,512]{1,0:T(8,128)(2,1)S(1)}, bf16[128,512]{1,0:T(8,128)(2,1)S(1)}, u32[]{:S(2)}, u32[]{:S(2)}) collective-permute-start(bf16[128,512]{1,0:T(8,128)(2,1)S(1)} %get-tuple-element.59), channel_id=1, source_target_pairs={{0,1},{1,0},{2,3},{3,2},{4,5},{5,4},{6,7},{7,6},{8,9},{9,8},{10,11... | collective-permute-start | bytes 393224 | tf_op jit(solution)/shard_map/ppermute | solution.py:419
  43.1 1.3 %collective-permute-start.8 = (bf16[16,2176]{1,0:T(8,128)(2,1)S(1)}, bf16[16,2176]{1,0:T(8,128)(2,1)S(1)}, u32[]{:S(2)}, u32[]{:S(2)}) collective-permute-start(bf16[16,2176]{1,0:T(8,128)(2,1)S(1)} %get-tuple-element.72.own), channel_id=1, source_target_pairs={{0,1},{1,0},{2,3},{3,2},{4,5},{5,4},{6,7},{7,6},{8,9},{9,8},{10,11... | collective-permute-start | bytes 208904 | tf_op jit(solution)/shard_map/ppermute | solution.py:419
  45.0 12.0 %collective-permute-start.11 = (bf16[16,2176]{1,0:T(8,128)(2,1)S(1)}, bf16[16,2176]{1,0:T(8,128)(2,1)S(1)}, u32[]{:S(2)}, u32[]{:S(2)}) collective-permute-start(bf16[16,2176]{1,0:T(8,128)(2,1)S(1)} %pair.1), channel_id=1, source_target_pairs={{0,6},{1,7},{8,14},{9,15},{16,22},{17,23},{24,30},{25,31}} | collective-permute-start | bytes 208904 | tf_op jit(solution)/shard_map/ppermute | solution.py:424
  51.4 5.5 %collective-permute-start.10 = (bf16[16,2176]{1,0:T(8,128)(2,1)S(1)}, bf16[16,2176]{1,0:T(8,128)(2,1)S(1)}, u32[]{:S(2)}, u32[]{:S(2)}) collective-permute-start(bf16[16,2176]{1,0:T(8,128)(2,1)S(1)} %pair.1), channel_id=1, source_target_pairs={{0,4},{1,5},{2,6},{3,7},{8,12},{9,13},{10,14},{11,15},{16,20},{17,... | collective-permute-start | bytes 208904 | tf_op jit(solution)/shard_map/ppermute | solution.py:424
  52.7 4.4 %collective-permute-start.9 = (bf16[16,2176]{1,0:T(8,128)(2,1)S(1)}, bf16[16,2176]{1,0:T(8,128)(2,1)S(1)}, u32[]{:S(2)}, u32[]{:S(2)}) collective-permute-start(bf16[16,2176]{1,0:T(8,128)(2,1)S(1)} %pair.1), channel_id=1, source_target_pairs={{0,2},{1,3},{2,4},{3,5},{4,6},{5,7},{8,10},{9,11},{10,12},{11,13},... | collective-permute-start | bytes 208904 | tf_op jit(solution)/shard_map/ppermute | solution.py:424
  60.5 13.6 %collective-permute-start.12 = (bf16[64,2048]{1,0:T(8,128)(2,1)S(1)}, bf16[64,2048]{1,0:T(8,128)(2,1)S(1)}, u32[]{:S(2)}, u32[]{:S(2)}) collective-permute-start(bf16[64,2048]{1,0:T(8,128)(2,1)S(1)} %get-tuple-element.78), channel_id=1, source_target_pairs={{0,2},{1,3},{2,0},{3,1},{4,6},{5,7},{6,4},{7,5},{8,10},{9,11},{10,... | collective-permute-start | bytes 786440 | tf_op jit(solution)/shard_map/ppermute | solution.py:419
  62.9 11.2 %collective-permute-start.13 = (bf16[64,2048]{1,0:T(8,128)(2,1)S(1)}, bf16[64,2048]{1,0:T(8,128)(2,1)S(1)}, u32[]{:S(2)}, u32[]{:S(2)}) collective-permute-start(bf16[64,2048]{1,0:T(8,128)(2,1)S(1)} %get-tuple-element.79), channel_id=1, source_target_pairs={{0,4},{1,5},{2,6},{3,7},{4,0},{5,1},{6,2},{7,3},{8,12},{9,13},{10,... | collective-permute-start | bytes 786440 | tf_op jit(solution)/shard_map/ppermute | solution.py:419
  62.9 12.5 %collective-permute-start.14 = (bf16[64,2048]{1,0:T(8,128)(2,1)S(1)}, bf16[64,2048]{1,0:T(8,128)(2,1)S(1)}, u32[]{:S(2)}, u32[]{:S(2)}) collective-permute-start(bf16[64,2048]{1,0:T(8,128)(2,1)S(1)} %get-tuple-element.80), channel_id=1, source_target_pairs={{0,6},{1,7},{2,4},{3,5},{4,2},{5,3},{6,0},{7,1},{8,14},{9,15},{10,... | collective-permute-start | bytes 786440 | tf_op jit(solution)/shard_map/ppermute | solution.py:419
  75.5 4.1 %collective-permute-start.15 = (bf16[256,2048]{1,0:T(8,128)(2,1)S(1)}, bf16[256,2048]{1,0:T(8,128)(2,1)S(1)}, u32[]{:S(2)}, u32[]{:S(2)}) collective-permute-start(bf16[256,2048]{1,0:T(8,128)(2,1)S(1)} %gather.1.tokens), channel_id=1, source_target_pairs={{0,1},{1,0},{2,3},{3,2},{4,5},{5,4},{6,7},{7,6},{8,9},{9,8},{10,11... | collective-permute-start | bytes 3145736 | tf_op jit(solution)/shard_map/ppermute | solution.py:419
  87.5 4.6 %collective-permute-start.21 = (bf16[256,1024]{1,0:T(8,128)(2,1)S(1)}, bf16[256,1024]{1,0:T(8,128)(2,1)S(1)}, u32[]{:S(2)}, u32[]{:S(2)}) collective-permute-start(bf16[256,1024]{1,0:T(8,128)(2,1)S(1)} %get-tuple-element.88), channel_id=1, source_target_pairs={{0,1},{1,0},{2,3},{3,2},{4,5},{5,4},{6,7},{7,6},{8,9},{9,8},{10,11... | collective-permute-start | bytes 1572872 | tf_op jit(solution)/shard_map/ppermute | solution.py:419
  92.0 3.8 %collective-permute-start.16 = (bf16[256,1024]{1,0:T(8,128)(2,1)S(1)}, bf16[256,1024]{1,0:T(8,128)(2,1)S(1)}, u32[]{:S(2)}, u32[]{:S(2)}) collective-permute-start(bf16[256,1024]{1,0:T(8,128)(2,1)S(1)} %get-tuple-element.82), channel_id=1, source_target_pairs={{0,1},{1,0},{2,3},{3,2},{4,5},{5,4},{6,7},{7,6},{8,9},{9,8},{10,11... | collective-permute-start | bytes 1572872 | tf_op jit(solution)/shard_map/ppermute | solution.py:419
  92.2 6.4 %collective-permute-start.22 = (bf16[64,1024]{1,0:T(8,128)(2,1)S(1)}, bf16[64,1024]{1,0:T(8,128)(2,1)S(1)}, u32[]{:S(2)}, u32[]{:S(2)}) collective-permute-start(bf16[64,1024]{1,0:T(8,128)(2,1)S(1)} %get-tuple-element.90), channel_id=1, source_target_pairs={{0,2},{1,3},{2,0},{3,1},{4,6},{5,7},{6,4},{7,5},{8,10},{9,11},{10,... | collective-permute-start | bytes 393224 | tf_op jit(solution)/shard_map/ppermute | solution.py:419
  93.0 8.5 %collective-permute-start.23 = (bf16[64,1024]{1,0:T(8,128)(2,1)S(1)}, bf16[64,1024]{1,0:T(8,128)(2,1)S(1)}, u32[]{:S(2)}, u32[]{:S(2)}) collective-permute-start(bf16[64,1024]{1,0:T(8,128)(2,1)S(1)} %get-tuple-element.91), channel_id=1, source_target_pairs={{0,4},{1,5},{2,6},{3,7},{4,0},{5,1},{6,2},{7,3},{8,12},{9,13},{10,... | collective-permute-start | bytes 393224 | tf_op jit(solution)/shard_map/ppermute | solution.py:419
  94.5 7.3 %collective-permute-start.24 = (bf16[64,1024]{1,0:T(8,128)(2,1)S(1)}, bf16[64,1024]{1,0:T(8,128)(2,1)S(1)}, u32[]{:S(2)}, u32[]{:S(2)}) collective-permute-start(bf16[64,1024]{1,0:T(8,128)(2,1)S(1)} %get-tuple-element.92), channel_id=1, source_target_pairs={{0,6},{1,7},{2,4},{3,5},{4,2},{5,3},{6,0},{7,1},{8,14},{9,15},{10,... | collective-permute-start | bytes 393224 | tf_op jit(solution)/shard_map/ppermute | solution.py:419
  95.9 8.3 %collective-permute-start.17 = (bf16[64,1024]{1,0:T(8,128)(2,1)S(1)}, bf16[64,1024]{1,0:T(8,128)(2,1)S(1)}, u32[]{:S(2)}, u32[]{:S(2)}) collective-permute-start(bf16[64,1024]{1,0:T(8,128)(2,1)S(1)} %get-tuple-element.84), channel_id=1, source_target_pairs={{0,2},{1,3},{2,0},{3,1},{4,6},{5,7},{6,4},{7,5},{8,10},{9,11},{10,... | collective-permute-start | bytes 393224 | tf_op jit(solution)/shard_map/ppermute | solution.py:419
  96.6 10.3 %collective-permute-start.18 = (bf16[64,1024]{1,0:T(8,128)(2,1)S(1)}, bf16[64,1024]{1,0:T(8,128)(2,1)S(1)}, u32[]{:S(2)}, u32[]{:S(2)}) collective-permute-start(bf16[64,1024]{1,0:T(8,128)(2,1)S(1)} %get-tuple-element.85), channel_id=1, source_target_pairs={{0,4},{1,5},{2,6},{3,7},{4,0},{5,1},{6,2},{7,3},{8,12},{9,13},{10,... | collective-permute-start | bytes 393224 | tf_op jit(solution)/shard_map/ppermute | solution.py:419
  98.5 8.4 %collective-permute-start.19 = (bf16[64,1024]{1,0:T(8,128)(2,1)S(1)}, bf16[64,1024]{1,0:T(8,128)(2,1)S(1)}, u32[]{:S(2)}, u32[]{:S(2)}) collective-permute-start(bf16[64,1024]{1,0:T(8,128)(2,1)S(1)} %get-tuple-element.86), channel_id=1, source_target_pairs={{0,6},{1,7},{2,4},{3,5},{4,2},{5,3},{6,0},{7,1},{8,14},{9,15},{10,... | collective-permute-start | bytes 393224 | tf_op jit(solution)/shard_map/ppermute | solution.py:419
  102.1 8.6 %collective-permute-start.25 = (bf16[128,1024]{1,0:T(8,128)(2,1)S(1)}, bf16[128,1024]{1,0:T(8,128)(2,1)S(1)}, u32[]{:S(2)}, u32[]{:S(2)}) collective-permute-start(bf16[128,1024]{1,0:T(8,128)(2,1)S(1)} %finish.3), channel_id=1, source_target_pairs={{0,8},{8,16},{16,24},{24,0},{1,9},{9,17},{17,25},{25,1},{2,10},{10... | collective-permute-start | bytes 786440 | tf_op jit(solution)/shard_map/ppermute | solution.py:429
  107.3 10.0 %collective-permute-start.20 = (bf16[128,1024]{1,0:T(8,128)(2,1)S(1)}, bf16[128,1024]{1,0:T(8,128)(2,1)S(1)}, u32[]{:S(2)}, u32[]{:S(2)}) collective-permute-start(bf16[128,1024]{1,0:T(8,128)(2,1)S(1)} %finish.2), channel_id=1, source_target_pairs={{0,8},{8,16},{16,24},{24,0},{1,9},{9,17},{17,25},{25,1},{2,10},{10... | collective-permute-start | bytes 786440 | tf_op jit(solution)/shard_map/ppermute | solution.py:429

commit v2 on v1

--- a/solution.py
+++ b/solution.py
@@ -16,10 +16,12 @@
 STRIP = 16
 LANES = 128
 PAIR = 2
+BATCHES = ((0, 3), (1, 2))
 CHUNKS = 2
 F32 = jnp.float32
 BF16 = jnp.bfloat16
 VMEM = pl.BlockSpec(memory_space=pltpu.VMEM)
+ANY = pl.BlockSpec(memory_space=pl.ANY)
 SMEM = pl.BlockSpec(memory_space=pltpu.SMEM)
 
 
@@ -65,42 +67,59 @@
 def dot_split(a, b, dims=((1,), (0,))):
     a_high, a_low = a
     b_high, b_low = b
-    return dot(a_high, b_high, dims) + (dot(a_high, b_low, dims) + dot(a_low, b_high, dims))
+    count = a_high.shape[0]
+    both = dot(jnp.concatenate([a_high, a_low], 0), b_high, dims)
+    return both[:count] + (both[count:] + dot(a_high, b_low, dims))
 
 
 def iota(dims, axis):
     return lax.broadcasted_iota(jnp.int32, dims, axis)
 
 
-def norm_kernel(gains, *refs):
-    xs, out = refs[:-1], refs[-1]
-    rows = xs[0].shape[0]
-    for slot, x in enumerate(xs):
-
-        def body(at, slot=slot, x=x):
-            out[slot, at, :] = rms_norm(x[at, :].astype(F32), gains[0]).astype(BF16)
-
-        strips(rows, body)
-
-
-def project_kernel(place, gains, near, w_own, w_other, *refs):
-    xs, (q_out, kv_out, far, weights) = refs[:-4], refs[-4:]
-    rows, width = xs[0].shape
+def norm_into(out, x, gain):
+    def body(at):
+        out[at, :] = rms_norm(x[at, :].astype(F32), gain).astype(BF16)
+
+    strips(x.shape[0], body)
+
+
+def norm_kernel(place, gains, x, after, out):
+    norm_into(out, x, gains[0])
+
+
+def queries_into(q_out, slots, normed, head):
+    rows = normed.shape[0] // len(slots)
+    for at, slot in enumerate(slots):
+        for part in range(GROUP):
+            cols = pl.ds(pl.multiple_of((head * GROUP + part) * HD, HD), HD)
+            q_out[slot, pl.ds(part * rows, rows), :] = normed[at * rows : (at + 1) * rows, cols]
+
+
+def project_kernel(
+    place, gains, normed_own, beside, normed_near, w_own, w_other, q_out, kv_out, weights, normed
+):
+    rows = beside.shape[0]
     head = place[0] % KVH
     key_at = place[1]
     weights[:, pl.ds(pl.multiple_of(key_at * HD, HD), HD)] = w_own[...]
     weights[:, pl.ds(pl.multiple_of((1 - key_at) * HD, HD), HD)] = w_other[...]
-    norm_kernel(gains, *xs, far)
-    for half, normed in enumerate((near, far)):
-        count = normed.shape[0]
-        both = dot(normed[...].reshape(count * rows, width), weights[...]).astype(BF16)
-        here = pl.ds(half * count * rows, count * rows)
-        kv_out[0, here, :] = both[:, :HD]
-        kv_out[1, here, :] = both[:, HD:]
-        for slot in range(count):
-            for part in range(GROUP):
-                cols = pl.ds(pl.multiple_of((head * GROUP + part) * HD, HD), HD)
-                q_out[half * count + slot, pl.ds(part * rows, rows), :] = normed[slot, :, cols]
+    normed[:rows, :] = normed_own[...]
+    norm_into(normed.at[pl.ds(rows, rows)], beside, gains[0])
+    normed[2 * rows :, :] = normed_near[...]
+    both = dot(normed[...], weights[...]).astype(BF16)
+    kv_out[0, : 3 * rows, :] = both[:, :HD]
+    kv_out[1, : 3 * rows, :] = both[:, HD:]
+    queries_into(q_out, (0, 1, 2), normed, head)
+
+
+def project_last_kernel(place, normed, weights, q_in, kv_in, q_out, kv_out):
+    rows = normed.shape[0]
+    q_out[:3] = q_in[:3]
+    kv_out[:, : 3 * rows, :] = kv_in[:, : 3 * rows, :]
+    both = dot(normed[...], weights[...]).astype(BF16)
+    kv_out[0, 3 * rows :, :] = both[:, :HD]
+    kv_out[1, 3 * rows :, :] = both[:, HD:]
+    queries_into(q_out, (3,), normed, place[0] % KVH)
 
 
 def near_kernel(place, q, kv, largest_out, total_out, summed):
@@ -183,8 +202,8 @@
     strips(rows, normalize)
     low_rank = dot(mixed[...], dt_in[...]).astype(BF16)
     pre[...] = dot(low_rank, dt_out[...])
-    bc = dot(mixed[...], w_bct[...], ((1,), (1,)))
     bct = dot(w_bct[...], mixed[...], ((1,), (1,)))
+    bc = bct.T
     bc_out[...] = bc
     b_rows = bct[:state]
     coupling = dot_split(split(bc[:, state:]), split(b_rows))
@@ -279,21 +298,26 @@
 def route_kernel(
     place, before, faded, chunk_state, chunk_keep, bc, gains, router_t, routes_t, beside, *refs
 ):
-    ends, (second, weighting), packed = refs[:-10], refs[-10:-8], refs[-8:-4]
-    state_high, state_low, carried, expert_in = refs[-4:]
+    ends, (second, weighting), packed = refs[:-11], refs[-11:-9], refs[-9:-5]
+    state_high, state_low, carried, expert_in, stack = refs[-5:]
     rows, width = before.shape
     chunks = chunk_keep.shape[0]
     state = chunk_state.shape[0] // chunks
     me = place[0]
     own = place[2]
-    fades = [end[:, width:].astype(F32) for end in ends]
+    chip = me // 2
+    stack[0] = jnp.zeros_like(beside)
+    for slot, end in enumerate(ends, 1):
+        stack[slot] = end[...]
+    fades = [stack[chip ^ at, :, width:].astype(F32) for at in range(len(ends))]
     last_fade = beside[:, width:].astype(F32)
     second_core = lax.rem(me, 2) == 1
     for tile in range(width // LANES):
         cols = pl.ds(tile * LANES, LANES)
         total = jnp.zeros((state, LANES), F32)
-        for end, fade in zip(ends[::-1], fades[::-1]):
-            total = total * fade[tile : tile + 1] + end[:, cols].astype(F32)
+        for at, fade in enumerate(fades):
+            joined = total * fade[tile : tile + 1] + stack[chip ^ at, :, cols].astype(F32)
+            total = jnp.where(at < chip, joined, total)
         joined = total * last_fade[tile : tile + 1] + beside[:, cols].astype(F32)
         total = jnp.where(second_core, joined, total)
         for chunk in range(chunks):
@@ -327,14 +351,17 @@
     ranks = jnp.where(uses, ranks, -1.0).astype(jnp.int32)
     capacity = packed[0].shape[0]
     place_row = iota((capacity, rows), 0)
-    weights = []
+    weights, placings = [], []
     for slot in range(EXPERTS):
         mine = expert == (own ^ slot)
         rank = jnp.sum(jnp.where(mine, ranks, 0), 0, keepdims=True)
         gate = jnp.sum(jnp.where(mine, gates, 0.0), 0, keepdims=True)
         placing = place_row == rank
         weights.append(jnp.where(placing, gate, 0.0))
-        packed[slot][...] = dot(placing.astype(BF16), expert_in[...]).astype(BF16)
+        placings.append(placing.astype(BF16))
+    chosen = dot(jnp.concatenate(placings, 0), expert_in[...]).astype(BF16)
+    for slot in range(EXPERTS):
+        packed[slot][...] = chosen[slot * capacity : (slot + 1) * capacity]
     weighting[...] = jnp.concatenate(weights, 0).T
 
 
@@ -359,7 +386,7 @@
     return pl.pallas_call(
         functools.partial(fetch_kernel, pieces),
         out_shape=tuple(shape(array.shape, array.dtype) for array in arrays),
-        in_specs=[pl.BlockSpec(memory_space=pl.ANY)] * (len(arrays) + 1),
+        in_specs=[ANY] * (len(arrays) + 1),
         out_specs=(VMEM,) * len(arrays),
         scratch_shapes=[pltpu.SemaphoreType.DMA((sum(pieces),))],
         compiler_params=params(4),
@@ -375,34 +402,41 @@
         out[at * capacity : (at + 1) * capacity, :] = block[...]
 
 
-def up_kernel(w_up, tokens, hidden):
+def up_kernel(w_up, own, other, hidden):
+    tokens = jnp.concatenate([own[...], other[...]], 0)
     tile = 256 if hidden.shape[1] % 256 == 0 else LANES
     for low in range(0, hidden.shape[1], tile):
         cols = slice(low, low + tile)
-        raised = dot(tokens[...], w_up[:, cols])
+        raised = dot(tokens, w_up[:, cols])
         hidden[:, cols] = (raised * jax.nn.sigmoid(raised)).astype(BF16)
 
 
-def down_kernel(start, w_down, *refs):
-    hiddens, outs = refs[:-PAIR], refs[-PAIR:]
+def down_kernel(start, done, w_down, *refs):
+    outs = refs[-PAIR:]
+    earlier, hiddens = refs[: PAIR * done], refs[PAIR * done : -PAIR]
     hidden = jnp.concatenate([block[...] for block in hiddens], 0)
-    rows, width = outs[0].shape
+    rows = hiddens[0].shape[0] // PAIR
     tile = 256
-    for low in range(0, width, tile):
+    for at, block in enumerate(earlier):
+        outs[at % PAIR][at // PAIR * rows : (at // PAIR + 1) * rows, :] = block[...]
+    for low in range(0, outs[0].shape[1], tile):
         result = dot(hidden, w_down[:, start + low : start + low + tile]).astype(BF16)
-        for at, out in enumerate(outs):
-            out[:, low : low + tile] = result[at * rows : (at + 1) * rows]
+        for at in range(PAIR * len(hiddens)):
+            batch = done + at // PAIR
+            outs[at % PAIR][batch * rows : (batch + 1) * rows, low : low + tile] = result[
+                at * rows : (at + 1) * rows
+            ]
 
 
 def join_kernel(*refs):
     parts, outs = refs[:-EXPERTS], refs[-EXPERTS:]
     capacity = outs[0].shape[0]
-    for slot, out in enumerate(outs):
-        at = slice(slot * capacity, (slot + 1) * capacity)
+    for place, slot in enumerate(sum(BATCHES, ())):
+        at = slice(place * capacity, (place + 1) * capacity)
         total = parts[0][at, :].astype(F32)
         for part in parts[1:]:
             total = total + part[at, :].astype(F32)
-        out[...] = total.astype(BF16)
+        outs[slot][...] = total.astype(BF16)
 
 
 def finish_kernel(start, second, weighting, *refs):
@@ -413,15 +447,9 @@
     out[...] = (second[:, cols] + (dot(high, rows) + dot(low, rows))).astype(BF16)
 
 
-def exchange(value, axis, mask, later_only=False):
+def exchange(value, axis, mask):
     count = lax.axis_size(axis)
-    pairs = [(at, at ^ mask) for at in range(count) if not later_only or at < at ^ mask]
-    return lax.ppermute(value, axis, pairs)
-
-
-def handed_on(value, axis, steps):
-    count = lax.axis_size(axis)
-    return lax.ppermute(value, axis, [(at, at + steps) for at in range(count - steps)])
+    return lax.ppermute(value, axis, [(at, at ^ mask) for at in range(count)])
 
 
 def shifted(value, axis, steps):
@@ -470,35 +498,56 @@
     near_tokens = exchange(tokens, "ctx", 2)
     w_own, w_other, key_at = head_weights(w_kv[0], shard_count, me)
     beside = exchange(tokens, "ctx", 1)
-    far_tokens = exchange(near_tokens, "ctx", 1)
     place = jnp.stack([me, key_at, me // parts]).astype(jnp.int32)
-    near_normed = pl.pallas_call(
-        norm_kernel,
-        out_shape=shape((2, rows, width), BF16),
-        in_specs=[VMEM] * 3,
-        out_specs=VMEM,
-        compiler_params=params(16),
-        cost_estimate=cost(16 * rows * width, 8 * rows * width),
-        name="norm",
-    )(in_hbm(gains), in_hbm(tokens), beside)
+
+    def norm(block, after):
+        return pl.pallas_call(
+            norm_kernel,
+            out_shape=shape((rows, width), BF16),
+            in_specs=[SMEM, VMEM, VMEM, ANY],
+            out_specs=VMEM,
+            compiler_params=params(4),
+            cost_estimate=cost(8 * rows * width, 4 * rows * width),
+            name="norm",
+        )(place, in_hbm(gains), block, after)
+
+    normed_own = norm(in_hbm(tokens), in_hbm(tokens))
+    raising, lowering = fetch([w_up[0], w_down[0]], (16, 16), normed_own)
+    normed_near = norm(near_tokens, raising)
+    normed_far = exchange(normed_near, "ctx", 1)
+    projected = (
+        shape((KVH, GROUP * rows, HD), BF16),
+        shape((2, group_rows, HD), BF16),
+    )
+    queries, kv, weights = pl.pallas_call(
+        project_kernel,
+        out_shape=projected + (shape((width, 2 * HD), BF16),),
+        in_specs=[SMEM] + [VMEM] * 6,
+        out_specs=(VMEM,) * 3,
+        scratch_shapes=[pltpu.VMEM((3 * rows, width), BF16)],
+        compiler_params=params(12),
+        cost_estimate=cost(12 * rows * width * HD, 24 * rows * width),
+        name="project",
+    )(
+        place,
+        in_hbm(gains),
+        normed_own,
+        beside,
+        normed_near,
+        in_hbm(w_own),
+        w_other,
+    )
     queries, kv = pl.pallas_call(
-        project_kernel,
-        out_shape=(
-            shape((KVH, GROUP * rows, HD), BF16),
-            shape((2, group_rows, HD), BF16),
-        ),
-        in_specs=[SMEM] + [VMEM] * 6,
-        out_specs=(VMEM, VMEM),
-        scratch_shapes=[
-            pltpu.VMEM((2, rows, width), BF16),
-            pltpu.VMEM((width, 2 * HD), BF16),
-        ],
-        compiler_params=params(24),
-        cost_estimate=cost(4 * group_rows * width * HD, 8 * group_rows * width),
-        name="project",
-    )(place, in_hbm(gains), near_normed, in_hbm(w_own), w_other, near_tokens, far_tokens)
+        project_last_kernel,
+        out_shape=projected,
+        in_specs=[SMEM] + [VMEM] * 4,
+        out_specs=(VMEM,) * 2,
+        compiler_params=params(12),
+        cost_estimate=cost(4 * rows * width * HD, 8 * rows * width),
+        name="project_last",
+    )(place, normed_far, weights, queries, kv)
     turns = shard_count // KVH
-    pasts = [exchange(kv, "ctx", turn * KVH, later_only=True) for turn in range(1, turns)]
+    pasts = [exchange(kv, "ctx", turn * KVH) for turn in range(1, turns)]
     small = [dt_in[0], dt_out[0], w_bc[0].T, tokens, w_router[0].T]
     in_one, in_two, in_bct, in_tokens, in_router = fetch(small, (2, 2, 1, 2, 1), kv)
     scored = GROUP * rows * group_rows * KVH
@@ -551,7 +600,7 @@
             pltpu.VMEM((rows, width), BF16),
             pltpu.VMEM((rows, width), BF16),
         ],
-        compiler_params=params(32),
+        compiler_params=params(20),
         cost_estimate=cost(10 * rows * width * 256, 30 * rows * width, 3 * rows * width),
         name="prepare",
     )(
@@ -576,7 +625,7 @@
         cost_estimate=cost(4 * ends.size, 8 * ends.size),
         name="pair",
     )(place, ends, beside_ends)
-    earlier_ends = [handed_on(chip_ends, "ctx", steps) for steps in range(2, shard_count, 2)]
+    earlier_ends = [exchange(chip_ends, "ctx", mask) for mask in range(2, shard_count, 2)]
     before, faded = pl.pallas_call(
         within_kernel,
         out_shape=(shape((rows, width), F32), shape((rows, width), F32)),
@@ -597,8 +646,9 @@
             pltpu.VMEM((chunks * state, width), BF16),
             pltpu.VMEM((rows, width), F32),
             pltpu.VMEM((rows, width), BF16),
+            pltpu.VMEM((shard_count // 2, state, width + LANES), BF16),
         ],
-        compiler_params=params(24),
+        compiler_params=params(16),
         cost_estimate=cost(10 * rows * width * 256, 30 * rows * width),
         name="route",
     )(
@@ -618,48 +668,61 @@
     arrived = [packed[0]] + [
         exchange(packed[slot], "ctx", slot * parts) for slot in range(1, EXPERTS)
     ]
-    raising, lowering = fetch([w_up[0], w_down[0]], (16, 16), packed[0])
     units = raising.shape[1]
-    expert_rows = EXPERTS * capacity
-    arrived = pl.pallas_call(
-        gather_kernel,
-        out_shape=shape((expert_rows, width), BF16),
-        in_specs=[pl.BlockSpec(memory_space=pl.ANY)] + [VMEM] * EXPERTS,
-        out_specs=VMEM,
-        compiler_params=params(8),
-        cost_estimate=cost(0, 4 * expert_rows * width),
-        name="gather",
-    )(raising, *arrived)
-    hiddens = []
-    for turn in range(parts):
-        hiddens.append(
-            pl.pallas_call(
+    batch_rows = 2 * capacity
+    hiddens = [[] for _ in range(0, parts, PAIR)]
+    after = packed[0]
+    for batch in BATCHES:
+        tokens_here = pl.pallas_call(
+            gather_kernel,
+            out_shape=shape((batch_rows, width), BF16),
+            in_specs=[ANY] + [VMEM] * 2,
+            out_specs=VMEM,
+            compiler_params=params(4),
+            cost_estimate=cost(0, 4 * batch_rows * width),
+            name="gather",
+        )(after, *[arrived[slot] for slot in batch])
+        held = [tokens_here] + [
+            exchange(tokens_here, "ctx", turn) for turn in range(1, parts)
+        ]
+        for turn in range(0, parts, PAIR):
+            after = pl.pallas_call(
                 up_kernel,
-                out_shape=shape((expert_rows, units), BF16),
-                in_specs=[VMEM, VMEM],
+                out_shape=shape((PAIR * batch_rows, units), BF16),
+                in_specs=[VMEM] * (1 + PAIR),
                 out_specs=VMEM,
-                compiler_params=params(14),
-                cost_estimate=cost(2 * expert_rows * width * units, 2 * width * units),
+                compiler_params=params(12),
+                cost_estimate=cost(2 * PAIR * batch_rows * width, 2 * width),
                 name="up",
-            )(raising, exchange(arrived, "ctx", turn) if turn else arrived)
-        )
+            )(raising, *held[turn : turn + PAIR])
+            hiddens[turn // PAIR].append(after)
+
+    def lower(start, span, blocks, earlier=()):
+        done = len(earlier) // PAIR
+        out_rows = batch_rows * (done + len(blocks))
+        return pl.pallas_call(
+            functools.partial(down_kernel, start, done),
+            out_shape=(shape((out_rows, span), BF16),) * PAIR,
+            in_specs=[VMEM] * (1 + len(earlier) + len(blocks)),
+            out_specs=(VMEM,) * PAIR,
+            compiler_params=params(12),
+            cost_estimate=cost(
+                2 * PAIR * batch_rows * len(blocks) * span * units, 2 * span * units
+            ),
+            name="down",
+        )(lowering, *earlier, *blocks)
+
     chunk_width = width // CHUNKS
     results = []
     for chunk in range(CHUNKS):
         start = chunk * chunk_width
         part_out = []
-        for turn in range(0, parts, PAIR):
-            part_out += pl.pallas_call(
-                functools.partial(down_kernel, start),
-                out_shape=(shape((expert_rows, chunk_width), BF16),) * PAIR,
-                in_specs=[VMEM] * (1 + PAIR),
-                out_specs=(VMEM,) * PAIR,
-                compiler_params=params(14),
-                cost_estimate=cost(
-                    2 * PAIR * expert_rows * chunk_width * units, 2 * chunk_width * units
-                ),
-                name="down",
-            )(lowering, *hiddens[turn : turn + PAIR])
+        for first_batch, last_batch in hiddens:
+            if chunk == 0:
+                earlier = lower(start, chunk_width, [first_batch])
+                part_out += lower(start, chunk_width, [last_batch], earlier)
+            else:
+                part_out += lower(start, chunk_width, [first_batch, last_batch])
         sums = [part_out[0]] + [
             exchange(part_out[turn], "ctx", turn) for turn in range(1, parts)
         ]

time: 118 us -> 114 us (0.966)
  starting transfers between devices: 36.2 us -> 28.9 us
  Pallas kernels: 47.3 us -> 49.1 us
    ppermute x24 -> x25, starting transfers between devices: 33 us -> 25.7 us  [exchange(): return lax.ppermute(value, axis, [(at, at ^ mask) for at in range(count)])]
    pallas_call x7 -> x11, Pallas kernels: 20.2 us -> 21.7 us  [the longest x3 8.05 us: lower(): pl.pallas_call(functools.partial(down_kernel, start, done), out_shape=(sh...]
    ppermute x24 -> x25, waiting for transfers between devices: 25.1 us -> 26 us  [exchange(): return lax.ppermute(value, axis, [(at, at ^ mask) for at in range(count)])]
  transfers between devices with their start and end apart: 26 -> 27, of which waited for: 15 -> 19; matrix products, arithmetic and copies ran while one was open for 0% -> 0% of each run, Pallas kernels for 22% -> 26%
where the time goes in v2:
time: 114 us; the launch traced here: 113 us
  Pallas kernels  49.1 us (43%)
  waiting for transfers between devices  34.4 us (30%)
  starting transfers between devices  28.9 us (25%)
    ppermute x25, waiting for transfers between devices, exchange(): return lax.ppermute(value, axis, [(at, at ^ mask) for at in range(count)])  26 us
    ppermute x25, starting transfers between devices, exchange(): return lax.ppermute(value, axis, [(at, at ^ mask) for at in range(count)])  25.7 us
    pallas_call x2, Pallas kernels, fetch(): pl.pallas_call(functools.partial(fetch_kernel, pieces), out_shape=tuple((...  11.1 us
    ppermute x2, waiting for transfers between devices, shifted(): lax.ppermute(value, axis, [(at, (at + steps) % count) for at in range(cou...  8.33 us
    pallas_call x3, Pallas kernels, lower(): pl.pallas_call(functools.partial(down_kernel, start, done), out_shape=(sh...  8.05 us
    pallas_call x2, Pallas kernels, on_device(): pl.pallas_call(up_kernel, out_shape=shape((PAIR * batch_rows, units), BF1...  7.94 us
    pallas_call x1, Pallas kernels, on_device(): pl.pallas_call(prepare_kernel, out_shape=(shape((rows, width), F32), shap...  5.75 us
    pallas_call x1, Pallas kernels, on_device(): pl.pallas_call(route_kernel, out_shape=(shape((rows, width), F32), shape(...  3.51 us
  transfers between devices with their start and end apart: 27, of which 19 were waited for; matrix products, arithmetic and copies ran while one was open for 0% of the time, Pallas kernels for 26%

profile of v2, /device:TPU:0, one launch (start us, length us, event | category | flops | bytes accessed | tf_op | source)
XLA Modules:
  0.0 113.5 jit_solution(8643904976423889901)
XLA Ops:
  0.0 2.9 %collective-permute-start = (bf16[128,2048]{1,0:T(8,128)(2,1)}, bf16[128,2048]{1,0:T(8,128)(2,1)S(1)}, u32[]{:S(2)}, u32[]{:S(2)}) collective-permute-start(bf16[128,2048]{1,0:T(8,128)(2,1)} %bitcast.23), channel_id=1, source_target_pairs={{0,2},{1,3},{2,0},{3,1},{4,6},{5,7},{6,4},{7,5},{8,10},{9,11},{10,... | collective-permute-start | bytes 1572872 | tf_op jit(solution)/shard_map/ppermute | solution.py:452
  2.9 1.5 %collective-permute-start.3 = (bf16[2048,128]{1,0:T(8,128)(2,1)}, bf16[2048,128]{1,0:T(8,128)(2,1)S(1)}, u32[]{:S(2)}, u32[]{:S(2)}) collective-permute-start(bf16[2048,128]{1,0:T(8,128)(2,1)} %bitcast.28), channel_id=1, source_target_pairs={{0,4},{1,5},{2,6},{3,7},{4,0},{5,1},{6,2},{7,3},{8,12},{9,13},{10,... | collective-permute-start | bytes 1572872 | tf_op jit(solution)/shard_map/ppermute | solution.py:452
  4.5 1.4 %norm.2.refs_2_.normed_own = bf16[128,2048]{1,0:T(8,128)(2,1)S(1)} custom-call(s32[3]{0:T(128)S(1)} %pad_add_fusion.place, f32[3,1,2048]{2,1,0:T(1,128)} %bitcast.32, bf16[128,2048]{1,0:T(8,128)(2,1)} %bitcast.25, bf16[128,2048]{1,0:T(8,128)(2,1)} %bitcast.26), custom_call_target="tpu_custom_call" | custom-call | flops 2097152 | bytes 1048576 | tf_op jit(solution)/shard_map/norm/pallas_call | solution.py:504
  5.9 9.6 %fetch.2 = (bf16[2048,3584]{1,0:T(8,128)(2,1)S(1)}, bf16[3584,2048]{1,0:T(8,128)(2,1)S(1)}) custom-call(bf16[2048,3584]{1,0:T(8,128)(2,1)} %bitcast.21, bf16[3584,2048]{1,0:T(8,128)(2,1)} %bitcast.22, bf16[128,2048]{1,0:T(8,128)(2,1)S(1)} %norm.2.refs_2_.normed_own), custom_call_target="tpu_custom_call" | custom-call | bytes 58720256 | tf_op jit(solution)/shard_map/fetch/pallas_call | solution.py:386
  15.6 1.1 norm.3.normed_near
  16.7 0.3 collective-permute-start.1
  17.0 0.5 collective-permute-done.3.w_other
  17.5 2.2 %project.1 = (bf16[4,512,128]{2,1,0:T(8,128)(2,1)S(1)}, bf16[2,512,128]{2,1,0:T(8,128)(2,1)S(1)}, bf16[2048,256]{1,0:T(8,128)(2,1)S(1)}) custom-call(s32[3]{0:T(128)S(1)} %pad_add_fusion.place, f32[3,1,2048]{2,1,0:T(1,128)} %bitcast.34, bf16[128,2048]{1,0:T(8,128)(2,1)S(1)} %norm.2.refs_2_.normed_own, bf16[128,2048]{1,0:T(8,128)(2,1)S(1)} %collective-permute-done.2.beside, ...), custom_call_target="tpu_custom_call" | custom-call | flops 402653184 | bytes 6291456 | tf_op jit(solution)/shard_map/project/pallas_call | solution.py:522
  19.7 0.9 project_last.1
  20.6 1.6 %collective-permute-start.4 = (bf16[2,512,128]{2,1,0:T(8,128)(2,1)S(1)}, bf16[2,512,128]{2,1,0:T(8,128)(2,1)S(1)}, u32[]{:S(2)}, u32[]{:S(2)}) collective-permute-start(bf16[2,512,128]{2,1,0:T(8,128)(2,1)S(1)} %get-tuple-element.58.refs_5_.kv), channel_id=1, source_target_pairs={{0,4},{1,5},{2,6},{3,7},{4,0},{5,1},{6,2},{7,3},{8,12},{9,13},{10,... | collective-permute-start | bytes 786440 | tf_op jit(solution)/shard_map/ppermute | solution.py:452
  22.2 2.5 %near.1 = (f32[4,512,128]{2,1,0:T(8,128)S(1)}, f32[4,512,128]{2,1,0:T(8,128)S(1)}, f32[4,512,128]{2,1,0:T(8,128)S(1)}) custom-call(s32[3]{0:T(128)S(1)} %pad_add_fusion.place, bf16[4,512,128]{2,1,0:T(8,128)(2,1)S(1)} %get-tuple-element.63.q, bf16[2,512,128]{2,1,0:T(8,128)(2,1)S(1)} %get-tuple-element.58.refs_5_.kv), custom_call_target="tpu_custom_call" | custom-call | flops 536870912 | bytes 4194304 | tf_op jit(solution)/shard_map/near/pallas_call | solution.py:557
  24.8 3.9 %collective-permute-done.4.past = bf16[2,512,128]{2,1,0:T(8,128)(2,1)S(1)} collective-permute-done((bf16[2,512,128]{2,1,0:T(8,128)(2,1)S(1)}, bf16[2,512,128]{2,1,0:T(8,128)(2,1)S(1)}, u32[]{:S(2)}, u32[]{:S(2)}) %collective-permute-start.4) | collective-permute-done | bytes 262176 | tf_op jit(solution)/shard_map/ppermute | solution.py:452
  28.7 0.6 far.3
  29.3 1.3 %collective-permute-start.6 = (bf16[128,512]{1,0:T(8,128)(2,1)S(1)}, bf16[128,512]{1,0:T(8,128)(2,1)S(1)}, u32[]{:S(2)}, u32[]{:S(2)}) collective-permute-start(bf16[128,512]{1,0:T(8,128)(2,1)S(1)} %get-tuple-element.69), channel_id=1, source_target_pairs={{0,2},{1,3},{2,0},{3,1},{4,6},{5,7},{6,4},{7,5},{8,10},{9,11},{10,... | collective-permute-start | bytes 393224 | tf_op jit(solution)/shard_map/ppermute | solution.py:452
  30.6 0.6 far.2
  31.3 1.0 collective-permute-start.5
  32.3 1.5 %fetch.3 = (bf16[2048,128]{1,0:T(8,128)(2,1)S(1)}, bf16[128,2048]{1,0:T(8,128)(2,1)S(1)}, bf16[32,2048]{1,0:T(8,128)(2,1)S(1)}, bf16[128,2048]{1,0:T(8,128)(2,1)S(1)}, bf16[4,2048]{1,0:T(4,128)(2,1)S(1)}) custom-call(bf16[2048,128]{1,0:T(8,128)(2,1)} %bitcast.30, bf16[128,2048]{1,0:T(8,128)(2,1)} %bitcast.31, bf16[32,2048]{1,0:T(8,128)(2,1)} %bitcast.37, ...), custom_call_target="tpu_custom_call" | custom-call | bytes 3440640 | tf_op jit(solution)/shard_map/fetch/pallas_call | solution.py:386
  33.8 1.4 %collective-permute-done.6.refs_2_ = bf16[128,512]{1,0:T(8,128)(2,1)S(1)} collective-permute-done((bf16[128,512]{1,0:T(8,128)(2,1)S(1)}, bf16[128,512]{1,0:T(8,128)(2,1)S(1)}, u32[]{:S(2)}, u32[]{:S(2)}) %collective-permute-start.6) | collective-permute-done | bytes 131104 | tf_op jit(solution)/shard_map/ppermute | solution.py:452
  35.2 1.1 %collective-permute-done.7.refs_3_ = bf16[128,512]{1,0:T(8,128)(2,1)S(1)} collective-permute-done((bf16[128,512]{1,0:T(8,128)(2,1)S(1)}, bf16[128,512]{1,0:T(8,128)(2,1)S(1)}, u32[]{:S(2)}, u32[]{:S(2)}) %collective-permute-start.7) | collective-permute-done | bytes 131104 | tf_op jit(solution)/shard_map/ppermute | solution.py:452
  36.4 5.8 %prepare.1 = (f32[128,2048]{1,0:T(8,128)S(1)}, f32[128,2048]{1,0:T(8,128)S(1)}, f32[128,2048]{1,0:T(8,128)S(1)}, f32[256,2048]{1,0:T(8,128)S(1)}, f32[16,2048]{1...) custom-call(s32[3]{0:T(128)S(1)} %pad_add_fusion.place, ...), custom_call_target="tpu_custom_call" | custom-call | flops 671088640 | bytes 7864320 | tf_op jit(solution)/shard_map/prepare/pallas_call | solution.py:583
  42.1 0.7 collective-permute-start.8
  42.8 0.9 collective-permute-done.8.other.beside
  43.7 0.6 pair.1
  44.3 3.4 %collective-permute-start.11 = (bf16[16,2176]{1,0:T(8,128)(2,1)S(1)}, bf16[16,2176]{1,0:T(8,128)(2,1)S(1)}, u32[]{:S(2)}, u32[]{:S(2)}) collective-permute-start(bf16[16,2176]{1,0:T(8,128)(2,1)S(1)} %pair.1), channel_id=1, source_target_pairs={{0,6},{1,7},{2,4},{3,5},{4,2},{5,3},{6,0},{7,1},{8,14},{9,15},{10,... | collective-permute-start | bytes 208904 | tf_op jit(solution)/shard_map/ppermute | solution.py:452
  47.8 0.7 collective-permute-start.9
  48.4 1.7 %within.1 = (f32[128,2048]{1,0:T(8,128)S(1)}, f32[128,2048]{1,0:T(8,128)S(1)}) custom-call(f32[128,128]{1,0:T(8,128)S(1)} %get-tuple-element.71.coef, f32[128,2048]{1,0:T(8,128)S(1)} %get-tuple-element.72.base, f32[128,2048]{1,0:T(8,128)S(1)} %get-tuple-element.73.keep, f32[128,2048]{1,0:T(8,128)S(1)} %get-tuple-element.74.drive), custom_call_target="tpu_custom_call" | custom-call | flops 10485760 | bytes 5242880 | tf_op jit(solution)/shard_map/within/pallas_call | solution.py:629
  50.2 0.3 collective-permute-done.11.refs_2_
  50.4 1.6 %collective-permute-done.10.refs_1_ = bf16[16,2176]{1,0:T(8,128)(2,1)S(1)} collective-permute-done((bf16[16,2176]{1,0:T(8,128)(2,1)S(1)}, bf16[16,2176]{1,0:T(8,128)(2,1)S(1)}, u32[]{:S(2)}, u32[]{:S(2)}) %collective-permute-start.10) | collective-permute-done | bytes 69664 | tf_op jit(solution)/shard_map/ppermute | solution.py:452
  52.1 0.3 collective-permute-done.9.refs_0_
  52.4 3.5 %route.1 = (f32[128,2048]{1,0:T(8,128)S(1)}, f32[128,256]{1,0:T(8,128)S(1)}, bf16[64,2048]{1,0:T(8,128)(2,1)S(1)}, bf16[64,2048]{1,0:T(8,128)(2,1)S(1)}, bf16[64...) custom-call(s32[3]{0:T(128)S(1)} %pad_add_fusion.place, f32[128,2048]{1,0:T(8,128)S(1)} %get-tuple-element.75.before, ...), custom_call_target="tpu_custom_call" | custom-call | flops 671088640 | bytes 7864320 | tf_op jit(solution)/shard_map/route/pallas_call | solution.py:638
  55.9 1.9 %collective-permute-start.12 = (bf16[64,2048]{1,0:T(8,128)(2,1)S(1)}, bf16[64,2048]{1,0:T(8,128)(2,1)S(1)}, u32[]{:S(2)}, u32[]{:S(2)}) collective-permute-start(bf16[64,2048]{1,0:T(8,128)(2,1)S(1)} %get-tuple-element.86), channel_id=1, source_target_pairs={{0,6},{1,7},{2,4},{3,5},{4,2},{5,3},{6,0},{7,1},{8,14},{9,15},{10,... | collective-permute-start | bytes 786440 | tf_op jit(solution)/shard_map/ppermute | solution.py:452
  57.8 6.9 %collective-permute-done.12.refs_1_ = bf16[64,2048]{1,0:T(8,128)(2,1)S(1)} collective-permute-done((bf16[64,2048]{1,0:T(8,128)(2,1)S(1)}, bf16[64,2048]{1,0:T(8,128)(2,1)S(1)}, u32[]{:S(2)}, u32[]{:S(2)}) %collective-permute-start.12) | collective-permute-done | bytes 262176 | tf_op jit(solution)/shard_map/ppermute | solution.py:452
  64.8 1.3 %collective-permute-start.14 = (bf16[64,2048]{1,0:T(8,128)(2,1)S(1)}, bf16[64,2048]{1,0:T(8,128)(2,1)S(1)}, u32[]{:S(2)}, u32[]{:S(2)}) collective-permute-start(bf16[64,2048]{1,0:T(8,128)(2,1)S(1)} %get-tuple-element.89), channel_id=1, source_target_pairs={{0,2},{1,3},{2,0},{3,1},{4,6},{5,7},{6,4},{7,5},{8,10},{9,11},{10,... | collective-permute-start | bytes 786440 | tf_op jit(solution)/shard_map/ppermute | solution.py:452
  66.1 0.5 collective-permute-start.15
  66.6 0.2 collective-permute-done.13.other
  66.7 4.0 %up.2.refs_0_.after = bf16[256,3584]{1,0:T(8,128)(2,1)S(1)} custom-call(bf16[2048,3584]{1,0:T(8,128)(2,1)S(1)} %get-tuple-element.54.after.w_up, bf16[128,2048]{1,0:T(8,128)(2,1)S(1)} %gather.2.own, bf16[128,2048]{1,0:T(8,128)(2,1)S(1)} %collective-permute-done.13.other), custom_call_target="tpu_custom_call" | custom-call | flops 1048576 | bytes 4096 | tf_op jit(solution)/shard_map/up/pallas_call | solution.py:689
  70.7 2.8 %collective-permute-done.14.refs_0_ = bf16[64,2048]{1,0:T(8,128)(2,1)S(1)} collective-permute-done((bf16[64,2048]{1,0:T(8,128)(2,1)S(1)}, bf16[64,2048]{1,0:T(8,128)(2,1)S(1)}, u32[]{:S(2)}, u32[]{:S(2)}) %collective-permute-start.14) | collective-permute-done | bytes 262176 | tf_op jit(solution)/shard_map/ppermute | solution.py:452
  73.6 0.9 collective-permute-done.15.refs_1_
  74.6 2.1 %down.3 = (bf16[128,1024]{1,0:T(8,128)(2,1)S(1)}, bf16[128,1024]{1,0:T(8,128)(2,1)S(1)}) custom-call(bf16[3584,2048]{1,0:T(8,128)(2,1)S(1)} %get-tuple-element.84.w_down, bf16[256,3584]{1,0:T(8,128)(2,1)S(1)} %up.2.refs_0_.after), custom_call_target="tpu_custom_call" | custom-call | flops 1879048192 | bytes 7340032 | tf_op jit(solution)/shard_map/down/pallas_call | solution.py:703
  76.7 4.0 %up.3.refs_2_.refs_1_ = bf16[256,3584]{1,0:T(8,128)(2,1)S(1)} custom-call(bf16[2048,3584]{1,0:T(8,128)(2,1)S(1)} %get-tuple-element.54.after.w_up, bf16[128,2048]{1,0:T(8,128)(2,1)S(1)} %gather.3.own, bf16[128,2048]{1,0:T(8,128)(2,1)S(1)} %collective-permute-done.16.other), custom_call_target="tpu_custom_call" | custom-call | flops 1048576 | bytes 4096 | tf_op jit(solution)/shard_map/up/pallas_call | solution.py:689
  80.7 3.9 %down.5 = (bf16[256,1024]{1,0:T(8,128)(2,1)S(1)}, bf16[256,1024]{1,0:T(8,128)(2,1)S(1)}) custom-call(bf16[3584,2048]{1,0:T(8,128)(2,1)S(1)} %get-tuple-element.84.w_down, bf16[256,3584]{1,0:T(8,128)(2,1)S(1)} %up.2.refs_0_.after, bf16[256,3584]{1,0:T(8,128)(2,1)S(1)} %up.3.refs_2_.refs_1_), custom_call_target="tpu_custom_call" | custom-call | flops 3758096384 | bytes 7340032 | tf_op jit(solution)/shard_map/down/pallas_call | solution.py:703
  84.6 0.6 collective-permute-start.22
  85.2 2.1 %down.4 = (bf16[256,1024]{1,0:T(8,128)(2,1)S(1)}, bf16[256,1024]{1,0:T(8,128)(2,1)S(1)}) custom-call(bf16[3584,2048]{1,0:T(8,128)(2,1)S(1)} %get-tuple-element.84.w_down, bf16[128,1024]{1,0:T(8,128)(2,1)S(1)} %get-tuple-element.87.refs_0_, bf16[128,1024]{1,0:T(8,128)(2,1)S(1)} %get-tuple-element.88.refs_1_, bf16[256,3584]{1,0:T(8,128)(2,1)S(1)} %up.3.refs_2_.refs_1_), custom_call_target="tpu_custom_call" | custom-call | flops 1879048192 | bytes 7340032 | tf_op jit(solution)/shard_map/down/pallas_call | solution.py:703
  87.2 0.1 collective-permute-start.17
  87.3 0.1 join.3
  87.5 0.9 collective-permute-start.23
  88.3 1.6 %collective-permute-start.24 = (bf16[64,1024]{1,0:T(8,128)(2,1)S(1)}, bf16[64,1024]{1,0:T(8,128)(2,1)S(1)}, u32[]{:S(2)}, u32[]{:S(2)}) collective-permute-start(bf16[64,1024]{1,0:T(8,128)(2,1)S(1)} %get-tuple-element.101), channel_id=1, source_target_pairs={{0,4},{1,5},{2,6},{3,7},{4,0},{5,1},{6,2},{7,3},{8,12},{9,13},{10,... | collective-permute-start | bytes 393224 | tf_op jit(solution)/shard_map/ppermute | solution.py:452
  89.9 1.1 collective-permute-start.25
  91.0 0.1 join.2
  91.2 0.9 collective-permute-start.18
  92.0 1.6 %collective-permute-start.19 = (bf16[64,1024]{1,0:T(8,128)(2,1)S(1)}, bf16[64,1024]{1,0:T(8,128)(2,1)S(1)}, u32[]{:S(2)}, u32[]{:S(2)}) collective-permute-start(bf16[64,1024]{1,0:T(8,128)(2,1)S(1)} %get-tuple-element.95), channel_id=1, source_target_pairs={{0,4},{1,5},{2,6},{3,7},{4,0},{5,1},{6,2},{7,3},{8,12},{9,13},{10,... | collective-permute-start | bytes 393224 | tf_op jit(solution)/shard_map/ppermute | solution.py:452
  93.6 0.2 collective-permute-done.23.refs_1_
  93.8 1.8 %collective-permute-start.20 = (bf16[64,1024]{1,0:T(8,128)(2,1)S(1)}, bf16[64,1024]{1,0:T(8,128)(2,1)S(1)}, u32[]{:S(2)}, u32[]{:S(2)}) collective-permute-start(bf16[64,1024]{1,0:T(8,128)(2,1)S(1)} %get-tuple-element.96), channel_id=1, source_target_pairs={{0,6},{1,7},{2,4},{3,5},{4,2},{5,3},{6,0},{7,1},{8,14},{9,15},{10,... | collective-permute-start | bytes 393224 | tf_op jit(solution)/shard_map/ppermute | solution.py:452
  95.6 1.2 %collective-permute-done.24.refs_2_ = bf16[64,1024]{1,0:T(8,128)(2,1)S(1)} collective-permute-done((bf16[64,1024]{1,0:T(8,128)(2,1)S(1)}, bf16[64,1024]{1,0:T(8,128)(2,1)S(1)}, u32[]{:S(2)}, u32[]{:S(2)}) %collective-permute-start.24) | collective-permute-done | bytes 131104 | tf_op jit(solution)/shard_map/ppermute | solution.py:452
  96.9 0.4 collective-permute-done.25.refs_3_
  97.2 0.3 finish.3
  97.5 1.6 %collective-permute-start.26 = (bf16[128,1024]{1,0:T(8,128)(2,1)S(1)}, bf16[128,1024]{1,0:T(8,128)(2,1)S(1)}, u32[]{:S(2)}, u32[]{:S(2)}) collective-permute-start(bf16[128,1024]{1,0:T(8,128)(2,1)S(1)} %finish.3), channel_id=1, source_target_pairs={{0,8},{8,16},{16,24},{24,0},{1,9},{9,17},{17,25},{25,1},{2,10},{10... | collective-permute-start | bytes 786440 | tf_op jit(solution)/shard_map/ppermute | solution.py:457
  99.2 0.3 collective-permute-done.18.refs_1_
  99.5 2.9 %collective-permute-done.19.refs_2_ = bf16[64,1024]{1,0:T(8,128)(2,1)S(1)} collective-permute-done((bf16[64,1024]{1,0:T(8,128)(2,1)S(1)}, bf16[64,1024]{1,0:T(8,128)(2,1)S(1)}, u32[]{:S(2)}, u32[]{:S(2)}) %collective-permute-start.19) | collective-permute-done | bytes 131104 | tf_op jit(solution)/shard_map/ppermute | solution.py:452
  102.4 0.3 finish.2
  102.7 1.6 %collective-permute-start.21 = (bf16[128,1024]{1,0:T(8,128)(2,1)S(1)}, bf16[128,1024]{1,0:T(8,128)(2,1)S(1)}, u32[]{:S(2)}, u32[]{:S(2)}) collective-permute-start(bf16[128,1024]{1,0:T(8,128)(2,1)S(1)} %finish.2), channel_id=1, source_target_pairs={{0,8},{8,16},{16,24},{24,0},{1,9},{9,17},{17,25},{25,1},{2,10},{10... | collective-permute-start | bytes 786440 | tf_op jit(solution)/shard_map/ppermute | solution.py:457
  104.3 1.7 %collective-permute-done.26 = bf16[128,1024]{1,0:T(8,128)(2,1)S(1)} collective-permute-done((bf16[128,1024]{1,0:T(8,128)(2,1)S(1)}, bf16[128,1024]{1,0:T(8,128)(2,1)S(1)}, u32[]{:S(2)}, u32[]{:S(2)}) %collective-permute-start.26) | collective-permute-done | bytes 262176 | tf_op jit(solution)/shard_map/ppermute | solution.py:457
  106.0 6.6 %collective-permute-done.21 = bf16[128,1024]{1,0:T(8,128)(2,1)S(1)} collective-permute-done((bf16[128,1024]{1,0:T(8,128)(2,1)S(1)}, bf16[128,1024]{1,0:T(8,128)(2,1)S(1)}, u32[]{:S(2)}, u32[]{:S(2)}) %collective-permute-start.21) | collective-permute-done | bytes 262176 | tf_op jit(solution)/shard_map/ppermute | solution.py:457
  112.6 0.8 maximum_bitcast_fusion
  (16 shorter events, 0.3 us)
Async XLA Ops:
  0.0 15.6 %collective-permute-start = (bf16[128,2048]{1,0:T(8,128)(2,1)}, bf16[128,2048]{1,0:T(8,128)(2,1)S(1)}, u32[]{:S(2)}, u32[]{:S(2)}) collective-permute-start(bf16[128,2048]{1,0:T(8,128)(2,1)} %bitcast.23), channel_id=1, source_target_pairs={{0,2},{1,3},{2,0},{3,1},{4,6},{5,7},{6,4},{7,5},{8,10},{9,11},{10,... | collective-permute-start | bytes 1572872 | tf_op jit(solution)/shard_map/ppermute | solution.py:452
  2.9 14.0 %collective-permute-start.2 = (bf16[128,2048]{1,0:T(8,128)(2,1)}, bf16[128,2048]{1,0:T(8,128)(2,1)S(1)}, u32[]{:S(2)}, u32[]{:S(2)}) collective-permute-start(bf16[128,2048]{1,0:T(8,128)(2,1)} %bitcast.24), channel_id=1, source_target_pairs={{0,1},{1,0},{2,3},{3,2},{4,5},{5,4},{6,7},{7,6},{8,9},{9,8},{10,11... | collective-permute-start | bytes 1572872 | tf_op jit(solution)/shard_map/ppermute | solution.py:452
  2.9 14.5 %collective-permute-start.3 = (bf16[2048,128]{1,0:T(8,128)(2,1)}, bf16[2048,128]{1,0:T(8,128)(2,1)S(1)}, u32[]{:S(2)}, u32[]{:S(2)}) collective-permute-start(bf16[2048,128]{1,0:T(8,128)(2,1)} %bitcast.28), channel_id=1, source_target_pairs={{0,4},{1,5},{2,6},{3,7},{4,0},{5,1},{6,2},{7,3},{8,12},{9,13},{10,... | collective-permute-start | bytes 1572872 | tf_op jit(solution)/shard_map/ppermute | solution.py:452
  16.7 3.1 %collective-permute-start.1 = (bf16[128,2048]{1,0:T(8,128)(2,1)S(1)}, bf16[128,2048]{1,0:T(8,128)(2,1)S(1)}, u32[]{:S(2)}, u32[]{:S(2)}) collective-permute-start(bf16[128,2048]{1,0:T(8,128)(2,1)S(1)} %norm.3.normed_near), channel_id=1, source_target_pairs={{0,1},{1,0},{2,3},{3,2},{4,5},{5,4},{6,7},{7,6},{8,9},{9,8},{10,11... | collective-permute-start | bytes 1572872 | tf_op jit(solution)/shard_map/ppermute | solution.py:452
  20.6 8.1 %collective-permute-start.4 = (bf16[2,512,128]{2,1,0:T(8,128)(2,1)S(1)}, bf16[2,512,128]{2,1,0:T(8,128)(2,1)S(1)}, u32[]{:S(2)}, u32[]{:S(2)}) collective-permute-start(bf16[2,512,128]{2,1,0:T(8,128)(2,1)S(1)} %get-tuple-element.58.refs_5_.kv), channel_id=1, source_target_pairs={{0,4},{1,5},{2,6},{3,7},{4,0},{5,1},{6,2},{7,3},{8,12},{9,13},{10,... | collective-permute-start | bytes 786440 | tf_op jit(solution)/shard_map/ppermute | solution.py:452
  29.3 5.9 %collective-permute-start.6 = (bf16[128,512]{1,0:T(8,128)(2,1)S(1)}, bf16[128,512]{1,0:T(8,128)(2,1)S(1)}, u32[]{:S(2)}, u32[]{:S(2)}) collective-permute-start(bf16[128,512]{1,0:T(8,128)(2,1)S(1)} %get-tuple-element.69), channel_id=1, source_target_pairs={{0,2},{1,3},{2,0},{3,1},{4,6},{5,7},{6,4},{7,5},{8,10},{9,11},{10,... | collective-permute-start | bytes 393224 | tf_op jit(solution)/shard_map/ppermute | solution.py:452
  30.6 5.7 %collective-permute-start.7 = (bf16[128,512]{1,0:T(8,128)(2,1)S(1)}, bf16[128,512]{1,0:T(8,128)(2,1)S(1)}, u32[]{:S(2)}, u32[]{:S(2)}) collective-permute-start(bf16[128,512]{1,0:T(8,128)(2,1)S(1)} %get-tuple-element.70), channel_id=1, source_target_pairs={{0,3},{1,2},{2,1},{3,0},{4,7},{5,6},{6,5},{7,4},{8,11},{9,10},{10,... | collective-permute-start | bytes 393224 | tf_op jit(solution)/shard_map/ppermute | solution.py:452
  31.3 5.1 %collective-permute-start.5 = (bf16[128,512]{1,0:T(8,128)(2,1)S(1)}, bf16[128,512]{1,0:T(8,128)(2,1)S(1)}, u32[]{:S(2)}, u32[]{:S(2)}) collective-permute-start(bf16[128,512]{1,0:T(8,128)(2,1)S(1)} %get-tuple-element.68), channel_id=1, source_target_pairs={{0,1},{1,0},{2,3},{3,2},{4,5},{5,4},{6,7},{7,6},{8,9},{9,8},{10,11... | collective-permute-start | bytes 393224 | tf_op jit(solution)/shard_map/ppermute | solution.py:452
  42.1 1.6 %collective-permute-start.8 = (bf16[16,2176]{1,0:T(8,128)(2,1)S(1)}, bf16[16,2176]{1,0:T(8,128)(2,1)S(1)}, u32[]{:S(2)}, u32[]{:S(2)}) collective-permute-start(bf16[16,2176]{1,0:T(8,128)(2,1)S(1)} %get-tuple-element.81.own), channel_id=1, source_target_pairs={{0,1},{1,0},{2,3},{3,2},{4,5},{5,4},{6,7},{7,6},{8,9},{9,8},{10,11... | collective-permute-start | bytes 208904 | tf_op jit(solution)/shard_map/ppermute | solution.py:452
  44.3 6.1 %collective-permute-start.11 = (bf16[16,2176]{1,0:T(8,128)(2,1)S(1)}, bf16[16,2176]{1,0:T(8,128)(2,1)S(1)}, u32[]{:S(2)}, u32[]{:S(2)}) collective-permute-start(bf16[16,2176]{1,0:T(8,128)(2,1)S(1)} %pair.1), channel_id=1, source_target_pairs={{0,6},{1,7},{2,4},{3,5},{4,2},{5,3},{6,0},{7,1},{8,14},{9,15},{10,... | collective-permute-start | bytes 208904 | tf_op jit(solution)/shard_map/ppermute | solution.py:452
  47.7 4.3 %collective-permute-start.10 = (bf16[16,2176]{1,0:T(8,128)(2,1)S(1)}, bf16[16,2176]{1,0:T(8,128)(2,1)S(1)}, u32[]{:S(2)}, u32[]{:S(2)}) collective-permute-start(bf16[16,2176]{1,0:T(8,128)(2,1)S(1)} %pair.1), channel_id=1, source_target_pairs={{0,4},{1,5},{2,6},{3,7},{4,0},{5,1},{6,2},{7,3},{8,12},{9,13},{10,... | collective-permute-start | bytes 208904 | tf_op jit(solution)/shard_map/ppermute | solution.py:452
  47.8 4.6 %collective-permute-start.9 = (bf16[16,2176]{1,0:T(8,128)(2,1)S(1)}, bf16[16,2176]{1,0:T(8,128)(2,1)S(1)}, u32[]{:S(2)}, u32[]{:S(2)}) collective-permute-start(bf16[16,2176]{1,0:T(8,128)(2,1)S(1)} %pair.1), channel_id=1, source_target_pairs={{0,2},{1,3},{2,0},{3,1},{4,6},{5,7},{6,4},{7,5},{8,10},{9,11},{10,... | collective-permute-start | bytes 208904 | tf_op jit(solution)/shard_map/ppermute | solution.py:452
  55.9 8.8 %collective-permute-start.12 = (bf16[64,2048]{1,0:T(8,128)(2,1)S(1)}, bf16[64,2048]{1,0:T(8,128)(2,1)S(1)}, u32[]{:S(2)}, u32[]{:S(2)}) collective-permute-start(bf16[64,2048]{1,0:T(8,128)(2,1)S(1)} %get-tuple-element.86), channel_id=1, source_target_pairs={{0,6},{1,7},{2,4},{3,5},{4,2},{5,3},{6,0},{7,1},{8,14},{9,15},{10,... | collective-permute-start | bytes 786440 | tf_op jit(solution)/shard_map/ppermute | solution.py:452
  64.8 2.0 %collective-permute-start.13 = (bf16[128,2048]{1,0:T(8,128)(2,1)S(1)}, bf16[128,2048]{1,0:T(8,128)(2,1)S(1)}, u32[]{:S(2)}, u32[]{:S(2)}) collective-permute-start(bf16[128,2048]{1,0:T(8,128)(2,1)S(1)} %gather.2.own), channel_id=1, source_target_pairs={{0,1},{1,0},{2,3},{3,2},{4,5},{5,4},{6,7},{7,6},{8,9},{9,8},{10,11... | collective-permute-start | bytes 1572872 | tf_op jit(solution)/shard_map/ppermute | solution.py:452
  64.8 8.7 %collective-permute-start.14 = (bf16[64,2048]{1,0:T(8,128)(2,1)S(1)}, bf16[64,2048]{1,0:T(8,128)(2,1)S(1)}, u32[]{:S(2)}, u32[]{:S(2)}) collective-permute-start(bf16[64,2048]{1,0:T(8,128)(2,1)S(1)} %get-tuple-element.89), channel_id=1, source_target_pairs={{0,2},{1,3},{2,0},{3,1},{4,6},{5,7},{6,4},{7,5},{8,10},{9,11},{10,... | collective-permute-start | bytes 786440 | tf_op jit(solution)/shard_map/ppermute | solution.py:452
  66.1 8.4 %collective-permute-start.15 = (bf16[64,2048]{1,0:T(8,128)(2,1)S(1)}, bf16[64,2048]{1,0:T(8,128)(2,1)S(1)}, u32[]{:S(2)}, u32[]{:S(2)}) collective-permute-start(bf16[64,2048]{1,0:T(8,128)(2,1)S(1)} %get-tuple-element.90), channel_id=1, source_target_pairs={{0,4},{1,5},{2,6},{3,7},{4,0},{5,1},{6,2},{7,3},{8,12},{9,13},{10,... | collective-permute-start | bytes 786440 | tf_op jit(solution)/shard_map/ppermute | solution.py:452
  74.5 2.1 %collective-permute-start.16 = (bf16[128,2048]{1,0:T(8,128)(2,1)S(1)}, bf16[128,2048]{1,0:T(8,128)(2,1)S(1)}, u32[]{:S(2)}, u32[]{:S(2)}) collective-permute-start(bf16[128,2048]{1,0:T(8,128)(2,1)S(1)} %gather.3.own), channel_id=1, source_target_pairs={{0,1},{1,0},{2,3},{3,2},{4,5},{5,4},{6,7},{7,6},{8,9},{9,8},{10,11... | collective-permute-start | bytes 1572872 | tf_op jit(solution)/shard_map/ppermute | solution.py:452
  84.6 2.7 %collective-permute-start.22 = (bf16[256,1024]{1,0:T(8,128)(2,1)S(1)}, bf16[256,1024]{1,0:T(8,128)(2,1)S(1)}, u32[]{:S(2)}, u32[]{:S(2)}) collective-permute-start(bf16[256,1024]{1,0:T(8,128)(2,1)S(1)} %get-tuple-element.98), channel_id=1, source_target_pairs={{0,1},{1,0},{2,3},{3,2},{4,5},{5,4},{6,7},{7,6},{8,9},{9,8},{10,11... | collective-permute-start | bytes 1572872 | tf_op jit(solution)/shard_map/ppermute | solution.py:452
  87.2 3.8 %collective-permute-start.17 = (bf16[256,1024]{1,0:T(8,128)(2,1)S(1)}, bf16[256,1024]{1,0:T(8,128)(2,1)S(1)}, u32[]{:S(2)}, u32[]{:S(2)}) collective-permute-start(bf16[256,1024]{1,0:T(8,128)(2,1)S(1)} %get-tuple-element.92), channel_id=1, source_target_pairs={{0,1},{1,0},{2,3},{3,2},{4,5},{5,4},{6,7},{7,6},{8,9},{9,8},{10,11... | collective-permute-start | bytes 1572872 | tf_op jit(solution)/shard_map/ppermute | solution.py:452
  87.5 6.4 %collective-permute-start.23 = (bf16[64,1024]{1,0:T(8,128)(2,1)S(1)}, bf16[64,1024]{1,0:T(8,128)(2,1)S(1)}, u32[]{:S(2)}, u32[]{:S(2)}) collective-permute-start(bf16[64,1024]{1,0:T(8,128)(2,1)S(1)} %get-tuple-element.100), channel_id=1, source_target_pairs={{0,2},{1,3},{2,0},{3,1},{4,6},{5,7},{6,4},{7,5},{8,10},{9,11},{10,... | collective-permute-start | bytes 393224 | tf_op jit(solution)/shard_map/ppermute | solution.py:452
  88.3 8.5 %collective-permute-start.24 = (bf16[64,1024]{1,0:T(8,128)(2,1)S(1)}, bf16[64,1024]{1,0:T(8,128)(2,1)S(1)}, u32[]{:S(2)}, u32[]{:S(2)}) collective-permute-start(bf16[64,1024]{1,0:T(8,128)(2,1)S(1)} %get-tuple-element.101), channel_id=1, source_target_pairs={{0,4},{1,5},{2,6},{3,7},{4,0},{5,1},{6,2},{7,3},{8,12},{9,13},{10,... | collective-permute-start | bytes 393224 | tf_op jit(solution)/shard_map/ppermute | solution.py:452
  89.9 7.3 %collective-permute-start.25 = (bf16[64,1024]{1,0:T(8,128)(2,1)S(1)}, bf16[64,1024]{1,0:T(8,128)(2,1)S(1)}, u32[]{:S(2)}, u32[]{:S(2)}) collective-permute-start(bf16[64,1024]{1,0:T(8,128)(2,1)S(1)} %get-tuple-element.102), channel_id=1, source_target_pairs={{0,6},{1,7},{2,4},{3,5},{4,2},{5,3},{6,0},{7,1},{8,14},{9,15},{10,... | collective-permute-start | bytes 393224 | tf_op jit(solution)/shard_map/ppermute | solution.py:452
  91.2 8.3 %collective-permute-start.18 = (bf16[64,1024]{1,0:T(8,128)(2,1)S(1)}, bf16[64,1024]{1,0:T(8,128)(2,1)S(1)}, u32[]{:S(2)}, u32[]{:S(2)}) collective-permute-start(bf16[64,1024]{1,0:T(8,128)(2,1)S(1)} %get-tuple-element.94), channel_id=1, source_target_pairs={{0,2},{1,3},{2,0},{3,1},{4,6},{5,7},{6,4},{7,5},{8,10},{9,11},{10,... | collective-permute-start | bytes 393224 | tf_op jit(solution)/shard_map/ppermute | solution.py:452
  92.0 10.3 %collective-permute-start.19 = (bf16[64,1024]{1,0:T(8,128)(2,1)S(1)}, bf16[64,1024]{1,0:T(8,128)(2,1)S(1)}, u32[]{:S(2)}, u32[]{:S(2)}) collective-permute-start(bf16[64,1024]{1,0:T(8,128)(2,1)S(1)} %get-tuple-element.95), channel_id=1, source_target_pairs={{0,4},{1,5},{2,6},{3,7},{4,0},{5,1},{6,2},{7,3},{8,12},{9,13},{10,... | collective-permute-start | bytes 393224 | tf_op jit(solution)/shard_map/ppermute | solution.py:452
  93.8 8.6 %collective-permute-start.20 = (bf16[64,1024]{1,0:T(8,128)(2,1)S(1)}, bf16[64,1024]{1,0:T(8,128)(2,1)S(1)}, u32[]{:S(2)}, u32[]{:S(2)}) collective-permute-start(bf16[64,1024]{1,0:T(8,128)(2,1)S(1)} %get-tuple-element.96), channel_id=1, source_target_pairs={{0,6},{1,7},{2,4},{3,5},{4,2},{5,3},{6,0},{7,1},{8,14},{9,15},{10,... | collective-permute-start | bytes 393224 | tf_op jit(solution)/shard_map/ppermute | solution.py:452
  97.5 8.5 %collective-permute-start.26 = (bf16[128,1024]{1,0:T(8,128)(2,1)S(1)}, bf16[128,1024]{1,0:T(8,128)(2,1)S(1)}, u32[]{:S(2)}, u32[]{:S(2)}) collective-permute-start(bf16[128,1024]{1,0:T(8,128)(2,1)S(1)} %finish.3), channel_id=1, source_target_pairs={{0,8},{8,16},{16,24},{24,0},{1,9},{9,17},{17,25},{25,1},{2,10},{10... | collective-permute-start | bytes 786440 | tf_op jit(solution)/shard_map/ppermute | solution.py:457
  102.7 9.9 %collective-permute-start.21 = (bf16[128,1024]{1,0:T(8,128)(2,1)S(1)}, bf16[128,1024]{1,0:T(8,128)(2,1)S(1)}, u32[]{:S(2)}, u32[]{:S(2)}) collective-permute-start(bf16[128,1024]{1,0:T(8,128)(2,1)S(1)} %finish.2), channel_id=1, source_target_pairs={{0,8},{8,16},{16,24},{24,0},{1,9},{9,17},{17,25},{25,1},{2,10},{10... | collective-permute-start | bytes 786440 | tf_op jit(solution)/shard_map/ppermute | solution.py:457

commit v3 on v2

--- a/solution.py
+++ b/solution.py
@@ -15,8 +15,6 @@
 EIGHT = 8
 STRIP = 16
 LANES = 128
-PAIR = 2
-BATCHES = ((0, 3), (1, 2))
 CHUNKS = 2
 F32 = jnp.float32
 BF16 = jnp.bfloat16
@@ -182,7 +180,7 @@
     place, x, gains, skip, dt_in, dt_out, bias, rate, w_bct, *refs
 ):
     attended = refs[:KVH]
-    base, keep_out, drive_out, chunk_state, chunk_keep, bc_out, coef_out, ends = refs[KVH:-4]
+    base, keep_out, drive_out, chunk_state, chunk_keep, bc_out, bct_out, ends = refs[KVH:-4]
     mixed, pre, tail_high, tail_low = refs[-4:]
     rows, width = x.shape
     state = w_bct.shape[0] // 2
@@ -205,38 +203,35 @@
     bct = dot(w_bct[...], mixed[...], ((1,), (1,)))
     bc = bct.T
     bc_out[...] = bc
+    bct_out[...] = bct
     b_rows = bct[:state]
-    coupling = dot_split(split(bc[:, state:]), split(b_rows))
-    row, lane = iota((rows, rows), 0), iota((rows, rows), 1)
-    coef = jnp.zeros((rows, rows), F32)
-    for back in range(EIGHT):
-        diagonal = jnp.sum(jnp.where(lane == row - back, coupling, 0.0), 1, keepdims=True)
-        coef = coef + jnp.where((lane == back) & (row % EIGHT >= back), diagonal, 0.0)
-    coef_out[...] = coef
-
-    edge = iota((EIGHT, width), 0)
+    block = width // 4
+    edge = iota((EIGHT, block), 0)
 
     def steps(index, carry):
         at = pl.ds(pl.multiple_of(index * STRIP, STRIP), STRIP)
-        raw = pre[at, :] + bias[...]
-        step_size = jnp.maximum(raw, 0.0) + jnp.log1p(jnp.exp(-jnp.abs(raw)))
-        keep = jnp.exp(-step_size * rate[...])
-        drive = step_size * mixed[at, :].astype(F32)
-        keep_out[at, :] = keep
-        drive_out[at, :] = drive
-        tails = []
-        for part in range(STRIP // EIGHT):
-            kept = keep[part * EIGHT : (part + 1) * EIGHT]
-            after = jnp.where(edge < EIGHT - 1, pltpu.roll(kept, EIGHT - 1, 0), 1.0)
-            for hop in (1, 2, 4):
-                after = after * jnp.where(
-                    edge < EIGHT - hop, pltpu.roll(after, EIGHT - hop, 0), 1.0
-                )
-            chunk_keep[pl.ds(index * (STRIP // EIGHT) + part, 1), :] = after[0:1] * kept[0:1]
-            tails.append(after * drive[part * EIGHT : (part + 1) * EIGHT])
-        high, low = split(jnp.concatenate(tails, 0))
-        tail_high[at, :] = high
-        tail_low[at, :] = low
+        for low in range(0, width, block):
+            cols = pl.ds(low, block)
+            raw = pre[at, cols] + bias[:, cols]
+            step_size = jnp.maximum(raw, 0.0) + jnp.log1p(jnp.exp(-jnp.abs(raw)))
+            keep = jnp.exp(-step_size * rate[:, cols])
+            drive = step_size * mixed[at, cols].astype(F32)
+            keep_out[at, cols] = keep
+            drive_out[at, cols] = drive
+            tails = []
+            for part in range(STRIP // EIGHT):
+                kept = keep[part * EIGHT : (part + 1) * EIGHT]
+                after = jnp.where(edge < EIGHT - 1, pltpu.roll(kept, EIGHT - 1, 0), 1.0)
+                for hop in (1, 2, 4):
+                    after = after * jnp.where(
+                        edge < EIGHT - hop, pltpu.roll(after, EIGHT - hop, 0), 1.0
+                    )
+                whole = after[0:1] * kept[0:1]
+                chunk_keep[pl.ds(index * (STRIP // EIGHT) + part, 1), cols] = whole
+                tails.append(after * drive[part * EIGHT : (part + 1) * EIGHT])
+            high, low_part = split(jnp.concatenate(tails, 0))
+            tail_high[at, cols] = high
+            tail_low[at, cols] = low_part
         return carry
 
     lax.fori_loop(0, rows // STRIP, steps, 0, unroll=2)
@@ -273,8 +268,16 @@
     ends[:, width:] = (earlier[:, width:] * fade).astype(BF16)
 
 
-def within_kernel(coef, base, keep, drive, second, faded):
+def within_kernel(bc, bct, base, keep, drive, second, faded, coef):
     rows, width = base.shape
+    state = bct.shape[0] // 2
+    coupling = dot_split(split(bc[:, state:]), split(bct[:state]))
+    row, lane = iota((rows, rows), 0), iota((rows, rows), 1)
+    total = jnp.zeros((rows, rows), F32)
+    for back in range(EIGHT):
+        diagonal = jnp.sum(jnp.where(lane == row - back, coupling, 0.0), 1, keepdims=True)
+        total = total + jnp.where((lane == back) & (row % EIGHT >= back), diagonal, 0.0)
+    coef[...] = total
     edge = iota((EIGHT, width), 0)
 
     def chunk(index, carry):
@@ -395,48 +398,37 @@
     )(*[in_hbm(array) for array in arrays], after)
 
 
-def gather_kernel(after, *refs):
+def gather_kernel(*refs):
     blocks, out = refs[:-1], refs[-1]
     capacity = blocks[0].shape[0]
     for at, block in enumerate(blocks):
         out[at * capacity : (at + 1) * capacity, :] = block[...]
 
 
-def up_kernel(w_up, own, other, hidden):
-    tokens = jnp.concatenate([own[...], other[...]], 0)
+def up_kernel(w_up, tokens, after, hidden):
     tile = 256 if hidden.shape[1] % 256 == 0 else LANES
     for low in range(0, hidden.shape[1], tile):
         cols = slice(low, low + tile)
-        raised = dot(tokens, w_up[:, cols])
+        raised = dot(tokens[...], w_up[:, cols])
         hidden[:, cols] = (raised * jax.nn.sigmoid(raised)).astype(BF16)
 
 
-def down_kernel(start, done, w_down, *refs):
-    outs = refs[-PAIR:]
-    earlier, hiddens = refs[: PAIR * done], refs[PAIR * done : -PAIR]
-    hidden = jnp.concatenate([block[...] for block in hiddens], 0)
-    rows = hiddens[0].shape[0] // PAIR
+def down_kernel(start, w_down, hidden, after, out):
     tile = 256
-    for at, block in enumerate(earlier):
-        outs[at % PAIR][at // PAIR * rows : (at // PAIR + 1) * rows, :] = block[...]
-    for low in range(0, outs[0].shape[1], tile):
-        result = dot(hidden, w_down[:, start + low : start + low + tile]).astype(BF16)
-        for at in range(PAIR * len(hiddens)):
-            batch = done + at // PAIR
-            outs[at % PAIR][batch * rows : (batch + 1) * rows, low : low + tile] = result[
-                at * rows : (at + 1) * rows
-            ]
+    for low in range(0, out.shape[1], tile):
+        part = w_down[:, start + low : start + low + tile]
+        out[:, low : low + tile] = dot(hidden[...], part).astype(BF16)
 
 
 def join_kernel(*refs):
     parts, outs = refs[:-EXPERTS], refs[-EXPERTS:]
     capacity = outs[0].shape[0]
-    for place, slot in enumerate(sum(BATCHES, ())):
-        at = slice(place * capacity, (place + 1) * capacity)
+    for slot, out in enumerate(outs):
+        at = slice(slot * capacity, (slot + 1) * capacity)
         total = parts[0][at, :].astype(F32)
         for part in parts[1:]:
             total = total + part[at, :].astype(F32)
-        outs[slot][...] = total.astype(BF16)
+        out[...] = total.astype(BF16)
 
 
 def finish_kernel(start, second, weighting, *refs):
@@ -580,7 +572,7 @@
         for slot, block in zip(slots, state_now):
             attended[slot] = exchange(block, "ctx", slot) if slot else block
 
-    base, keep, drive, chunk_state, chunk_keep, bc, coef, ends = pl.pallas_call(
+    base, keep, drive, chunk_state, chunk_keep, bc, bct, ends = pl.pallas_call(
         prepare_kernel,
         out_shape=(
             shape((rows, width), F32),
@@ -589,7 +581,7 @@
             shape((chunks * state, width), F32),
             shape((chunks, width), F32),
             shape((rows, 2 * state), F32),
-            shape((rows, rows), F32),
+            shape((2 * state, rows), F32),
             shape((state, width + LANES), BF16),
         ),
         in_specs=[SMEM] + [VMEM] * (8 + KVH),
@@ -629,12 +621,13 @@
     before, faded = pl.pallas_call(
         within_kernel,
         out_shape=(shape((rows, width), F32), shape((rows, width), F32)),
-        in_specs=[VMEM] * 4,
+        in_specs=[VMEM] * 5,
         out_specs=(VMEM, VMEM),
-        compiler_params=params(16),
+        scratch_shapes=[pltpu.VMEM((rows, rows), F32)],
+        compiler_params=params(12),
         cost_estimate=cost(40 * rows * width, 20 * rows * width),
         name="within",
-    )(coef, base, keep, drive)
+    )(bc, bct, base, keep, drive)
     second, weighting, *packed = pl.pallas_call(
         route_kernel,
         out_shape=(shape((rows, width), F32), shape((rows, EXPERTS * capacity), F32))
@@ -665,67 +658,53 @@
         *earlier_ends,
     )
 
-    arrived = [packed[0]] + [
-        exchange(packed[slot], "ctx", slot * parts) for slot in range(1, EXPERTS)
-    ]
+    def between_experts(blocks):
+        moved = {slot: exchange(blocks[slot], "ctx", slot * parts) for slot in (3, 1, 2)}
+        return [blocks[0]] + [moved[slot] for slot in range(1, EXPERTS)]
+
     units = raising.shape[1]
-    batch_rows = 2 * capacity
-    hiddens = [[] for _ in range(0, parts, PAIR)]
-    after = packed[0]
-    for batch in BATCHES:
-        tokens_here = pl.pallas_call(
-            gather_kernel,
-            out_shape=shape((batch_rows, width), BF16),
-            in_specs=[ANY] + [VMEM] * 2,
+    expert_rows = EXPERTS * capacity
+    arrived = pl.pallas_call(
+        gather_kernel,
+        out_shape=shape((expert_rows, width), BF16),
+        in_specs=[VMEM] * EXPERTS,
+        out_specs=VMEM,
+        compiler_params=params(4),
+        cost_estimate=cost(0, 4 * expert_rows * width),
+        name="gather",
+    )(*between_experts(packed))
+    hiddens = []
+    after = arrived
+    for turn in range(parts):
+        after = pl.pallas_call(
+            up_kernel,
+            out_shape=shape((expert_rows, units), BF16),
+            in_specs=[VMEM, VMEM, ANY],
             out_specs=VMEM,
-            compiler_params=params(4),
-            cost_estimate=cost(0, 4 * batch_rows * width),
-            name="gather",
-        )(after, *[arrived[slot] for slot in batch])
-        held = [tokens_here] + [
-            exchange(tokens_here, "ctx", turn) for turn in range(1, parts)
-        ]
-        for turn in range(0, parts, PAIR):
-            after = pl.pallas_call(
-                up_kernel,
-                out_shape=shape((PAIR * batch_rows, units), BF16),
-                in_specs=[VMEM] * (1 + PAIR),
-                out_specs=VMEM,
-                compiler_params=params(12),
-                cost_estimate=cost(2 * PAIR * batch_rows * width, 2 * width),
-                name="up",
-            )(raising, *held[turn : turn + PAIR])
-            hiddens[turn // PAIR].append(after)
-
-    def lower(start, span, blocks, earlier=()):
-        done = len(earlier) // PAIR
-        out_rows = batch_rows * (done + len(blocks))
-        return pl.pallas_call(
-            functools.partial(down_kernel, start, done),
-            out_shape=(shape((out_rows, span), BF16),) * PAIR,
-            in_specs=[VMEM] * (1 + len(earlier) + len(blocks)),
-            out_specs=(VMEM,) * PAIR,
             compiler_params=params(12),
-            cost_estimate=cost(
-                2 * PAIR * batch_rows * len(blocks) * span * units, 2 * span * units
-            ),
-            name="down",
-        )(lowering, *earlier, *blocks)
-
+            cost_estimate=cost(2 * expert_rows * width * units, 2 * width * units),
+            name="up",
+        )(raising, exchange(arrived, "ctx", turn) if turn else arrived, after)
+        hiddens.append(after)
     chunk_width = width // CHUNKS
     results = []
     for chunk in range(CHUNKS):
         start = chunk * chunk_width
-        part_out = []
-        for first_batch, last_batch in hiddens:
-            if chunk == 0:
-                earlier = lower(start, chunk_width, [first_batch])
-                part_out += lower(start, chunk_width, [last_batch], earlier)
-            else:
-                part_out += lower(start, chunk_width, [first_batch, last_batch])
-        sums = [part_out[0]] + [
-            exchange(part_out[turn], "ctx", turn) for turn in range(1, parts)
-        ]
+        sums = []
+        for turn in reversed(range(parts)):
+            part_out = pl.pallas_call(
+                functools.partial(down_kernel, start),
+                out_shape=shape((expert_rows, chunk_width), BF16),
+                in_specs=[VMEM, VMEM, ANY],
+                out_specs=VMEM,
+                compiler_params=params(12),
+                cost_estimate=cost(
+                    2 * expert_rows * chunk_width * units, 2 * chunk_width * units
+                ),
+                name="down",
+            )(lowering, hiddens[turn], after)
+            sums.append(exchange(part_out, "ctx", turn) if turn else part_out)
+            after = part_out
         joined = pl.pallas_call(
             join_kernel,
             out_shape=(shape((capacity, chunk_width), BF16),) * EXPERTS,
@@ -737,9 +716,8 @@
             ),
             name="join",
         )(*sums)
-        returned = [joined[0]] + [
-            exchange(joined[slot], "ctx", slot * parts) for slot in range(1, EXPERTS)
-        ]
+        after = joined[0]
+        returned = between_experts(joined)
         finished = pl.pallas_call(
             functools.partial(finish_kernel, start),
             out_shape=shape((rows, chunk_width), BF16),

time: 114 us -> 111 us (0.974)
  waiting for transfers between devices: 34.4 us -> 31.7 us
    ppermute x25 -> x24, waiting for transfers between devices: 26 us -> 24.3 us  [exchange(): return lax.ppermute(value, axis, [(at, at ^ mask) for at in range(count)])]
    ppermute x25 -> x24, starting transfers between devices: 25.7 us -> 24.8 us  [exchange(): return lax.ppermute(value, axis, [(at, at ^ mask) for at in range(count)])]
  transfers between devices with their start and end apart: 27 -> 26, of which waited for: 19 -> 15; matrix products, arithmetic and copies ran while one was open for 0% -> 0% of each run, Pallas kernels for 26% -> 27%
where the time goes in v3:
time: 111 us; the launch traced here: 110 us
  Pallas kernels  49.4 us (45%)
  waiting for transfers between devices  31.7 us (29%)
  starting transfers between devices  28.1 us (25%)
    ppermute x24, starting transfers between devices, exchange(): return lax.ppermute(value, axis, [(at, at ^ mask) for at in range(count)])  24.8 us
    ppermute x24, waiting for transfers between devices, exchange(): return lax.ppermute(value, axis, [(at, at ^ mask) for at in range(count)])  24.3 us
    pallas_call x2, Pallas kernels, fetch(): pl.pallas_call(functools.partial(fetch_kernel, pieces), out_shape=tuple((...  11.1 us
    pallas_call x4, Pallas kernels, on_device(): pl.pallas_call(functools.partial(down_kernel, start), out_shape=shape((ex...  8.21 us
    pallas_call x2, Pallas kernels, on_device(): pl.pallas_call(up_kernel, out_shape=shape((expert_rows, units), BF16), in...  8.09 us
    ppermute x2, waiting for transfers between devices, shifted(): lax.ppermute(value, axis, [(at, (at + steps) % count) for at in range(cou...  7.41 us
    pallas_call x1, Pallas kernels, on_device(): pl.pallas_call(prepare_kernel, out_shape=(shape((rows, width), F32), shap...  5.41 us
    pallas_call x1, Pallas kernels, on_device(): pl.pallas_call(route_kernel, out_shape=(shape((rows, width), F32), shape(...  3.51 us
  transfers between devices with their start and end apart: 26, of which 15 were waited for; matrix products, arithmetic and copies ran while one was open for 0% of the time, Pallas kernels for 27%

profile of v3, /device:TPU:0, one launch (start us, length us, event | category | flops | bytes accessed | tf_op | source)
XLA Modules:
  0.0 110.3 jit_solution(8504285553373481004)
XLA Ops:
  0.0 2.9 %collective-permute-start = (bf16[128,2048]{1,0:T(8,128)(2,1)}, bf16[128,2048]{1,0:T(8,128)(2,1)S(1)}, u32[]{:S(2)}, u32[]{:S(2)}) collective-permute-start(bf16[128,2048]{1,0:T(8,128)(2,1)} %bitcast.23), channel_id=1, source_target_pairs={{0,2},{1,3},{2,0},{3,1},{4,6},{5,7},{6,4},{7,5},{8,10},{9,11},{10,... | collective-permute-start | bytes 1572872 | tf_op jit(solution)/shard_map/ppermute | solution.py:444
  2.9 1.5 %collective-permute-start.3 = (bf16[2048,128]{1,0:T(8,128)(2,1)}, bf16[2048,128]{1,0:T(8,128)(2,1)S(1)}, u32[]{:S(2)}, u32[]{:S(2)}) collective-permute-start(bf16[2048,128]{1,0:T(8,128)(2,1)} %bitcast.28), channel_id=1, source_target_pairs={{0,4},{1,5},{2,6},{3,7},{4,0},{5,1},{6,2},{7,3},{8,12},{9,13},{10,... | collective-permute-start | bytes 1572872 | tf_op jit(solution)/shard_map/ppermute | solution.py:444
  4.5 0.1 pad_add_fusion.place
  4.5 1.4 %norm.2.refs_2_.normed_own = bf16[128,2048]{1,0:T(8,128)(2,1)S(1)} custom-call(s32[3]{0:T(128)S(1)} %pad_add_fusion.place, f32[3,1,2048]{2,1,0:T(1,128)} %bitcast.32, bf16[128,2048]{1,0:T(8,128)(2,1)} %bitcast.25, bf16[128,2048]{1,0:T(8,128)(2,1)} %bitcast.26), custom_call_target="tpu_custom_call" | custom-call | flops 2097152 | bytes 1048576 | tf_op jit(solution)/shard_map/norm/pallas_call | solution.py:496
  5.9 9.6 %fetch.2 = (bf16[2048,3584]{1,0:T(8,128)(2,1)S(1)}, bf16[3584,2048]{1,0:T(8,128)(2,1)S(1)}) custom-call(bf16[2048,3584]{1,0:T(8,128)(2,1)} %bitcast.21, bf16[3584,2048]{1,0:T(8,128)(2,1)} %bitcast.22, bf16[128,2048]{1,0:T(8,128)(2,1)S(1)} %norm.2.refs_2_.normed_own), custom_call_target="tpu_custom_call" | custom-call | bytes 58720256 | tf_op jit(solution)/shard_map/fetch/pallas_call | solution.py:389
  15.6 1.1 norm.3.normed_near
  16.7 0.3 collective-permute-start.1
  17.0 0.5 collective-permute-done.3.w_other
  17.5 2.2 %project.1 = (bf16[4,512,128]{2,1,0:T(8,128)(2,1)S(1)}, bf16[2,512,128]{2,1,0:T(8,128)(2,1)S(1)}, bf16[2048,256]{1,0:T(8,128)(2,1)S(1)}) custom-call(s32[3]{0:T(128)S(1)} %pad_add_fusion.place, f32[3,1,2048]{2,1,0:T(1,128)} %bitcast.34, bf16[128,2048]{1,0:T(8,128)(2,1)S(1)} %norm.2.refs_2_.normed_own, bf16[128,2048]{1,0:T(8,128)(2,1)S(1)} %collective-permute-done.2.beside, ...), custom_call_target="tpu_custom_call" | custom-call | flops 402653184 | bytes 6291456 | tf_op jit(solution)/shard_map/project/pallas_call | solution.py:514
  19.7 0.9 project_last.1
  20.6 1.6 %collective-permute-start.4 = (bf16[2,512,128]{2,1,0:T(8,128)(2,1)S(1)}, bf16[2,512,128]{2,1,0:T(8,128)(2,1)S(1)}, u32[]{:S(2)}, u32[]{:S(2)}) collective-permute-start(bf16[2,512,128]{2,1,0:T(8,128)(2,1)S(1)} %get-tuple-element.52.refs_5_.kv), channel_id=1, source_target_pairs={{0,4},{1,5},{2,6},{3,7},{4,0},{5,1},{6,2},{7,3},{8,12},{9,13},{10,... | collective-permute-start | bytes 786440 | tf_op jit(solution)/shard_map/ppermute | solution.py:444
  22.2 2.5 %near.1 = (f32[4,512,128]{2,1,0:T(8,128)S(1)}, f32[4,512,128]{2,1,0:T(8,128)S(1)}, f32[4,512,128]{2,1,0:T(8,128)S(1)}) custom-call(s32[3]{0:T(128)S(1)} %pad_add_fusion.place, bf16[4,512,128]{2,1,0:T(8,128)(2,1)S(1)} %get-tuple-element.57.q, bf16[2,512,128]{2,1,0:T(8,128)(2,1)S(1)} %get-tuple-element.52.refs_5_.kv), custom_call_target="tpu_custom_call" | custom-call | flops 536870912 | bytes 4194304 | tf_op jit(solution)/shard_map/near/pallas_call | solution.py:549
  24.8 3.9 %collective-permute-done.4.past = bf16[2,512,128]{2,1,0:T(8,128)(2,1)S(1)} collective-permute-done((bf16[2,512,128]{2,1,0:T(8,128)(2,1)S(1)}, bf16[2,512,128]{2,1,0:T(8,128)(2,1)S(1)}, u32[]{:S(2)}, u32[]{:S(2)}) %collective-permute-start.4) | collective-permute-done | bytes 262176 | tf_op jit(solution)/shard_map/ppermute | solution.py:444
  28.7 0.6 far.3
  29.3 1.3 %collective-permute-start.6 = (bf16[128,512]{1,0:T(8,128)(2,1)S(1)}, bf16[128,512]{1,0:T(8,128)(2,1)S(1)}, u32[]{:S(2)}, u32[]{:S(2)}) collective-permute-start(bf16[128,512]{1,0:T(8,128)(2,1)S(1)} %get-tuple-element.63), channel_id=1, source_target_pairs={{0,2},{1,3},{2,0},{3,1},{4,6},{5,7},{6,4},{7,5},{8,10},{9,11},{10,... | collective-permute-start | bytes 393224 | tf_op jit(solution)/shard_map/ppermute | solution.py:444
  30.6 0.6 far.2
  31.3 1.0 collective-permute-start.5
  32.3 1.5 %fetch.3 = (bf16[2048,128]{1,0:T(8,128)(2,1)S(1)}, bf16[128,2048]{1,0:T(8,128)(2,1)S(1)}, bf16[32,2048]{1,0:T(8,128)(2,1)S(1)}, bf16[128,2048]{1,0:T(8,128)(2,1)S(1)}, bf16[4,2048]{1,0:T(4,128)(2,1)S(1)}) custom-call(bf16[2048,128]{1,0:T(8,128)(2,1)} %bitcast.30, bf16[128,2048]{1,0:T(8,128)(2,1)} %bitcast.31, bf16[32,2048]{1,0:T(8,128)(2,1)} %bitcast.37, ...), custom_call_target="tpu_custom_call" | custom-call | bytes 3440640 | tf_op jit(solution)/shard_map/fetch/pallas_call | solution.py:389
  33.8 1.4 %collective-permute-done.6.refs_2_ = bf16[128,512]{1,0:T(8,128)(2,1)S(1)} collective-permute-done((bf16[128,512]{1,0:T(8,128)(2,1)S(1)}, bf16[128,512]{1,0:T(8,128)(2,1)S(1)}, u32[]{:S(2)}, u32[]{:S(2)}) %collective-permute-start.6) | collective-permute-done | bytes 131104 | tf_op jit(solution)/shard_map/ppermute | solution.py:444
  35.2 1.1 %collective-permute-done.7.refs_3_ = bf16[128,512]{1,0:T(8,128)(2,1)S(1)} collective-permute-done((bf16[128,512]{1,0:T(8,128)(2,1)S(1)}, bf16[128,512]{1,0:T(8,128)(2,1)S(1)}, u32[]{:S(2)}, u32[]{:S(2)}) %collective-permute-start.7) | collective-permute-done | bytes 131104 | tf_op jit(solution)/shard_map/ppermute | solution.py:444
  36.4 5.4 %prepare.1 = (f32[128,2048]{1,0:T(8,128)S(1)}, f32[128,2048]{1,0:T(8,128)S(1)}, f32[128,2048]{1,0:T(8,128)S(1)}, f32[256,2048]{1,0:T(8,128)S(1)}, f32[16,2048]{1...) custom-call(s32[3]{0:T(128)S(1)} %pad_add_fusion.place, ...), custom_call_target="tpu_custom_call" | custom-call | flops 671088640 | bytes 7864320 | tf_op jit(solution)/shard_map/prepare/pallas_call | solution.py:575
  41.8 0.7 collective-permute-start.8
  42.5 0.9 collective-permute-done.8.other.beside
  43.4 0.6 pair.1
  44.0 3.4 %collective-permute-start.11 = (bf16[16,2176]{1,0:T(8,128)(2,1)S(1)}, bf16[16,2176]{1,0:T(8,128)(2,1)S(1)}, u32[]{:S(2)}, u32[]{:S(2)}) collective-permute-start(bf16[16,2176]{1,0:T(8,128)(2,1)S(1)} %pair.1), channel_id=1, source_target_pairs={{0,6},{1,7},{2,4},{3,5},{4,2},{5,3},{6,0},{7,1},{8,14},{9,15},{10,... | collective-permute-start | bytes 208904 | tf_op jit(solution)/shard_map/ppermute | solution.py:444
  47.4 0.7 collective-permute-start.9
  48.1 2.1 %within.1 = (f32[128,2048]{1,0:T(8,128)S(1)}, f32[128,2048]{1,0:T(8,128)S(1)}) custom-call(f32[128,32]{1,0:T(8,128)S(1)} %get-tuple-element.65.bc, f32[32,128]{1,0:T(8,128)S(1)} %get-tuple-element.66.bct, f32[128,2048]{1,0:T(8,128)S(1)} %get-tuple-element.67.base, f32[128,2048]{1,0:T(8,128)S(1)} %get-tuple-element.68.keep, ...), custom_call_target="tpu_custom_call" | custom-call | flops 10485760 | bytes 5242880 | tf_op jit(solution)/shard_map/within/pallas_call | solution.py:621
  50.2 1.5 %collective-permute-done.10.refs_1_ = bf16[16,2176]{1,0:T(8,128)(2,1)S(1)} collective-permute-done((bf16[16,2176]{1,0:T(8,128)(2,1)S(1)}, bf16[16,2176]{1,0:T(8,128)(2,1)S(1)}, u32[]{:S(2)}, u32[]{:S(2)}) %collective-permute-start.10) | collective-permute-done | bytes 69664 | tf_op jit(solution)/shard_map/ppermute | solution.py:444
  51.7 0.3 collective-permute-done.9.refs_0_
  52.1 3.5 %route.1 = (f32[128,2048]{1,0:T(8,128)S(1)}, f32[128,256]{1,0:T(8,128)S(1)}, bf16[64,2048]{1,0:T(8,128)(2,1)S(1)}, bf16[64,2048]{1,0:T(8,128)(2,1)S(1)}, bf16[64...) custom-call(s32[3]{0:T(128)S(1)} %pad_add_fusion.place, f32[128,2048]{1,0:T(8,128)S(1)} %get-tuple-element.70.before, ...), custom_call_target="tpu_custom_call" | custom-call | flops 671088640 | bytes 7864320 | tf_op jit(solution)/shard_map/route/pallas_call | solution.py:631
  55.6 1.4 %collective-permute-start.12 = (bf16[64,2048]{1,0:T(8,128)(2,1)S(1)}, bf16[64,2048]{1,0:T(8,128)(2,1)S(1)}, u32[]{:S(2)}, u32[]{:S(2)}) collective-permute-start(bf16[64,2048]{1,0:T(8,128)(2,1)S(1)} %get-tuple-element.80), channel_id=1, source_target_pairs={{0,2},{1,3},{2,0},{3,1},{4,6},{5,7},{6,4},{7,5},{8,10},{9,11},{10,... | collective-permute-start | bytes 786440 | tf_op jit(solution)/shard_map/ppermute | solution.py:444
  56.9 1.1 collective-permute-start.13
  58.0 1.1 %collective-permute-start.14 = (bf16[64,2048]{1,0:T(8,128)(2,1)S(1)}, bf16[64,2048]{1,0:T(8,128)(2,1)S(1)}, u32[]{:S(2)}, u32[]{:S(2)}) collective-permute-start(bf16[64,2048]{1,0:T(8,128)(2,1)S(1)} %get-tuple-element.82), channel_id=1, source_target_pairs={{0,6},{1,7},{2,4},{3,5},{4,2},{5,3},{6,0},{7,1},{8,14},{9,15},{10,... | collective-permute-start | bytes 786440 | tf_op jit(solution)/shard_map/ppermute | solution.py:444
  59.1 5.7 %collective-permute-done.12.refs_1_ = bf16[64,2048]{1,0:T(8,128)(2,1)S(1)} collective-permute-done((bf16[64,2048]{1,0:T(8,128)(2,1)S(1)}, bf16[64,2048]{1,0:T(8,128)(2,1)S(1)}, u32[]{:S(2)}, u32[]{:S(2)}) %collective-permute-start.12) | collective-permute-done | bytes 262176 | tf_op jit(solution)/shard_map/ppermute | solution.py:444
  64.9 1.0 collective-permute-done.13.refs_2_
  65.9 4.2 %collective-permute-done.14.refs_3_ = bf16[64,2048]{1,0:T(8,128)(2,1)S(1)} collective-permute-done((bf16[64,2048]{1,0:T(8,128)(2,1)S(1)}, bf16[64,2048]{1,0:T(8,128)(2,1)S(1)}, u32[]{:S(2)}, u32[]{:S(2)}) %collective-permute-start.14) | collective-permute-done | bytes 262176 | tf_op jit(solution)/shard_map/ppermute | solution.py:444
  70.1 0.1 gather.1.tokens.after
  70.2 0.1 collective-permute-start.15
  70.2 4.0 %up.2.after.hidden = bf16[256,3584]{1,0:T(8,128)(2,1)S(1)} custom-call(bf16[2048,3584]{1,0:T(8,128)(2,1)S(1)} %get-tuple-element.48.after.w_up, bf16[256,2048]{1,0:T(8,128)(2,1)S(1)} %gather.1.tokens.after, bf16[256,2048]{1,0:T(8,128)(2,1)S(1)} %gather.1.tokens.after), custom_call_target="tpu_custom_call" | custom-call | flops 3758096384 | bytes 14680064 | tf_op jit(solution)/shard_map/up/pallas_call | solution.py:679
  74.2 4.1 %up.3.hidden.after = bf16[256,3584]{1,0:T(8,128)(2,1)S(1)} custom-call(bf16[2048,3584]{1,0:T(8,128)(2,1)S(1)} %get-tuple-element.48.after.w_up, bf16[256,2048]{1,0:T(8,128)(2,1)S(1)} %collective-permute-done.15.tokens, bf16[256,3584]{1,0:T(8,128)(2,1)S(1)} %up.2.after.hidden), custom_call_target="tpu_custom_call" | custom-call | flops 3758096384 | bytes 14680064 | tf_op jit(solution)/shard_map/up/pallas_call | solution.py:679
  78.4 2.1 %down.4.after = bf16[256,1024]{1,0:T(8,128)(2,1)S(1)} custom-call(bf16[3584,2048]{1,0:T(8,128)(2,1)S(1)} %get-tuple-element.78.w_down, bf16[256,3584]{1,0:T(8,128)(2,1)S(1)} %up.3.hidden.after, bf16[256,3584]{1,0:T(8,128)(2,1)S(1)} %up.3.hidden.after), custom_call_target="tpu_custom_call" | custom-call | flops 1879048192 | bytes 7340032 | tf_op jit(solution)/shard_map/down/pallas_call | solution.py:695
  80.4 0.6 collective-permute-start.16
  81.0 2.0 %down.5.refs_1_ = bf16[256,1024]{1,0:T(8,128)(2,1)S(1)} custom-call(bf16[3584,2048]{1,0:T(8,128)(2,1)S(1)} %get-tuple-element.78.w_down, bf16[256,3584]{1,0:T(8,128)(2,1)S(1)} %up.2.after.hidden, bf16[256,1024]{1,0:T(8,128)(2,1)S(1)} %down.4.after), custom_call_target="tpu_custom_call" | custom-call | flops 1879048192 | bytes 7340032 | tf_op jit(solution)/shard_map/down/pallas_call | solution.py:695
  83.0 0.1 join.2
  83.2 2.1 %down.6.after = bf16[256,1024]{1,0:T(8,128)(2,1)S(1)} custom-call(bf16[3584,2048]{1,0:T(8,128)(2,1)S(1)} %get-tuple-element.78.w_down, bf16[256,3584]{1,0:T(8,128)(2,1)S(1)} %up.3.hidden.after, bf16[64,1024]{1,0:T(8,128)(2,1)S(1)} %get-tuple-element.83.refs_0_.after), custom_call_target="tpu_custom_call" | custom-call | flops 1879048192 | bytes 7340032 | tf_op jit(solution)/shard_map/down/pallas_call | solution.py:695
  85.2 0.1 collective-permute-start.21
  85.3 0.8 collective-permute-start.17
  86.2 1.5 %collective-permute-start.18 = (bf16[64,1024]{1,0:T(8,128)(2,1)S(1)}, bf16[64,1024]{1,0:T(8,128)(2,1)S(1)}, u32[]{:S(2)}, u32[]{:S(2)}) collective-permute-start(bf16[64,1024]{1,0:T(8,128)(2,1)S(1)} %get-tuple-element.85), channel_id=1, source_target_pairs={{0,4},{1,5},{2,6},{3,7},{4,0},{5,1},{6,2},{7,3},{8,12},{9,13},{10,... | collective-permute-start | bytes 393224 | tf_op jit(solution)/shard_map/ppermute | solution.py:444
  87.7 1.2 %collective-permute-start.19 = (bf16[64,1024]{1,0:T(8,128)(2,1)S(1)}, bf16[64,1024]{1,0:T(8,128)(2,1)S(1)}, u32[]{:S(2)}, u32[]{:S(2)}) collective-permute-start(bf16[64,1024]{1,0:T(8,128)(2,1)S(1)} %get-tuple-element.86), channel_id=1, source_target_pairs={{0,6},{1,7},{2,4},{3,5},{4,2},{5,3},{6,0},{7,1},{8,14},{9,15},{10,... | collective-permute-start | bytes 393224 | tf_op jit(solution)/shard_map/ppermute | solution.py:444
  88.9 2.1 %down.7.refs_1_ = bf16[256,1024]{1,0:T(8,128)(2,1)S(1)} custom-call(bf16[3584,2048]{1,0:T(8,128)(2,1)S(1)} %get-tuple-element.78.w_down, bf16[256,3584]{1,0:T(8,128)(2,1)S(1)} %up.2.after.hidden, bf16[256,1024]{1,0:T(8,128)(2,1)S(1)} %down.6.after), custom_call_target="tpu_custom_call" | custom-call | flops 1879048192 | bytes 7340032 | tf_op jit(solution)/shard_map/down/pallas_call | solution.py:695
  90.9 0.1 join.3
  91.1 0.8 collective-permute-start.22
  91.9 1.5 %collective-permute-start.23 = (bf16[64,1024]{1,0:T(8,128)(2,1)S(1)}, bf16[64,1024]{1,0:T(8,128)(2,1)S(1)}, u32[]{:S(2)}, u32[]{:S(2)}) collective-permute-start(bf16[64,1024]{1,0:T(8,128)(2,1)S(1)} %get-tuple-element.89), channel_id=1, source_target_pairs={{0,4},{1,5},{2,6},{3,7},{4,0},{5,1},{6,2},{7,3},{8,12},{9,13},{10,... | collective-permute-start | bytes 393224 | tf_op jit(solution)/shard_map/ppermute | solution.py:444
  93.5 1.2 %collective-permute-start.24 = (bf16[64,1024]{1,0:T(8,128)(2,1)S(1)}, bf16[64,1024]{1,0:T(8,128)(2,1)S(1)}, u32[]{:S(2)}, u32[]{:S(2)}) collective-permute-start(bf16[64,1024]{1,0:T(8,128)(2,1)S(1)} %get-tuple-element.90), channel_id=1, source_target_pairs={{0,6},{1,7},{2,4},{3,5},{4,2},{5,3},{6,0},{7,1},{8,14},{9,15},{10,... | collective-permute-start | bytes 393224 | tf_op jit(solution)/shard_map/ppermute | solution.py:444
  94.6 0.3 collective-permute-done.19.refs_3_
  94.9 0.3 finish.2
  95.2 1.6 %collective-permute-start.20 = (bf16[128,1024]{1,0:T(8,128)(2,1)S(1)}, bf16[128,1024]{1,0:T(8,128)(2,1)S(1)}, u32[]{:S(2)}, u32[]{:S(2)}) collective-permute-start(bf16[128,1024]{1,0:T(8,128)(2,1)S(1)} %finish.2), channel_id=1, source_target_pairs={{0,8},{8,16},{16,24},{24,0},{1,9},{9,17},{17,25},{25,1},{2,10},{10... | collective-permute-start | bytes 786440 | tf_op jit(solution)/shard_map/ppermute | solution.py:449
  96.8 0.7 collective-permute-done.22.refs_1_
  97.6 2.6 %collective-permute-done.23.refs_2_ = bf16[64,1024]{1,0:T(8,128)(2,1)S(1)} collective-permute-done((bf16[64,1024]{1,0:T(8,128)(2,1)S(1)}, bf16[64,1024]{1,0:T(8,128)(2,1)S(1)}, u32[]{:S(2)}, u32[]{:S(2)}) %collective-permute-start.23) | collective-permute-done | bytes 131104 | tf_op jit(solution)/shard_map/ppermute | solution.py:444
  100.1 0.3 finish.3
  100.5 1.6 %collective-permute-start.25 = (bf16[128,1024]{1,0:T(8,128)(2,1)S(1)}, bf16[128,1024]{1,0:T(8,128)(2,1)S(1)}, u32[]{:S(2)}, u32[]{:S(2)}) collective-permute-start(bf16[128,1024]{1,0:T(8,128)(2,1)S(1)} %finish.3), channel_id=1, source_target_pairs={{0,8},{8,16},{16,24},{24,0},{1,9},{9,17},{17,25},{25,1},{2,10},{10... | collective-permute-start | bytes 786440 | tf_op jit(solution)/shard_map/ppermute | solution.py:449
  102.1 1.8 %collective-permute-done.20 = bf16[128,1024]{1,0:T(8,128)(2,1)S(1)} collective-permute-done((bf16[128,1024]{1,0:T(8,128)(2,1)S(1)}, bf16[128,1024]{1,0:T(8,128)(2,1)S(1)}, u32[]{:S(2)}, u32[]{:S(2)}) %collective-permute-start.20) | collective-permute-done | bytes 262176 | tf_op jit(solution)/shard_map/ppermute | solution.py:449
  103.9 5.6 %collective-permute-done.25 = bf16[128,1024]{1,0:T(8,128)(2,1)S(1)} collective-permute-done((bf16[128,1024]{1,0:T(8,128)(2,1)S(1)}, bf16[128,1024]{1,0:T(8,128)(2,1)S(1)}, u32[]{:S(2)}, u32[]{:S(2)}) %collective-permute-start.25) | collective-permute-done | bytes 262176 | tf_op jit(solution)/shard_map/ppermute | solution.py:449
  109.5 0.8 maximum_bitcast_fusion
  (14 shorter events, 0.0 us)
Async XLA Ops:
  0.0 15.6 %collective-permute-start = (bf16[128,2048]{1,0:T(8,128)(2,1)}, bf16[128,2048]{1,0:T(8,128)(2,1)S(1)}, u32[]{:S(2)}, u32[]{:S(2)}) collective-permute-start(bf16[128,2048]{1,0:T(8,128)(2,1)} %bitcast.23), channel_id=1, source_target_pairs={{0,2},{1,3},{2,0},{3,1},{4,6},{5,7},{6,4},{7,5},{8,10},{9,11},{10,... | collective-permute-start | bytes 1572872 | tf_op jit(solution)/shard_map/ppermute | solution.py:444
  2.9 14.0 %collective-permute-start.2 = (bf16[128,2048]{1,0:T(8,128)(2,1)}, bf16[128,2048]{1,0:T(8,128)(2,1)S(1)}, u32[]{:S(2)}, u32[]{:S(2)}) collective-permute-start(bf16[128,2048]{1,0:T(8,128)(2,1)} %bitcast.24), channel_id=1, source_target_pairs={{0,1},{1,0},{2,3},{3,2},{4,5},{5,4},{6,7},{7,6},{8,9},{9,8},{10,11... | collective-permute-start | bytes 1572872 | tf_op jit(solution)/shard_map/ppermute | solution.py:444
  2.9 14.5 %collective-permute-start.3 = (bf16[2048,128]{1,0:T(8,128)(2,1)}, bf16[2048,128]{1,0:T(8,128)(2,1)S(1)}, u32[]{:S(2)}, u32[]{:S(2)}) collective-permute-start(bf16[2048,128]{1,0:T(8,128)(2,1)} %bitcast.28), channel_id=1, source_target_pairs={{0,4},{1,5},{2,6},{3,7},{4,0},{5,1},{6,2},{7,3},{8,12},{9,13},{10,... | collective-permute-start | bytes 1572872 | tf_op jit(solution)/shard_map/ppermute | solution.py:444
  16.7 3.1 %collective-permute-start.1 = (bf16[128,2048]{1,0:T(8,128)(2,1)S(1)}, bf16[128,2048]{1,0:T(8,128)(2,1)S(1)}, u32[]{:S(2)}, u32[]{:S(2)}) collective-permute-start(bf16[128,2048]{1,0:T(8,128)(2,1)S(1)} %norm.3.normed_near), channel_id=1, source_target_pairs={{0,1},{1,0},{2,3},{3,2},{4,5},{5,4},{6,7},{7,6},{8,9},{9,8},{10,11... | collective-permute-start | bytes 1572872 | tf_op jit(solution)/shard_map/ppermute | solution.py:444
  20.6 8.1 %collective-permute-start.4 = (bf16[2,512,128]{2,1,0:T(8,128)(2,1)S(1)}, bf16[2,512,128]{2,1,0:T(8,128)(2,1)S(1)}, u32[]{:S(2)}, u32[]{:S(2)}) collective-permute-start(bf16[2,512,128]{2,1,0:T(8,128)(2,1)S(1)} %get-tuple-element.52.refs_5_.kv), channel_id=1, source_target_pairs={{0,4},{1,5},{2,6},{3,7},{4,0},{5,1},{6,2},{7,3},{8,12},{9,13},{10,... | collective-permute-start | bytes 786440 | tf_op jit(solution)/shard_map/ppermute | solution.py:444
  29.3 5.9 %collective-permute-start.6 = (bf16[128,512]{1,0:T(8,128)(2,1)S(1)}, bf16[128,512]{1,0:T(8,128)(2,1)S(1)}, u32[]{:S(2)}, u32[]{:S(2)}) collective-permute-start(bf16[128,512]{1,0:T(8,128)(2,1)S(1)} %get-tuple-element.63), channel_id=1, source_target_pairs={{0,2},{1,3},{2,0},{3,1},{4,6},{5,7},{6,4},{7,5},{8,10},{9,11},{10,... | collective-permute-start | bytes 393224 | tf_op jit(solution)/shard_map/ppermute | solution.py:444
  30.6 5.7 %collective-permute-start.7 = (bf16[128,512]{1,0:T(8,128)(2,1)S(1)}, bf16[128,512]{1,0:T(8,128)(2,1)S(1)}, u32[]{:S(2)}, u32[]{:S(2)}) collective-permute-start(bf16[128,512]{1,0:T(8,128)(2,1)S(1)} %get-tuple-element.64), channel_id=1, source_target_pairs={{0,3},{1,2},{2,1},{3,0},{4,7},{5,6},{6,5},{7,4},{8,11},{9,10},{10,... | collective-permute-start | bytes 393224 | tf_op jit(solution)/shard_map/ppermute | solution.py:444
  31.3 5.1 %collective-permute-start.5 = (bf16[128,512]{1,0:T(8,128)(2,1)S(1)}, bf16[128,512]{1,0:T(8,128)(2,1)S(1)}, u32[]{:S(2)}, u32[]{:S(2)}) collective-permute-start(bf16[128,512]{1,0:T(8,128)(2,1)S(1)} %get-tuple-element.62), channel_id=1, source_target_pairs={{0,1},{1,0},{2,3},{3,2},{4,5},{5,4},{6,7},{7,6},{8,9},{9,8},{10,11... | collective-permute-start | bytes 393224 | tf_op jit(solution)/shard_map/ppermute | solution.py:444
  41.8 1.6 %collective-permute-start.8 = (bf16[16,2176]{1,0:T(8,128)(2,1)S(1)}, bf16[16,2176]{1,0:T(8,128)(2,1)S(1)}, u32[]{:S(2)}, u32[]{:S(2)}) collective-permute-start(bf16[16,2176]{1,0:T(8,128)(2,1)S(1)} %get-tuple-element.75.own), channel_id=1, source_target_pairs={{0,1},{1,0},{2,3},{3,2},{4,5},{5,4},{6,7},{7,6},{8,9},{9,8},{10,11... | collective-permute-start | bytes 208904 | tf_op jit(solution)/shard_map/ppermute | solution.py:444
  44.0 6.2 %collective-permute-start.11 = (bf16[16,2176]{1,0:T(8,128)(2,1)S(1)}, bf16[16,2176]{1,0:T(8,128)(2,1)S(1)}, u32[]{:S(2)}, u32[]{:S(2)}) collective-permute-start(bf16[16,2176]{1,0:T(8,128)(2,1)S(1)} %pair.1), channel_id=1, source_target_pairs={{0,6},{1,7},{2,4},{3,5},{4,2},{5,3},{6,0},{7,1},{8,14},{9,15},{10,... | collective-permute-start | bytes 208904 | tf_op jit(solution)/shard_map/ppermute | solution.py:444
  47.4 4.3 %collective-permute-start.10 = (bf16[16,2176]{1,0:T(8,128)(2,1)S(1)}, bf16[16,2176]{1,0:T(8,128)(2,1)S(1)}, u32[]{:S(2)}, u32[]{:S(2)}) collective-permute-start(bf16[16,2176]{1,0:T(8,128)(2,1)S(1)} %pair.1), channel_id=1, source_target_pairs={{0,4},{1,5},{2,6},{3,7},{4,0},{5,1},{6,2},{7,3},{8,12},{9,13},{10,... | collective-permute-start | bytes 208904 | tf_op jit(solution)/shard_map/ppermute | solution.py:444
  47.4 4.6 %collective-permute-start.9 = (bf16[16,2176]{1,0:T(8,128)(2,1)S(1)}, bf16[16,2176]{1,0:T(8,128)(2,1)S(1)}, u32[]{:S(2)}, u32[]{:S(2)}) collective-permute-start(bf16[16,2176]{1,0:T(8,128)(2,1)S(1)} %pair.1), channel_id=1, source_target_pairs={{0,2},{1,3},{2,0},{3,1},{4,6},{5,7},{6,4},{7,5},{8,10},{9,11},{10,... | collective-permute-start | bytes 208904 | tf_op jit(solution)/shard_map/ppermute | solution.py:444
  55.6 9.3 %collective-permute-start.12 = (bf16[64,2048]{1,0:T(8,128)(2,1)S(1)}, bf16[64,2048]{1,0:T(8,128)(2,1)S(1)}, u32[]{:S(2)}, u32[]{:S(2)}) collective-permute-start(bf16[64,2048]{1,0:T(8,128)(2,1)S(1)} %get-tuple-element.80), channel_id=1, source_target_pairs={{0,2},{1,3},{2,0},{3,1},{4,6},{5,7},{6,4},{7,5},{8,10},{9,11},{10,... | collective-permute-start | bytes 786440 | tf_op jit(solution)/shard_map/ppermute | solution.py:444
  56.9 9.0 %collective-permute-start.13 = (bf16[64,2048]{1,0:T(8,128)(2,1)S(1)}, bf16[64,2048]{1,0:T(8,128)(2,1)S(1)}, u32[]{:S(2)}, u32[]{:S(2)}) collective-permute-start(bf16[64,2048]{1,0:T(8,128)(2,1)S(1)} %get-tuple-element.81), channel_id=1, source_target_pairs={{0,4},{1,5},{2,6},{3,7},{4,0},{5,1},{6,2},{7,3},{8,12},{9,13},{10,... | collective-permute-start | bytes 786440 | tf_op jit(solution)/shard_map/ppermute | solution.py:444
  58.0 12.1 %collective-permute-start.14 = (bf16[64,2048]{1,0:T(8,128)(2,1)S(1)}, bf16[64,2048]{1,0:T(8,128)(2,1)S(1)}, u32[]{:S(2)}, u32[]{:S(2)}) collective-permute-start(bf16[64,2048]{1,0:T(8,128)(2,1)S(1)} %get-tuple-element.82), channel_id=1, source_target_pairs={{0,6},{1,7},{2,4},{3,5},{4,2},{5,3},{6,0},{7,1},{8,14},{9,15},{10,... | collective-permute-start | bytes 786440 | tf_op jit(solution)/shard_map/ppermute | solution.py:444
  70.2 4.1 %collective-permute-start.15 = (bf16[256,2048]{1,0:T(8,128)(2,1)S(1)}, bf16[256,2048]{1,0:T(8,128)(2,1)S(1)}, u32[]{:S(2)}, u32[]{:S(2)}) collective-permute-start(bf16[256,2048]{1,0:T(8,128)(2,1)S(1)} %gather.1.tokens.after), channel_id=1, source_target_pairs={{0,1},{1,0},{2,3},{3,2},{4,5},{5,4},{6,7},{7,6},{8,9},{9,8},{10,11... | collective-permute-start | bytes 3145736 | tf_op jit(solution)/shard_map/ppermute | solution.py:444
  80.4 2.6 %collective-permute-start.16 = (bf16[256,1024]{1,0:T(8,128)(2,1)S(1)}, bf16[256,1024]{1,0:T(8,128)(2,1)S(1)}, u32[]{:S(2)}, u32[]{:S(2)}) collective-permute-start(bf16[256,1024]{1,0:T(8,128)(2,1)S(1)} %down.4.after), channel_id=1, source_target_pairs={{0,1},{1,0},{2,3},{3,2},{4,5},{5,4},{6,7},{7,6},{8,9},{9,8},{10,11... | collective-permute-start | bytes 1572872 | tf_op jit(solution)/shard_map/ppermute | solution.py:444
  85.2 5.7 %collective-permute-start.21 = (bf16[256,1024]{1,0:T(8,128)(2,1)S(1)}, bf16[256,1024]{1,0:T(8,128)(2,1)S(1)}, u32[]{:S(2)}, u32[]{:S(2)}) collective-permute-start(bf16[256,1024]{1,0:T(8,128)(2,1)S(1)} %down.6.after), channel_id=1, source_target_pairs={{0,1},{1,0},{2,3},{3,2},{4,5},{5,4},{6,7},{7,6},{8,9},{9,8},{10,11... | collective-permute-start | bytes 1572872 | tf_op jit(solution)/shard_map/ppermute | solution.py:444
  85.3 8.1 %collective-permute-start.17 = (bf16[64,1024]{1,0:T(8,128)(2,1)S(1)}, bf16[64,1024]{1,0:T(8,128)(2,1)S(1)}, u32[]{:S(2)}, u32[]{:S(2)}) collective-permute-start(bf16[64,1024]{1,0:T(8,128)(2,1)S(1)} %get-tuple-element.84), channel_id=1, source_target_pairs={{0,2},{1,3},{2,0},{3,1},{4,6},{5,7},{6,4},{7,5},{8,10},{9,11},{10,... | collective-permute-start | bytes 393224 | tf_op jit(solution)/shard_map/ppermute | solution.py:444
  86.2 8.5 %collective-permute-start.18 = (bf16[64,1024]{1,0:T(8,128)(2,1)S(1)}, bf16[64,1024]{1,0:T(8,128)(2,1)S(1)}, u32[]{:S(2)}, u32[]{:S(2)}) collective-permute-start(bf16[64,1024]{1,0:T(8,128)(2,1)S(1)} %get-tuple-element.85), channel_id=1, source_target_pairs={{0,4},{1,5},{2,6},{3,7},{4,0},{5,1},{6,2},{7,3},{8,12},{9,13},{10,... | collective-permute-start | bytes 393224 | tf_op jit(solution)/shard_map/ppermute | solution.py:444
  87.7 7.2 %collective-permute-start.19 = (bf16[64,1024]{1,0:T(8,128)(2,1)S(1)}, bf16[64,1024]{1,0:T(8,128)(2,1)S(1)}, u32[]{:S(2)}, u32[]{:S(2)}) collective-permute-start(bf16[64,1024]{1,0:T(8,128)(2,1)S(1)} %get-tuple-element.86), channel_id=1, source_target_pairs={{0,6},{1,7},{2,4},{3,5},{4,2},{5,3},{6,0},{7,1},{8,14},{9,15},{10,... | collective-permute-start | bytes 393224 | tf_op jit(solution)/shard_map/ppermute | solution.py:444
  91.1 6.5 %collective-permute-start.22 = (bf16[64,1024]{1,0:T(8,128)(2,1)S(1)}, bf16[64,1024]{1,0:T(8,128)(2,1)S(1)}, u32[]{:S(2)}, u32[]{:S(2)}) collective-permute-start(bf16[64,1024]{1,0:T(8,128)(2,1)S(1)} %get-tuple-element.88), channel_id=1, source_target_pairs={{0,2},{1,3},{2,0},{3,1},{4,6},{5,7},{6,4},{7,5},{8,10},{9,11},{10,... | collective-permute-start | bytes 393224 | tf_op jit(solution)/shard_map/ppermute | solution.py:444
  91.9 8.2 %collective-permute-start.23 = (bf16[64,1024]{1,0:T(8,128)(2,1)S(1)}, bf16[64,1024]{1,0:T(8,128)(2,1)S(1)}, u32[]{:S(2)}, u32[]{:S(2)}) collective-permute-start(bf16[64,1024]{1,0:T(8,128)(2,1)S(1)} %get-tuple-element.89), channel_id=1, source_target_pairs={{0,4},{1,5},{2,6},{3,7},{4,0},{5,1},{6,2},{7,3},{8,12},{9,13},{10,... | collective-permute-start | bytes 393224 | tf_op jit(solution)/shard_map/ppermute | solution.py:444
  93.5 6.7 %collective-permute-start.24 = (bf16[64,1024]{1,0:T(8,128)(2,1)S(1)}, bf16[64,1024]{1,0:T(8,128)(2,1)S(1)}, u32[]{:S(2)}, u32[]{:S(2)}) collective-permute-start(bf16[64,1024]{1,0:T(8,128)(2,1)S(1)} %get-tuple-element.90), channel_id=1, source_target_pairs={{0,6},{1,7},{2,4},{3,5},{4,2},{5,3},{6,0},{7,1},{8,14},{9,15},{10,... | collective-permute-start | bytes 393224 | tf_op jit(solution)/shard_map/ppermute | solution.py:444
  95.2 8.7 %collective-permute-start.20 = (bf16[128,1024]{1,0:T(8,128)(2,1)S(1)}, bf16[128,1024]{1,0:T(8,128)(2,1)S(1)}, u32[]{:S(2)}, u32[]{:S(2)}) collective-permute-start(bf16[128,1024]{1,0:T(8,128)(2,1)S(1)} %finish.2), channel_id=1, source_target_pairs={{0,8},{8,16},{16,24},{24,0},{1,9},{9,17},{17,25},{25,1},{2,10},{10... | collective-permute-start | bytes 786440 | tf_op jit(solution)/shard_map/ppermute | solution.py:449
  100.5 9.0 %collective-permute-start.25 = (bf16[128,1024]{1,0:T(8,128)(2,1)S(1)}, bf16[128,1024]{1,0:T(8,128)(2,1)S(1)}, u32[]{:S(2)}, u32[]{:S(2)}) collective-permute-start(bf16[128,1024]{1,0:T(8,128)(2,1)S(1)} %finish.3), channel_id=1, source_target_pairs={{0,8},{8,16},{16,24},{24,0},{1,9},{9,17},{17,25},{25,1},{2,10},{10... | collective-permute-start | bytes 786440 | tf_op jit(solution)/shard_map/ppermute | solution.py:449

commit v4 on v3

--- a/solution.py
+++ b/solution.py
@@ -376,9 +376,8 @@
         rows = source.shape[0] // number
         for piece in range(number):
             at = pl.ds(piece * rows, rows)
-            copies.append(
-                pltpu.make_async_copy(source.at[at], out.at[at], sems.at[len(copies)])
-            )
+            start, end = (source, out) if number == 1 else (source.at[at], out.at[at])
+            copies.append(pltpu.make_async_copy(start, end, sems.at[len(copies)]))
     for copy in copies:
         copy.start()
     for copy in copies:
@@ -398,44 +397,52 @@
     )(*[in_hbm(array) for array in arrays], after)
 
 
-def gather_kernel(*refs):
+def gather_kernel(after, *refs):
     blocks, out = refs[:-1], refs[-1]
     capacity = blocks[0].shape[0]
     for at, block in enumerate(blocks):
         out[at * capacity : (at + 1) * capacity, :] = block[...]
 
 
-def up_kernel(w_up, tokens, after, hidden):
+def up_kernel(w_up, after, *refs):
+    blocks, hidden = refs[:-1], refs[-1]
+    tokens = jnp.concatenate([block[...] for block in blocks], 0)
     tile = 256 if hidden.shape[1] % 256 == 0 else LANES
     for low in range(0, hidden.shape[1], tile):
         cols = slice(low, low + tile)
-        raised = dot(tokens[...], w_up[:, cols])
+        raised = dot(tokens, w_up[:, cols])
         hidden[:, cols] = (raised * jax.nn.sigmoid(raised)).astype(BF16)
 
 
-def down_kernel(start, w_down, hidden, after, out):
+def down_kernel(start, w_down, hidden, after, *outs):
+    rows, width = outs[0].shape
     tile = 256
-    for low in range(0, out.shape[1], tile):
+    for low in range(0, width, tile):
         part = w_down[:, start + low : start + low + tile]
-        out[:, low : low + tile] = dot(hidden[...], part).astype(BF16)
+        result = dot(hidden[...], part).astype(BF16)
+        for at, out in enumerate(outs):
+            out[:, low : low + tile] = result[at * rows : (at + 1) * rows]
 
 
 def join_kernel(*refs):
-    parts, outs = refs[:-EXPERTS], refs[-EXPERTS:]
+    parts, outs = refs[: 1 - EXPERTS], refs[1 - EXPERTS :]
     capacity = outs[0].shape[0]
-    for slot, out in enumerate(outs):
-        at = slice(slot * capacity, (slot + 1) * capacity)
-        total = parts[0][at, :].astype(F32)
+    for at, out in enumerate(outs):
+        here = slice(at * capacity, (at + 1) * capacity)
+        total = parts[0][here, :].astype(F32)
         for part in parts[1:]:
-            total = total + part[at, :].astype(F32)
+            total = total + part[here, :].astype(F32)
         out[...] = total.astype(BF16)
 
 
 def finish_kernel(start, second, weighting, *refs):
-    blocks, out = refs[:-1], refs[-1]
-    rows = jnp.concatenate([block[...] for block in blocks], 0)
+    blocks, parts, out = refs[: EXPERTS - 1], refs[EXPERTS - 1 : -1], refs[-1]
+    cols = slice(start, start + out.shape[1])
+    total = parts[0][:, cols].astype(F32)
+    for part in parts[1:]:
+        total = total + part[:, cols].astype(F32)
+    rows = jnp.concatenate([total.astype(BF16)] + [block[...] for block in blocks], 0)
     high, low = split(weighting[...])
-    cols = slice(start, start + out.shape[1])
     out[...] = (second[:, cols] + (dot(high, rows) + dot(low, rows))).astype(BF16)
 
 
@@ -492,7 +499,7 @@
     beside = exchange(tokens, "ctx", 1)
     place = jnp.stack([me, key_at, me // parts]).astype(jnp.int32)
 
-    def norm(block, after):
+    def norm(gains, block, after):
         return pl.pallas_call(
             norm_kernel,
             out_shape=shape((rows, width), BF16),
@@ -501,11 +508,15 @@
             compiler_params=params(4),
             cost_estimate=cost(8 * rows * width, 4 * rows * width),
             name="norm",
-        )(place, in_hbm(gains), block, after)
-
-    normed_own = norm(in_hbm(tokens), in_hbm(tokens))
-    raising, lowering = fetch([w_up[0], w_down[0]], (16, 16), normed_own)
-    normed_near = norm(near_tokens, raising)
+        )(place, gains, block, after)
+
+    normed_own = norm(in_hbm(gains), in_hbm(tokens), in_hbm(tokens))
+    here = [w_up[0], w_down[0], gains, w_own, tokens, dt_in[0], dt_out[0], w_bc[0].T]
+    here += [skip_gain, dt_bias, decay_rate, w_router[0].T, routes[0].T]
+    here = fetch(here, (16, 16) + (1,) * 11, normed_own)
+    raising, lowering, gains, w_own, tokens, dt_first, dt_second, w_bct = here[:8]
+    skip_gain, dt_bias, decay_rate, router_t, routes_t = here[8:]
+    normed_near = norm(gains, near_tokens, raising)
     normed_far = exchange(normed_near, "ctx", 1)
     projected = (
         shape((KVH, GROUP * rows, HD), BF16),
@@ -522,11 +533,11 @@
         name="project",
     )(
         place,
-        in_hbm(gains),
+        gains,
         normed_own,
         beside,
         normed_near,
-        in_hbm(w_own),
+        w_own,
         w_other,
     )
     queries, kv = pl.pallas_call(
@@ -540,8 +551,6 @@
     )(place, normed_far, weights, queries, kv)
     turns = shard_count // KVH
     pasts = [exchange(kv, "ctx", turn * KVH) for turn in range(1, turns)]
-    small = [dt_in[0], dt_out[0], w_bc[0].T, tokens, w_router[0].T]
-    in_one, in_two, in_bct, in_tokens, in_router = fetch(small, (2, 2, 1, 2, 1), kv)
     scored = GROUP * rows * group_rows * KVH
     tallies = (shape((KVH, GROUP * rows, LANES), F32),) * 2 + (
         shape((KVH, GROUP * rows, HD), F32),
@@ -597,14 +606,14 @@
         name="prepare",
     )(
         place,
-        in_tokens,
-        in_hbm(gains),
-        in_hbm(skip_gain),
-        in_one,
-        in_two,
-        in_hbm(dt_bias),
-        in_hbm(decay_rate),
-        in_bct,
+        tokens,
+        gains,
+        skip_gain,
+        dt_first,
+        dt_second,
+        dt_bias,
+        decay_rate,
+        w_bct,
         *attended,
     )
     beside_ends = exchange(ends, "ctx", 1)
@@ -651,40 +660,64 @@
         chunk_state,
         chunk_keep,
         bc,
-        in_hbm(gains),
-        in_router,
-        in_hbm(routes[0].T),
+        gains,
+        router_t,
+        routes_t,
         beside_ends,
         *earlier_ends,
     )
 
+    units = raising.shape[1]
+
+    def lift(blocks, after):
+        count = sum(block.shape[0] for block in blocks)
+        return pl.pallas_call(
+            up_kernel,
+            out_shape=shape((count, units), BF16),
+            in_specs=[VMEM, ANY] + [VMEM] * len(blocks),
+            out_specs=VMEM,
+            compiler_params=params(12),
+            cost_estimate=cost(2 * count * width * units, 2 * width * units),
+            name="up",
+        )(raising, after, *blocks)
+
+    def lower(start, span, hidden, after, outs=1):
+        count = hidden.shape[0]
+        return pl.pallas_call(
+            functools.partial(down_kernel, start),
+            out_shape=(shape((count // outs, span), BF16),) * outs,
+            in_specs=[VMEM, VMEM, ANY],
+            out_specs=(VMEM,) * outs,
+            compiler_params=params(12),
+            cost_estimate=cost(2 * count * span * units, 2 * span * units),
+            name="down",
+        )(lowering, hidden, after)
+
     def between_experts(blocks):
-        moved = {slot: exchange(blocks[slot], "ctx", slot * parts) for slot in (3, 1, 2)}
-        return [blocks[0]] + [moved[slot] for slot in range(1, EXPERTS)]
-
-    units = raising.shape[1]
-    expert_rows = EXPERTS * capacity
+        moved = {slot: exchange(blocks[slot - 1], "ctx", slot * parts) for slot in (3, 1, 2)}
+        return [moved[slot] for slot in range(1, EXPERTS)]
+
+    moved = between_experts(packed[1:])
+    stay = [exchange(packed[0], "ctx", turn) if turn else packed[0] for turn in range(parts)]
+    stay_out = lower(0, width, lift(stay, packed[0]), packed[0], parts)
+    stay_sums = [stay_out[0]] + [
+        exchange(stay_out[turn], "ctx", turn) for turn in range(1, parts)
+    ]
+
+    moved_rows = (EXPERTS - 1) * capacity
     arrived = pl.pallas_call(
         gather_kernel,
-        out_shape=shape((expert_rows, width), BF16),
-        in_specs=[VMEM] * EXPERTS,
+        out_shape=shape((moved_rows, width), BF16),
+        in_specs=[ANY] + [VMEM] * (EXPERTS - 1),
         out_specs=VMEM,
         compiler_params=params(4),
-        cost_estimate=cost(0, 4 * expert_rows * width),
+        cost_estimate=cost(0, 4 * moved_rows * width),
         name="gather",
-    )(*between_experts(packed))
+    )(stay_sums[-1], *moved)
     hiddens = []
     after = arrived
     for turn in range(parts):
-        after = pl.pallas_call(
-            up_kernel,
-            out_shape=shape((expert_rows, units), BF16),
-            in_specs=[VMEM, VMEM, ANY],
-            out_specs=VMEM,
-            compiler_params=params(12),
-            cost_estimate=cost(2 * expert_rows * width * units, 2 * width * units),
-            name="up",
-        )(raising, exchange(arrived, "ctx", turn) if turn else arrived, after)
+        after = lift([exchange(arrived, "ctx", turn) if turn else arrived], after)
         hiddens.append(after)
     chunk_width = width // CHUNKS
     results = []
@@ -692,28 +725,16 @@
         start = chunk * chunk_width
         sums = []
         for turn in reversed(range(parts)):
-            part_out = pl.pallas_call(
-                functools.partial(down_kernel, start),
-                out_shape=shape((expert_rows, chunk_width), BF16),
-                in_specs=[VMEM, VMEM, ANY],
-                out_specs=VMEM,
-                compiler_params=params(12),
-                cost_estimate=cost(
-                    2 * expert_rows * chunk_width * units, 2 * chunk_width * units
-                ),
-                name="down",
-            )(lowering, hiddens[turn], after)
+            (part_out,) = lower(start, chunk_width, hiddens[turn], after)
             sums.append(exchange(part_out, "ctx", turn) if turn else part_out)
             after = part_out
         joined = pl.pallas_call(
             join_kernel,
-            out_shape=(shape((capacity, chunk_width), BF16),) * EXPERTS,
+            out_shape=(shape((capacity, chunk_width), BF16),) * (EXPERTS - 1),
             in_specs=[VMEM] * parts,
-            out_specs=(VMEM,) * EXPERTS,
+            out_specs=(VMEM,) * (EXPERTS - 1),
             compiler_params=params(8),
-            cost_estimate=cost(
-                4 * EXPERTS * capacity * chunk_width, 8 * EXPERTS * capacity * chunk_width
-            ),
+            cost_estimate=cost(4 * moved_rows * chunk_width, 8 * moved_rows * chunk_width),
             name="join",
         )(*sums)
         after = joined[0]
@@ -721,14 +742,14 @@
         finished = pl.pallas_call(
             functools.partial(finish_kernel, start),
             out_shape=shape((rows, chunk_width), BF16),
-            in_specs=[VMEM] * (2 + EXPERTS),
+            in_specs=[VMEM] * (1 + EXPERTS + parts),
             out_specs=VMEM,
             compiler_params=params(8),
             cost_estimate=cost(
                 4 * rows * EXPERTS * capacity * chunk_width, 10 * rows * chunk_width
             ),
             name="finish",
-        )(second, weighting, *returned)
+        )(second, weighting, *returned, *stay_sums)
         results.append(shifted(finished, "segment", 1))
     return jnp.concatenate(results, 1)[None]
 

time: 111 us -> 110 us (level)
  waiting for transfers between devices: 31.7 us -> 28.7 us
  starting transfers between devices: 28.1 us -> 30.5 us
    ppermute x24 -> x26, waiting for transfers between devices: 24.3 us -> 19.9 us  [exchange(): return lax.ppermute(value, axis, [(at, at ^ mask) for at in range(count)])]
    ppermute x24 -> x26, starting transfers between devices: 24.8 us -> 27.2 us  [exchange(): return lax.ppermute(value, axis, [(at, at ^ mask) for at in range(count)])]
    pallas_call x7 -> x9, Pallas kernels: 16.4 us -> 17.8 us  [the longest x5 9.23 us: lower(): pl.pallas_call(functools.partial(down_kernel, start), out_shape=(shape((c...]
    ppermute x2, waiting for transfers between devices: 7.41 us -> 8.78 us  [shifted(): lax.ppermute(value, axis, [(at, (at + steps) % count) for at in range(cou...]
    pallas_call x2 -> x1, Pallas kernels: 11.1 us -> 10.3 us  [fetch(): pl.pallas_call(functools.partial(fetch_kernel, pieces), out_shape=tuple((...]
  transfers between devices with their start and end apart: 26 -> 28, of which waited for: 15 -> 13; matrix products, arithmetic and copies ran while one was open for 0% -> 0% of each run, Pallas kernels for 27% -> 29%
where the time goes in v4:
time: 110 us; the launch traced here: 109 us
  Pallas kernels  49.2 us (45%)
  starting transfers between devices  30.5 us (28%)
  waiting for transfers between devices  28.7 us (26%)
    ppermute x26, starting transfers between devices, exchange(): return lax.ppermute(value, axis, [(at, at ^ mask) for at in range(count)])  27.2 us
    ppermute x26, waiting for transfers between devices, exchange(): return lax.ppermute(value, axis, [(at, at ^ mask) for at in range(count)])  19.9 us
    pallas_call x1, Pallas kernels, fetch(): pl.pallas_call(functools.partial(fetch_kernel, pieces), out_shape=tuple((...  10.3 us
    pallas_call x5, Pallas kernels, lower(): pl.pallas_call(functools.partial(down_kernel, start), out_shape=(shape((c...  9.23 us
    ppermute x2, waiting for transfers between devices, shifted(): lax.ppermute(value, axis, [(at, (at + steps) % count) for at in range(cou...  8.78 us
    pallas_call x3, Pallas kernels, lift(): pl.pallas_call(up_kernel, out_shape=shape((count, units), BF16), in_specs...  8.49 us
    pallas_call x1, Pallas kernels, on_device(): pl.pallas_call(prepare_kernel, out_shape=(shape((rows, width), F32), shap...  5.15 us
    ppermute x2, starting transfers between devices, shifted(): lax.ppermute(value, axis, [(at, (at + steps) % count) for at in range(cou...  3.25 us
  transfers between devices with their start and end apart: 28, of which 13 were waited for; matrix products, arithmetic and copies ran while one was open for 0% of the time, Pallas kernels for 29%

profile of v4, /device:TPU:0, one launch (start us, length us, event | category | flops | bytes accessed | tf_op | source)
XLA Modules:
  0.0 109.5 jit_solution(1532058095060915967)
XLA Ops:
  0.0 2.9 %collective-permute-start = (bf16[128,2048]{1,0:T(8,128)(2,1)}, bf16[128,2048]{1,0:T(8,128)(2,1)S(1)}, u32[]{:S(2)}, u32[]{:S(2)}) collective-permute-start(bf16[128,2048]{1,0:T(8,128)(2,1)} %bitcast.23), channel_id=1, source_target_pairs={{0,2},{1,3},{2,0},{3,1},{4,6},{5,7},{6,4},{7,5},{8,10},{9,11},{10,... | collective-permute-start | bytes 1572872 | tf_op jit(solution)/shard_map/ppermute | solution.py:451
  2.9 1.5 %collective-permute-start.3 = (bf16[2048,128]{1,0:T(8,128)(2,1)}, bf16[2048,128]{1,0:T(8,128)(2,1)}, u32[]{:S(2)}, u32[]{:S(2)}) collective-permute-start(bf16[2048,128]{1,0:T(8,128)(2,1)} %bitcast.30), channel_id=1, source_target_pairs={{0,4},{1,5},{2,6},{3,7},{4,0},{5,1},{6,2},{7,3},{8,12},{9,13},{10,... | collective-permute-start | bytes 1572872 | tf_op jit(solution)/shard_map/ppermute | solution.py:451
  4.5 0.1 pad_add_fusion.place
  4.5 1.4 %norm.2.refs_13_.normed_own = bf16[128,2048]{1,0:T(8,128)(2,1)S(1)} custom-call(s32[3]{0:T(128)S(1)} %pad_add_fusion.place, f32[3,1,2048]{2,1,0:T(1,128)} %bitcast.33, bf16[128,2048]{1,0:T(8,128)(2,1)} %bitcast.25, bf16[128,2048]{1,0:T(8,128)(2,1)} %bitcast.26), custom_call_target="tpu_custom_call" | custom-call | flops 2097152 | bytes 1048576 | tf_op jit(solution)/shard_map/norm/pallas_call | solution.py:503
  5.9 10.3 %fetch.1 = (bf16[2048,3584]{1,0:T(8,128)(2,1)S(1)}, bf16[3584,2048]{1,0:T(8,128)(2,1)S(1)}, f32[3,1,2048]{2,1,0:T(1,128)S(1)}, bf16[2048,128]{1,0:T(8,128)(2,1)S...) custom-call(bf16[2048,3584]{1,0:T(8,128)(2,1)} %bitcast.21, ...), custom_call_target="tpu_custom_call" | custom-call | bytes 63259648 | tf_op jit(solution)/shard_map/fetch/pallas_call | solution.py:388
  16.3 0.9 norm.3.normed_near
  17.2 0.3 collective-permute-start.1
  17.5 0.1 collective-permute-done.3.w_other
  17.6 2.2 %project.1 = (bf16[4,512,128]{2,1,0:T(8,128)(2,1)S(1)}, bf16[2,512,128]{2,1,0:T(8,128)(2,1)S(1)}, bf16[2048,256]{1,0:T(8,128)(2,1)S(1)}) custom-call(s32[3]{0:T(128)S(1)} %pad_add_fusion.place, f32[3,1,2048]{2,1,0:T(1,128)S(1)} %get-tuple-element.55.gains, bf16[128,2048]{1,0:T(8,128)(2,1)S(1)} %norm.2.refs_13_.normed_own, ...), custom_call_target="tpu_custom_call" | custom-call | flops 402653184 | bytes 6291456 | tf_op jit(solution)/shard_map/project/pallas_call | solution.py:525
  19.8 0.9 project_last.1
  20.7 1.6 %collective-permute-start.4 = (bf16[2,512,128]{2,1,0:T(8,128)(2,1)S(1)}, bf16[2,512,128]{2,1,0:T(8,128)(2,1)S(1)}, u32[]{:S(2)}, u32[]{:S(2)}) collective-permute-start(bf16[2,512,128]{2,1,0:T(8,128)(2,1)S(1)} %get-tuple-element.68.kv), channel_id=1, source_target_pairs={{0,4},{1,5},{2,6},{3,7},{4,0},{5,1},{6,2},{7,3},{8,12},{9,13},{10,... | collective-permute-start | bytes 786440 | tf_op jit(solution)/shard_map/ppermute | solution.py:451
  22.3 2.5 %near.1 = (f32[4,512,128]{2,1,0:T(8,128)S(1)}, f32[4,512,128]{2,1,0:T(8,128)S(1)}, f32[4,512,128]{2,1,0:T(8,128)S(1)}) custom-call(s32[3]{0:T(128)S(1)} %pad_add_fusion.place, bf16[4,512,128]{2,1,0:T(8,128)(2,1)S(1)} %get-tuple-element.67.q, bf16[2,512,128]{2,1,0:T(8,128)(2,1)S(1)} %get-tuple-element.68.kv), custom_call_target="tpu_custom_call" | custom-call | flops 536870912 | bytes 4194304 | tf_op jit(solution)/shard_map/near/pallas_call | solution.py:558
  24.9 4.3 %collective-permute-done.4.past = bf16[2,512,128]{2,1,0:T(8,128)(2,1)S(1)} collective-permute-done((bf16[2,512,128]{2,1,0:T(8,128)(2,1)S(1)}, bf16[2,512,128]{2,1,0:T(8,128)(2,1)S(1)}, u32[]{:S(2)}, u32[]{:S(2)}) %collective-permute-start.4) | collective-permute-done | bytes 262176 | tf_op jit(solution)/shard_map/ppermute | solution.py:451
  29.2 0.6 far.3
  29.8 0.6 collective-permute-start.6
  30.4 0.1 collective-permute-start.7
  30.6 0.6 far.2
  31.2 1.5 %collective-permute-start.5 = (bf16[128,512]{1,0:T(8,128)(2,1)S(1)}, bf16[128,512]{1,0:T(8,128)(2,1)S(1)}, u32[]{:S(2)}, u32[]{:S(2)}) collective-permute-start(bf16[128,512]{1,0:T(8,128)(2,1)S(1)} %get-tuple-element.73), channel_id=1, source_target_pairs={{0,1},{1,0},{2,3},{3,2},{4,5},{5,4},{6,7},{7,6},{8,9},{9,8},{10,11... | collective-permute-start | bytes 393224 | tf_op jit(solution)/shard_map/ppermute | solution.py:451
  32.7 3.5 %collective-permute-done.6.refs_2_ = bf16[128,512]{1,0:T(8,128)(2,1)S(1)} collective-permute-done((bf16[128,512]{1,0:T(8,128)(2,1)S(1)}, bf16[128,512]{1,0:T(8,128)(2,1)S(1)}, u32[]{:S(2)}, u32[]{:S(2)}) %collective-permute-start.6) | collective-permute-done | bytes 131104 | tf_op jit(solution)/shard_map/ppermute | solution.py:451
  36.2 5.2 %prepare.1 = (f32[128,2048]{1,0:T(8,128)S(1)}, f32[128,2048]{1,0:T(8,128)S(1)}, f32[128,2048]{1,0:T(8,128)S(1)}, f32[256,2048]{1,0:T(8,128)S(1)}, f32[16,2048]{1...) custom-call(s32[3]{0:T(128)S(1)} %pad_add_fusion.place, ...), custom_call_target="tpu_custom_call" | custom-call | flops 671088640 | bytes 7864320 | tf_op jit(solution)/shard_map/prepare/pallas_call | solution.py:584
  41.4 1.3 %collective-permute-start.8 = (bf16[16,2176]{1,0:T(8,128)(2,1)S(1)}, bf16[16,2176]{1,0:T(8,128)(2,1)S(1)}, u32[]{:S(2)}, u32[]{:S(2)}) collective-permute-start(bf16[16,2176]{1,0:T(8,128)(2,1)S(1)} %get-tuple-element.87.own), channel_id=1, source_target_pairs={{0,1},{1,0},{2,3},{3,2},{4,5},{5,4},{6,7},{7,6},{8,9},{9,8},{10,11... | collective-permute-start | bytes 208904 | tf_op jit(solution)/shard_map/ppermute | solution.py:451
  42.7 0.9 collective-permute-done.8.other.beside
  43.6 0.6 pair.1
  44.2 2.7 %collective-permute-start.11 = (bf16[16,2176]{1,0:T(8,128)(2,1)S(1)}, bf16[16,2176]{1,0:T(8,128)(2,1)S(1)}, u32[]{:S(2)}, u32[]{:S(2)}) collective-permute-start(bf16[16,2176]{1,0:T(8,128)(2,1)S(1)} %pair.1), channel_id=1, source_target_pairs={{0,6},{1,7},{2,4},{3,5},{4,2},{5,3},{6,0},{7,1},{8,14},{9,15},{10,... | collective-permute-start | bytes 208904 | tf_op jit(solution)/shard_map/ppermute | solution.py:451
  46.8 1.1 collective-permute-start.9
  47.9 2.1 %within.1 = (f32[128,2048]{1,0:T(8,128)S(1)}, f32[128,2048]{1,0:T(8,128)S(1)}) custom-call(f32[128,32]{1,0:T(8,128)S(1)} %get-tuple-element.76.bc, f32[32,128]{1,0:T(8,128)S(1)} %get-tuple-element.77.bct, f32[128,2048]{1,0:T(8,128)S(1)} %get-tuple-element.78.base, f32[128,2048]{1,0:T(8,128)S(1)} %get-tuple-element.79.keep, ...), custom_call_target="tpu_custom_call" | custom-call | flops 10485760 | bytes 5242880 | tf_op jit(solution)/shard_map/within/pallas_call | solution.py:630
  50.1 1.1 collective-permute-done.10.refs_1_
  51.1 0.7 collective-permute-done.9.refs_0_
  51.8 3.2 %route.1 = (f32[128,2048]{1,0:T(8,128)S(1)}, f32[128,256]{1,0:T(8,128)S(1)}, bf16[64,2048]{1,0:T(8,128)(2,1)S(1)}, bf16[64,2048]{1,0:T(8,128)(2,1)S(1)}, bf16[64...) custom-call(s32[3]{0:T(128)S(1)} %pad_add_fusion.place, f32[128,2048]{1,0:T(8,128)S(1)} %get-tuple-element.81.before, ...), custom_call_target="tpu_custom_call" | custom-call | flops 671088640 | bytes 7864320 | tf_op jit(solution)/shard_map/route/pallas_call | solution.py:640
  55.1 0.1 collective-permute-start.12
  55.1 1.0 collective-permute-start.14
  56.1 1.5 %collective-permute-start.15 = (bf16[64,2048]{1,0:T(8,128)(2,1)S(1)}, bf16[64,2048]{1,0:T(8,128)(2,1)S(1)}, u32[]{:S(2)}, u32[]{:S(2)}) collective-permute-start(bf16[64,2048]{1,0:T(8,128)(2,1)S(1)} %get-tuple-element.94), channel_id=1, source_target_pairs={{0,4},{1,5},{2,6},{3,7},{4,0},{5,1},{6,2},{7,3},{8,12},{9,13},{10,... | collective-permute-start | bytes 786440 | tf_op jit(solution)/shard_map/ppermute | solution.py:451
  57.6 1.1 collective-permute-start.16
  58.7 2.1 %up.3.hidden = bf16[128,3584]{1,0:T(8,128)(2,1)S(1)} custom-call(bf16[2048,3584]{1,0:T(8,128)(2,1)S(1)} %get-tuple-element.62.after.w_up, bf16[64,2048]{1,0:T(8,128)(2,1)S(1)} %get-tuple-element.91.after.refs_0_, bf16[64,2048]{1,0:T(8,128)(2,1)S(1)} %get-tuple-element.91.after.refs_0_, bf16[64,2048]{1,0:T(8,128)(2,1)S(1)} %collective-permute-done.12.refs_1_), custom_call_target="tpu_custom_call" | custom-call | flops 1879048192 | bytes 14680064 | tf_op jit(solution)/shard_map/up/pallas_call | solution.py:674
  60.8 2.3 %down.5 = (bf16[64,2048]{1,0:T(8,128)(2,1)S(1)}, bf16[64,2048]{1,0:T(8,128)(2,1)S(1)}) custom-call(bf16[3584,2048]{1,0:T(8,128)(2,1)S(1)} %get-tuple-element.90.w_down, bf16[128,3584]{1,0:T(8,128)(2,1)S(1)} %up.3.hidden, bf16[64,2048]{1,0:T(8,128)(2,1)S(1)} %get-tuple-element.91.after.refs_0_), custom_call_target="tpu_custom_call" | custom-call | flops 1879048192 | bytes 14680064 | tf_op jit(solution)/shard_map/down/pallas_call | solution.py:686
  63.2 1.1 collective-permute-done.14.refs_0_
  64.3 4.9 %collective-permute-done.15.refs_1_ = bf16[64,2048]{1,0:T(8,128)(2,1)S(1)} collective-permute-done((bf16[64,2048]{1,0:T(8,128)(2,1)S(1)}, bf16[64,2048]{1,0:T(8,128)(2,1)S(1)}, u32[]{:S(2)}, u32[]{:S(2)}) %collective-permute-start.15) | collective-permute-done | bytes 262176 | tf_op jit(solution)/shard_map/ppermute | solution.py:451
  69.2 1.1 collective-permute-done.16.refs_2_
  70.3 0.1 collective-permute-start.17
  70.4 3.2 %up.4.after.hidden = bf16[192,3584]{1,0:T(8,128)(2,1)S(1)} custom-call(bf16[2048,3584]{1,0:T(8,128)(2,1)S(1)} %get-tuple-element.62.after.w_up, bf16[192,2048]{1,0:T(8,128)(2,1)S(1)} %gather.1.after.refs_0_, bf16[192,2048]{1,0:T(8,128)(2,1)S(1)} %gather.1.after.refs_0_), custom_call_target="tpu_custom_call" | custom-call | flops 2818572288 | bytes 14680064 | tf_op jit(solution)/shard_map/up/pallas_call | solution.py:674
  73.6 3.2 %up.5.hidden.after = bf16[192,3584]{1,0:T(8,128)(2,1)S(1)} custom-call(bf16[2048,3584]{1,0:T(8,128)(2,1)S(1)} %get-tuple-element.62.after.w_up, bf16[192,3584]{1,0:T(8,128)(2,1)S(1)} %up.4.after.hidden, bf16[192,2048]{1,0:T(8,128)(2,1)S(1)} %collective-permute-done.17.refs_0_), custom_call_target="tpu_custom_call" | custom-call | flops 2818572288 | bytes 14680064 | tf_op jit(solution)/shard_map/up/pallas_call | solution.py:674
  76.8 1.7 %down.6.after = bf16[192,1024]{1,0:T(8,128)(2,1)S(1)} custom-call(bf16[3584,2048]{1,0:T(8,128)(2,1)S(1)} %get-tuple-element.90.w_down, bf16[192,3584]{1,0:T(8,128)(2,1)S(1)} %up.5.hidden.after, bf16[192,3584]{1,0:T(8,128)(2,1)S(1)} %up.5.hidden.after), custom_call_target="tpu_custom_call" | custom-call | flops 1409286144 | bytes 7340032 | tf_op jit(solution)/shard_map/down/pallas_call | solution.py:686
  78.5 0.5 collective-permute-start.18
  79.0 1.7 %down.7.refs_1_ = bf16[192,1024]{1,0:T(8,128)(2,1)S(1)} custom-call(bf16[3584,2048]{1,0:T(8,128)(2,1)S(1)} %get-tuple-element.90.w_down, bf16[192,3584]{1,0:T(8,128)(2,1)S(1)} %up.4.after.hidden, bf16[192,1024]{1,0:T(8,128)(2,1)S(1)} %down.6.after), custom_call_target="tpu_custom_call" | custom-call | flops 1409286144 | bytes 7340032 | tf_op jit(solution)/shard_map/down/pallas_call | solution.py:686
  80.7 0.1 join.2
  80.8 1.9 %down.8.after = bf16[192,1024]{1,0:T(8,128)(2,1)S(1)} custom-call(bf16[3584,2048]{1,0:T(8,128)(2,1)S(1)} %get-tuple-element.90.w_down, bf16[192,3584]{1,0:T(8,128)(2,1)S(1)} %up.5.hidden.after, bf16[64,1024]{1,0:T(8,128)(2,1)S(1)} %get-tuple-element.96.after), custom_call_target="tpu_custom_call" | custom-call | flops 1409286144 | bytes 7340032 | tf_op jit(solution)/shard_map/down/pallas_call | solution.py:686
  82.7 0.1 collective-permute-start.23
  82.8 1.1 %collective-permute-start.19 = (bf16[64,1024]{1,0:T(8,128)(2,1)S(1)}, bf16[64,1024]{1,0:T(8,128)(2,1)S(1)}, u32[]{:S(2)}, u32[]{:S(2)}) collective-permute-start(bf16[64,1024]{1,0:T(8,128)(2,1)S(1)} %get-tuple-element.96.after), channel_id=1, source_target_pairs={{0,2},{1,3},{2,0},{3,1},{4,6},{5,7},{6,4},{7,5},{8,10},{9,11},{10,... | collective-permute-start | bytes 393224 | tf_op jit(solution)/shard_map/ppermute | solution.py:451
  83.9 1.2 %collective-permute-start.20 = (bf16[64,1024]{1,0:T(8,128)(2,1)S(1)}, bf16[64,1024]{1,0:T(8,128)(2,1)S(1)}, u32[]{:S(2)}, u32[]{:S(2)}) collective-permute-start(bf16[64,1024]{1,0:T(8,128)(2,1)S(1)} %get-tuple-element.97), channel_id=1, source_target_pairs={{0,4},{1,5},{2,6},{3,7},{4,0},{5,1},{6,2},{7,3},{8,12},{9,13},{10,... | collective-permute-start | bytes 393224 | tf_op jit(solution)/shard_map/ppermute | solution.py:451
  85.1 1.3 %collective-permute-start.21 = (bf16[64,1024]{1,0:T(8,128)(2,1)S(1)}, bf16[64,1024]{1,0:T(8,128)(2,1)S(1)}, u32[]{:S(2)}, u32[]{:S(2)}) collective-permute-start(bf16[64,1024]{1,0:T(8,128)(2,1)S(1)} %get-tuple-element.98), channel_id=1, source_target_pairs={{0,6},{1,7},{2,4},{3,5},{4,2},{5,3},{6,0},{7,1},{8,14},{9,15},{10,... | collective-permute-start | bytes 393224 | tf_op jit(solution)/shard_map/ppermute | solution.py:451
  86.4 1.7 %down.9.refs_1_ = bf16[192,1024]{1,0:T(8,128)(2,1)S(1)} custom-call(bf16[3584,2048]{1,0:T(8,128)(2,1)S(1)} %get-tuple-element.90.w_down, bf16[192,3584]{1,0:T(8,128)(2,1)S(1)} %up.4.after.hidden, bf16[192,1024]{1,0:T(8,128)(2,1)S(1)} %down.8.after), custom_call_target="tpu_custom_call" | custom-call | flops 1409286144 | bytes 7340032 | tf_op jit(solution)/shard_map/down/pallas_call | solution.py:686
  88.0 0.1 join.3
  88.1 1.1 %collective-permute-start.24 = (bf16[64,1024]{1,0:T(8,128)(2,1)S(1)}, bf16[64,1024]{1,0:T(8,128)(2,1)S(1)}, u32[]{:S(2)}, u32[]{:S(2)}) collective-permute-start(bf16[64,1024]{1,0:T(8,128)(2,1)S(1)} %get-tuple-element.100), channel_id=1, source_target_pairs={{0,2},{1,3},{2,0},{3,1},{4,6},{5,7},{6,4},{7,5},{8,10},{9,11},{10,... | collective-permute-start | bytes 393224 | tf_op jit(solution)/shard_map/ppermute | solution.py:451
  89.3 1.2 %collective-permute-start.25 = (bf16[64,1024]{1,0:T(8,128)(2,1)S(1)}, bf16[64,1024]{1,0:T(8,128)(2,1)S(1)}, u32[]{:S(2)}, u32[]{:S(2)}) collective-permute-start(bf16[64,1024]{1,0:T(8,128)(2,1)S(1)} %get-tuple-element.101), channel_id=1, source_target_pairs={{0,4},{1,5},{2,6},{3,7},{4,0},{5,1},{6,2},{7,3},{8,12},{9,13},{10,... | collective-permute-start | bytes 393224 | tf_op jit(solution)/shard_map/ppermute | solution.py:451
  90.5 0.7 collective-permute-done.20.refs_1_
  91.2 3.3 %collective-permute-start.26 = (bf16[64,1024]{1,0:T(8,128)(2,1)S(1)}, bf16[64,1024]{1,0:T(8,128)(2,1)S(1)}, u32[]{:S(2)}, u32[]{:S(2)}) collective-permute-start(bf16[64,1024]{1,0:T(8,128)(2,1)S(1)} %get-tuple-element.102), channel_id=1, source_target_pairs={{0,6},{1,7},{2,4},{3,5},{4,2},{5,3},{6,0},{7,1},{8,14},{9,15},{10,... | collective-permute-start | bytes 393224 | tf_op jit(solution)/shard_map/ppermute | solution.py:451
  94.5 0.3 finish.2
  94.8 1.6 %collective-permute-start.22 = (bf16[128,1024]{1,0:T(8,128)(2,1)S(1)}, bf16[128,1024]{1,0:T(8,128)(2,1)S(1)}, u32[]{:S(2)}, u32[]{:S(2)}) collective-permute-start(bf16[128,1024]{1,0:T(8,128)(2,1)S(1)} %finish.2), channel_id=1, source_target_pairs={{0,8},{8,16},{16,24},{24,0},{1,9},{9,17},{17,25},{25,1},{2,10},{10... | collective-permute-start | bytes 786440 | tf_op jit(solution)/shard_map/ppermute | solution.py:456
  96.5 1.5 %collective-permute-done.26.refs_2_ = bf16[64,1024]{1,0:T(8,128)(2,1)S(1)} collective-permute-done((bf16[64,1024]{1,0:T(8,128)(2,1)S(1)}, bf16[64,1024]{1,0:T(8,128)(2,1)S(1)}, u32[]{:S(2)}, u32[]{:S(2)}) %collective-permute-start.26) | collective-permute-done | bytes 131104 | tf_op jit(solution)/shard_map/ppermute | solution.py:451
  97.9 0.3 finish.3
  98.3 1.6 %collective-permute-start.27 = (bf16[128,1024]{1,0:T(8,128)(2,1)S(1)}, bf16[128,1024]{1,0:T(8,128)(2,1)S(1)}, u32[]{:S(2)}, u32[]{:S(2)}) collective-permute-start(bf16[128,1024]{1,0:T(8,128)(2,1)S(1)} %finish.3), channel_id=1, source_target_pairs={{0,8},{8,16},{16,24},{24,0},{1,9},{9,17},{17,25},{25,1},{2,10},{10... | collective-permute-start | bytes 786440 | tf_op jit(solution)/shard_map/ppermute | solution.py:456
  99.9 4.2 %collective-permute-done.22 = bf16[128,1024]{1,0:T(8,128)(2,1)S(1)} collective-permute-done((bf16[128,1024]{1,0:T(8,128)(2,1)S(1)}, bf16[128,1024]{1,0:T(8,128)(2,1)S(1)}, u32[]{:S(2)}, u32[]{:S(2)}) %collective-permute-start.22) | collective-permute-done | bytes 262176 | tf_op jit(solution)/shard_map/ppermute | solution.py:456
  104.1 4.5 %collective-permute-done.27 = bf16[128,1024]{1,0:T(8,128)(2,1)S(1)} collective-permute-done((bf16[128,1024]{1,0:T(8,128)(2,1)S(1)}, bf16[128,1024]{1,0:T(8,128)(2,1)S(1)}, u32[]{:S(2)}, u32[]{:S(2)}) %collective-permute-start.27) | collective-permute-done | bytes 262176 | tf_op jit(solution)/shard_map/ppermute | solution.py:456
  108.7 0.8 maximum_bitcast_fusion
  (19 shorter events, 0.2 us)
Async XLA Ops:
  0.0 16.3 %collective-permute-start = (bf16[128,2048]{1,0:T(8,128)(2,1)}, bf16[128,2048]{1,0:T(8,128)(2,1)S(1)}, u32[]{:S(2)}, u32[]{:S(2)}) collective-permute-start(bf16[128,2048]{1,0:T(8,128)(2,1)} %bitcast.23), channel_id=1, source_target_pairs={{0,2},{1,3},{2,0},{3,1},{4,6},{5,7},{6,4},{7,5},{8,10},{9,11},{10,... | collective-permute-start | bytes 1572872 | tf_op jit(solution)/shard_map/ppermute | solution.py:451
  2.9 14.5 %collective-permute-start.2 = (bf16[128,2048]{1,0:T(8,128)(2,1)}, bf16[128,2048]{1,0:T(8,128)(2,1)S(1)}, u32[]{:S(2)}, u32[]{:S(2)}) collective-permute-start(bf16[128,2048]{1,0:T(8,128)(2,1)} %bitcast.24), channel_id=1, source_target_pairs={{0,1},{1,0},{2,3},{3,2},{4,5},{5,4},{6,7},{7,6},{8,9},{9,8},{10,11... | collective-permute-start | bytes 1572872 | tf_op jit(solution)/shard_map/ppermute | solution.py:451
  2.9 14.7 %collective-permute-start.3 = (bf16[2048,128]{1,0:T(8,128)(2,1)}, bf16[2048,128]{1,0:T(8,128)(2,1)}, u32[]{:S(2)}, u32[]{:S(2)}) collective-permute-start(bf16[2048,128]{1,0:T(8,128)(2,1)} %bitcast.30), channel_id=1, source_target_pairs={{0,4},{1,5},{2,6},{3,7},{4,0},{5,1},{6,2},{7,3},{8,12},{9,13},{10,... | collective-permute-start | bytes 1572872 | tf_op jit(solution)/shard_map/ppermute | solution.py:451
  17.2 2.7 %collective-permute-start.1 = (bf16[128,2048]{1,0:T(8,128)(2,1)S(1)}, bf16[128,2048]{1,0:T(8,128)(2,1)S(1)}, u32[]{:S(2)}, u32[]{:S(2)}) collective-permute-start(bf16[128,2048]{1,0:T(8,128)(2,1)S(1)} %norm.3.normed_near), channel_id=1, source_target_pairs={{0,1},{1,0},{2,3},{3,2},{4,5},{5,4},{6,7},{7,6},{8,9},{9,8},{10,11... | collective-permute-start | bytes 1572872 | tf_op jit(solution)/shard_map/ppermute | solution.py:451
  20.7 8.4 %collective-permute-start.4 = (bf16[2,512,128]{2,1,0:T(8,128)(2,1)S(1)}, bf16[2,512,128]{2,1,0:T(8,128)(2,1)S(1)}, u32[]{:S(2)}, u32[]{:S(2)}) collective-permute-start(bf16[2,512,128]{2,1,0:T(8,128)(2,1)S(1)} %get-tuple-element.68.kv), channel_id=1, source_target_pairs={{0,4},{1,5},{2,6},{3,7},{4,0},{5,1},{6,2},{7,3},{8,12},{9,13},{10,... | collective-permute-start | bytes 786440 | tf_op jit(solution)/shard_map/ppermute | solution.py:451
  29.8 6.4 %collective-permute-start.6 = (bf16[128,512]{1,0:T(8,128)(2,1)S(1)}, bf16[128,512]{1,0:T(8,128)(2,1)S(1)}, u32[]{:S(2)}, u32[]{:S(2)}) collective-permute-start(bf16[128,512]{1,0:T(8,128)(2,1)S(1)} %get-tuple-element.74), channel_id=1, source_target_pairs={{0,2},{1,3},{2,0},{3,1},{4,6},{5,7},{6,4},{7,5},{8,10},{9,11},{10,... | collective-permute-start | bytes 393224 | tf_op jit(solution)/shard_map/ppermute | solution.py:451
  30.4 5.8 %collective-permute-start.7 = (bf16[128,512]{1,0:T(8,128)(2,1)S(1)}, bf16[128,512]{1,0:T(8,128)(2,1)S(1)}, u32[]{:S(2)}, u32[]{:S(2)}) collective-permute-start(bf16[128,512]{1,0:T(8,128)(2,1)S(1)} %get-tuple-element.75), channel_id=1, source_target_pairs={{0,3},{1,2},{2,1},{3,0},{4,7},{5,6},{6,5},{7,4},{8,11},{9,10},{10,... | collective-permute-start | bytes 393224 | tf_op jit(solution)/shard_map/ppermute | solution.py:451
  31.2 5.0 %collective-permute-start.5 = (bf16[128,512]{1,0:T(8,128)(2,1)S(1)}, bf16[128,512]{1,0:T(8,128)(2,1)S(1)}, u32[]{:S(2)}, u32[]{:S(2)}) collective-permute-start(bf16[128,512]{1,0:T(8,128)(2,1)S(1)} %get-tuple-element.73), channel_id=1, source_target_pairs={{0,1},{1,0},{2,3},{3,2},{4,5},{5,4},{6,7},{7,6},{8,9},{9,8},{10,11... | collective-permute-start | bytes 393224 | tf_op jit(solution)/shard_map/ppermute | solution.py:451
  41.4 2.2 %collective-permute-start.8 = (bf16[16,2176]{1,0:T(8,128)(2,1)S(1)}, bf16[16,2176]{1,0:T(8,128)(2,1)S(1)}, u32[]{:S(2)}, u32[]{:S(2)}) collective-permute-start(bf16[16,2176]{1,0:T(8,128)(2,1)S(1)} %get-tuple-element.87.own), channel_id=1, source_target_pairs={{0,1},{1,0},{2,3},{3,2},{4,5},{5,4},{6,7},{7,6},{8,9},{9,8},{10,11... | collective-permute-start | bytes 208904 | tf_op jit(solution)/shard_map/ppermute | solution.py:451
  44.2 5.9 %collective-permute-start.11 = (bf16[16,2176]{1,0:T(8,128)(2,1)S(1)}, bf16[16,2176]{1,0:T(8,128)(2,1)S(1)}, u32[]{:S(2)}, u32[]{:S(2)}) collective-permute-start(bf16[16,2176]{1,0:T(8,128)(2,1)S(1)} %pair.1), channel_id=1, source_target_pairs={{0,6},{1,7},{2,4},{3,5},{4,2},{5,3},{6,0},{7,1},{8,14},{9,15},{10,... | collective-permute-start | bytes 208904 | tf_op jit(solution)/shard_map/ppermute | solution.py:451
  46.8 4.3 %collective-permute-start.10 = (bf16[16,2176]{1,0:T(8,128)(2,1)S(1)}, bf16[16,2176]{1,0:T(8,128)(2,1)S(1)}, u32[]{:S(2)}, u32[]{:S(2)}) collective-permute-start(bf16[16,2176]{1,0:T(8,128)(2,1)S(1)} %pair.1), channel_id=1, source_target_pairs={{0,4},{1,5},{2,6},{3,7},{4,0},{5,1},{6,2},{7,3},{8,12},{9,13},{10,... | collective-permute-start | bytes 208904 | tf_op jit(solution)/shard_map/ppermute | solution.py:451
  46.8 5.0 %collective-permute-start.9 = (bf16[16,2176]{1,0:T(8,128)(2,1)S(1)}, bf16[16,2176]{1,0:T(8,128)(2,1)S(1)}, u32[]{:S(2)}, u32[]{:S(2)}) collective-permute-start(bf16[16,2176]{1,0:T(8,128)(2,1)S(1)} %pair.1), channel_id=1, source_target_pairs={{0,2},{1,3},{2,0},{3,1},{4,6},{5,7},{6,4},{7,5},{8,10},{9,11},{10,... | collective-permute-start | bytes 208904 | tf_op jit(solution)/shard_map/ppermute | solution.py:451
  55.1 3.6 %collective-permute-start.12 = (bf16[64,2048]{1,0:T(8,128)(2,1)S(1)}, bf16[64,2048]{1,0:T(8,128)(2,1)S(1)}, u32[]{:S(2)}, u32[]{:S(2)}) collective-permute-start(bf16[64,2048]{1,0:T(8,128)(2,1)S(1)} %get-tuple-element.91.after.refs_0_), channel_id=1, source_target_pairs={{0,1},{1,0},{2,3},{3,2},{4,5},{5,4},{6,7},{7,6},{8,9},{9,8},{10,11... | collective-permute-start | bytes 786440 | tf_op jit(solution)/shard_map/ppermute | solution.py:451
  55.1 9.2 %collective-permute-start.14 = (bf16[64,2048]{1,0:T(8,128)(2,1)S(1)}, bf16[64,2048]{1,0:T(8,128)(2,1)S(1)}, u32[]{:S(2)}, u32[]{:S(2)}) collective-permute-start(bf16[64,2048]{1,0:T(8,128)(2,1)S(1)} %get-tuple-element.93), channel_id=1, source_target_pairs={{0,2},{1,3},{2,0},{3,1},{4,6},{5,7},{6,4},{7,5},{8,10},{9,11},{10,... | collective-permute-start | bytes 786440 | tf_op jit(solution)/shard_map/ppermute | solution.py:451
  56.1 13.0 %collective-permute-start.15 = (bf16[64,2048]{1,0:T(8,128)(2,1)S(1)}, bf16[64,2048]{1,0:T(8,128)(2,1)S(1)}, u32[]{:S(2)}, u32[]{:S(2)}) collective-permute-start(bf16[64,2048]{1,0:T(8,128)(2,1)S(1)} %get-tuple-element.94), channel_id=1, source_target_pairs={{0,4},{1,5},{2,6},{3,7},{4,0},{5,1},{6,2},{7,3},{8,12},{9,13},{10,... | collective-permute-start | bytes 786440 | tf_op jit(solution)/shard_map/ppermute | solution.py:451
  57.6 12.6 %collective-permute-start.16 = (bf16[64,2048]{1,0:T(8,128)(2,1)S(1)}, bf16[64,2048]{1,0:T(8,128)(2,1)S(1)}, u32[]{:S(2)}, u32[]{:S(2)}) collective-permute-start(bf16[64,2048]{1,0:T(8,128)(2,1)S(1)} %get-tuple-element.95), channel_id=1, source_target_pairs={{0,6},{1,7},{2,4},{3,5},{4,2},{5,3},{6,0},{7,1},{8,14},{9,15},{10,... | collective-permute-start | bytes 786440 | tf_op jit(solution)/shard_map/ppermute | solution.py:451
  63.1 7.1 %collective-permute-start.13 = (bf16[64,2048]{1,0:T(8,128)(2,1)S(1)}, bf16[64,2048]{1,0:T(8,128)(2,1)S(1)}, u32[]{:S(2)}, u32[]{:S(2)}) collective-permute-start(bf16[64,2048]{1,0:T(8,128)(2,1)S(1)} %get-tuple-element.92), channel_id=1, source_target_pairs={{0,1},{1,0},{2,3},{3,2},{4,5},{5,4},{6,7},{7,6},{8,9},{9,8},{10,11... | collective-permute-start | bytes 786440 | tf_op jit(solution)/shard_map/ppermute | solution.py:451
  70.3 3.3 %collective-permute-start.17 = (bf16[192,2048]{1,0:T(8,128)(2,1)S(1)}, bf16[192,2048]{1,0:T(8,128)(2,1)S(1)}, u32[]{:S(2)}, u32[]{:S(2)}) collective-permute-start(bf16[192,2048]{1,0:T(8,128)(2,1)S(1)} %gather.1.after.refs_0_), channel_id=1, source_target_pairs={{0,1},{1,0},{2,3},{3,2},{4,5},{5,4},{6,7},{7,6},{8,9},{9,8},{10,11... | collective-permute-start | bytes 2359304 | tf_op jit(solution)/shard_map/ppermute | solution.py:451
  78.5 2.2 %collective-permute-start.18 = (bf16[192,1024]{1,0:T(8,128)(2,1)S(1)}, bf16[192,1024]{1,0:T(8,128)(2,1)S(1)}, u32[]{:S(2)}, u32[]{:S(2)}) collective-permute-start(bf16[192,1024]{1,0:T(8,128)(2,1)S(1)} %down.6.after), channel_id=1, source_target_pairs={{0,1},{1,0},{2,3},{3,2},{4,5},{5,4},{6,7},{7,6},{8,9},{9,8},{10,11... | collective-permute-start | bytes 1179656 | tf_op jit(solution)/shard_map/ppermute | solution.py:451
  82.7 5.3 %collective-permute-start.23 = (bf16[192,1024]{1,0:T(8,128)(2,1)S(1)}, bf16[192,1024]{1,0:T(8,128)(2,1)S(1)}, u32[]{:S(2)}, u32[]{:S(2)}) collective-permute-start(bf16[192,1024]{1,0:T(8,128)(2,1)S(1)} %down.8.after), channel_id=1, source_target_pairs={{0,1},{1,0},{2,3},{3,2},{4,5},{5,4},{6,7},{7,6},{8,9},{9,8},{10,11... | collective-permute-start | bytes 1179656 | tf_op jit(solution)/shard_map/ppermute | solution.py:451
  82.8 11.7 %collective-permute-start.19 = (bf16[64,1024]{1,0:T(8,128)(2,1)S(1)}, bf16[64,1024]{1,0:T(8,128)(2,1)S(1)}, u32[]{:S(2)}, u32[]{:S(2)}) collective-permute-start(bf16[64,1024]{1,0:T(8,128)(2,1)S(1)} %get-tuple-element.96.after), channel_id=1, source_target_pairs={{0,2},{1,3},{2,0},{3,1},{4,6},{5,7},{6,4},{7,5},{8,10},{9,11},{10,... | collective-permute-start | bytes 393224 | tf_op jit(solution)/shard_map/ppermute | solution.py:451
  83.9 7.3 %collective-permute-start.20 = (bf16[64,1024]{1,0:T(8,128)(2,1)S(1)}, bf16[64,1024]{1,0:T(8,128)(2,1)S(1)}, u32[]{:S(2)}, u32[]{:S(2)}) collective-permute-start(bf16[64,1024]{1,0:T(8,128)(2,1)S(1)} %get-tuple-element.97), channel_id=1, source_target_pairs={{0,4},{1,5},{2,6},{3,7},{4,0},{5,1},{6,2},{7,3},{8,12},{9,13},{10,... | collective-permute-start | bytes 393224 | tf_op jit(solution)/shard_map/ppermute | solution.py:451
  85.1 9.4 %collective-permute-start.21 = (bf16[64,1024]{1,0:T(8,128)(2,1)S(1)}, bf16[64,1024]{1,0:T(8,128)(2,1)S(1)}, u32[]{:S(2)}, u32[]{:S(2)}) collective-permute-start(bf16[64,1024]{1,0:T(8,128)(2,1)S(1)} %get-tuple-element.98), channel_id=1, source_target_pairs={{0,6},{1,7},{2,4},{3,5},{4,2},{5,3},{6,0},{7,1},{8,14},{9,15},{10,... | collective-permute-start | bytes 393224 | tf_op jit(solution)/shard_map/ppermute | solution.py:451
  88.1 8.3 %collective-permute-start.24 = (bf16[64,1024]{1,0:T(8,128)(2,1)S(1)}, bf16[64,1024]{1,0:T(8,128)(2,1)S(1)}, u32[]{:S(2)}, u32[]{:S(2)}) collective-permute-start(bf16[64,1024]{1,0:T(8,128)(2,1)S(1)} %get-tuple-element.100), channel_id=1, source_target_pairs={{0,2},{1,3},{2,0},{3,1},{4,6},{5,7},{6,4},{7,5},{8,10},{9,11},{10,... | collective-permute-start | bytes 393224 | tf_op jit(solution)/shard_map/ppermute | solution.py:451
  89.3 7.2 %collective-permute-start.25 = (bf16[64,1024]{1,0:T(8,128)(2,1)S(1)}, bf16[64,1024]{1,0:T(8,128)(2,1)S(1)}, u32[]{:S(2)}, u32[]{:S(2)}) collective-permute-start(bf16[64,1024]{1,0:T(8,128)(2,1)S(1)} %get-tuple-element.101), channel_id=1, source_target_pairs={{0,4},{1,5},{2,6},{3,7},{4,0},{5,1},{6,2},{7,3},{8,12},{9,13},{10,... | collective-permute-start | bytes 393224 | tf_op jit(solution)/shard_map/ppermute | solution.py:451
  91.2 6.8 %collective-permute-start.26 = (bf16[64,1024]{1,0:T(8,128)(2,1)S(1)}, bf16[64,1024]{1,0:T(8,128)(2,1)S(1)}, u32[]{:S(2)}, u32[]{:S(2)}) collective-permute-start(bf16[64,1024]{1,0:T(8,128)(2,1)S(1)} %get-tuple-element.102), channel_id=1, source_target_pairs={{0,6},{1,7},{2,4},{3,5},{4,2},{5,3},{6,0},{7,1},{8,14},{9,15},{10,... | collective-permute-start | bytes 393224 | tf_op jit(solution)/shard_map/ppermute | solution.py:451
  94.8 9.3 %collective-permute-start.22 = (bf16[128,1024]{1,0:T(8,128)(2,1)S(1)}, bf16[128,1024]{1,0:T(8,128)(2,1)S(1)}, u32[]{:S(2)}, u32[]{:S(2)}) collective-permute-start(bf16[128,1024]{1,0:T(8,128)(2,1)S(1)} %finish.2), channel_id=1, source_target_pairs={{0,8},{8,16},{16,24},{24,0},{1,9},{9,17},{17,25},{25,1},{2,10},{10... | collective-permute-start | bytes 786440 | tf_op jit(solution)/shard_map/ppermute | solution.py:456
  98.3 10.4 %collective-permute-start.27 = (bf16[128,1024]{1,0:T(8,128)(2,1)S(1)}, bf16[128,1024]{1,0:T(8,128)(2,1)S(1)}, u32[]{:S(2)}, u32[]{:S(2)}) collective-permute-start(bf16[128,1024]{1,0:T(8,128)(2,1)S(1)} %finish.3), channel_id=1, source_target_pairs={{0,8},{8,16},{16,24},{24,0},{1,9},{9,17},{17,25},{25,1},{2,10},{10... | collective-permute-start | bytes 786440 | tf_op jit(solution)/shard_map/ppermute | solution.py:456

commit v5 on v4

--- a/solution.py
+++ b/solution.py
@@ -1,4 +1,5 @@
 import functools
+import math
 
 import jax
 import jax.numpy as jnp
@@ -15,6 +16,7 @@
 EIGHT = 8
 STRIP = 16
 LANES = 128
+SCALE = HD ** (-0.5) * math.log2(math.e)
 CHUNKS = 2
 F32 = jnp.float32
 BF16 = jnp.bfloat16
@@ -81,69 +83,65 @@
     strips(x.shape[0], body)
 
 
-def norm_kernel(place, gains, x, after, out):
-    norm_into(out, x, gains[0])
-
-
-def queries_into(q_out, slots, normed, head):
-    rows = normed.shape[0] // len(slots)
-    for at, slot in enumerate(slots):
+def norm_kernel(gains, after, *refs):
+    count = len(refs) // 2
+    for x, out in zip(refs[:count], refs[count:]):
+        norm_into(out, x, gains[0])
+
+
+def project(head, weights, first, second, q_out, kv_out):
+    rows = first.shape[0]
+    normed = jnp.concatenate([first[...], second[...]], 0)
+    both = dot(normed, weights[...]).astype(BF16)
+    kv_out[0] = both[:, :HD]
+    kv_out[1] = both[:, HD:]
+    for slot, shard in enumerate((first, second)):
         for part in range(GROUP):
             cols = pl.ds(pl.multiple_of((head * GROUP + part) * HD, HD), HD)
-            q_out[slot, pl.ds(part * rows, rows), :] = normed[at * rows : (at + 1) * rows, cols]
-
-
-def project_kernel(
-    place, gains, normed_own, beside, normed_near, w_own, w_other, q_out, kv_out, weights, normed
-):
-    rows = beside.shape[0]
-    head = place[0] % KVH
+            q_out[slot, pl.ds(part * rows, rows), :] = shard[:, cols]
+
+
+def project_kernel(place, w_own, w_other, first, second, q_out, kv_out, weights):
     key_at = place[1]
     weights[:, pl.ds(pl.multiple_of(key_at * HD, HD), HD)] = w_own[...]
     weights[:, pl.ds(pl.multiple_of((1 - key_at) * HD, HD), HD)] = w_other[...]
-    normed[:rows, :] = normed_own[...]
-    norm_into(normed.at[pl.ds(rows, rows)], beside, gains[0])
-    normed[2 * rows :, :] = normed_near[...]
-    both = dot(normed[...], weights[...]).astype(BF16)
-    kv_out[0, : 3 * rows, :] = both[:, :HD]
-    kv_out[1, : 3 * rows, :] = both[:, HD:]
-    queries_into(q_out, (0, 1, 2), normed, head)
-
-
-def project_last_kernel(place, normed, weights, q_in, kv_in, q_out, kv_out):
-    rows = normed.shape[0]
-    q_out[:3] = q_in[:3]
-    kv_out[:, : 3 * rows, :] = kv_in[:, : 3 * rows, :]
-    both = dot(normed[...], weights[...]).astype(BF16)
-    kv_out[0, 3 * rows :, :] = both[:, :HD]
-    kv_out[1, 3 * rows :, :] = both[:, HD:]
-    queries_into(q_out, (3,), normed, place[0] % KVH)
-
-
-def near_kernel(place, q, kv, largest_out, total_out, summed):
+    project(place[0] % KVH, weights, first, second, q_out, kv_out)
+
+
+def project_more_kernel(place, weights, first, second, q_out, kv_out):
+    project(place[0] % KVH, weights, first, second, q_out, kv_out)
+
+
+def joined_keys(halves, which):
+    return jnp.concatenate([half[which] for half in halves], 0)
+
+
+def near_kernel(place, *refs):
+    queries, halves, (largest_out, total_out, summed) = refs[:2], refs[2:4], refs[4:]
     me = place[0]
-    rows = q.shape[1] // GROUP
-    count = kv.shape[1]
+    keys, values = joined_keys(halves, 0), joined_keys(halves, 1)
+    count = keys.shape[0]
+    rows = count // KVH
     lane = iota((rows, count), 1)
     key_shard = me ^ (lane // rows)
     later = lane % rows > iota((rows, count), 0)
     for slot in range(KVH):
         shard = me ^ slot
         hidden = (key_shard > shard) | ((key_shard == shard) & later)
-        scores = dot(q[slot], kv[0], ((1,), (1,))) * HD ** (-0.5)
+        scores = dot(queries[slot // 2][slot % 2], keys, ((1,), (1,)))
         scores = scores.reshape(GROUP, rows, count)
         scores = jnp.where(hidden[None], -1e30, scores).reshape(GROUP * rows, count)
         largest = jnp.max(scores, -1, keepdims=True)
-        weights = jnp.exp(scores - largest)
+        weights = jnp.exp2(scores * SCALE - largest * SCALE)
         total = jnp.sum(weights, -1, keepdims=True)
-        summed[slot] = dot(weights.astype(BF16), kv[1])
+        summed[slot] = dot(weights.astype(BF16), values)
         largest_out[slot] = jnp.broadcast_to(largest, (GROUP * rows, LANES))
         total_out[slot] = jnp.broadcast_to(total, (GROUP * rows, LANES))
 
 
-def far_kernel(turn, slots, last, place, q, largest, total, summed, past, *outs):
-    rows = q.shape[1] // GROUP
-    wide = past.shape[1] // LANES
+def far_kernel(turn, slots, last, place, after, *refs):
+    queries, (largest, total, summed), halves, outs = refs[:2], refs[2:5], refs[5:7], refs[7:]
+    rows = queries[0].shape[1] // GROUP
     mine = place[0] // KVH
     seen = (mine ^ turn) < mine
 
@@ -160,14 +158,17 @@
 
     @pl.when(seen)
     def _():
+        keys, values = joined_keys(halves, 0), joined_keys(halves, 1)
+        wide = keys.shape[0] // LANES
         for at, slot in enumerate(slots):
-            scores = dot(q[slot], past[0], ((1,), (1,))) * HD ** (-0.5)
+            scores = dot(queries[slot // 2][slot % 2], keys, ((1,), (1,)))
             top = jnp.broadcast_to(jnp.max(scores, -1, keepdims=True), (GROUP * rows, LANES))
             newest = jnp.maximum(largest[slot], top)
-            weights = jnp.exp(scores - jnp.concatenate([newest] * wide, 1))
-            fade = jnp.exp(largest[slot] - newest)
+            offset = newest * SCALE
+            weights = jnp.exp2(scores * SCALE - jnp.concatenate([offset] * wide, 1))
+            fade = jnp.exp2(largest[slot] * SCALE - offset)
             weight = jnp.broadcast_to(jnp.sum(weights, -1, keepdims=True), (GROUP * rows, LANES))
-            value = summed[slot] * fade + dot(weights.astype(BF16), past[1])
+            value = summed[slot] * fade + dot(weights.astype(BF16), values)
             keep(at, newest, total[slot] * fade + weight, value)
 
     @pl.when(jnp.logical_not(seen))
@@ -368,26 +369,32 @@
     weighting[...] = jnp.concatenate(weights, 0).T
 
 
-def fetch_kernel(pieces, *refs):
+def fetch_kernel(pieces, starts, *refs):
     count = len(pieces)
     sources, outs, sems = refs[:count], refs[-count - 1 : -1], refs[-1]
     copies = []
-    for source, out, number in zip(sources, outs, pieces):
-        rows = source.shape[0] // number
+    for source, out, number, start in zip(sources, outs, pieces, starts):
+        rows = out.shape[0] // number
         for piece in range(number):
-            at = pl.ds(piece * rows, rows)
-            start, end = (source, out) if number == 1 else (source.at[at], out.at[at])
-            copies.append(pltpu.make_async_copy(start, end, sems.at[len(copies)]))
+            begin, end = source, out
+            if number > 1:
+                at = pl.ds(piece * rows, rows)
+                begin, end = source.at[at, pl.ds(start, out.shape[1])], out.at[at]
+            copies.append(pltpu.make_async_copy(begin, end, sems.at[len(copies)]))
     for copy in copies:
         copy.start()
     for copy in copies:
         copy.wait()
 
 
-def fetch(arrays, pieces, after):
+def fetch(items, after):
+    arrays, pieces, starts, widths = zip(*items)
     return pl.pallas_call(
-        functools.partial(fetch_kernel, pieces),
-        out_shape=tuple(shape(array.shape, array.dtype) for array in arrays),
+        functools.partial(fetch_kernel, pieces, starts),
+        out_shape=tuple(
+            shape(array.shape[:-1] + (width,), array.dtype)
+            for array, width in zip(arrays, widths)
+        ),
         in_specs=[ANY] * (len(arrays) + 1),
         out_specs=(VMEM,) * len(arrays),
         scratch_shapes=[pltpu.SemaphoreType.DMA((sum(pieces),))],
@@ -414,24 +421,27 @@
         hidden[:, cols] = (raised * jax.nn.sigmoid(raised)).astype(BF16)
 
 
-def down_kernel(start, w_down, hidden, after, *outs):
-    rows, width = outs[0].shape
+def down_kernel(weights, hidden, after, *refs):
+    w_downs, outs = refs[:weights], refs[weights:]
+    rows = outs[0].shape[0]
     tile = 256
-    for low in range(0, width, tile):
-        part = w_down[:, start + low : start + low + tile]
-        result = dot(hidden[...], part).astype(BF16)
-        for at, out in enumerate(outs):
-            out[:, low : low + tile] = result[at * rows : (at + 1) * rows]
-
-
-def join_kernel(*refs):
+    begin = 0
+    for w_down in w_downs:
+        for low in range(0, w_down.shape[1], tile):
+            result = dot(hidden[...], w_down[:, low : low + tile]).astype(BF16)
+            for at, out in enumerate(outs):
+                out[:, begin + low : begin + low + tile] = result[at * rows : (at + 1) * rows]
+        begin += w_down.shape[1]
+
+
+def join_kernel(start, own, *refs):
     parts, outs = refs[: 1 - EXPERTS], refs[1 - EXPERTS :]
-    capacity = outs[0].shape[0]
+    capacity, width = outs[0].shape
     for at, out in enumerate(outs):
         here = slice(at * capacity, (at + 1) * capacity)
-        total = parts[0][here, :].astype(F32)
-        for part in parts[1:]:
-            total = total + part[here, :].astype(F32)
+        total = own[here, :].astype(F32)
+        for part in parts:
+            total = total + part[here, start : start + width].astype(F32)
         out[...] = total.astype(BF16)
 
 
@@ -499,58 +509,54 @@
     beside = exchange(tokens, "ctx", 1)
     place = jnp.stack([me, key_at, me // parts]).astype(jnp.int32)
 
-    def norm(gains, block, after):
+    def norm(gains, blocks, after):
         return pl.pallas_call(
             norm_kernel,
-            out_shape=shape((rows, width), BF16),
-            in_specs=[SMEM, VMEM, VMEM, ANY],
-            out_specs=VMEM,
-            compiler_params=params(4),
+            out_shape=(shape((rows, width), BF16),) * len(blocks),
+            in_specs=[VMEM, ANY] + [VMEM] * len(blocks),
+            out_specs=(VMEM,) * len(blocks),
+            compiler_params=params(6),
             cost_estimate=cost(8 * rows * width, 4 * rows * width),
             name="norm",
-        )(place, gains, block, after)
-
-    normed_own = norm(in_hbm(gains), in_hbm(tokens), in_hbm(tokens))
-    here = [w_up[0], w_down[0], gains, w_own, tokens, dt_in[0], dt_out[0], w_bc[0].T]
+        )(gains, after, *blocks)
+
+    normed = list(norm(in_hbm(gains), [in_hbm(tokens), beside], place))
+    half = width // CHUNKS
+    here = [gains, w_own, tokens, dt_in[0], dt_out[0], w_bc[0].T]
     here += [skip_gain, dt_bias, decay_rate, w_router[0].T, routes[0].T]
-    here = fetch(here, (16, 16) + (1,) * 11, normed_own)
-    raising, lowering, gains, w_own, tokens, dt_first, dt_second, w_bct = here[:8]
-    skip_gain, dt_bias, decay_rate, router_t, routes_t = here[8:]
-    normed_near = norm(gains, near_tokens, raising)
-    normed_far = exchange(normed_near, "ctx", 1)
-    projected = (
-        shape((KVH, GROUP * rows, HD), BF16),
-        shape((2, group_rows, HD), BF16),
-    )
-    queries, kv, weights = pl.pallas_call(
+    here = [(array, 1, 0, array.shape[-1]) for array in here]
+    here = [(w_up[0], 16, 0, w_up.shape[2]), (w_down[0], 16, 0, half)] + here
+    raising, *here = fetch(here, normed[1])
+    lowering, gains, w_own, tokens, dt_first, dt_second, w_bct = here[:7]
+    lowering = [lowering]
+    skip_gain, dt_bias, decay_rate, router_t, routes_t = here[7:]
+    normed += norm(gains, [near_tokens], raising)
+    normed.append(exchange(normed[2], "ctx", 1))
+    projected = (shape((2, GROUP * rows, HD), BF16), shape((2, 2 * rows, HD), BF16))
+    first_q, first_kv, weights = pl.pallas_call(
         project_kernel,
         out_shape=projected + (shape((width, 2 * HD), BF16),),
-        in_specs=[SMEM] + [VMEM] * 6,
+        in_specs=[SMEM] + [VMEM] * 4,
         out_specs=(VMEM,) * 3,
-        scratch_shapes=[pltpu.VMEM((3 * rows, width), BF16)],
-        compiler_params=params(12),
-        cost_estimate=cost(12 * rows * width * HD, 24 * rows * width),
+        compiler_params=params(8),
+        cost_estimate=cost(8 * rows * width * HD, 16 * rows * width),
         name="project",
-    )(
-        place,
-        gains,
-        normed_own,
-        beside,
-        normed_near,
-        w_own,
-        w_other,
-    )
-    queries, kv = pl.pallas_call(
-        project_last_kernel,
+    )(place, w_own, w_other, *normed[:2])
+    last_q, last_kv = pl.pallas_call(
+        project_more_kernel,
         out_shape=projected,
-        in_specs=[SMEM] + [VMEM] * 4,
+        in_specs=[SMEM] + [VMEM] * 3,
         out_specs=(VMEM,) * 2,
-        compiler_params=params(12),
-        cost_estimate=cost(4 * rows * width * HD, 8 * rows * width),
-        name="project_last",
-    )(place, normed_far, weights, queries, kv)
+        compiler_params=params(8),
+        cost_estimate=cost(8 * rows * width * HD, 16 * rows * width),
+        name="project_more",
+    )(place, weights, *normed[2:])
+    queries, kv = (first_q, last_q), (first_kv, last_kv)
     turns = shard_count // KVH
-    pasts = [exchange(kv, "ctx", turn * KVH) for turn in range(1, turns)]
+    pasts = [
+        [exchange(half, "ctx", turn * KVH) for half in kv] for turn in range(1, turns)
+    ]
+    lowering += fetch([(w_down[0], 16, half, half)], last_kv)
     scored = GROUP * rows * group_rows * KVH
     tallies = (shape((KVH, GROUP * rows, LANES), F32),) * 2 + (
         shape((KVH, GROUP * rows, HD), F32),
@@ -558,12 +564,12 @@
     tally = pl.pallas_call(
         near_kernel,
         out_shape=tallies,
-        in_specs=[SMEM, VMEM, VMEM],
+        in_specs=[SMEM] + [VMEM] * 4,
         out_specs=(VMEM,) * 3,
         compiler_params=params(16),
         cost_estimate=cost(4 * scored * HD, 4 * group_rows * GROUP * HD * 4, scored),
         name="near",
-    )(place, queries, kv)
+    )(place, *queries, *kv)
     attended = [None] * KVH
     for slots in ((2, 3), (0, 1)):
         state_now = tally
@@ -572,12 +578,12 @@
             state_now = pl.pallas_call(
                 functools.partial(far_kernel, turn, slots, last),
                 out_shape=(shape((rows, GROUP * HD), BF16),) * len(slots) if last else tallies,
-                in_specs=[SMEM] + [VMEM] * 5,
+                in_specs=[SMEM, ANY] + [VMEM] * 7,
                 out_specs=(VMEM,) * (len(slots) if last else 3),
                 compiler_params=params(16),
                 cost_estimate=cost(2 * scored * HD, 2 * group_rows * GROUP * HD * 4, scored // 2),
                 name="far",
-            )(place, queries, *state_now, past)
+            )(place, lowering[1], *queries, *state_now, *past)
         for slot, block in zip(slots, state_now):
             attended[slot] = exchange(block, "ctx", slot) if slot else block
 
@@ -681,17 +687,18 @@
             name="up",
         )(raising, after, *blocks)
 
-    def lower(start, span, hidden, after, outs=1):
-        count = hidden.shape[0]
+    def lower(weights, hidden, after, outs=1, hurry=False):
+        count, span = hidden.shape[0], half * len(weights)
+        work = 1 if hurry else units
         return pl.pallas_call(
-            functools.partial(down_kernel, start),
+            functools.partial(down_kernel, len(weights)),
             out_shape=(shape((count // outs, span), BF16),) * outs,
-            in_specs=[VMEM, VMEM, ANY],
+            in_specs=[VMEM, ANY] + [VMEM] * len(weights),
             out_specs=(VMEM,) * outs,
             compiler_params=params(12),
-            cost_estimate=cost(2 * count * span * units, 2 * span * units),
+            cost_estimate=cost(2 * count * span * work, 2 * span * work),
             name="down",
-        )(lowering, hidden, after)
+        )(hidden, after, *weights)
 
     def between_experts(blocks):
         moved = {slot: exchange(blocks[slot - 1], "ctx", slot * parts) for slot in (3, 1, 2)}
@@ -699,11 +706,10 @@
 
     moved = between_experts(packed[1:])
     stay = [exchange(packed[0], "ctx", turn) if turn else packed[0] for turn in range(parts)]
-    stay_out = lower(0, width, lift(stay, packed[0]), packed[0], parts)
+    stay_out = lower(lowering, lift(stay, packed[0]), packed[0], parts)
     stay_sums = [stay_out[0]] + [
         exchange(stay_out[turn], "ctx", turn) for turn in range(1, parts)
     ]
-
     moved_rows = (EXPERTS - 1) * capacity
     arrived = pl.pallas_call(
         gather_kernel,
@@ -719,34 +725,32 @@
     for turn in range(parts):
         after = lift([exchange(arrived, "ctx", turn) if turn else arrived], after)
         hiddens.append(after)
-    chunk_width = width // CHUNKS
+    others = []
+    for turn in range(1, parts):
+        (after,) = lower(lowering, hiddens[turn], after)
+        others.append(exchange(after, "ctx", turn))
     results = []
     for chunk in range(CHUNKS):
-        start = chunk * chunk_width
-        sums = []
-        for turn in reversed(range(parts)):
-            (part_out,) = lower(start, chunk_width, hiddens[turn], after)
-            sums.append(exchange(part_out, "ctx", turn) if turn else part_out)
-            after = part_out
+        (own,) = lower(lowering[chunk : chunk + 1], hiddens[0], after, hurry=chunk > 0)
         joined = pl.pallas_call(
-            join_kernel,
-            out_shape=(shape((capacity, chunk_width), BF16),) * (EXPERTS - 1),
+            functools.partial(join_kernel, chunk * half),
+            out_shape=(shape((capacity, half), BF16),) * (EXPERTS - 1),
             in_specs=[VMEM] * parts,
             out_specs=(VMEM,) * (EXPERTS - 1),
             compiler_params=params(8),
-            cost_estimate=cost(4 * moved_rows * chunk_width, 8 * moved_rows * chunk_width),
+            cost_estimate=cost(4 * moved_rows * half, 8 * moved_rows * half),
             name="join",
-        )(*sums)
+        )(own, *others)
         after = joined[0]
         returned = between_experts(joined)
         finished = pl.pallas_call(
-            functools.partial(finish_kernel, start),
-            out_shape=shape((rows, chunk_width), BF16),
+            functools.partial(finish_kernel, chunk * half),
+            out_shape=shape((rows, half), BF16),
             in_specs=[VMEM] * (1 + EXPERTS + parts),
             out_specs=VMEM,
             compiler_params=params(8),
             cost_estimate=cost(
-                4 * rows * EXPERTS * capacity * chunk_width, 10 * rows * chunk_width
+                4 * rows * EXPERTS * capacity * half, 10 * rows * half
             ),
             name="finish",
         )(second, weighting, *returned, *stay_sums)

time: 110 us -> 108 us (0.982)
  transfers between devices with their start and end apart: 28 -> 28, of which waited for: 13 -> 16; matrix products, arithmetic and copies ran while one was open for 0% -> 0% of each run, Pallas kernels for 29% -> 30%
where the time goes in v5:
time: 108 us; the launch traced here: 107 us
  Pallas kernels  48.2 us (45%)
  starting transfers between devices  29.7 us (28%)
  waiting for transfers between devices  28.3 us (26%)
    ppermute x26, starting transfers between devices, exchange(): return lax.ppermute(value, axis, [(at, at ^ mask) for at in range(count)])  26.4 us
    ppermute x26, waiting for transfers between devices, exchange(): return lax.ppermute(value, axis, [(at, at ^ mask) for at in range(count)])  20.5 us
    pallas_call x2, Pallas kernels, fetch(): pl.pallas_call(functools.partial(fetch_kernel, pieces, starts), out_shape...  11.6 us
    pallas_call x4, Pallas kernels, lower(): pl.pallas_call(functools.partial(down_kernel, len(weights)), out_shape=(s...  8.49 us
    pallas_call x3, Pallas kernels, lift(): pl.pallas_call(up_kernel, out_shape=shape((count, units), BF16), in_specs...  8.16 us
    ppermute x2, waiting for transfers between devices, shifted(): lax.ppermute(value, axis, [(at, (at + steps) % count) for at in range(cou...  7.73 us
    pallas_call x1, Pallas kernels, on_device(): pl.pallas_call(prepare_kernel, out_shape=(shape((rows, width), F32), shap...  5.16 us
    ppermute x2, starting transfers between devices, shifted(): lax.ppermute(value, axis, [(at, (at + steps) % count) for at in range(cou...  3.26 us
  transfers between devices with their start and end apart: 28, of which 16 were waited for; matrix products, arithmetic and copies ran while one was open for 0% of the time, Pallas kernels for 30%

profile of v5, /device:TPU:0, one launch (start us, length us, event | category | flops | bytes accessed | tf_op | source)
XLA Modules:
  0.0 107.4 jit_solution(58143525748610618)
XLA Ops:
  0.0 0.5 collective-permute-start
  0.5 2.5 %collective-permute-start.2 = (bf16[128,2048]{1,0:T(8,128)(2,1)}, bf16[128,2048]{1,0:T(8,128)(2,1)S(1)}, u32[]{:S(2)}, u32[]{:S(2)}) collective-permute-start(bf16[128,2048]{1,0:T(8,128)(2,1)} %bitcast.25), channel_id=1, source_target_pairs={{0,2},{1,3},{2,0},{3,1},{4,6},{5,7},{6,4},{7,5},{8,10},{9,11},{10,... | collective-permute-start | bytes 1572872 | tf_op jit(solution)/shard_map/ppermute | solution.py:461
  2.9 1.5 %collective-permute-start.1 = (bf16[2048,128]{1,0:T(8,128)(2,1)}, bf16[2048,128]{1,0:T(8,128)(2,1)S(1)}, u32[]{:S(2)}, u32[]{:S(2)}) collective-permute-start(bf16[2048,128]{1,0:T(8,128)(2,1)} %bitcast.30), channel_id=1, source_target_pairs={{0,4},{1,5},{2,6},{3,7},{4,0},{5,1},{6,2},{7,3},{8,12},{9,13},{10,... | collective-permute-start | bytes 1572872 | tf_op jit(solution)/shard_map/ppermute | solution.py:461
  4.5 0.1 pad_add_fusion.after.place
  4.5 1.7 %norm.2 = (bf16[128,2048]{1,0:T(8,128)(2,1)S(1)}, bf16[128,2048]{1,0:T(8,128)(2,1)S(1)}) custom-call(f32[3,1,2048]{2,1,0:T(1,128)} %bitcast.33, s32[3]{0:T(128)S(1)} %pad_add_fusion.after.place, bf16[128,2048]{1,0:T(8,128)(2,1)} %bitcast.26, bf16[128,2048]{1,0:T(8,128)(2,1)S(1)} %collective-permute-done.refs_1_), custom_call_target="tpu_custom_call" | custom-call | flops 2097152 | bytes 1048576 | tf_op jit(solution)/shard_map/norm/pallas_call | solution.py:513
  6.3 8.4 %fetch.2 = (bf16[2048,3584]{1,0:T(8,128)(2,1)S(1)}, bf16[3584,1024]{1,0:T(8,128)(2,1)S(1)}, f32[3,1,2048]{2,1,0:T(1,128)S(1)}, bf16[2048,128]{1,0:T(8,128)(2,1)S...) custom-call(bf16[2048,3584]{1,0:T(8,128)(2,1)} %bitcast.23, ...), custom_call_target="tpu_custom_call" | custom-call | bytes 63259648 | tf_op jit(solution)/shard_map/fetch/pallas_call | solution.py:392
  14.7 1.1 collective-permute-done.2.refs_0_
  15.7 0.3 norm.3.first
  16.2 1.1 collective-permute-done.1.w_other
  17.2 1.2 %project.1 = (bf16[2,512,128]{2,1,0:T(8,128)(2,1)S(1)}, bf16[2,256,128]{2,1,0:T(8,128)(2,1)S(1)}, bf16[2048,256]{1,0:T(8,128)(2,1)S(1)}) custom-call(s32[3]{0:T(128)S(1)} %pad_add_fusion.after.place, bf16[2048,128]{1,0:T(8,128)(2,1)S(1)} %get-tuple-element.65.w_own, bf16[2048,128]{1,0:T(8,128)(2,1)S(1)} %collective-permute-done.1.w_other, ...), custom_call_target="tpu_custom_call" | custom-call | flops 268435456 | bytes 4194304 | tf_op jit(solution)/shard_map/project/pallas_call | solution.py:536
  18.5 1.6 %collective-permute-start.4 = (bf16[2,256,128]{2,1,0:T(8,128)(2,1)S(1)}, bf16[2,256,128]{2,1,0:T(8,128)(2,1)S(1)}, u32[]{:S(2)}, u32[]{:S(2)}) collective-permute-start(bf16[2,256,128]{2,1,0:T(8,128)(2,1)S(1)} %get-tuple-element.72.refs_2_), channel_id=1, source_target_pairs={{0,4},{1,5},{2,6},{3,7},{4,0},{5,1},{6,2},{7,3},{8,12},{9,13},{10,... | collective-permute-start | bytes 393224 | tf_op jit(solution)/shard_map/ppermute | solution.py:461
  20.1 1.0 project_more.1
  21.0 0.6 collective-permute-start.5
  21.6 3.2 %fetch.3.after.refs_1_.refs_0_ = bf16[3584,1024]{1,0:T(8,128)(2,1)S(1)} custom-call(bf16[3584,2048]{1,0:T(8,128)(2,1)} %bitcast.22, bf16[2,256,128]{2,1,0:T(8,128)(2,1)S(1)} %get-tuple-element.69.refs_1_.refs_3_), custom_call_target="tpu_custom_call" | custom-call | bytes 29360128 | tf_op jit(solution)/shard_map/fetch/pallas_call | solution.py:392
  24.8 2.5 %near.1 = (f32[4,512,128]{2,1,0:T(8,128)S(1)}, f32[4,512,128]{2,1,0:T(8,128)S(1)}, f32[4,512,128]{2,1,0:T(8,128)S(1)}) custom-call(s32[3]{0:T(128)S(1)} %pad_add_fusion.after.place, bf16[2,512,128]{2,1,0:T(8,128)(2,1)S(1)} %get-tuple-element.70.refs_0_, bf16[2,512,128]{2,1,0:T(8,128)(2,1)S(1)} %get-tuple-element.71.refs_1_, ...), custom_call_target="tpu_custom_call" | custom-call | flops 536870912 | bytes 4194304 | tf_op jit(solution)/shard_map/near/pallas_call | solution.py:564
  27.3 0.6 far.3
  28.0 0.8 collective-permute-start.7
  28.8 0.6 far.2
  29.4 1.4 %collective-permute-start.6 = (bf16[128,512]{1,0:T(8,128)(2,1)S(1)}, bf16[128,512]{1,0:T(8,128)(2,1)S(1)}, u32[]{:S(2)}, u32[]{:S(2)}) collective-permute-start(bf16[128,512]{1,0:T(8,128)(2,1)S(1)} %get-tuple-element.77), channel_id=1, source_target_pairs={{0,1},{1,0},{2,3},{3,2},{4,5},{5,4},{6,7},{7,6},{8,9},{9,8},{10,11... | collective-permute-start | bytes 393224 | tf_op jit(solution)/shard_map/ppermute | solution.py:461
  30.9 3.3 %collective-permute-done.7.refs_2_ = bf16[128,512]{1,0:T(8,128)(2,1)S(1)} collective-permute-done((bf16[128,512]{1,0:T(8,128)(2,1)S(1)}, bf16[128,512]{1,0:T(8,128)(2,1)S(1)}, u32[]{:S(2)}, u32[]{:S(2)}) %collective-permute-start.7) | collective-permute-done | bytes 131104 | tf_op jit(solution)/shard_map/ppermute | solution.py:461
  34.2 0.4 collective-permute-done.8.refs_3_
  34.6 5.2 %prepare.1 = (f32[128,2048]{1,0:T(8,128)S(1)}, f32[128,2048]{1,0:T(8,128)S(1)}, f32[128,2048]{1,0:T(8,128)S(1)}, f32[256,2048]{1,0:T(8,128)S(1)}, f32[16,2048]{1...) custom-call(s32[3]{0:T(128)S(1)} %pad_add_fusion.after.place, ...), custom_call_target="tpu_custom_call" | custom-call | flops 671088640 | bytes 7864320 | tf_op jit(solution)/shard_map/prepare/pallas_call | solution.py:590
  39.8 1.1 %collective-permute-start.9 = (bf16[16,2176]{1,0:T(8,128)(2,1)S(1)}, bf16[16,2176]{1,0:T(8,128)(2,1)S(1)}, u32[]{:S(2)}, u32[]{:S(2)}) collective-permute-start(bf16[16,2176]{1,0:T(8,128)(2,1)S(1)} %get-tuple-element.91.own), channel_id=1, source_target_pairs={{0,1},{1,0},{2,3},{3,2},{4,5},{5,4},{6,7},{7,6},{8,9},{9,8},{10,11... | collective-permute-start | bytes 208904 | tf_op jit(solution)/shard_map/ppermute | solution.py:461
  40.9 0.9 collective-permute-done.9.other.beside
  41.8 0.6 pair.1
  42.4 3.1 %collective-permute-start.12 = (bf16[16,2176]{1,0:T(8,128)(2,1)S(1)}, bf16[16,2176]{1,0:T(8,128)(2,1)S(1)}, u32[]{:S(2)}, u32[]{:S(2)}) collective-permute-start(bf16[16,2176]{1,0:T(8,128)(2,1)S(1)} %pair.1), channel_id=1, source_target_pairs={{0,6},{1,7},{2,4},{3,5},{4,2},{5,3},{6,0},{7,1},{8,14},{9,15},{10,... | collective-permute-start | bytes 208904 | tf_op jit(solution)/shard_map/ppermute | solution.py:461
  45.4 1.0 collective-permute-start.10
  46.4 2.1 %within.1 = (f32[128,2048]{1,0:T(8,128)S(1)}, f32[128,2048]{1,0:T(8,128)S(1)}) custom-call(f32[128,32]{1,0:T(8,128)S(1)} %get-tuple-element.80.bc, f32[32,128]{1,0:T(8,128)S(1)} %get-tuple-element.81.bct, f32[128,2048]{1,0:T(8,128)S(1)} %get-tuple-element.82.base, f32[128,2048]{1,0:T(8,128)S(1)} %get-tuple-element.83.keep, ...), custom_call_target="tpu_custom_call" | custom-call | flops 10485760 | bytes 5242880 | tf_op jit(solution)/shard_map/within/pallas_call | solution.py:636
  48.5 1.2 %collective-permute-done.11.refs_1_ = bf16[16,2176]{1,0:T(8,128)(2,1)S(1)} collective-permute-done((bf16[16,2176]{1,0:T(8,128)(2,1)S(1)}, bf16[16,2176]{1,0:T(8,128)(2,1)S(1)}, u32[]{:S(2)}, u32[]{:S(2)}) %collective-permute-start.11) | collective-permute-done | bytes 69664 | tf_op jit(solution)/shard_map/ppermute | solution.py:461
  49.7 0.6 collective-permute-done.10.refs_0_
  50.3 3.2 %route.1 = (f32[128,2048]{1,0:T(8,128)S(1)}, f32[128,256]{1,0:T(8,128)S(1)}, bf16[64,2048]{1,0:T(8,128)(2,1)S(1)}, bf16[64,2048]{1,0:T(8,128)(2,1)S(1)}, bf16[64...) custom-call(s32[3]{0:T(128)S(1)} %pad_add_fusion.after.place, f32[128,2048]{1,0:T(8,128)S(1)} %get-tuple-element.85.before, ...), custom_call_target="tpu_custom_call" | custom-call | flops 671088640 | bytes 7864320 | tf_op jit(solution)/shard_map/route/pallas_call | solution.py:646
  53.6 1.1 %collective-permute-start.15 = (bf16[64,2048]{1,0:T(8,128)(2,1)S(1)}, bf16[64,2048]{1,0:T(8,128)(2,1)S(1)}, u32[]{:S(2)}, u32[]{:S(2)}) collective-permute-start(bf16[64,2048]{1,0:T(8,128)(2,1)S(1)} %get-tuple-element.97), channel_id=1, source_target_pairs={{0,2},{1,3},{2,0},{3,1},{4,6},{5,7},{6,4},{7,5},{8,10},{9,11},{10,... | collective-permute-start | bytes 786440 | tf_op jit(solution)/shard_map/ppermute | solution.py:461
  54.7 1.4 %collective-permute-start.16 = (bf16[64,2048]{1,0:T(8,128)(2,1)S(1)}, bf16[64,2048]{1,0:T(8,128)(2,1)S(1)}, u32[]{:S(2)}, u32[]{:S(2)}) collective-permute-start(bf16[64,2048]{1,0:T(8,128)(2,1)S(1)} %get-tuple-element.98), channel_id=1, source_target_pairs={{0,4},{1,5},{2,6},{3,7},{4,0},{5,1},{6,2},{7,3},{8,12},{9,13},{10,... | collective-permute-start | bytes 786440 | tf_op jit(solution)/shard_map/ppermute | solution.py:461
  56.1 1.1 collective-permute-start.17
  57.2 2.1 %up.3.hidden = bf16[128,3584]{1,0:T(8,128)(2,1)S(1)} custom-call(bf16[2048,3584]{1,0:T(8,128)(2,1)S(1)} %get-tuple-element.68.after.w_up, bf16[64,2048]{1,0:T(8,128)(2,1)S(1)} %get-tuple-element.94.after.refs_0_, bf16[64,2048]{1,0:T(8,128)(2,1)S(1)} %get-tuple-element.94.after.refs_0_, bf16[64,2048]{1,0:T(8,128)(2,1)S(1)} %collective-permute-done.13.refs_1_), custom_call_target="tpu_custom_call" | custom-call | flops 1879048192 | bytes 14680064 | tf_op jit(solution)/shard_map/up/pallas_call | solution.py:680
  59.3 2.1 %down.4 = (bf16[64,2048]{1,0:T(8,128)(2,1)S(1)}, bf16[64,2048]{1,0:T(8,128)(2,1)S(1)}) custom-call(bf16[128,3584]{1,0:T(8,128)(2,1)S(1)} %up.3.hidden, bf16[64,2048]{1,0:T(8,128)(2,1)S(1)} %get-tuple-element.94.after.refs_0_, bf16[3584,1024]{1,0:T(8,128)(2,1)S(1)} %get-tuple-element.95.refs_0_, bf16[3584,1024]{1,0:T(8,128)(2,1)S(1)} %fetch.3.after.refs_1_.refs_0_), custom_call_target="tpu_custom_call" | custom-call | flops 1879048192 | bytes 14680064 | tf_op jit(solution)/shard_map/down/pallas_call | solution.py:693
  61.4 1.4 %collective-permute-done.15.refs_0_ = bf16[64,2048]{1,0:T(8,128)(2,1)S(1)} collective-permute-done((bf16[64,2048]{1,0:T(8,128)(2,1)S(1)}, bf16[64,2048]{1,0:T(8,128)(2,1)S(1)}, u32[]{:S(2)}, u32[]{:S(2)}) %collective-permute-start.15) | collective-permute-done | bytes 262176 | tf_op jit(solution)/shard_map/ppermute | solution.py:461
  62.8 4.9 %collective-permute-done.16.refs_1_ = bf16[64,2048]{1,0:T(8,128)(2,1)S(1)} collective-permute-done((bf16[64,2048]{1,0:T(8,128)(2,1)S(1)}, bf16[64,2048]{1,0:T(8,128)(2,1)S(1)}, u32[]{:S(2)}, u32[]{:S(2)}) %collective-permute-start.16) | collective-permute-done | bytes 262176 | tf_op jit(solution)/shard_map/ppermute | solution.py:461
  67.7 1.2 %collective-permute-done.17.refs_2_ = bf16[64,2048]{1,0:T(8,128)(2,1)S(1)} collective-permute-done((bf16[64,2048]{1,0:T(8,128)(2,1)S(1)}, bf16[64,2048]{1,0:T(8,128)(2,1)S(1)}, u32[]{:S(2)}, u32[]{:S(2)}) %collective-permute-start.17) | collective-permute-done | bytes 262176 | tf_op jit(solution)/shard_map/ppermute | solution.py:461
  69.0 3.0 %up.4.after.hidden = bf16[192,3584]{1,0:T(8,128)(2,1)S(1)} custom-call(bf16[2048,3584]{1,0:T(8,128)(2,1)S(1)} %get-tuple-element.68.after.w_up, bf16[192,2048]{1,0:T(8,128)(2,1)S(1)} %gather.1.after.refs_0_, bf16[192,2048]{1,0:T(8,128)(2,1)S(1)} %gather.1.after.refs_0_), custom_call_target="tpu_custom_call" | custom-call | flops 2818572288 | bytes 14680064 | tf_op jit(solution)/shard_map/up/pallas_call | solution.py:680
  72.0 3.0 %up.5.hidden.after = bf16[192,3584]{1,0:T(8,128)(2,1)S(1)} custom-call(bf16[2048,3584]{1,0:T(8,128)(2,1)S(1)} %get-tuple-element.68.after.w_up, bf16[192,3584]{1,0:T(8,128)(2,1)S(1)} %up.4.after.hidden, bf16[192,2048]{1,0:T(8,128)(2,1)S(1)} %collective-permute-done.18.refs_0_), custom_call_target="tpu_custom_call" | custom-call | flops 2818572288 | bytes 14680064 | tf_op jit(solution)/shard_map/up/pallas_call | solution.py:680
  75.1 3.0 %down.5.after = bf16[192,2048]{1,0:T(8,128)(2,1)S(1)} custom-call(bf16[192,3584]{1,0:T(8,128)(2,1)S(1)} %up.5.hidden.after, bf16[192,3584]{1,0:T(8,128)(2,1)S(1)} %up.5.hidden.after, bf16[3584,1024]{1,0:T(8,128)(2,1)S(1)} %get-tuple-element.95.refs_0_, bf16[3584,1024]{1,0:T(8,128)(2,1)S(1)} %fetch.3.after.refs_1_.refs_0_), custom_call_target="tpu_custom_call" | custom-call | flops 2818572288 | bytes 14680064 | tf_op jit(solution)/shard_map/down/pallas_call | solution.py:693
  78.1 0.6 collective-permute-start.19
  78.7 1.8 %down.6.own = bf16[192,1024]{1,0:T(8,128)(2,1)S(1)} custom-call(bf16[192,3584]{1,0:T(8,128)(2,1)S(1)} %up.4.after.hidden, bf16[192,2048]{1,0:T(8,128)(2,1)S(1)} %down.5.after, bf16[3584,1024]{1,0:T(8,128)(2,1)S(1)} %get-tuple-element.95.refs_0_), custom_call_target="tpu_custom_call" | custom-call | flops 1409286144 | bytes 7340032 | tf_op jit(solution)/shard_map/down/pallas_call | solution.py:693
  80.5 0.1 collective-permute-done.19.refs_0_
  80.6 0.1 join.2
  80.7 1.4 %collective-permute-start.21 = (bf16[64,1024]{1,0:T(8,128)(2,1)S(1)}, bf16[64,1024]{1,0:T(8,128)(2,1)S(1)}, u32[]{:S(2)}, u32[]{:S(2)}) collective-permute-start(bf16[64,1024]{1,0:T(8,128)(2,1)S(1)} %get-tuple-element.101), channel_id=1, source_target_pairs={{0,4},{1,5},{2,6},{3,7},{4,0},{5,1},{6,2},{7,3},{8,12},{9,13},{10,... | collective-permute-start | bytes 393224 | tf_op jit(solution)/shard_map/ppermute | solution.py:461
  82.0 1.2 %collective-permute-start.22 = (bf16[64,1024]{1,0:T(8,128)(2,1)S(1)}, bf16[64,1024]{1,0:T(8,128)(2,1)S(1)}, u32[]{:S(2)}, u32[]{:S(2)}) collective-permute-start(bf16[64,1024]{1,0:T(8,128)(2,1)S(1)} %get-tuple-element.102), channel_id=1, source_target_pairs={{0,6},{1,7},{2,4},{3,5},{4,2},{5,3},{6,0},{7,1},{8,14},{9,15},{10,... | collective-permute-start | bytes 393224 | tf_op jit(solution)/shard_map/ppermute | solution.py:461
  83.2 1.0 collective-permute-start.20
  84.2 1.6 %down.7.own = bf16[192,1024]{1,0:T(8,128)(2,1)S(1)} custom-call(bf16[192,3584]{1,0:T(8,128)(2,1)S(1)} %up.4.after.hidden, bf16[64,1024]{1,0:T(8,128)(2,1)S(1)} %get-tuple-element.100.after, bf16[3584,1024]{1,0:T(8,128)(2,1)S(1)} %fetch.3.after.refs_1_.refs_0_), custom_call_target="tpu_custom_call" | custom-call | flops 393216 | bytes 2048 | tf_op jit(solution)/shard_map/down/pallas_call | solution.py:693
  85.8 0.1 join.3
  85.9 1.1 collective-permute-start.24
  87.0 1.4 %collective-permute-start.25 = (bf16[64,1024]{1,0:T(8,128)(2,1)S(1)}, bf16[64,1024]{1,0:T(8,128)(2,1)S(1)}, u32[]{:S(2)}, u32[]{:S(2)}) collective-permute-start(bf16[64,1024]{1,0:T(8,128)(2,1)S(1)} %get-tuple-element.105), channel_id=1, source_target_pairs={{0,4},{1,5},{2,6},{3,7},{4,0},{5,1},{6,2},{7,3},{8,12},{9,13},{10,... | collective-permute-start | bytes 393224 | tf_op jit(solution)/shard_map/ppermute | solution.py:461
  88.3 1.2 %collective-permute-done.21.refs_1_ = bf16[64,1024]{1,0:T(8,128)(2,1)S(1)} collective-permute-done((bf16[64,1024]{1,0:T(8,128)(2,1)S(1)}, bf16[64,1024]{1,0:T(8,128)(2,1)S(1)}, u32[]{:S(2)}, u32[]{:S(2)}) %collective-permute-start.21) | collective-permute-done | bytes 131104 | tf_op jit(solution)/shard_map/ppermute | solution.py:461
  89.5 2.0 %collective-permute-start.26 = (bf16[64,1024]{1,0:T(8,128)(2,1)S(1)}, bf16[64,1024]{1,0:T(8,128)(2,1)S(1)}, u32[]{:S(2)}, u32[]{:S(2)}) collective-permute-start(bf16[64,1024]{1,0:T(8,128)(2,1)S(1)} %get-tuple-element.106), channel_id=1, source_target_pairs={{0,6},{1,7},{2,4},{3,5},{4,2},{5,3},{6,0},{7,1},{8,14},{9,15},{10,... | collective-permute-start | bytes 393224 | tf_op jit(solution)/shard_map/ppermute | solution.py:461
  91.5 0.3 finish.2
  91.9 1.6 %collective-permute-start.23 = (bf16[128,1024]{1,0:T(8,128)(2,1)S(1)}, bf16[128,1024]{1,0:T(8,128)(2,1)S(1)}, u32[]{:S(2)}, u32[]{:S(2)}) collective-permute-start(bf16[128,1024]{1,0:T(8,128)(2,1)S(1)} %finish.2), channel_id=1, source_target_pairs={{0,8},{8,16},{16,24},{24,0},{1,9},{9,17},{17,25},{25,1},{2,10},{10... | collective-permute-start | bytes 786440 | tf_op jit(solution)/shard_map/ppermute | solution.py:466
  93.5 0.7 collective-permute-done.24.refs_0_
  94.2 2.6 %collective-permute-done.26.refs_2_ = bf16[64,1024]{1,0:T(8,128)(2,1)S(1)} collective-permute-done((bf16[64,1024]{1,0:T(8,128)(2,1)S(1)}, bf16[64,1024]{1,0:T(8,128)(2,1)S(1)}, u32[]{:S(2)}, u32[]{:S(2)}) %collective-permute-start.26) | collective-permute-done | bytes 131104 | tf_op jit(solution)/shard_map/ppermute | solution.py:461
  96.9 0.3 finish.3
  97.2 1.6 %collective-permute-start.27 = (bf16[128,1024]{1,0:T(8,128)(2,1)S(1)}, bf16[128,1024]{1,0:T(8,128)(2,1)S(1)}, u32[]{:S(2)}, u32[]{:S(2)}) collective-permute-start(bf16[128,1024]{1,0:T(8,128)(2,1)S(1)} %finish.3), channel_id=1, source_target_pairs={{0,8},{8,16},{16,24},{24,0},{1,9},{9,17},{17,25},{25,1},{2,10},{10... | collective-permute-start | bytes 786440 | tf_op jit(solution)/shard_map/ppermute | solution.py:466
  98.8 2.0 %collective-permute-done.23 = bf16[128,1024]{1,0:T(8,128)(2,1)S(1)} collective-permute-done((bf16[128,1024]{1,0:T(8,128)(2,1)S(1)}, bf16[128,1024]{1,0:T(8,128)(2,1)S(1)}, u32[]{:S(2)}, u32[]{:S(2)}) %collective-permute-start.23) | collective-permute-done | bytes 262176 | tf_op jit(solution)/shard_map/ppermute | solution.py:466
  100.8 5.7 %collective-permute-done.27 = bf16[128,1024]{1,0:T(8,128)(2,1)S(1)} collective-permute-done((bf16[128,1024]{1,0:T(8,128)(2,1)S(1)}, bf16[128,1024]{1,0:T(8,128)(2,1)S(1)}, u32[]{:S(2)}, u32[]{:S(2)}) %collective-permute-start.27) | collective-permute-done | bytes 262176 | tf_op jit(solution)/shard_map/ppermute | solution.py:466
  106.5 0.8 maximum_bitcast_fusion
  (19 shorter events, 0.4 us)
Async XLA Ops:
  0.0 4.5 %collective-permute-start = (bf16[128,2048]{1,0:T(8,128)(2,1)}, bf16[128,2048]{1,0:T(8,128)(2,1)S(1)}, u32[]{:S(2)}, u32[]{:S(2)}) collective-permute-start(bf16[128,2048]{1,0:T(8,128)(2,1)} %bitcast.24), channel_id=1, source_target_pairs={{0,1},{1,0},{2,3},{3,2},{4,5},{5,4},{6,7},{7,6},{8,9},{9,8},{10,11... | collective-permute-start | bytes 1572872 | tf_op jit(solution)/shard_map/ppermute | solution.py:461
  0.5 15.3 %collective-permute-start.2 = (bf16[128,2048]{1,0:T(8,128)(2,1)}, bf16[128,2048]{1,0:T(8,128)(2,1)S(1)}, u32[]{:S(2)}, u32[]{:S(2)}) collective-permute-start(bf16[128,2048]{1,0:T(8,128)(2,1)} %bitcast.25), channel_id=1, source_target_pairs={{0,2},{1,3},{2,0},{3,1},{4,6},{5,7},{6,4},{7,5},{8,10},{9,11},{10,... | collective-permute-start | bytes 1572872 | tf_op jit(solution)/shard_map/ppermute | solution.py:461
  2.9 14.3 %collective-permute-start.1 = (bf16[2048,128]{1,0:T(8,128)(2,1)}, bf16[2048,128]{1,0:T(8,128)(2,1)S(1)}, u32[]{:S(2)}, u32[]{:S(2)}) collective-permute-start(bf16[2048,128]{1,0:T(8,128)(2,1)} %bitcast.30), channel_id=1, source_target_pairs={{0,4},{1,5},{2,6},{3,7},{4,0},{5,1},{6,2},{7,3},{8,12},{9,13},{10,... | collective-permute-start | bytes 1572872 | tf_op jit(solution)/shard_map/ppermute | solution.py:461
  16.1 4.0 %collective-permute-start.3 = (bf16[128,2048]{1,0:T(8,128)(2,1)S(1)}, bf16[128,2048]{1,0:T(8,128)(2,1)S(1)}, u32[]{:S(2)}, u32[]{:S(2)}) collective-permute-start(bf16[128,2048]{1,0:T(8,128)(2,1)S(1)} %norm.3.first), channel_id=1, source_target_pairs={{0,1},{1,0},{2,3},{3,2},{4,5},{5,4},{6,7},{7,6},{8,9},{9,8},{10,11... | collective-permute-start | bytes 1572872 | tf_op jit(solution)/shard_map/ppermute | solution.py:461
  18.5 8.8 %collective-permute-start.4 = (bf16[2,256,128]{2,1,0:T(8,128)(2,1)S(1)}, bf16[2,256,128]{2,1,0:T(8,128)(2,1)S(1)}, u32[]{:S(2)}, u32[]{:S(2)}) collective-permute-start(bf16[2,256,128]{2,1,0:T(8,128)(2,1)S(1)} %get-tuple-element.72.refs_2_), channel_id=1, source_target_pairs={{0,4},{1,5},{2,6},{3,7},{4,0},{5,1},{6,2},{7,3},{8,12},{9,13},{10,... | collective-permute-start | bytes 393224 | tf_op jit(solution)/shard_map/ppermute | solution.py:461
  21.0 6.3 %collective-permute-start.5 = (bf16[2,256,128]{2,1,0:T(8,128)(2,1)S(1)}, bf16[2,256,128]{2,1,0:T(8,128)(2,1)S(1)}, u32[]{:S(2)}, u32[]{:S(2)}) collective-permute-start(bf16[2,256,128]{2,1,0:T(8,128)(2,1)S(1)} %get-tuple-element.69.refs_1_.refs_3_), channel_id=1, source_target_pairs={{0,4},{1,5},{2,6},{3,7},{4,0},{5,1},{6,2},{7,3},{8,12},{9,13},{10,... | collective-permute-start | bytes 393224 | tf_op jit(solution)/shard_map/ppermute | solution.py:461
  28.0 6.3 %collective-permute-start.7 = (bf16[128,512]{1,0:T(8,128)(2,1)S(1)}, bf16[128,512]{1,0:T(8,128)(2,1)S(1)}, u32[]{:S(2)}, u32[]{:S(2)}) collective-permute-start(bf16[128,512]{1,0:T(8,128)(2,1)S(1)} %get-tuple-element.78), channel_id=1, source_target_pairs={{0,2},{1,3},{2,0},{3,1},{4,6},{5,7},{6,4},{7,5},{8,10},{9,11},{10,... | collective-permute-start | bytes 393224 | tf_op jit(solution)/shard_map/ppermute | solution.py:461
  28.8 5.8 %collective-permute-start.8 = (bf16[128,512]{1,0:T(8,128)(2,1)S(1)}, bf16[128,512]{1,0:T(8,128)(2,1)S(1)}, u32[]{:S(2)}, u32[]{:S(2)}) collective-permute-start(bf16[128,512]{1,0:T(8,128)(2,1)S(1)} %get-tuple-element.79), channel_id=1, source_target_pairs={{0,3},{1,2},{2,1},{3,0},{4,7},{5,6},{6,5},{7,4},{8,11},{9,10},{10,... | collective-permute-start | bytes 393224 | tf_op jit(solution)/shard_map/ppermute | solution.py:461
  29.4 5.2 %collective-permute-start.6 = (bf16[128,512]{1,0:T(8,128)(2,1)S(1)}, bf16[128,512]{1,0:T(8,128)(2,1)S(1)}, u32[]{:S(2)}, u32[]{:S(2)}) collective-permute-start(bf16[128,512]{1,0:T(8,128)(2,1)S(1)} %get-tuple-element.77), channel_id=1, source_target_pairs={{0,1},{1,0},{2,3},{3,2},{4,5},{5,4},{6,7},{7,6},{8,9},{9,8},{10,11... | collective-permute-start | bytes 393224 | tf_op jit(solution)/shard_map/ppermute | solution.py:461
  39.8 2.0 %collective-permute-start.9 = (bf16[16,2176]{1,0:T(8,128)(2,1)S(1)}, bf16[16,2176]{1,0:T(8,128)(2,1)S(1)}, u32[]{:S(2)}, u32[]{:S(2)}) collective-permute-start(bf16[16,2176]{1,0:T(8,128)(2,1)S(1)} %get-tuple-element.91.own), channel_id=1, source_target_pairs={{0,1},{1,0},{2,3},{3,2},{4,5},{5,4},{6,7},{7,6},{8,9},{9,8},{10,11... | collective-permute-start | bytes 208904 | tf_op jit(solution)/shard_map/ppermute | solution.py:461
  42.4 6.2 %collective-permute-start.12 = (bf16[16,2176]{1,0:T(8,128)(2,1)S(1)}, bf16[16,2176]{1,0:T(8,128)(2,1)S(1)}, u32[]{:S(2)}, u32[]{:S(2)}) collective-permute-start(bf16[16,2176]{1,0:T(8,128)(2,1)S(1)} %pair.1), channel_id=1, source_target_pairs={{0,6},{1,7},{2,4},{3,5},{4,2},{5,3},{6,0},{7,1},{8,14},{9,15},{10,... | collective-permute-start | bytes 208904 | tf_op jit(solution)/shard_map/ppermute | solution.py:461
  45.4 4.3 %collective-permute-start.11 = (bf16[16,2176]{1,0:T(8,128)(2,1)S(1)}, bf16[16,2176]{1,0:T(8,128)(2,1)S(1)}, u32[]{:S(2)}, u32[]{:S(2)}) collective-permute-start(bf16[16,2176]{1,0:T(8,128)(2,1)S(1)} %pair.1), channel_id=1, source_target_pairs={{0,4},{1,5},{2,6},{3,7},{4,0},{5,1},{6,2},{7,3},{8,12},{9,13},{10,... | collective-permute-start | bytes 208904 | tf_op jit(solution)/shard_map/ppermute | solution.py:461
  45.4 4.9 %collective-permute-start.10 = (bf16[16,2176]{1,0:T(8,128)(2,1)S(1)}, bf16[16,2176]{1,0:T(8,128)(2,1)S(1)}, u32[]{:S(2)}, u32[]{:S(2)}) collective-permute-start(bf16[16,2176]{1,0:T(8,128)(2,1)S(1)} %pair.1), channel_id=1, source_target_pairs={{0,2},{1,3},{2,0},{3,1},{4,6},{5,7},{6,4},{7,5},{8,10},{9,11},{10,... | collective-permute-start | bytes 208904 | tf_op jit(solution)/shard_map/ppermute | solution.py:461
  53.5 3.6 %collective-permute-start.13 = (bf16[64,2048]{1,0:T(8,128)(2,1)S(1)}, bf16[64,2048]{1,0:T(8,128)(2,1)S(1)}, u32[]{:S(2)}, u32[]{:S(2)}) collective-permute-start(bf16[64,2048]{1,0:T(8,128)(2,1)S(1)} %get-tuple-element.94.after.refs_0_), channel_id=1, source_target_pairs={{0,1},{1,0},{2,3},{3,2},{4,5},{5,4},{6,7},{7,6},{8,9},{9,8},{10,11... | collective-permute-start | bytes 786440 | tf_op jit(solution)/shard_map/ppermute | solution.py:461
  53.6 9.2 %collective-permute-start.15 = (bf16[64,2048]{1,0:T(8,128)(2,1)S(1)}, bf16[64,2048]{1,0:T(8,128)(2,1)S(1)}, u32[]{:S(2)}, u32[]{:S(2)}) collective-permute-start(bf16[64,2048]{1,0:T(8,128)(2,1)S(1)} %get-tuple-element.97), channel_id=1, source_target_pairs={{0,2},{1,3},{2,0},{3,1},{4,6},{5,7},{6,4},{7,5},{8,10},{9,11},{10,... | collective-permute-start | bytes 786440 | tf_op jit(solution)/shard_map/ppermute | solution.py:461
  54.7 12.9 %collective-permute-start.16 = (bf16[64,2048]{1,0:T(8,128)(2,1)S(1)}, bf16[64,2048]{1,0:T(8,128)(2,1)S(1)}, u32[]{:S(2)}, u32[]{:S(2)}) collective-permute-start(bf16[64,2048]{1,0:T(8,128)(2,1)S(1)} %get-tuple-element.98), channel_id=1, source_target_pairs={{0,4},{1,5},{2,6},{3,7},{4,0},{5,1},{6,2},{7,3},{8,12},{9,13},{10,... | collective-permute-start | bytes 786440 | tf_op jit(solution)/shard_map/ppermute | solution.py:461
  56.1 12.7 %collective-permute-start.17 = (bf16[64,2048]{1,0:T(8,128)(2,1)S(1)}, bf16[64,2048]{1,0:T(8,128)(2,1)S(1)}, u32[]{:S(2)}, u32[]{:S(2)}) collective-permute-start(bf16[64,2048]{1,0:T(8,128)(2,1)S(1)} %get-tuple-element.99), channel_id=1, source_target_pairs={{0,6},{1,7},{2,4},{3,5},{4,2},{5,3},{6,0},{7,1},{8,14},{9,15},{10,... | collective-permute-start | bytes 786440 | tf_op jit(solution)/shard_map/ppermute | solution.py:461
  61.4 7.5 %collective-permute-start.14 = (bf16[64,2048]{1,0:T(8,128)(2,1)S(1)}, bf16[64,2048]{1,0:T(8,128)(2,1)S(1)}, u32[]{:S(2)}, u32[]{:S(2)}) collective-permute-start(bf16[64,2048]{1,0:T(8,128)(2,1)S(1)} %get-tuple-element.96), channel_id=1, source_target_pairs={{0,1},{1,0},{2,3},{3,2},{4,5},{5,4},{6,7},{7,6},{8,9},{9,8},{10,11... | collective-permute-start | bytes 786440 | tf_op jit(solution)/shard_map/ppermute | solution.py:461
  68.9 3.1 %collective-permute-start.18 = (bf16[192,2048]{1,0:T(8,128)(2,1)S(1)}, bf16[192,2048]{1,0:T(8,128)(2,1)S(1)}, u32[]{:S(2)}, u32[]{:S(2)}) collective-permute-start(bf16[192,2048]{1,0:T(8,128)(2,1)S(1)} %gather.1.after.refs_0_), channel_id=1, source_target_pairs={{0,1},{1,0},{2,3},{3,2},{4,5},{5,4},{6,7},{7,6},{8,9},{9,8},{10,11... | collective-permute-start | bytes 2359304 | tf_op jit(solution)/shard_map/ppermute | solution.py:461
  78.1 2.5 %collective-permute-start.19 = (bf16[192,2048]{1,0:T(8,128)(2,1)S(1)}, bf16[192,2048]{1,0:T(8,128)(2,1)S(1)}, u32[]{:S(2)}, u32[]{:S(2)}) collective-permute-start(bf16[192,2048]{1,0:T(8,128)(2,1)S(1)} %down.5.after), channel_id=1, source_target_pairs={{0,1},{1,0},{2,3},{3,2},{4,5},{5,4},{6,7},{7,6},{8,9},{9,8},{10,11... | collective-permute-start | bytes 2359304 | tf_op jit(solution)/shard_map/ppermute | solution.py:461
  80.7 8.8 %collective-permute-start.21 = (bf16[64,1024]{1,0:T(8,128)(2,1)S(1)}, bf16[64,1024]{1,0:T(8,128)(2,1)S(1)}, u32[]{:S(2)}, u32[]{:S(2)}) collective-permute-start(bf16[64,1024]{1,0:T(8,128)(2,1)S(1)} %get-tuple-element.101), channel_id=1, source_target_pairs={{0,4},{1,5},{2,6},{3,7},{4,0},{5,1},{6,2},{7,3},{8,12},{9,13},{10,... | collective-permute-start | bytes 393224 | tf_op jit(solution)/shard_map/ppermute | solution.py:461
  82.0 9.5 %collective-permute-start.22 = (bf16[64,1024]{1,0:T(8,128)(2,1)S(1)}, bf16[64,1024]{1,0:T(8,128)(2,1)S(1)}, u32[]{:S(2)}, u32[]{:S(2)}) collective-permute-start(bf16[64,1024]{1,0:T(8,128)(2,1)S(1)} %get-tuple-element.102), channel_id=1, source_target_pairs={{0,6},{1,7},{2,4},{3,5},{4,2},{5,3},{6,0},{7,1},{8,14},{9,15},{10,... | collective-permute-start | bytes 393224 | tf_op jit(solution)/shard_map/ppermute | solution.py:461
  83.2 8.3 %collective-permute-start.20 = (bf16[64,1024]{1,0:T(8,128)(2,1)S(1)}, bf16[64,1024]{1,0:T(8,128)(2,1)S(1)}, u32[]{:S(2)}, u32[]{:S(2)}) collective-permute-start(bf16[64,1024]{1,0:T(8,128)(2,1)S(1)} %get-tuple-element.100.after), channel_id=1, source_target_pairs={{0,2},{1,3},{2,0},{3,1},{4,6},{5,7},{6,4},{7,5},{8,10},{9,11},{10,... | collective-permute-start | bytes 393224 | tf_op jit(solution)/shard_map/ppermute | solution.py:461
  85.9 8.3 %collective-permute-start.24 = (bf16[64,1024]{1,0:T(8,128)(2,1)S(1)}, bf16[64,1024]{1,0:T(8,128)(2,1)S(1)}, u32[]{:S(2)}, u32[]{:S(2)}) collective-permute-start(bf16[64,1024]{1,0:T(8,128)(2,1)S(1)} %get-tuple-element.104), channel_id=1, source_target_pairs={{0,2},{1,3},{2,0},{3,1},{4,6},{5,7},{6,4},{7,5},{8,10},{9,11},{10,... | collective-permute-start | bytes 393224 | tf_op jit(solution)/shard_map/ppermute | solution.py:461
  87.0 7.2 %collective-permute-start.25 = (bf16[64,1024]{1,0:T(8,128)(2,1)S(1)}, bf16[64,1024]{1,0:T(8,128)(2,1)S(1)}, u32[]{:S(2)}, u32[]{:S(2)}) collective-permute-start(bf16[64,1024]{1,0:T(8,128)(2,1)S(1)} %get-tuple-element.105), channel_id=1, source_target_pairs={{0,4},{1,5},{2,6},{3,7},{4,0},{5,1},{6,2},{7,3},{8,12},{9,13},{10,... | collective-permute-start | bytes 393224 | tf_op jit(solution)/shard_map/ppermute | solution.py:461
  89.5 7.4 %collective-permute-start.26 = (bf16[64,1024]{1,0:T(8,128)(2,1)S(1)}, bf16[64,1024]{1,0:T(8,128)(2,1)S(1)}, u32[]{:S(2)}, u32[]{:S(2)}) collective-permute-start(bf16[64,1024]{1,0:T(8,128)(2,1)S(1)} %get-tuple-element.106), channel_id=1, source_target_pairs={{0,6},{1,7},{2,4},{3,5},{4,2},{5,3},{6,0},{7,1},{8,14},{9,15},{10,... | collective-permute-start | bytes 393224 | tf_op jit(solution)/shard_map/ppermute | solution.py:461
  91.9 9.0 %collective-permute-start.23 = (bf16[128,1024]{1,0:T(8,128)(2,1)S(1)}, bf16[128,1024]{1,0:T(8,128)(2,1)S(1)}, u32[]{:S(2)}, u32[]{:S(2)}) collective-permute-start(bf16[128,1024]{1,0:T(8,128)(2,1)S(1)} %finish.2), channel_id=1, source_target_pairs={{0,8},{8,16},{16,24},{24,0},{1,9},{9,17},{17,25},{25,1},{2,10},{10... | collective-permute-start | bytes 786440 | tf_op jit(solution)/shard_map/ppermute | solution.py:466
  97.2 9.3 %collective-permute-start.27 = (bf16[128,1024]{1,0:T(8,128)(2,1)S(1)}, bf16[128,1024]{1,0:T(8,128)(2,1)S(1)}, u32[]{:S(2)}, u32[]{:S(2)}) collective-permute-start(bf16[128,1024]{1,0:T(8,128)(2,1)S(1)} %finish.3), channel_id=1, source_target_pairs={{0,8},{8,16},{16,24},{24,0},{1,9},{9,17},{17,25},{25,1},{2,10},{10... | collective-permute-start | bytes 786440 | tf_op jit(solution)/shard_map/ppermute | solution.py:466

commit v6 on v5

--- a/solution.py
+++ b/solution.py
@@ -62,6 +62,12 @@
 
 def dot(a, b, dims=((1,), (0,))):
     return lax.dot_general(a, b, (dims, ((), ())), preferred_element_type=F32)
+
+
+def dot_high(a, b):
+    count = a[0].shape[0]
+    both = dot(jnp.concatenate(a, 0), b)
+    return both[:count] + both[count:]
 
 
 def dot_split(a, b, dims=((1,), (0,))):
@@ -139,7 +145,7 @@
         total_out[slot] = jnp.broadcast_to(total, (GROUP * rows, LANES))
 
 
-def far_kernel(turn, slots, last, place, after, *refs):
+def far_kernel(turn, slots, last, place, *refs):
     queries, (largest, total, summed), halves, outs = refs[:2], refs[2:5], refs[5:7], refs[7:]
     rows = queries[0].shape[1] // GROUP
     mine = place[0] // KVH
@@ -181,8 +187,8 @@
     place, x, gains, skip, dt_in, dt_out, bias, rate, w_bct, *refs
 ):
     attended = refs[:KVH]
-    base, keep_out, drive_out, chunk_state, chunk_keep, bc_out, bct_out, ends = refs[KVH:-4]
-    mixed, pre, tail_high, tail_low = refs[-4:]
+    base, keep_out, drive_out, chunk_state, chunk_keep, bc_out, bct_out, ends = refs[KVH:-3]
+    mixed, pre, tail = refs[-3:]
     rows, width = x.shape
     state = w_bct.shape[0] // 2
     chunks = rows // EIGHT
@@ -214,7 +220,7 @@
         for low in range(0, width, block):
             cols = pl.ds(low, block)
             raw = pre[at, cols] + bias[:, cols]
-            step_size = jnp.maximum(raw, 0.0) + jnp.log1p(jnp.exp(-jnp.abs(raw)))
+            step_size = jnp.maximum(raw, 0.0) + jnp.log(1.0 + jnp.exp(-jnp.abs(raw)))
             keep = jnp.exp(-step_size * rate[:, cols])
             drive = step_size * mixed[at, cols].astype(F32)
             keep_out[at, cols] = keep
@@ -230,17 +236,14 @@
                 whole = after[0:1] * kept[0:1]
                 chunk_keep[pl.ds(index * (STRIP // EIGHT) + part, 1), cols] = whole
                 tails.append(after * drive[part * EIGHT : (part + 1) * EIGHT])
-            high, low_part = split(jnp.concatenate(tails, 0))
-            tail_high[at, cols] = high
-            tail_low[at, cols] = low_part
+            tail[at, cols] = jnp.concatenate(tails, 0).astype(BF16)
         return carry
 
     lax.fori_loop(0, rows // STRIP, steps, 0, unroll=2)
 
     spread = jnp.concatenate([b_rows] * chunks, 0)
     own = iota(spread.shape, 0) // state == iota(spread.shape, 1) // EIGHT
-    spread = split(jnp.where(own, spread, 0.0))
-    chunk_state[...] = dot_split(spread, (tail_high[...], tail_low[...]))
+    chunk_state[...] = dot_high(split(jnp.where(own, spread, 0.0)), tail[...])
     products = []
     for tile in range(width // LANES):
         cols = pl.ds(tile * LANES, LANES)
@@ -255,7 +258,7 @@
     ends[:, width:] = jnp.concatenate(products, 0).astype(BF16)
 
 
-def pair_kernel(place, own, other, ends):
+def pair_kernel(place, after, own, other, ends):
     width = own.shape[1] - LANES
     first = lax.rem(place[0], 2) == 0
     mine = own[...].astype(F32)
@@ -269,8 +272,8 @@
     ends[:, width:] = (earlier[:, width:] * fade).astype(BF16)
 
 
-def within_kernel(bc, bct, base, keep, drive, second, faded, coef):
-    rows, width = base.shape
+def couple_kernel(bc, bct, coef):
+    rows = bc.shape[0]
     state = bct.shape[0] // 2
     coupling = dot_split(split(bc[:, state:]), split(bct[:state]))
     row, lane = iota((rows, rows), 0), iota((rows, rows), 1)
@@ -279,6 +282,10 @@
         diagonal = jnp.sum(jnp.where(lane == row - back, coupling, 0.0), 1, keepdims=True)
         total = total + jnp.where((lane == back) & (row % EIGHT >= back), diagonal, 0.0)
     coef[...] = total
+
+
+def within_kernel(coef, base, keep, drive, second, faded):
+    rows, width = base.shape
     edge = iota((EIGHT, width), 0)
 
     def chunk(index, carry):
@@ -302,8 +309,8 @@
 def route_kernel(
     place, before, faded, chunk_state, chunk_keep, bc, gains, router_t, routes_t, beside, *refs
 ):
-    ends, (second, weighting), packed = refs[:-11], refs[-11:-9], refs[-9:-5]
-    state_high, state_low, carried, expert_in, stack = refs[-5:]
+    ends, (second, weighting), packed = refs[:-10], refs[-10:-8], refs[-8:-4]
+    states, carried, expert_in, stack = refs[-4:]
     rows, width = before.shape
     chunks = chunk_keep.shape[0]
     state = chunk_state.shape[0] // chunks
@@ -326,9 +333,7 @@
         total = jnp.where(second_core, joined, total)
         for chunk in range(chunks):
             at = pl.ds(chunk * state, state)
-            high, low = split(total)
-            state_high[at, cols] = high
-            state_low[at, cols] = low
+            states[at, cols] = total.astype(BF16)
             total = total * chunk_keep[chunk : chunk + 1, cols] + chunk_state[at, cols]
     wide = chunks * state
     repeat = (iota((state, wide), 1) % state == iota((state, wide), 0)).astype(BF16)
@@ -336,7 +341,7 @@
     spread = [
         jnp.where(here, dot(part, repeat), 0.0).astype(BF16) for part in split(bc[:, state:])
     ]
-    carried[...] = dot_split(spread, (state_high[...], state_low[...]))
+    carried[...] = dot_high(spread, states[...])
 
     def normalize(at):
         values = before[at, :] + carried[at, :] * faded[at, :]
@@ -387,7 +392,7 @@
         copy.wait()
 
 
-def fetch(items, after):
+def fetch(items, after, hurry=False):
     arrays, pieces, starts, widths = zip(*items)
     return pl.pallas_call(
         functools.partial(fetch_kernel, pieces, starts),
@@ -399,7 +404,7 @@
         out_specs=(VMEM,) * len(arrays),
         scratch_shapes=[pltpu.SemaphoreType.DMA((sum(pieces),))],
         compiler_params=params(4),
-        cost_estimate=cost(0, sum(array.size * 4 for array in arrays)),
+        cost_estimate=cost(0, 0 if hurry else sum(array.size * 4 for array in arrays)),
         name="fetch",
     )(*[in_hbm(array) for array in arrays], after)
 
@@ -556,7 +561,6 @@
     pasts = [
         [exchange(half, "ctx", turn * KVH) for half in kv] for turn in range(1, turns)
     ]
-    lowering += fetch([(w_down[0], 16, half, half)], last_kv)
     scored = GROUP * rows * group_rows * KVH
     tallies = (shape((KVH, GROUP * rows, LANES), F32),) * 2 + (
         shape((KVH, GROUP * rows, HD), F32),
@@ -578,12 +582,12 @@
             state_now = pl.pallas_call(
                 functools.partial(far_kernel, turn, slots, last),
                 out_shape=(shape((rows, GROUP * HD), BF16),) * len(slots) if last else tallies,
-                in_specs=[SMEM, ANY] + [VMEM] * 7,
+                in_specs=[SMEM] + [VMEM] * 7,
                 out_specs=(VMEM,) * (len(slots) if last else 3),
                 compiler_params=params(16),
                 cost_estimate=cost(2 * scored * HD, 2 * group_rows * GROUP * HD * 4, scored // 2),
                 name="far",
-            )(place, lowering[1], *queries, *state_now, *past)
+            )(place, *queries, *state_now, *past)
         for slot, block in zip(slots, state_now):
             attended[slot] = exchange(block, "ctx", slot) if slot else block
 
@@ -605,7 +609,6 @@
             pltpu.VMEM((rows, width), BF16),
             pltpu.VMEM((rows, width), F32),
             pltpu.VMEM((rows, width), BF16),
-            pltpu.VMEM((rows, width), BF16),
         ],
         compiler_params=params(20),
         cost_estimate=cost(10 * rows * width * 256, 30 * rows * width, 3 * rows * width),
@@ -623,26 +626,34 @@
         *attended,
     )
     beside_ends = exchange(ends, "ctx", 1)
+    coef = pl.pallas_call(
+        couple_kernel,
+        out_shape=shape((rows, rows), F32),
+        in_specs=[VMEM, VMEM],
+        out_specs=VMEM,
+        compiler_params=params(4),
+        cost_estimate=cost(20 * rows * rows, 20 * rows * rows),
+        name="couple",
+    )(bc, bct)
     chip_ends = pl.pallas_call(
         pair_kernel,
         out_shape=shape(ends.shape, BF16),
-        in_specs=[SMEM, VMEM, VMEM],
+        in_specs=[SMEM, ANY, VMEM, VMEM],
         out_specs=VMEM,
         compiler_params=params(8),
         cost_estimate=cost(4 * ends.size, 8 * ends.size),
         name="pair",
-    )(place, ends, beside_ends)
+    )(place, coef, ends, beside_ends)
     earlier_ends = [exchange(chip_ends, "ctx", mask) for mask in range(2, shard_count, 2)]
     before, faded = pl.pallas_call(
         within_kernel,
         out_shape=(shape((rows, width), F32), shape((rows, width), F32)),
-        in_specs=[VMEM] * 5,
+        in_specs=[VMEM] * 4,
         out_specs=(VMEM, VMEM),
-        scratch_shapes=[pltpu.VMEM((rows, rows), F32)],
         compiler_params=params(12),
         cost_estimate=cost(40 * rows * width, 20 * rows * width),
         name="within",
-    )(bc, bct, base, keep, drive)
+    )(coef, base, keep, drive)
     second, weighting, *packed = pl.pallas_call(
         route_kernel,
         out_shape=(shape((rows, width), F32), shape((rows, EXPERTS * capacity), F32))
@@ -650,7 +661,6 @@
         in_specs=[SMEM] + [VMEM] * (9 + len(earlier_ends)),
         out_specs=(VMEM,) * (2 + EXPERTS),
         scratch_shapes=[
-            pltpu.VMEM((chunks * state, width), BF16),
             pltpu.VMEM((chunks * state, width), BF16),
             pltpu.VMEM((rows, width), F32),
             pltpu.VMEM((rows, width), BF16),
@@ -706,7 +716,9 @@
 
     moved = between_experts(packed[1:])
     stay = [exchange(packed[0], "ctx", turn) if turn else packed[0] for turn in range(parts)]
-    stay_out = lower(lowering, lift(stay, packed[0]), packed[0], parts)
+    stay_hidden = lift(stay, packed[0])
+    lowering += fetch([(w_down[0], 16, half, half)], stay_hidden, hurry=True)
+    stay_out = lower(lowering, stay_hidden, packed[0], parts)
     stay_sums = [stay_out[0]] + [
         exchange(stay_out[turn], "ctx", turn) for turn in range(1, parts)
     ]

time: 108 us -> 106 us (0.981)
  transfers between devices with their start and end apart: 28 -> 28, of which waited for: 16 -> 16; matrix products, arithmetic and copies ran while one was open for 0% -> 0% of each run, Pallas kernels for 30% -> 31%
where the time goes in v6:
time: 106 us
  Pallas kernels  47.2 us (45%)
  waiting for transfers between devices  28.8 us (27%)
  starting transfers between devices  28.7 us (27%)
    ppermute x26, starting transfers between devices, exchange(): return lax.ppermute(value, axis, [(at, at ^ mask) for at in range(count)])  25.5 us
    ppermute x26, waiting for transfers between devices, exchange(): return lax.ppermute(value, axis, [(at, at ^ mask) for at in range(count)])  20.6 us
    pallas_call x2, Pallas kernels, fetch(): pl.pallas_call(functools.partial(fetch_kernel, pieces, starts), out_shape...  11.6 us
    pallas_call x4, Pallas kernels, lower(): pl.pallas_call(functools.partial(down_kernel, len(weights)), out_shape=(s...  8.5 us
    ppermute x2, waiting for transfers between devices, shifted(): lax.ppermute(value, axis, [(at, (at + steps) % count) for at in range(cou...  8.17 us
    pallas_call x3, Pallas kernels, lift(): pl.pallas_call(up_kernel, out_shape=shape((count, units), BF16), in_specs...  8.16 us
    pallas_call x1, Pallas kernels, on_device(): pl.pallas_call(prepare_kernel, out_shape=(shape((rows, width), F32), shap...  4.59 us
    ppermute x2, starting transfers between devices, shifted(): lax.ppermute(value, axis, [(at, (at + steps) % count) for at in range(cou...  3.26 us
  transfers between devices with their start and end apart: 28, of which 16 were waited for; matrix products, arithmetic and copies ran while one was open for 0% of the time, Pallas kernels for 31%

profile of v6, /device:TPU:0, one launch (start us, length us, event | category | flops | bytes accessed | tf_op | source)
XLA Modules:
  0.0 105.9 jit_solution(14447249000953627848)
XLA Ops:
  0.0 0.5 collective-permute-start
  0.5 2.5 %collective-permute-start.2 = (bf16[128,2048]{1,0:T(8,128)(2,1)}, bf16[128,2048]{1,0:T(8,128)(2,1)S(1)}, u32[]{:S(2)}, u32[]{:S(2)}) collective-permute-start(bf16[128,2048]{1,0:T(8,128)(2,1)} %bitcast.25), channel_id=1, source_target_pairs={{0,2},{1,3},{2,0},{3,1},{4,6},{5,7},{6,4},{7,5},{8,10},{9,11},{10,... | collective-permute-start | bytes 1572872 | tf_op jit(solution)/shard_map/ppermute | solution.py:466
  2.9 1.5 %collective-permute-start.1 = (bf16[2048,128]{1,0:T(8,128)(2,1)}, bf16[2048,128]{1,0:T(8,128)(2,1)S(1)}, u32[]{:S(2)}, u32[]{:S(2)}) collective-permute-start(bf16[2048,128]{1,0:T(8,128)(2,1)} %bitcast.30), channel_id=1, source_target_pairs={{0,4},{1,5},{2,6},{3,7},{4,0},{5,1},{6,2},{7,3},{8,12},{9,13},{10,... | collective-permute-start | bytes 1572872 | tf_op jit(solution)/shard_map/ppermute | solution.py:466
  4.5 1.7 %norm.2 = (bf16[128,2048]{1,0:T(8,128)(2,1)S(1)}, bf16[128,2048]{1,0:T(8,128)(2,1)S(1)}) custom-call(f32[3,1,2048]{2,1,0:T(1,128)} %bitcast.33, s32[3]{0:T(128)S(1)} %pad_add_fusion.after.place, bf16[128,2048]{1,0:T(8,128)(2,1)} %bitcast.26, bf16[128,2048]{1,0:T(8,128)(2,1)S(1)} %collective-permute-done.refs_1_), custom_call_target="tpu_custom_call" | custom-call | flops 2097152 | bytes 1048576 | tf_op jit(solution)/shard_map/norm/pallas_call | solution.py:518
  6.3 8.4 %fetch.2 = (bf16[2048,3584]{1,0:T(8,128)(2,1)S(1)}, bf16[3584,1024]{1,0:T(8,128)(2,1)S(1)}, f32[3,1,2048]{2,1,0:T(1,128)S(1)}, bf16[2048,128]{1,0:T(8,128)(2,1)S...) custom-call(bf16[2048,3584]{1,0:T(8,128)(2,1)} %bitcast.23, ...), custom_call_target="tpu_custom_call" | custom-call | bytes 63259648 | tf_op jit(solution)/shard_map/fetch/pallas_call | solution.py:397
  14.7 1.1 %collective-permute-done.2.refs_0_ = bf16[128,2048]{1,0:T(8,128)(2,1)S(1)} collective-permute-done((bf16[128,2048]{1,0:T(8,128)(2,1)}, bf16[128,2048]{1,0:T(8,128)(2,1)S(1)}, u32[]{:S(2)}, u32[]{:S(2)}) %collective-permute-start.2) | collective-permute-done | bytes 524320 | tf_op jit(solution)/shard_map/ppermute | solution.py:466
  15.7 0.3 norm.3.first
  16.2 1.1 collective-permute-done.1.w_other
  17.2 1.2 %project.1 = (bf16[2,512,128]{2,1,0:T(8,128)(2,1)S(1)}, bf16[2,256,128]{2,1,0:T(8,128)(2,1)S(1)}, bf16[2048,256]{1,0:T(8,128)(2,1)S(1)}) custom-call(s32[3]{0:T(128)S(1)} %pad_add_fusion.after.place, bf16[2048,128]{1,0:T(8,128)(2,1)S(1)} %get-tuple-element.65.w_own, bf16[2048,128]{1,0:T(8,128)(2,1)S(1)} %collective-permute-done.1.w_other, ...), custom_call_target="tpu_custom_call" | custom-call | flops 268435456 | bytes 4194304 | tf_op jit(solution)/shard_map/project/pallas_call | solution.py:541
  18.5 1.6 %collective-permute-start.4 = (bf16[2,256,128]{2,1,0:T(8,128)(2,1)S(1)}, bf16[2,256,128]{2,1,0:T(8,128)(2,1)S(1)}, u32[]{:S(2)}, u32[]{:S(2)}) collective-permute-start(bf16[2,256,128]{2,1,0:T(8,128)(2,1)S(1)} %get-tuple-element.71.refs_2_), channel_id=1, source_target_pairs={{0,4},{1,5},{2,6},{3,7},{4,0},{5,1},{6,2},{7,3},{8,12},{9,13},{10,... | collective-permute-start | bytes 393224 | tf_op jit(solution)/shard_map/ppermute | solution.py:466
  20.0 1.0 project_more.1
  21.0 0.6 collective-permute-start.5
  21.6 2.5 %near.1 = (f32[4,512,128]{2,1,0:T(8,128)S(1)}, f32[4,512,128]{2,1,0:T(8,128)S(1)}, f32[4,512,128]{2,1,0:T(8,128)S(1)}) custom-call(s32[3]{0:T(128)S(1)} %pad_add_fusion.after.place, bf16[2,512,128]{2,1,0:T(8,128)(2,1)S(1)} %get-tuple-element.67.refs_0_, bf16[2,512,128]{2,1,0:T(8,128)(2,1)S(1)} %get-tuple-element.70.refs_1_, ...), custom_call_target="tpu_custom_call" | custom-call | flops 536870912 | bytes 4194304 | tf_op jit(solution)/shard_map/near/pallas_call | solution.py:568
  24.1 2.2 %collective-permute-done.5.refs_6_ = bf16[2,256,128]{2,1,0:T(8,128)(2,1)S(1)} collective-permute-done((bf16[2,256,128]{2,1,0:T(8,128)(2,1)S(1)}, bf16[2,256,128]{2,1,0:T(8,128)(2,1)S(1)}, u32[]{:S(2)}, u32[]{:S(2)}) %collective-permute-start.5) | collective-permute-done | bytes 131104 | tf_op jit(solution)/shard_map/ppermute | solution.py:466
  26.3 0.6 far.3
  26.9 1.7 %collective-permute-start.7 = (bf16[128,512]{1,0:T(8,128)(2,1)S(1)}, bf16[128,512]{1,0:T(8,128)(2,1)S(1)}, u32[]{:S(2)}, u32[]{:S(2)}) collective-permute-start(bf16[128,512]{1,0:T(8,128)(2,1)S(1)} %get-tuple-element.78), channel_id=1, source_target_pairs={{0,2},{1,3},{2,0},{3,1},{4,6},{5,7},{6,4},{7,5},{8,10},{9,11},{10,... | collective-permute-start | bytes 393224 | tf_op jit(solution)/shard_map/ppermute | solution.py:466
  28.6 0.6 far.2
  29.3 0.6 collective-permute-start.6
  29.8 2.7 %collective-permute-done.7.refs_2_ = bf16[128,512]{1,0:T(8,128)(2,1)S(1)} collective-permute-done((bf16[128,512]{1,0:T(8,128)(2,1)S(1)}, bf16[128,512]{1,0:T(8,128)(2,1)S(1)}, u32[]{:S(2)}, u32[]{:S(2)}) %collective-permute-start.7) | collective-permute-done | bytes 131104 | tf_op jit(solution)/shard_map/ppermute | solution.py:466
  32.5 1.9 %collective-permute-done.8.refs_3_ = bf16[128,512]{1,0:T(8,128)(2,1)S(1)} collective-permute-done((bf16[128,512]{1,0:T(8,128)(2,1)S(1)}, bf16[128,512]{1,0:T(8,128)(2,1)S(1)}, u32[]{:S(2)}, u32[]{:S(2)}) %collective-permute-start.8) | collective-permute-done | bytes 131104 | tf_op jit(solution)/shard_map/ppermute | solution.py:466
  34.4 4.6 %prepare.1 = (f32[128,2048]{1,0:T(8,128)S(1)}, f32[128,2048]{1,0:T(8,128)S(1)}, f32[128,2048]{1,0:T(8,128)S(1)}, f32[256,2048]{1,0:T(8,128)S(1)}, f32[16,2048]{1...) custom-call(s32[3]{0:T(128)S(1)} %pad_add_fusion.after.place, ...), custom_call_target="tpu_custom_call" | custom-call | flops 671088640 | bytes 7864320 | tf_op jit(solution)/shard_map/prepare/pallas_call | solution.py:594
  39.0 0.3 collective-permute-start.9
  39.3 0.4 couple.1.coef.after
  39.7 0.6 collective-permute-done.9.other.beside
  40.3 0.6 pair.1
  40.9 3.6 %collective-permute-start.12 = (bf16[16,2176]{1,0:T(8,128)(2,1)S(1)}, bf16[16,2176]{1,0:T(8,128)(2,1)S(1)}, u32[]{:S(2)}, u32[]{:S(2)}) collective-permute-start(bf16[16,2176]{1,0:T(8,128)(2,1)S(1)} %pair.1), channel_id=1, source_target_pairs={{0,6},{1,7},{2,4},{3,5},{4,2},{5,3},{6,0},{7,1},{8,14},{9,15},{10,... | collective-permute-start | bytes 208904 | tf_op jit(solution)/shard_map/ppermute | solution.py:466
  44.5 0.6 collective-permute-start.10
  45.2 1.7 %within.1 = (f32[128,2048]{1,0:T(8,128)S(1)}, f32[128,2048]{1,0:T(8,128)S(1)}) custom-call(f32[128,128]{1,0:T(8,128)S(1)} %couple.1.coef.after, f32[128,2048]{1,0:T(8,128)S(1)} %get-tuple-element.82.base, f32[128,2048]{1,0:T(8,128)S(1)} %get-tuple-element.83.keep, f32[128,2048]{1,0:T(8,128)S(1)} %get-tuple-element.84.drive), custom_call_target="tpu_custom_call" | custom-call | flops 10485760 | bytes 5242880 | tf_op jit(solution)/shard_map/within/pallas_call | solution.py:648
  46.9 0.3 collective-permute-done.12.refs_2_
  47.2 1.6 %collective-permute-done.11.refs_1_ = bf16[16,2176]{1,0:T(8,128)(2,1)S(1)} collective-permute-done((bf16[16,2176]{1,0:T(8,128)(2,1)S(1)}, bf16[16,2176]{1,0:T(8,128)(2,1)S(1)}, u32[]{:S(2)}, u32[]{:S(2)}) %collective-permute-start.11) | collective-permute-done | bytes 69664 | tf_op jit(solution)/shard_map/ppermute | solution.py:466
  48.8 2.8 %route.1 = (f32[128,2048]{1,0:T(8,128)S(1)}, f32[128,256]{1,0:T(8,128)S(1)}, bf16[64,2048]{1,0:T(8,128)(2,1)S(1)}, bf16[64,2048]{1,0:T(8,128)(2,1)S(1)}, bf16[64...) custom-call(s32[3]{0:T(128)S(1)} %pad_add_fusion.after.place, f32[128,2048]{1,0:T(8,128)S(1)} %get-tuple-element.85.before, ...), custom_call_target="tpu_custom_call" | custom-call | flops 671088640 | bytes 7864320 | tf_op jit(solution)/shard_map/route/pallas_call | solution.py:657
  51.7 1.7 %collective-permute-start.15 = (bf16[64,2048]{1,0:T(8,128)(2,1)S(1)}, bf16[64,2048]{1,0:T(8,128)(2,1)S(1)}, u32[]{:S(2)}, u32[]{:S(2)}) collective-permute-start(bf16[64,2048]{1,0:T(8,128)(2,1)S(1)} %get-tuple-element.97), channel_id=1, source_target_pairs={{0,2},{1,3},{2,0},{3,1},{4,6},{5,7},{6,4},{7,5},{8,10},{9,11},{10,... | collective-permute-start | bytes 786440 | tf_op jit(solution)/shard_map/ppermute | solution.py:466
  53.4 0.8 collective-permute-start.16
  54.2 1.0 collective-permute-start.17
  55.3 2.1 %up.3.refs_1_.hidden = bf16[128,3584]{1,0:T(8,128)(2,1)S(1)} custom-call(bf16[2048,3584]{1,0:T(8,128)(2,1)S(1)} %get-tuple-element.69.after.w_up, bf16[64,2048]{1,0:T(8,128)(2,1)S(1)} %get-tuple-element.94.after.refs_0_, bf16[64,2048]{1,0:T(8,128)(2,1)S(1)} %get-tuple-element.94.after.refs_0_, bf16[64,2048]{1,0:T(8,128)(2,1)S(1)} %collective-permute-done.13.refs_1_), custom_call_target="tpu_custom_call" | custom-call | flops 1879048192 | bytes 14680064 | tf_op jit(solution)/shard_map/up/pallas_call | solution.py:690
  57.4 3.2 %fetch.3.refs_1_.refs_0_ = bf16[3584,1024]{1,0:T(8,128)(2,1)S(1)} custom-call(bf16[3584,2048]{1,0:T(8,128)(2,1)} %bitcast.22, bf16[128,3584]{1,0:T(8,128)(2,1)S(1)} %up.3.refs_1_.hidden), custom_call_target="tpu_custom_call" | custom-call | tf_op jit(solution)/shard_map/fetch/pallas_call | solution.py:397
  60.6 2.1 %down.4 = (bf16[64,2048]{1,0:T(8,128)(2,1)S(1)}, bf16[64,2048]{1,0:T(8,128)(2,1)S(1)}) custom-call(bf16[128,3584]{1,0:T(8,128)(2,1)S(1)} %up.3.refs_1_.hidden, bf16[64,2048]{1,0:T(8,128)(2,1)S(1)} %get-tuple-element.94.after.refs_0_, bf16[3584,1024]{1,0:T(8,128)(2,1)S(1)} %get-tuple-element.95.refs_0_, bf16[3584,1024]{1,0:T(8,128)(2,1)S(1)} %fetch.3.refs_1_.refs_0_), custom_call_target="tpu_custom_call" | custom-call | flops 1879048192 | bytes 14680064 | tf_op jit(solution)/shard_map/down/pallas_call | solution.py:703
  62.8 3.0 %collective-permute-done.16.refs_1_ = bf16[64,2048]{1,0:T(8,128)(2,1)S(1)} collective-permute-done((bf16[64,2048]{1,0:T(8,128)(2,1)S(1)}, bf16[64,2048]{1,0:T(8,128)(2,1)S(1)}, u32[]{:S(2)}, u32[]{:S(2)}) %collective-permute-start.16) | collective-permute-done | bytes 262176 | tf_op jit(solution)/shard_map/ppermute | solution.py:466
  65.8 1.7 %collective-permute-done.17.refs_2_ = bf16[64,2048]{1,0:T(8,128)(2,1)S(1)} collective-permute-done((bf16[64,2048]{1,0:T(8,128)(2,1)S(1)}, bf16[64,2048]{1,0:T(8,128)(2,1)S(1)}, u32[]{:S(2)}, u32[]{:S(2)}) %collective-permute-start.17) | collective-permute-done | bytes 262176 | tf_op jit(solution)/shard_map/ppermute | solution.py:466
  67.6 3.0 %up.4.after.hidden = bf16[192,3584]{1,0:T(8,128)(2,1)S(1)} custom-call(bf16[2048,3584]{1,0:T(8,128)(2,1)S(1)} %get-tuple-element.69.after.w_up, bf16[192,2048]{1,0:T(8,128)(2,1)S(1)} %gather.1.after.refs_0_, bf16[192,2048]{1,0:T(8,128)(2,1)S(1)} %gather.1.after.refs_0_), custom_call_target="tpu_custom_call" | custom-call | flops 2818572288 | bytes 14680064 | tf_op jit(solution)/shard_map/up/pallas_call | solution.py:690
  70.7 3.0 %up.5.hidden.after = bf16[192,3584]{1,0:T(8,128)(2,1)S(1)} custom-call(bf16[2048,3584]{1,0:T(8,128)(2,1)S(1)} %get-tuple-element.69.after.w_up, bf16[192,3584]{1,0:T(8,128)(2,1)S(1)} %up.4.after.hidden, bf16[192,2048]{1,0:T(8,128)(2,1)S(1)} %collective-permute-done.18.refs_0_), custom_call_target="tpu_custom_call" | custom-call | flops 2818572288 | bytes 14680064 | tf_op jit(solution)/shard_map/up/pallas_call | solution.py:690
  73.7 3.0 %down.5.after = bf16[192,2048]{1,0:T(8,128)(2,1)S(1)} custom-call(bf16[192,3584]{1,0:T(8,128)(2,1)S(1)} %up.5.hidden.after, bf16[192,3584]{1,0:T(8,128)(2,1)S(1)} %up.5.hidden.after, bf16[3584,1024]{1,0:T(8,128)(2,1)S(1)} %get-tuple-element.95.refs_0_, bf16[3584,1024]{1,0:T(8,128)(2,1)S(1)} %fetch.3.refs_1_.refs_0_), custom_call_target="tpu_custom_call" | custom-call | flops 2818572288 | bytes 14680064 | tf_op jit(solution)/shard_map/down/pallas_call | solution.py:703
  76.8 0.6 collective-permute-start.19
  77.3 1.8 %down.6.own = bf16[192,1024]{1,0:T(8,128)(2,1)S(1)} custom-call(bf16[192,3584]{1,0:T(8,128)(2,1)S(1)} %up.4.after.hidden, bf16[192,2048]{1,0:T(8,128)(2,1)S(1)} %down.5.after, bf16[3584,1024]{1,0:T(8,128)(2,1)S(1)} %get-tuple-element.95.refs_0_), custom_call_target="tpu_custom_call" | custom-call | flops 1409286144 | bytes 7340032 | tf_op jit(solution)/shard_map/down/pallas_call | solution.py:703
  79.2 0.1 collective-permute-done.19.refs_0_
  79.2 0.1 join.2
  79.3 0.8 collective-permute-start.21
  80.1 1.3 %collective-permute-start.22 = (bf16[64,1024]{1,0:T(8,128)(2,1)S(1)}, bf16[64,1024]{1,0:T(8,128)(2,1)S(1)}, u32[]{:S(2)}, u32[]{:S(2)}) collective-permute-start(bf16[64,1024]{1,0:T(8,128)(2,1)S(1)} %get-tuple-element.102), channel_id=1, source_target_pairs={{0,6},{1,7},{2,4},{3,5},{4,2},{5,3},{6,0},{7,1},{8,14},{9,15},{10,... | collective-permute-start | bytes 393224 | tf_op jit(solution)/shard_map/ppermute | solution.py:466
  81.4 1.5 %collective-permute-start.20 = (bf16[64,1024]{1,0:T(8,128)(2,1)S(1)}, bf16[64,1024]{1,0:T(8,128)(2,1)S(1)}, u32[]{:S(2)}, u32[]{:S(2)}) collective-permute-start(bf16[64,1024]{1,0:T(8,128)(2,1)S(1)} %get-tuple-element.100.after), channel_id=1, source_target_pairs={{0,2},{1,3},{2,0},{3,1},{4,6},{5,7},{6,4},{7,5},{8,10},{9,11},{10,... | collective-permute-start | bytes 393224 | tf_op jit(solution)/shard_map/ppermute | solution.py:466
  82.9 1.6 %down.7.own = bf16[192,1024]{1,0:T(8,128)(2,1)S(1)} custom-call(bf16[192,3584]{1,0:T(8,128)(2,1)S(1)} %up.4.after.hidden, bf16[64,1024]{1,0:T(8,128)(2,1)S(1)} %get-tuple-element.100.after, bf16[3584,1024]{1,0:T(8,128)(2,1)S(1)} %fetch.3.refs_1_.refs_0_), custom_call_target="tpu_custom_call" | custom-call | flops 393216 | bytes 2048 | tf_op jit(solution)/shard_map/down/pallas_call | solution.py:703
  84.5 0.1 join.3
  84.6 0.6 collective-permute-start.24
  85.2 1.7 %collective-permute-start.25 = (bf16[64,1024]{1,0:T(8,128)(2,1)S(1)}, bf16[64,1024]{1,0:T(8,128)(2,1)S(1)}, u32[]{:S(2)}, u32[]{:S(2)}) collective-permute-start(bf16[64,1024]{1,0:T(8,128)(2,1)S(1)} %get-tuple-element.105), channel_id=1, source_target_pairs={{0,4},{1,5},{2,6},{3,7},{4,0},{5,1},{6,2},{7,3},{8,12},{9,13},{10,... | collective-permute-start | bytes 393224 | tf_op jit(solution)/shard_map/ppermute | solution.py:466
  87.0 1.6 %collective-permute-done.21.refs_1_ = bf16[64,1024]{1,0:T(8,128)(2,1)S(1)} collective-permute-done((bf16[64,1024]{1,0:T(8,128)(2,1)S(1)}, bf16[64,1024]{1,0:T(8,128)(2,1)S(1)}, u32[]{:S(2)}, u32[]{:S(2)}) %collective-permute-start.21) | collective-permute-done | bytes 131104 | tf_op jit(solution)/shard_map/ppermute | solution.py:466
  88.5 1.7 %collective-permute-start.26 = (bf16[64,1024]{1,0:T(8,128)(2,1)S(1)}, bf16[64,1024]{1,0:T(8,128)(2,1)S(1)}, u32[]{:S(2)}, u32[]{:S(2)}) collective-permute-start(bf16[64,1024]{1,0:T(8,128)(2,1)S(1)} %get-tuple-element.106), channel_id=1, source_target_pairs={{0,6},{1,7},{2,4},{3,5},{4,2},{5,3},{6,0},{7,1},{8,14},{9,15},{10,... | collective-permute-start | bytes 393224 | tf_op jit(solution)/shard_map/ppermute | solution.py:466
  90.3 0.3 finish.2
  90.6 1.6 %collective-permute-start.23 = (bf16[128,1024]{1,0:T(8,128)(2,1)S(1)}, bf16[128,1024]{1,0:T(8,128)(2,1)S(1)}, u32[]{:S(2)}, u32[]{:S(2)}) collective-permute-start(bf16[128,1024]{1,0:T(8,128)(2,1)S(1)} %finish.2), channel_id=1, source_target_pairs={{0,8},{8,16},{16,24},{24,0},{1,9},{9,17},{17,25},{25,1},{2,10},{10... | collective-permute-start | bytes 786440 | tf_op jit(solution)/shard_map/ppermute | solution.py:471
  92.3 0.6 collective-permute-done.24.refs_0_
  92.9 2.1 %collective-permute-done.26.refs_2_ = bf16[64,1024]{1,0:T(8,128)(2,1)S(1)} collective-permute-done((bf16[64,1024]{1,0:T(8,128)(2,1)S(1)}, bf16[64,1024]{1,0:T(8,128)(2,1)S(1)}, u32[]{:S(2)}, u32[]{:S(2)}) %collective-permute-start.26) | collective-permute-done | bytes 131104 | tf_op jit(solution)/shard_map/ppermute | solution.py:466
  95.0 0.3 finish.3
  95.3 1.6 %collective-permute-start.27 = (bf16[128,1024]{1,0:T(8,128)(2,1)S(1)}, bf16[128,1024]{1,0:T(8,128)(2,1)S(1)}, u32[]{:S(2)}, u32[]{:S(2)}) collective-permute-start(bf16[128,1024]{1,0:T(8,128)(2,1)S(1)} %finish.3), channel_id=1, source_target_pairs={{0,8},{8,16},{16,24},{24,0},{1,9},{9,17},{17,25},{25,1},{2,10},{10... | collective-permute-start | bytes 786440 | tf_op jit(solution)/shard_map/ppermute | solution.py:471
  96.9 2.9 %collective-permute-done.23 = bf16[128,1024]{1,0:T(8,128)(2,1)S(1)} collective-permute-done((bf16[128,1024]{1,0:T(8,128)(2,1)S(1)}, bf16[128,1024]{1,0:T(8,128)(2,1)S(1)}, u32[]{:S(2)}, u32[]{:S(2)}) %collective-permute-start.23) | collective-permute-done | bytes 262176 | tf_op jit(solution)/shard_map/ppermute | solution.py:471
  99.8 5.3 %collective-permute-done.27 = bf16[128,1024]{1,0:T(8,128)(2,1)S(1)} collective-permute-done((bf16[128,1024]{1,0:T(8,128)(2,1)S(1)}, bf16[128,1024]{1,0:T(8,128)(2,1)S(1)}, u32[]{:S(2)}, u32[]{:S(2)}) %collective-permute-start.27) | collective-permute-done | bytes 262176 | tf_op jit(solution)/shard_map/ppermute | solution.py:471
  105.1 0.8 maximum_bitcast_fusion
  (20 shorter events, 0.4 us)
Async XLA Ops:
  0.0 4.5 %collective-permute-start = (bf16[128,2048]{1,0:T(8,128)(2,1)}, bf16[128,2048]{1,0:T(8,128)(2,1)S(1)}, u32[]{:S(2)}, u32[]{:S(2)}) collective-permute-start(bf16[128,2048]{1,0:T(8,128)(2,1)} %bitcast.24), channel_id=1, source_target_pairs={{0,1},{1,0},{2,3},{3,2},{4,5},{5,4},{6,7},{7,6},{8,9},{9,8},{10,11... | collective-permute-start | bytes 1572872 | tf_op jit(solution)/shard_map/ppermute | solution.py:466
  0.5 15.3 %collective-permute-start.2 = (bf16[128,2048]{1,0:T(8,128)(2,1)}, bf16[128,2048]{1,0:T(8,128)(2,1)S(1)}, u32[]{:S(2)}, u32[]{:S(2)}) collective-permute-start(bf16[128,2048]{1,0:T(8,128)(2,1)} %bitcast.25), channel_id=1, source_target_pairs={{0,2},{1,3},{2,0},{3,1},{4,6},{5,7},{6,4},{7,5},{8,10},{9,11},{10,... | collective-permute-start | bytes 1572872 | tf_op jit(solution)/shard_map/ppermute | solution.py:466
  2.9 14.3 %collective-permute-start.1 = (bf16[2048,128]{1,0:T(8,128)(2,1)}, bf16[2048,128]{1,0:T(8,128)(2,1)S(1)}, u32[]{:S(2)}, u32[]{:S(2)}) collective-permute-start(bf16[2048,128]{1,0:T(8,128)(2,1)} %bitcast.30), channel_id=1, source_target_pairs={{0,4},{1,5},{2,6},{3,7},{4,0},{5,1},{6,2},{7,3},{8,12},{9,13},{10,... | collective-permute-start | bytes 1572872 | tf_op jit(solution)/shard_map/ppermute | solution.py:466
  16.1 4.0 %collective-permute-start.3 = (bf16[128,2048]{1,0:T(8,128)(2,1)S(1)}, bf16[128,2048]{1,0:T(8,128)(2,1)S(1)}, u32[]{:S(2)}, u32[]{:S(2)}) collective-permute-start(bf16[128,2048]{1,0:T(8,128)(2,1)S(1)} %norm.3.first), channel_id=1, source_target_pairs={{0,1},{1,0},{2,3},{3,2},{4,5},{5,4},{6,7},{7,6},{8,9},{9,8},{10,11... | collective-permute-start | bytes 1572872 | tf_op jit(solution)/shard_map/ppermute | solution.py:466
  18.5 5.6 %collective-permute-start.4 = (bf16[2,256,128]{2,1,0:T(8,128)(2,1)S(1)}, bf16[2,256,128]{2,1,0:T(8,128)(2,1)S(1)}, u32[]{:S(2)}, u32[]{:S(2)}) collective-permute-start(bf16[2,256,128]{2,1,0:T(8,128)(2,1)S(1)} %get-tuple-element.71.refs_2_), channel_id=1, source_target_pairs={{0,4},{1,5},{2,6},{3,7},{4,0},{5,1},{6,2},{7,3},{8,12},{9,13},{10,... | collective-permute-start | bytes 393224 | tf_op jit(solution)/shard_map/ppermute | solution.py:466
  21.0 5.3 %collective-permute-start.5 = (bf16[2,256,128]{2,1,0:T(8,128)(2,1)S(1)}, bf16[2,256,128]{2,1,0:T(8,128)(2,1)S(1)}, u32[]{:S(2)}, u32[]{:S(2)}) collective-permute-start(bf16[2,256,128]{2,1,0:T(8,128)(2,1)S(1)} %get-tuple-element.72.refs_3_), channel_id=1, source_target_pairs={{0,4},{1,5},{2,6},{3,7},{4,0},{5,1},{6,2},{7,3},{8,12},{9,13},{10,... | collective-permute-start | bytes 393224 | tf_op jit(solution)/shard_map/ppermute | solution.py:466
  26.9 5.6 %collective-permute-start.7 = (bf16[128,512]{1,0:T(8,128)(2,1)S(1)}, bf16[128,512]{1,0:T(8,128)(2,1)S(1)}, u32[]{:S(2)}, u32[]{:S(2)}) collective-permute-start(bf16[128,512]{1,0:T(8,128)(2,1)S(1)} %get-tuple-element.78), channel_id=1, source_target_pairs={{0,2},{1,3},{2,0},{3,1},{4,6},{5,7},{6,4},{7,5},{8,10},{9,11},{10,... | collective-permute-start | bytes 393224 | tf_op jit(solution)/shard_map/ppermute | solution.py:466
  28.6 5.8 %collective-permute-start.8 = (bf16[128,512]{1,0:T(8,128)(2,1)S(1)}, bf16[128,512]{1,0:T(8,128)(2,1)S(1)}, u32[]{:S(2)}, u32[]{:S(2)}) collective-permute-start(bf16[128,512]{1,0:T(8,128)(2,1)S(1)} %get-tuple-element.79), channel_id=1, source_target_pairs={{0,3},{1,2},{2,1},{3,0},{4,7},{5,6},{6,5},{7,4},{8,11},{9,10},{10,... | collective-permute-start | bytes 393224 | tf_op jit(solution)/shard_map/ppermute | solution.py:466
  29.3 5.2 %collective-permute-start.6 = (bf16[128,512]{1,0:T(8,128)(2,1)S(1)}, bf16[128,512]{1,0:T(8,128)(2,1)S(1)}, u32[]{:S(2)}, u32[]{:S(2)}) collective-permute-start(bf16[128,512]{1,0:T(8,128)(2,1)S(1)} %get-tuple-element.77), channel_id=1, source_target_pairs={{0,1},{1,0},{2,3},{3,2},{4,5},{5,4},{6,7},{7,6},{8,9},{9,8},{10,11... | collective-permute-start | bytes 393224 | tf_op jit(solution)/shard_map/ppermute | solution.py:466
  39.0 1.3 %collective-permute-start.9 = (bf16[16,2176]{1,0:T(8,128)(2,1)S(1)}, bf16[16,2176]{1,0:T(8,128)(2,1)S(1)}, u32[]{:S(2)}, u32[]{:S(2)}) collective-permute-start(bf16[16,2176]{1,0:T(8,128)(2,1)S(1)} %get-tuple-element.91.own), channel_id=1, source_target_pairs={{0,1},{1,0},{2,3},{3,2},{4,5},{5,4},{6,7},{7,6},{8,9},{9,8},{10,11... | collective-permute-start | bytes 208904 | tf_op jit(solution)/shard_map/ppermute | solution.py:466
  40.9 6.3 %collective-permute-start.12 = (bf16[16,2176]{1,0:T(8,128)(2,1)S(1)}, bf16[16,2176]{1,0:T(8,128)(2,1)S(1)}, u32[]{:S(2)}, u32[]{:S(2)}) collective-permute-start(bf16[16,2176]{1,0:T(8,128)(2,1)S(1)} %pair.1), channel_id=1, source_target_pairs={{0,6},{1,7},{2,4},{3,5},{4,2},{5,3},{6,0},{7,1},{8,14},{9,15},{10,... | collective-permute-start | bytes 208904 | tf_op jit(solution)/shard_map/ppermute | solution.py:466
  44.5 4.3 %collective-permute-start.11 = (bf16[16,2176]{1,0:T(8,128)(2,1)S(1)}, bf16[16,2176]{1,0:T(8,128)(2,1)S(1)}, u32[]{:S(2)}, u32[]{:S(2)}) collective-permute-start(bf16[16,2176]{1,0:T(8,128)(2,1)S(1)} %pair.1), channel_id=1, source_target_pairs={{0,4},{1,5},{2,6},{3,7},{4,0},{5,1},{6,2},{7,3},{8,12},{9,13},{10,... | collective-permute-start | bytes 208904 | tf_op jit(solution)/shard_map/ppermute | solution.py:466
  44.5 4.3 %collective-permute-start.10 = (bf16[16,2176]{1,0:T(8,128)(2,1)S(1)}, bf16[16,2176]{1,0:T(8,128)(2,1)S(1)}, u32[]{:S(2)}, u32[]{:S(2)}) collective-permute-start(bf16[16,2176]{1,0:T(8,128)(2,1)S(1)} %pair.1), channel_id=1, source_target_pairs={{0,2},{1,3},{2,0},{3,1},{4,6},{5,7},{6,4},{7,5},{8,10},{9,11},{10,... | collective-permute-start | bytes 208904 | tf_op jit(solution)/shard_map/ppermute | solution.py:466
  51.6 3.6 %collective-permute-start.13 = (bf16[64,2048]{1,0:T(8,128)(2,1)S(1)}, bf16[64,2048]{1,0:T(8,128)(2,1)S(1)}, u32[]{:S(2)}, u32[]{:S(2)}) collective-permute-start(bf16[64,2048]{1,0:T(8,128)(2,1)S(1)} %get-tuple-element.94.after.refs_0_), channel_id=1, source_target_pairs={{0,1},{1,0},{2,3},{3,2},{4,5},{5,4},{6,7},{7,6},{8,9},{9,8},{10,11... | collective-permute-start | bytes 786440 | tf_op jit(solution)/shard_map/ppermute | solution.py:466
  51.7 11.0 %collective-permute-start.15 = (bf16[64,2048]{1,0:T(8,128)(2,1)S(1)}, bf16[64,2048]{1,0:T(8,128)(2,1)S(1)}, u32[]{:S(2)}, u32[]{:S(2)}) collective-permute-start(bf16[64,2048]{1,0:T(8,128)(2,1)S(1)} %get-tuple-element.97), channel_id=1, source_target_pairs={{0,2},{1,3},{2,0},{3,1},{4,6},{5,7},{6,4},{7,5},{8,10},{9,11},{10,... | collective-permute-start | bytes 786440 | tf_op jit(solution)/shard_map/ppermute | solution.py:466
  53.4 12.4 %collective-permute-start.16 = (bf16[64,2048]{1,0:T(8,128)(2,1)S(1)}, bf16[64,2048]{1,0:T(8,128)(2,1)S(1)}, u32[]{:S(2)}, u32[]{:S(2)}) collective-permute-start(bf16[64,2048]{1,0:T(8,128)(2,1)S(1)} %get-tuple-element.98), channel_id=1, source_target_pairs={{0,4},{1,5},{2,6},{3,7},{4,0},{5,1},{6,2},{7,3},{8,12},{9,13},{10,... | collective-permute-start | bytes 786440 | tf_op jit(solution)/shard_map/ppermute | solution.py:466
  54.2 13.3 %collective-permute-start.17 = (bf16[64,2048]{1,0:T(8,128)(2,1)S(1)}, bf16[64,2048]{1,0:T(8,128)(2,1)S(1)}, u32[]{:S(2)}, u32[]{:S(2)}) collective-permute-start(bf16[64,2048]{1,0:T(8,128)(2,1)S(1)} %get-tuple-element.99), channel_id=1, source_target_pairs={{0,6},{1,7},{2,4},{3,5},{4,2},{5,3},{6,0},{7,1},{8,14},{9,15},{10,... | collective-permute-start | bytes 786440 | tf_op jit(solution)/shard_map/ppermute | solution.py:466
  62.7 4.8 %collective-permute-start.14 = (bf16[64,2048]{1,0:T(8,128)(2,1)S(1)}, bf16[64,2048]{1,0:T(8,128)(2,1)S(1)}, u32[]{:S(2)}, u32[]{:S(2)}) collective-permute-start(bf16[64,2048]{1,0:T(8,128)(2,1)S(1)} %get-tuple-element.96), channel_id=1, source_target_pairs={{0,1},{1,0},{2,3},{3,2},{4,5},{5,4},{6,7},{7,6},{8,9},{9,8},{10,11... | collective-permute-start | bytes 786440 | tf_op jit(solution)/shard_map/ppermute | solution.py:466
  67.6 3.1 %collective-permute-start.18 = (bf16[192,2048]{1,0:T(8,128)(2,1)S(1)}, bf16[192,2048]{1,0:T(8,128)(2,1)S(1)}, u32[]{:S(2)}, u32[]{:S(2)}) collective-permute-start(bf16[192,2048]{1,0:T(8,128)(2,1)S(1)} %gather.1.after.refs_0_), channel_id=1, source_target_pairs={{0,1},{1,0},{2,3},{3,2},{4,5},{5,4},{6,7},{7,6},{8,9},{9,8},{10,11... | collective-permute-start | bytes 2359304 | tf_op jit(solution)/shard_map/ppermute | solution.py:466
  76.8 2.5 %collective-permute-start.19 = (bf16[192,2048]{1,0:T(8,128)(2,1)S(1)}, bf16[192,2048]{1,0:T(8,128)(2,1)S(1)}, u32[]{:S(2)}, u32[]{:S(2)}) collective-permute-start(bf16[192,2048]{1,0:T(8,128)(2,1)S(1)} %down.5.after), channel_id=1, source_target_pairs={{0,1},{1,0},{2,3},{3,2},{4,5},{5,4},{6,7},{7,6},{8,9},{9,8},{10,11... | collective-permute-start | bytes 2359304 | tf_op jit(solution)/shard_map/ppermute | solution.py:466
  79.3 9.2 %collective-permute-start.21 = (bf16[64,1024]{1,0:T(8,128)(2,1)S(1)}, bf16[64,1024]{1,0:T(8,128)(2,1)S(1)}, u32[]{:S(2)}, u32[]{:S(2)}) collective-permute-start(bf16[64,1024]{1,0:T(8,128)(2,1)S(1)} %get-tuple-element.101), channel_id=1, source_target_pairs={{0,4},{1,5},{2,6},{3,7},{4,0},{5,1},{6,2},{7,3},{8,12},{9,13},{10,... | collective-permute-start | bytes 393224 | tf_op jit(solution)/shard_map/ppermute | solution.py:466
  80.1 10.2 %collective-permute-start.22 = (bf16[64,1024]{1,0:T(8,128)(2,1)S(1)}, bf16[64,1024]{1,0:T(8,128)(2,1)S(1)}, u32[]{:S(2)}, u32[]{:S(2)}) collective-permute-start(bf16[64,1024]{1,0:T(8,128)(2,1)S(1)} %get-tuple-element.102), channel_id=1, source_target_pairs={{0,6},{1,7},{2,4},{3,5},{4,2},{5,3},{6,0},{7,1},{8,14},{9,15},{10,... | collective-permute-start | bytes 393224 | tf_op jit(solution)/shard_map/ppermute | solution.py:466
  81.4 8.8 %collective-permute-start.20 = (bf16[64,1024]{1,0:T(8,128)(2,1)S(1)}, bf16[64,1024]{1,0:T(8,128)(2,1)S(1)}, u32[]{:S(2)}, u32[]{:S(2)}) collective-permute-start(bf16[64,1024]{1,0:T(8,128)(2,1)S(1)} %get-tuple-element.100.after), channel_id=1, source_target_pairs={{0,2},{1,3},{2,0},{3,1},{4,6},{5,7},{6,4},{7,5},{8,10},{9,11},{10,... | collective-permute-start | bytes 393224 | tf_op jit(solution)/shard_map/ppermute | solution.py:466
  84.6 8.3 %collective-permute-start.24 = (bf16[64,1024]{1,0:T(8,128)(2,1)S(1)}, bf16[64,1024]{1,0:T(8,128)(2,1)S(1)}, u32[]{:S(2)}, u32[]{:S(2)}) collective-permute-start(bf16[64,1024]{1,0:T(8,128)(2,1)S(1)} %get-tuple-element.104), channel_id=1, source_target_pairs={{0,2},{1,3},{2,0},{3,1},{4,6},{5,7},{6,4},{7,5},{8,10},{9,11},{10,... | collective-permute-start | bytes 393224 | tf_op jit(solution)/shard_map/ppermute | solution.py:466
  85.2 7.7 %collective-permute-start.25 = (bf16[64,1024]{1,0:T(8,128)(2,1)S(1)}, bf16[64,1024]{1,0:T(8,128)(2,1)S(1)}, u32[]{:S(2)}, u32[]{:S(2)}) collective-permute-start(bf16[64,1024]{1,0:T(8,128)(2,1)S(1)} %get-tuple-element.105), channel_id=1, source_target_pairs={{0,4},{1,5},{2,6},{3,7},{4,0},{5,1},{6,2},{7,3},{8,12},{9,13},{10,... | collective-permute-start | bytes 393224 | tf_op jit(solution)/shard_map/ppermute | solution.py:466
  88.5 6.4 %collective-permute-start.26 = (bf16[64,1024]{1,0:T(8,128)(2,1)S(1)}, bf16[64,1024]{1,0:T(8,128)(2,1)S(1)}, u32[]{:S(2)}, u32[]{:S(2)}) collective-permute-start(bf16[64,1024]{1,0:T(8,128)(2,1)S(1)} %get-tuple-element.106), channel_id=1, source_target_pairs={{0,6},{1,7},{2,4},{3,5},{4,2},{5,3},{6,0},{7,1},{8,14},{9,15},{10,... | collective-permute-start | bytes 393224 | tf_op jit(solution)/shard_map/ppermute | solution.py:466
  90.6 9.2 %collective-permute-start.23 = (bf16[128,1024]{1,0:T(8,128)(2,1)S(1)}, bf16[128,1024]{1,0:T(8,128)(2,1)S(1)}, u32[]{:S(2)}, u32[]{:S(2)}) collective-permute-start(bf16[128,1024]{1,0:T(8,128)(2,1)S(1)} %finish.2), channel_id=1, source_target_pairs={{0,8},{8,16},{16,24},{24,0},{1,9},{9,17},{17,25},{25,1},{2,10},{10... | collective-permute-start | bytes 786440 | tf_op jit(solution)/shard_map/ppermute | solution.py:471
  95.3 9.8 %collective-permute-start.27 = (bf16[128,1024]{1,0:T(8,128)(2,1)S(1)}, bf16[128,1024]{1,0:T(8,128)(2,1)S(1)}, u32[]{:S(2)}, u32[]{:S(2)}) collective-permute-start(bf16[128,1024]{1,0:T(8,128)(2,1)S(1)} %finish.3), channel_id=1, source_target_pairs={{0,8},{8,16},{16,24},{24,0},{1,9},{9,17},{17,25},{25,1},{2,10},{10... | collective-permute-start | bytes 786440 | tf_op jit(solution)/shard_map/ppermute | solution.py:471

commit v7 on v6

--- a/solution.py
+++ b/solution.py
@@ -17,7 +17,7 @@
 STRIP = 16
 LANES = 128
 SCALE = HD ** (-0.5) * math.log2(math.e)
-CHUNKS = 2
+CUTS = (0, 9, 16)
 F32 = jnp.float32
 BF16 = jnp.bfloat16
 VMEM = pl.BlockSpec(memory_space=pltpu.VMEM)
@@ -145,8 +145,9 @@
         total_out[slot] = jnp.broadcast_to(total, (GROUP * rows, LANES))
 
 
-def far_kernel(turn, slots, last, place, *refs):
-    queries, (largest, total, summed), halves, outs = refs[:2], refs[2:5], refs[5:7], refs[7:]
+def far_kernel(turn, slots, last, parts, place, *refs):
+    queries, (largest, total, summed), refs = refs[:2], refs[2:5], refs[5:]
+    halves, outs = refs[:parts], refs[parts:]
     rows = queries[0].shape[1] // GROUP
     mine = place[0] // KVH
     seen = (mine ^ turn) < mine
@@ -433,14 +434,15 @@
     begin = 0
     for w_down in w_downs:
         for low in range(0, w_down.shape[1], tile):
-            result = dot(hidden[...], w_down[:, low : low + tile]).astype(BF16)
+            high = min(low + tile, w_down.shape[1])
+            result = dot(hidden[...], w_down[:, low:high]).astype(BF16)
             for at, out in enumerate(outs):
-                out[:, begin + low : begin + low + tile] = result[at * rows : (at + 1) * rows]
+                out[:, begin + low : begin + high] = result[at * rows : (at + 1) * rows]
         begin += w_down.shape[1]
 
 
-def join_kernel(start, own, *refs):
-    parts, outs = refs[: 1 - EXPERTS], refs[1 - EXPERTS :]
+def join_kernel(start, outs_count, after, own, *refs):
+    parts, outs = refs[:-outs_count], refs[-outs_count:]
     capacity, width = outs[0].shape
     for at, out in enumerate(outs):
         here = slice(at * capacity, (at + 1) * capacity)
@@ -451,12 +453,13 @@
 
 
 def finish_kernel(start, second, weighting, *refs):
-    blocks, parts, out = refs[: EXPERTS - 1], refs[EXPERTS - 1 : -1], refs[-1]
+    blocks, last, parts, out = refs[: EXPERTS - 2], refs[EXPERTS - 2], refs[EXPERTS - 1 : -1], refs[-1]
     cols = slice(start, start + out.shape[1])
     total = parts[0][:, cols].astype(F32)
     for part in parts[1:]:
         total = total + part[:, cols].astype(F32)
-    rows = jnp.concatenate([total.astype(BF16)] + [block[...] for block in blocks], 0)
+    rows = [total.astype(BF16)] + [block[...] for block in blocks] + [last[:, cols]]
+    rows = jnp.concatenate(rows, 0)
     high, low = split(weighting[...])
     out[...] = (second[:, cols] + (dot(high, rows) + dot(low, rows))).astype(BF16)
 
@@ -526,11 +529,12 @@
         )(gains, after, *blocks)
 
     normed = list(norm(in_hbm(gains), [in_hbm(tokens), beside], place))
-    half = width // CHUNKS
+    cuts = [width * cut // 16 for cut in CUTS]
+    spans = [high - low for low, high in zip(cuts, cuts[1:])]
     here = [gains, w_own, tokens, dt_in[0], dt_out[0], w_bc[0].T]
     here += [skip_gain, dt_bias, decay_rate, w_router[0].T, routes[0].T]
     here = [(array, 1, 0, array.shape[-1]) for array in here]
-    here = [(w_up[0], 16, 0, w_up.shape[2]), (w_down[0], 16, 0, half)] + here
+    here = [(w_up[0], 16, 0, w_up.shape[2]), (w_down[0], 16, 0, spans[0])] + here
     raising, *here = fetch(here, normed[1])
     lowering, gains, w_own, tokens, dt_first, dt_second, w_bct = here[:7]
     lowering = [lowering]
@@ -577,15 +581,20 @@
     attended = [None] * KVH
     for slots in ((2, 3), (0, 1)):
         state_now = tally
+        steps = []
         for turn, past in enumerate(pasts, 1):
-            last = turn == turns - 1
+            steps += [(turn, [half]) for half in past]
+        for step, (turn, past) in enumerate(steps, 1):
+            last = step == len(steps)
             state_now = pl.pallas_call(
-                functools.partial(far_kernel, turn, slots, last),
+                functools.partial(far_kernel, turn, slots, last, len(past)),
                 out_shape=(shape((rows, GROUP * HD), BF16),) * len(slots) if last else tallies,
-                in_specs=[SMEM] + [VMEM] * 7,
+                in_specs=[SMEM] + [VMEM] * (5 + len(past)),
                 out_specs=(VMEM,) * (len(slots) if last else 3),
                 compiler_params=params(16),
-                cost_estimate=cost(2 * scored * HD, 2 * group_rows * GROUP * HD * 4, scored // 2),
+                cost_estimate=cost(
+                    scored * HD * len(past), group_rows * GROUP * HD * 8, scored // 4 * len(past)
+                ),
                 name="far",
             )(place, *queries, *state_now, *past)
         for slot, block in zip(slots, state_now):
@@ -685,20 +694,21 @@
 
     units = raising.shape[1]
 
-    def lift(blocks, after):
+    def lift(blocks, after, hurry=False):
         count = sum(block.shape[0] for block in blocks)
+        work = 1 if hurry else units
         return pl.pallas_call(
             up_kernel,
             out_shape=shape((count, units), BF16),
             in_specs=[VMEM, ANY] + [VMEM] * len(blocks),
             out_specs=VMEM,
             compiler_params=params(12),
-            cost_estimate=cost(2 * count * width * units, 2 * width * units),
+            cost_estimate=cost(2 * count * width * work, 2 * width * work),
             name="up",
         )(raising, after, *blocks)
 
     def lower(weights, hidden, after, outs=1, hurry=False):
-        count, span = hidden.shape[0], half * len(weights)
+        count, span = hidden.shape[0], sum(weight.shape[1] for weight in weights)
         work = 1 if hurry else units
         return pl.pallas_call(
             functools.partial(down_kernel, len(weights)),
@@ -710,62 +720,74 @@
             name="down",
         )(hidden, after, *weights)
 
-    def between_experts(blocks):
-        moved = {slot: exchange(blocks[slot - 1], "ctx", slot * parts) for slot in (3, 1, 2)}
-        return [moved[slot] for slot in range(1, EXPERTS)]
-
-    moved = between_experts(packed[1:])
-    stay = [exchange(packed[0], "ctx", turn) if turn else packed[0] for turn in range(parts)]
-    stay_hidden = lift(stay, packed[0])
-    lowering += fetch([(w_down[0], 16, half, half)], stay_hidden, hurry=True)
+    def shared(blocks):
+        return [blocks[0]] + [
+            exchange(blocks[turn], "ctx", turn) for turn in range(1, parts)
+        ]
+
+    def join(start, span, sums, outs, after):
+        return pl.pallas_call(
+            functools.partial(join_kernel, start, outs),
+            out_shape=(shape((capacity, span), BF16),) * outs,
+            in_specs=[ANY] + [VMEM] * parts,
+            out_specs=(VMEM,) * outs,
+            compiler_params=params(8),
+            cost_estimate=cost(4 * outs * capacity * span, 8 * outs * capacity * span),
+            name="join",
+        )(after, *sums)
+
+    across = exchange(packed[3], "ctx", 3 * parts)
+    stay_hidden = lift(shared([packed[0]] * parts), packed[0])
+    lowering += fetch([(w_down[0], 16, cuts[1], spans[1])], stay_hidden, hurry=True)
     stay_out = lower(lowering, stay_hidden, packed[0], parts)
-    stay_sums = [stay_out[0]] + [
-        exchange(stay_out[turn], "ctx", turn) for turn in range(1, parts)
-    ]
-    moved_rows = (EXPERTS - 1) * capacity
+    stay_sums = shared(stay_out)
+
+    across_hidden = lift(shared([across] * parts), stay_sums[-1], True)
+    across_out = lower(lowering, across_hidden, packed[0], parts, True)
+    (across,) = join(0, width, shared(across_out), 1, across_hidden)
+    across_back = exchange(across, "ctx", 3 * parts)
+
+    near_slots = (1, 2)
+    near_rows = len(near_slots) * capacity
     arrived = pl.pallas_call(
         gather_kernel,
-        out_shape=shape((moved_rows, width), BF16),
-        in_specs=[ANY] + [VMEM] * (EXPERTS - 1),
+        out_shape=shape((near_rows, width), BF16),
+        in_specs=[ANY] + [VMEM] * len(near_slots),
         out_specs=VMEM,
         compiler_params=params(4),
-        cost_estimate=cost(0, 4 * moved_rows * width),
+        cost_estimate=cost(0, 4 * near_rows * width),
         name="gather",
-    )(stay_sums[-1], *moved)
+    )(across_out[0], *[exchange(packed[slot], "ctx", slot * parts) for slot in near_slots])
     hiddens = []
-    after = arrived
-    for turn in range(parts):
-        after = lift([exchange(arrived, "ctx", turn) if turn else arrived], after)
+    after = across
+    for block in shared([arrived] * parts):
+        after = lift([block], after, True)
         hiddens.append(after)
     others = []
+    after = across_back
     for turn in range(1, parts):
-        (after,) = lower(lowering, hiddens[turn], after)
+        (after,) = lower(lowering, hiddens[turn], after, hurry=True)
         others.append(exchange(after, "ctx", turn))
     results = []
-    for chunk in range(CHUNKS):
-        (own,) = lower(lowering[chunk : chunk + 1], hiddens[0], after, hurry=chunk > 0)
-        joined = pl.pallas_call(
-            functools.partial(join_kernel, chunk * half),
-            out_shape=(shape((capacity, half), BF16),) * (EXPERTS - 1),
-            in_specs=[VMEM] * parts,
-            out_specs=(VMEM,) * (EXPERTS - 1),
-            compiler_params=params(8),
-            cost_estimate=cost(4 * moved_rows * half, 8 * moved_rows * half),
-            name="join",
-        )(own, *others)
+    ready = hiddens[0]
+    for chunk, span in enumerate(spans):
+        (own,) = lower(lowering[chunk : chunk + 1], hiddens[0], after, hurry=True)
+        joined = join(cuts[chunk], span, [own] + others, len(near_slots), ready)
         after = joined[0]
-        returned = between_experts(joined)
+        returned = [
+            exchange(block, "ctx", slot * parts) for slot, block in zip(near_slots, joined)
+        ]
         finished = pl.pallas_call(
-            functools.partial(finish_kernel, chunk * half),
-            out_shape=shape((rows, half), BF16),
+            functools.partial(finish_kernel, cuts[chunk]),
+            out_shape=shape((rows, span), BF16),
             in_specs=[VMEM] * (1 + EXPERTS + parts),
             out_specs=VMEM,
             compiler_params=params(8),
             cost_estimate=cost(
-                4 * rows * EXPERTS * capacity * half, 10 * rows * half
+                4 * rows * EXPERTS * capacity * span, 10 * rows * span
             ),
             name="finish",
-        )(second, weighting, *returned, *stay_sums)
+        )(second, weighting, *returned, across_back, *stay_sums)
         results.append(shifted(finished, "segment", 1))
     return jnp.concatenate(results, 1)[None]
 

time: 106 us -> 111 us (1.047)
  Pallas kernels: 47.2 us -> 50.8 us
  waiting for transfers between devices: 28.8 us -> 32.1 us
  starting transfers between devices: 28.7 us -> 27.1 us
    ppermute x2, waiting for transfers between devices: 8.17 us -> 10.7 us  [shifted(): lax.ppermute(value, axis, [(at, (at + steps) % count) for at in range(cou...]
    ppermute x26 -> x27, starting transfers between devices: 25.5 us -> 23.9 us  [exchange(): return lax.ppermute(value, axis, [(at, at ^ mask) for at in range(count)])]
    pallas_call x4 -> x5, Pallas kernels: 8.5 us -> 10.1 us  [lower(): pl.pallas_call(functools.partial(down_kernel, len(weights)), out_shape=(s...]
    pallas_call x7 -> x10, Pallas kernels: 2.13 us -> 3.48 us  [the longest x4 2.58 us: on_device(): pl.pallas_call(functools.partial(far_kernel, turn, slots, last, len(past)...]
    ppermute x26 -> x27, waiting for transfers between devices: 20.6 us -> 21.4 us  [exchange(): return lax.ppermute(value, axis, [(at, at ^ mask) for at in range(count)])]
    pallas_call x3 -> x4, Pallas kernels: 8.16 us -> 8.85 us  [lift(): pl.pallas_call(up_kernel, out_shape=shape((count, units), BF16), in_specs...]
  transfers between devices with their start and end apart: 28 -> 29, of which waited for: 16 -> 17; matrix products, arithmetic and copies ran while one was open for 0% -> 0% of each run, Pallas kernels for 31% -> 36%
where the time goes in v7:
time: 111 us
  Pallas kernels  50.8 us (46%)
  waiting for transfers between devices  32.1 us (29%)
  starting transfers between devices  27.1 us (24%)
    ppermute x27, starting transfers between devices, exchange(): return lax.ppermute(value, axis, [(at, at ^ mask) for at in range(count)])  23.9 us
    ppermute x27, waiting for transfers between devices, exchange(): return lax.ppermute(value, axis, [(at, at ^ mask) for at in range(count)])  21.4 us
    pallas_call x2, Pallas kernels, fetch(): pl.pallas_call(functools.partial(fetch_kernel, pieces, starts), out_shape...  11.6 us
    ppermute x2, waiting for transfers between devices, shifted(): lax.ppermute(value, axis, [(at, (at + steps) % count) for at in range(cou...  10.7 us
    pallas_call x5, Pallas kernels, lower(): pl.pallas_call(functools.partial(down_kernel, len(weights)), out_shape=(s...  10.1 us
    pallas_call x4, Pallas kernels, lift(): pl.pallas_call(up_kernel, out_shape=shape((count, units), BF16), in_specs...  8.85 us
    pallas_call x1, Pallas kernels, on_device(): pl.pallas_call(prepare_kernel, out_shape=(shape((rows, width), F32), shap...  4.59 us
    ppermute x2, starting transfers between devices, shifted(): lax.ppermute(value, axis, [(at, (at + steps) % count) for at in range(cou...  3.24 us
  transfers between devices with their start and end apart: 29, of which 17 were waited for; matrix products, arithmetic and copies ran while one was open for 0% of the time, Pallas kernels for 36%

profile of v7, /device:TPU:0, one launch (start us, length us, event | category | flops | bytes accessed | tf_op | source)
XLA Modules:
  0.0 111.3 jit_solution(7205937364965989422)
XLA Ops:
  0.0 0.5 collective-permute-start
  0.5 2.5 %collective-permute-start.2 = (bf16[128,2048]{1,0:T(8,128)(2,1)}, bf16[128,2048]{1,0:T(8,128)(2,1)S(1)}, u32[]{:S(2)}, u32[]{:S(2)}) collective-permute-start(bf16[128,2048]{1,0:T(8,128)(2,1)} %bitcast.25), channel_id=1, source_target_pairs={{0,2},{1,3},{2,0},{3,1},{4,6},{5,7},{6,4},{7,5},{8,10},{9,11},{10,... | collective-permute-start | bytes 1572872 | tf_op jit(solution)/shard_map/ppermute | solution.py:469
  2.9 1.5 %collective-permute-start.1 = (bf16[2048,128]{1,0:T(8,128)(2,1)}, bf16[2048,128]{1,0:T(8,128)(2,1)S(1)}, u32[]{:S(2)}, u32[]{:S(2)}) collective-permute-start(bf16[2048,128]{1,0:T(8,128)(2,1)} %bitcast.30), channel_id=1, source_target_pairs={{0,4},{1,5},{2,6},{3,7},{4,0},{5,1},{6,2},{7,3},{8,12},{9,13},{10,... | collective-permute-start | bytes 1572872 | tf_op jit(solution)/shard_map/ppermute | solution.py:469
  4.5 1.7 %norm.2 = (bf16[128,2048]{1,0:T(8,128)(2,1)S(1)}, bf16[128,2048]{1,0:T(8,128)(2,1)S(1)}) custom-call(f32[3,1,2048]{2,1,0:T(1,128)} %bitcast.33, s32[3]{0:T(128)S(1)} %pad_add_fusion.after.place, bf16[128,2048]{1,0:T(8,128)(2,1)} %bitcast.26, bf16[128,2048]{1,0:T(8,128)(2,1)S(1)} %collective-permute-done.refs_1_), custom_call_target="tpu_custom_call" | custom-call | flops 2097152 | bytes 1048576 | tf_op jit(solution)/shard_map/norm/pallas_call | solution.py:521
  6.3 8.6 %fetch.2 = (bf16[2048,3584]{1,0:T(8,128)(2,1)S(1)}, bf16[3584,1152]{1,0:T(8,128)(2,1)S(1)}, f32[3,1,2048]{2,1,0:T(1,128)S(1)}, bf16[2048,128]{1,0:T(8,128)(2,1)S...) custom-call(bf16[2048,3584]{1,0:T(8,128)(2,1)} %bitcast.23, ...), custom_call_target="tpu_custom_call" | custom-call | bytes 63259648 | tf_op jit(solution)/shard_map/fetch/pallas_call | solution.py:398
  14.9 0.8 collective-permute-done.2.refs_0_
  15.7 0.3 norm.3.first
  16.2 1.1 collective-permute-done.1.w_other
  17.2 1.2 %project.1 = (bf16[2,512,128]{2,1,0:T(8,128)(2,1)S(1)}, bf16[2,256,128]{2,1,0:T(8,128)(2,1)S(1)}, bf16[2048,256]{1,0:T(8,128)(2,1)S(1)}) custom-call(s32[3]{0:T(128)S(1)} %pad_add_fusion.after.place, bf16[2048,128]{1,0:T(8,128)(2,1)S(1)} %get-tuple-element.71.w_own, bf16[2048,128]{1,0:T(8,128)(2,1)S(1)} %collective-permute-done.1.w_other, ...), custom_call_target="tpu_custom_call" | custom-call | flops 268435456 | bytes 4194304 | tf_op jit(solution)/shard_map/project/pallas_call | solution.py:545
  18.5 1.6 %collective-permute-start.4 = (bf16[2,256,128]{2,1,0:T(8,128)(2,1)S(1)}, bf16[2,256,128]{2,1,0:T(8,128)(2,1)S(1)}, u32[]{:S(2)}, u32[]{:S(2)}) collective-permute-start(bf16[2,256,128]{2,1,0:T(8,128)(2,1)S(1)} %get-tuple-element.77.refs_2_), channel_id=1, source_target_pairs={{0,4},{1,5},{2,6},{3,7},{4,0},{5,1},{6,2},{7,3},{8,12},{9,13},{10,... | collective-permute-start | bytes 393224 | tf_op jit(solution)/shard_map/ppermute | solution.py:469
  20.0 1.0 project_more.1
  21.0 0.6 collective-permute-start.5
  21.6 2.5 %near.1 = (f32[4,512,128]{2,1,0:T(8,128)S(1)}, f32[4,512,128]{2,1,0:T(8,128)S(1)}, f32[4,512,128]{2,1,0:T(8,128)S(1)}) custom-call(s32[3]{0:T(128)S(1)} %pad_add_fusion.after.place, bf16[2,512,128]{2,1,0:T(8,128)(2,1)S(1)} %get-tuple-element.73.refs_0_, bf16[2,512,128]{2,1,0:T(8,128)(2,1)S(1)} %get-tuple-element.76.refs_1_, ...), custom_call_target="tpu_custom_call" | custom-call | flops 536870912 | bytes 4194304 | tf_op jit(solution)/shard_map/near/pallas_call | solution.py:572
  24.1 0.7 far.4
  24.7 0.7 far.6
  25.4 0.9 collective-permute-done.5.refs_5_
  26.3 0.6 far.5
  27.0 0.6 far.7
  27.7 1.7 %collective-permute-start.7 = (bf16[128,512]{1,0:T(8,128)(2,1)S(1)}, bf16[128,512]{1,0:T(8,128)(2,1)S(1)}, u32[]{:S(2)}, u32[]{:S(2)}) collective-permute-start(bf16[128,512]{1,0:T(8,128)(2,1)S(1)} %get-tuple-element.90), channel_id=1, source_target_pairs={{0,2},{1,3},{2,0},{3,1},{4,6},{5,7},{6,4},{7,5},{8,10},{9,11},{10,... | collective-permute-start | bytes 393224 | tf_op jit(solution)/shard_map/ppermute | solution.py:469
  29.3 0.2 collective-permute-start.8
  29.6 4.4 %collective-permute-done.7.refs_2_ = bf16[128,512]{1,0:T(8,128)(2,1)S(1)} collective-permute-done((bf16[128,512]{1,0:T(8,128)(2,1)S(1)}, bf16[128,512]{1,0:T(8,128)(2,1)S(1)}, u32[]{:S(2)}, u32[]{:S(2)}) %collective-permute-start.7) | collective-permute-done | bytes 131104 | tf_op jit(solution)/shard_map/ppermute | solution.py:469
  34.0 2.0 %collective-permute-done.8.refs_3_ = bf16[128,512]{1,0:T(8,128)(2,1)S(1)} collective-permute-done((bf16[128,512]{1,0:T(8,128)(2,1)S(1)}, bf16[128,512]{1,0:T(8,128)(2,1)S(1)}, u32[]{:S(2)}, u32[]{:S(2)}) %collective-permute-start.8) | collective-permute-done | bytes 131104 | tf_op jit(solution)/shard_map/ppermute | solution.py:469
  36.0 4.6 %prepare.1 = (f32[128,2048]{1,0:T(8,128)S(1)}, f32[128,2048]{1,0:T(8,128)S(1)}, f32[128,2048]{1,0:T(8,128)S(1)}, f32[256,2048]{1,0:T(8,128)S(1)}, f32[16,2048]{1...) custom-call(s32[3]{0:T(128)S(1)} %pad_add_fusion.after.place, ...), custom_call_target="tpu_custom_call" | custom-call | flops 671088640 | bytes 7864320 | tf_op jit(solution)/shard_map/prepare/pallas_call | solution.py:603
  40.6 0.3 collective-permute-start.9
  40.9 0.4 couple.1.coef.after
  41.3 0.6 collective-permute-done.9.other.beside
  42.0 0.6 pair.1
  42.5 1.7 %collective-permute-start.10 = (bf16[16,2176]{1,0:T(8,128)(2,1)S(1)}, bf16[16,2176]{1,0:T(8,128)(2,1)S(1)}, u32[]{:S(2)}, u32[]{:S(2)}) collective-permute-start(bf16[16,2176]{1,0:T(8,128)(2,1)S(1)} %pair.1), channel_id=1, source_target_pairs={{0,2},{1,3},{2,0},{3,1},{4,6},{5,7},{6,4},{7,5},{8,10},{9,11},{10,... | collective-permute-start | bytes 208904 | tf_op jit(solution)/shard_map/ppermute | solution.py:469
  44.2 2.8 %collective-permute-start.11 = (bf16[16,2176]{1,0:T(8,128)(2,1)S(1)}, bf16[16,2176]{1,0:T(8,128)(2,1)S(1)}, u32[]{:S(2)}, u32[]{:S(2)}) collective-permute-start(bf16[16,2176]{1,0:T(8,128)(2,1)S(1)} %pair.1), channel_id=1, source_target_pairs={{0,4},{1,5},{2,6},{3,7},{4,0},{5,1},{6,2},{7,3},{8,12},{9,13},{10,... | collective-permute-start | bytes 208904 | tf_op jit(solution)/shard_map/ppermute | solution.py:469
  47.1 0.9 collective-permute-start.12
  47.9 1.7 %within.1 = (f32[128,2048]{1,0:T(8,128)S(1)}, f32[128,2048]{1,0:T(8,128)S(1)}) custom-call(f32[128,128]{1,0:T(8,128)S(1)} %couple.1.coef.after, f32[128,2048]{1,0:T(8,128)S(1)} %get-tuple-element.94.base, f32[128,2048]{1,0:T(8,128)S(1)} %get-tuple-element.95.keep, f32[128,2048]{1,0:T(8,128)S(1)} %get-tuple-element.96.drive), custom_call_target="tpu_custom_call" | custom-call | flops 10485760 | bytes 5242880 | tf_op jit(solution)/shard_map/within/pallas_call | solution.py:657
  49.7 0.6 collective-permute-done.11.refs_1_
  50.3 2.0 %collective-permute-done.12.refs_2_ = bf16[16,2176]{1,0:T(8,128)(2,1)S(1)} collective-permute-done((bf16[16,2176]{1,0:T(8,128)(2,1)S(1)}, bf16[16,2176]{1,0:T(8,128)(2,1)S(1)}, u32[]{:S(2)}, u32[]{:S(2)}) %collective-permute-start.12) | collective-permute-done | bytes 69664 | tf_op jit(solution)/shard_map/ppermute | solution.py:469
  52.3 2.8 %route.1 = (f32[128,2048]{1,0:T(8,128)S(1)}, f32[128,256]{1,0:T(8,128)S(1)}, bf16[64,2048]{1,0:T(8,128)(2,1)S(1)}, bf16[64,2048]{1,0:T(8,128)(2,1)S(1)}, bf16[64...) custom-call(s32[3]{0:T(128)S(1)} %pad_add_fusion.after.place, f32[128,2048]{1,0:T(8,128)S(1)} %get-tuple-element.97.before, ...), custom_call_target="tpu_custom_call" | custom-call | flops 671088640 | bytes 7864320 | tf_op jit(solution)/shard_map/route/pallas_call | solution.py:666
  55.2 1.4 %collective-permute-start.15 = (bf16[64,2048]{1,0:T(8,128)(2,1)S(1)}, bf16[64,2048]{1,0:T(8,128)(2,1)S(1)}, u32[]{:S(2)}, u32[]{:S(2)}) collective-permute-start(bf16[64,2048]{1,0:T(8,128)(2,1)S(1)} %get-tuple-element.109), channel_id=1, source_target_pairs={{0,6},{1,7},{2,4},{3,5},{4,2},{5,3},{6,0},{7,1},{8,14},{9,15},{10,... | collective-permute-start | bytes 786440 | tf_op jit(solution)/shard_map/ppermute | solution.py:469
  56.7 2.1 %up.4.refs_1_.hidden = bf16[128,3584]{1,0:T(8,128)(2,1)S(1)} custom-call(bf16[2048,3584]{1,0:T(8,128)(2,1)S(1)} %get-tuple-element.75.after.w_up, bf16[64,2048]{1,0:T(8,128)(2,1)S(1)} %get-tuple-element.106.after.refs_0_, bf16[64,2048]{1,0:T(8,128)(2,1)S(1)} %get-tuple-element.106.after.refs_0_, bf16[64,2048]{1,0:T(8,128)(2,1)S(1)} %collective-permute-done.13.refs_1_), custom_call_target="tpu_custom_call" | custom-call | flops 1879048192 | bytes 14680064 | tf_op jit(solution)/shard_map/up/pallas_call | solution.py:700
  58.8 3.0 %fetch.3.refs_1_.refs_0_ = bf16[3584,896]{1,0:T(8,128)(2,1)S(1)} custom-call(bf16[3584,2048]{1,0:T(8,128)(2,1)} %bitcast.22, bf16[128,3584]{1,0:T(8,128)(2,1)S(1)} %up.4.refs_1_.hidden), custom_call_target="tpu_custom_call" | custom-call | tf_op jit(solution)/shard_map/fetch/pallas_call | solution.py:398
  61.8 2.5 %down.5 = (bf16[64,2048]{1,0:T(8,128)(2,1)S(1)}, bf16[64,2048]{1,0:T(8,128)(2,1)S(1)}) custom-call(bf16[128,3584]{1,0:T(8,128)(2,1)S(1)} %up.4.refs_1_.hidden, bf16[64,2048]{1,0:T(8,128)(2,1)S(1)} %get-tuple-element.106.after.refs_0_, bf16[3584,1152]{1,0:T(8,128)(2,1)S(1)} %get-tuple-element.107.refs_0_, bf16[3584,896]{1,0:T(8,128)(2,1)S(1)} %fetch.3.refs_1_.refs_0_), custom_call_target="tpu_custom_call" | custom-call | flops 1879048192 | bytes 14680064 | tf_op jit(solution)/shard_map/down/pallas_call | solution.py:713
  64.5 0.3 collective-permute-done.15.refs_0_
  64.9 1.4 %collective-permute-start.18 = (bf16[64,2048]{1,0:T(8,128)(2,1)S(1)}, bf16[64,2048]{1,0:T(8,128)(2,1)S(1)}, u32[]{:S(2)}, u32[]{:S(2)}) collective-permute-start(bf16[64,2048]{1,0:T(8,128)(2,1)S(1)} %get-tuple-element.112), channel_id=1, source_target_pairs={{0,2},{1,3},{2,0},{3,1},{4,6},{5,7},{6,4},{7,5},{8,10},{9,11},{10,... | collective-permute-start | bytes 786440 | tf_op jit(solution)/shard_map/ppermute | solution.py:469
  66.3 0.6 collective-permute-start.19
  66.9 2.1 %up.5.hidden.after = bf16[128,3584]{1,0:T(8,128)(2,1)S(1)} custom-call(bf16[2048,3584]{1,0:T(8,128)(2,1)S(1)} %get-tuple-element.75.after.w_up, bf16[64,2048]{1,0:T(8,128)(2,1)S(1)} %collective-permute-done.14.after.refs_4_, bf16[64,2048]{1,0:T(8,128)(2,1)S(1)} %collective-permute-done.15.refs_0_, bf16[64,2048]{1,0:T(8,128)(2,1)S(1)} %collective-permute-done.16.refs_1_), custom_call_target="tpu_custom_call" | custom-call | flops 524288 | bytes 4096 | tf_op jit(solution)/shard_map/up/pallas_call | solution.py:700
  69.1 2.5 %down.6 = (bf16[64,2048]{1,0:T(8,128)(2,1)S(1)}, bf16[64,2048]{1,0:T(8,128)(2,1)S(1)}) custom-call(bf16[128,3584]{1,0:T(8,128)(2,1)S(1)} %up.5.hidden.after, bf16[64,2048]{1,0:T(8,128)(2,1)S(1)} %get-tuple-element.106.after.refs_0_, bf16[3584,1152]{1,0:T(8,128)(2,1)S(1)} %get-tuple-element.107.refs_0_, bf16[3584,896]{1,0:T(8,128)(2,1)S(1)} %fetch.3.refs_1_.refs_0_), custom_call_target="tpu_custom_call" | custom-call | flops 524288 | bytes 4096 | tf_op jit(solution)/shard_map/down/pallas_call | solution.py:713
  71.7 1.9 %collective-permute-done.18.refs_0_ = bf16[64,2048]{1,0:T(8,128)(2,1)S(1)} collective-permute-done((bf16[64,2048]{1,0:T(8,128)(2,1)S(1)}, bf16[64,2048]{1,0:T(8,128)(2,1)S(1)}, u32[]{:S(2)}, u32[]{:S(2)}) %collective-permute-start.18) | collective-permute-done | bytes 262176 | tf_op jit(solution)/shard_map/ppermute | solution.py:469
  73.5 1.2 %collective-permute-done.19.refs_1_ = bf16[64,2048]{1,0:T(8,128)(2,1)S(1)} collective-permute-done((bf16[64,2048]{1,0:T(8,128)(2,1)S(1)}, bf16[64,2048]{1,0:T(8,128)(2,1)S(1)}, u32[]{:S(2)}, u32[]{:S(2)}) %collective-permute-start.19) | collective-permute-done | bytes 262176 | tf_op jit(solution)/shard_map/ppermute | solution.py:469
  74.9 1.3 %collective-permute-start.21 = (bf16[64,2048]{1,0:T(8,128)(2,1)S(1)}, bf16[64,2048]{1,0:T(8,128)(2,1)S(1)}, u32[]{:S(2)}, u32[]{:S(2)}) collective-permute-start(bf16[64,2048]{1,0:T(8,128)(2,1)S(1)} %join.3.after), channel_id=1, source_target_pairs={{0,6},{1,7},{2,4},{3,5},{4,2},{5,3},{6,0},{7,1},{8,14},{9,15},{10,... | collective-permute-start | bytes 786440 | tf_op jit(solution)/shard_map/ppermute | solution.py:469
  76.2 2.1 %up.6.after.hidden = bf16[128,3584]{1,0:T(8,128)(2,1)S(1)} custom-call(bf16[2048,3584]{1,0:T(8,128)(2,1)S(1)} %get-tuple-element.75.after.w_up, bf16[64,2048]{1,0:T(8,128)(2,1)S(1)} %join.3.after, bf16[128,2048]{1,0:T(8,128)(2,1)S(1)} %gather.1.refs_0_), custom_call_target="tpu_custom_call" | custom-call | flops 524288 | bytes 4096 | tf_op jit(solution)/shard_map/up/pallas_call | solution.py:700
  78.3 2.4 %up.7.hidden = bf16[128,3584]{1,0:T(8,128)(2,1)S(1)} custom-call(bf16[2048,3584]{1,0:T(8,128)(2,1)S(1)} %get-tuple-element.75.after.w_up, bf16[128,3584]{1,0:T(8,128)(2,1)S(1)} %up.6.after.hidden, bf16[128,2048]{1,0:T(8,128)(2,1)S(1)} %collective-permute-done.20.refs_0_), custom_call_target="tpu_custom_call" | custom-call | flops 524288 | bytes 4096 | tf_op jit(solution)/shard_map/up/pallas_call | solution.py:700
  80.8 3.8 %collective-permute-done.21.after.refs_2_ = bf16[64,2048]{1,0:T(8,128)(2,1)S(1)} collective-permute-done((bf16[64,2048]{1,0:T(8,128)(2,1)S(1)}, bf16[64,2048]{1,0:T(8,128)(2,1)S(1)}, u32[]{:S(2)}, u32[]{:S(2)}) %collective-permute-start.21) | collective-permute-done | bytes 262176 | tf_op jit(solution)/shard_map/ppermute | solution.py:469
  84.5 2.5 %down.7.after = bf16[128,2048]{1,0:T(8,128)(2,1)S(1)} custom-call(bf16[128,3584]{1,0:T(8,128)(2,1)S(1)} %up.7.hidden, bf16[64,2048]{1,0:T(8,128)(2,1)S(1)} %collective-permute-done.21.after.refs_2_, bf16[3584,1152]{1,0:T(8,128)(2,1)S(1)} %get-tuple-element.107.refs_0_, bf16[3584,896]{1,0:T(8,128)(2,1)S(1)} %fetch.3.refs_1_.refs_0_), custom_call_target="tpu_custom_call" | custom-call | flops 524288 | bytes 4096 | tf_op jit(solution)/shard_map/down/pallas_call | solution.py:713
  87.1 1.4 %down.8.own = bf16[128,1152]{1,0:T(8,128)(2,1)S(1)} custom-call(bf16[128,3584]{1,0:T(8,128)(2,1)S(1)} %up.6.after.hidden, bf16[128,2048]{1,0:T(8,128)(2,1)S(1)} %down.7.after, bf16[3584,1152]{1,0:T(8,128)(2,1)S(1)} %get-tuple-element.107.refs_0_), custom_call_target="tpu_custom_call" | custom-call | flops 294912 | bytes 2304 | tf_op jit(solution)/shard_map/down/pallas_call | solution.py:713
  88.6 0.5 collective-permute-done.22.refs_0_
  89.1 0.6 collective-permute-start.23
  89.7 1.2 %collective-permute-start.24 = (bf16[64,1152]{1,0:T(8,128)(2,1)S(1)}, bf16[64,1152]{1,0:T(8,128)(2,1)S(1)}, u32[]{:S(2)}, u32[]{:S(2)}) collective-permute-start(bf16[64,1152]{1,0:T(8,128)(2,1)S(1)} %get-tuple-element.115), channel_id=1, source_target_pairs={{0,4},{1,5},{2,6},{3,7},{4,0},{5,1},{6,2},{7,3},{8,12},{9,13},{10,... | collective-permute-start | bytes 442376 | tf_op jit(solution)/shard_map/ppermute | solution.py:469
  90.9 1.2 %down.9.own = bf16[128,896]{1,0:T(8,128)(2,1)S(1)} custom-call(bf16[128,3584]{1,0:T(8,128)(2,1)S(1)} %up.6.after.hidden, bf16[64,1152]{1,0:T(8,128)(2,1)S(1)} %get-tuple-element.114.after, bf16[3584,896]{1,0:T(8,128)(2,1)S(1)} %fetch.3.refs_1_.refs_0_), custom_call_target="tpu_custom_call" | custom-call | flops 229376 | bytes 1792 | tf_op jit(solution)/shard_map/down/pallas_call | solution.py:713
  92.2 0.8 collective-permute-start.26
  92.9 1.6 %collective-permute-start.27 = (bf16[64,896]{1,0:T(8,128)(2,1)S(1)}, bf16[64,896]{1,0:T(8,128)(2,1)S(1)}, u32[]{:S(2)}, u32[]{:S(2)}) collective-permute-start(bf16[64,896]{1,0:T(8,128)(2,1)S(1)} %get-tuple-element.118), channel_id=1, source_target_pairs={{0,4},{1,5},{2,6},{3,7},{4,0},{5,1},{6,2},{7,3},{8,12},{9,13},{10,... | collective-permute-start | bytes 344072 | tf_op jit(solution)/shard_map/ppermute | solution.py:469
  94.5 1.1 %collective-permute-done.23.refs_0_ = bf16[64,1152]{1,0:T(8,128)(2,1)S(1)} collective-permute-done((bf16[64,1152]{1,0:T(8,128)(2,1)S(1)}, bf16[64,1152]{1,0:T(8,128)(2,1)S(1)}, u32[]{:S(2)}, u32[]{:S(2)}) %collective-permute-start.23) | collective-permute-done | bytes 147488 | tf_op jit(solution)/shard_map/ppermute | solution.py:469
  95.8 0.3 finish.2
  96.2 1.6 %collective-permute-start.25 = (bf16[128,1152]{1,0:T(8,128)(2,1)S(1)}, bf16[128,1152]{1,0:T(8,128)(2,1)S(1)}, u32[]{:S(2)}, u32[]{:S(2)}) collective-permute-start(bf16[128,1152]{1,0:T(8,128)(2,1)S(1)} %finish.2), channel_id=1, source_target_pairs={{0,8},{8,16},{16,24},{24,0},{1,9},{9,17},{17,25},{25,1},{2,10},{10... | collective-permute-start | bytes 884744 | tf_op jit(solution)/shard_map/ppermute | solution.py:474
  97.8 0.3 finish.3
  98.1 1.6 %collective-permute-start.28 = (bf16[128,896]{1,0:T(8,128)(2,1)S(1)}, bf16[128,896]{1,0:T(8,128)(2,1)S(1)}, u32[]{:S(2)}, u32[]{:S(2)}) collective-permute-start(bf16[128,896]{1,0:T(8,128)(2,1)S(1)} %finish.3), channel_id=1, source_target_pairs={{0,8},{8,16},{16,24},{24,0},{1,9},{9,17},{17,25},{25,1},{2,10},{10... | collective-permute-start | bytes 688136 | tf_op jit(solution)/shard_map/ppermute | solution.py:474
  99.8 10.7 %collective-permute-done.28 = bf16[128,896]{1,0:T(8,128)(2,1)S(1)} collective-permute-done((bf16[128,896]{1,0:T(8,128)(2,1)S(1)}, bf16[128,896]{1,0:T(8,128)(2,1)S(1)}, u32[]{:S(2)}, u32[]{:S(2)}) %collective-permute-start.28) | collective-permute-done | bytes 229408 | tf_op jit(solution)/shard_map/ppermute | solution.py:474
  110.4 0.9 maximum_bitcast_fusion
  (27 shorter events, 1.4 us)
Async XLA Ops:
  0.0 4.5 %collective-permute-start = (bf16[128,2048]{1,0:T(8,128)(2,1)}, bf16[128,2048]{1,0:T(8,128)(2,1)S(1)}, u32[]{:S(2)}, u32[]{:S(2)}) collective-permute-start(bf16[128,2048]{1,0:T(8,128)(2,1)} %bitcast.24), channel_id=1, source_target_pairs={{0,1},{1,0},{2,3},{3,2},{4,5},{5,4},{6,7},{7,6},{8,9},{9,8},{10,11... | collective-permute-start | bytes 1572872 | tf_op jit(solution)/shard_map/ppermute | solution.py:469
  0.5 15.3 %collective-permute-start.2 = (bf16[128,2048]{1,0:T(8,128)(2,1)}, bf16[128,2048]{1,0:T(8,128)(2,1)S(1)}, u32[]{:S(2)}, u32[]{:S(2)}) collective-permute-start(bf16[128,2048]{1,0:T(8,128)(2,1)} %bitcast.25), channel_id=1, source_target_pairs={{0,2},{1,3},{2,0},{3,1},{4,6},{5,7},{6,4},{7,5},{8,10},{9,11},{10,... | collective-permute-start | bytes 1572872 | tf_op jit(solution)/shard_map/ppermute | solution.py:469
  2.9 14.3 %collective-permute-start.1 = (bf16[2048,128]{1,0:T(8,128)(2,1)}, bf16[2048,128]{1,0:T(8,128)(2,1)S(1)}, u32[]{:S(2)}, u32[]{:S(2)}) collective-permute-start(bf16[2048,128]{1,0:T(8,128)(2,1)} %bitcast.30), channel_id=1, source_target_pairs={{0,4},{1,5},{2,6},{3,7},{4,0},{5,1},{6,2},{7,3},{8,12},{9,13},{10,... | collective-permute-start | bytes 1572872 | tf_op jit(solution)/shard_map/ppermute | solution.py:469
  16.1 4.0 %collective-permute-start.3 = (bf16[128,2048]{1,0:T(8,128)(2,1)S(1)}, bf16[128,2048]{1,0:T(8,128)(2,1)S(1)}, u32[]{:S(2)}, u32[]{:S(2)}) collective-permute-start(bf16[128,2048]{1,0:T(8,128)(2,1)S(1)} %norm.3.first), channel_id=1, source_target_pairs={{0,1},{1,0},{2,3},{3,2},{4,5},{5,4},{6,7},{7,6},{8,9},{9,8},{10,11... | collective-permute-start | bytes 1572872 | tf_op jit(solution)/shard_map/ppermute | solution.py:469
  18.5 5.6 %collective-permute-start.4 = (bf16[2,256,128]{2,1,0:T(8,128)(2,1)S(1)}, bf16[2,256,128]{2,1,0:T(8,128)(2,1)S(1)}, u32[]{:S(2)}, u32[]{:S(2)}) collective-permute-start(bf16[2,256,128]{2,1,0:T(8,128)(2,1)S(1)} %get-tuple-element.77.refs_2_), channel_id=1, source_target_pairs={{0,4},{1,5},{2,6},{3,7},{4,0},{5,1},{6,2},{7,3},{8,12},{9,13},{10,... | collective-permute-start | bytes 393224 | tf_op jit(solution)/shard_map/ppermute | solution.py:469
  21.0 5.3 %collective-permute-start.5 = (bf16[2,256,128]{2,1,0:T(8,128)(2,1)S(1)}, bf16[2,256,128]{2,1,0:T(8,128)(2,1)S(1)}, u32[]{:S(2)}, u32[]{:S(2)}) collective-permute-start(bf16[2,256,128]{2,1,0:T(8,128)(2,1)S(1)} %get-tuple-element.78.refs_3_), channel_id=1, source_target_pairs={{0,4},{1,5},{2,6},{3,7},{4,0},{5,1},{6,2},{7,3},{8,12},{9,13},{10,... | collective-permute-start | bytes 393224 | tf_op jit(solution)/shard_map/ppermute | solution.py:469
  26.9 2.6 %collective-permute-start.6 = (bf16[128,512]{1,0:T(8,128)(2,1)S(1)}, bf16[128,512]{1,0:T(8,128)(2,1)S(1)}, u32[]{:S(2)}, u32[]{:S(2)}) collective-permute-start(bf16[128,512]{1,0:T(8,128)(2,1)S(1)} %get-tuple-element.86), channel_id=1, source_target_pairs={{0,1},{1,0},{2,3},{3,2},{4,5},{5,4},{6,7},{7,6},{8,9},{9,8},{10,11... | collective-permute-start | bytes 393224 | tf_op jit(solution)/shard_map/ppermute | solution.py:469
  27.7 6.4 %collective-permute-start.7 = (bf16[128,512]{1,0:T(8,128)(2,1)S(1)}, bf16[128,512]{1,0:T(8,128)(2,1)S(1)}, u32[]{:S(2)}, u32[]{:S(2)}) collective-permute-start(bf16[128,512]{1,0:T(8,128)(2,1)S(1)} %get-tuple-element.90), channel_id=1, source_target_pairs={{0,2},{1,3},{2,0},{3,1},{4,6},{5,7},{6,4},{7,5},{8,10},{9,11},{10,... | collective-permute-start | bytes 393224 | tf_op jit(solution)/shard_map/ppermute | solution.py:469
  29.3 6.7 %collective-permute-start.8 = (bf16[128,512]{1,0:T(8,128)(2,1)S(1)}, bf16[128,512]{1,0:T(8,128)(2,1)S(1)}, u32[]{:S(2)}, u32[]{:S(2)}) collective-permute-start(bf16[128,512]{1,0:T(8,128)(2,1)S(1)} %get-tuple-element.91), channel_id=1, source_target_pairs={{0,3},{1,2},{2,1},{3,0},{4,7},{5,6},{6,5},{7,4},{8,11},{9,10},{10,... | collective-permute-start | bytes 393224 | tf_op jit(solution)/shard_map/ppermute | solution.py:469
  40.6 1.3 %collective-permute-start.9 = (bf16[16,2176]{1,0:T(8,128)(2,1)S(1)}, bf16[16,2176]{1,0:T(8,128)(2,1)S(1)}, u32[]{:S(2)}, u32[]{:S(2)}) collective-permute-start(bf16[16,2176]{1,0:T(8,128)(2,1)S(1)} %get-tuple-element.103.own), channel_id=1, source_target_pairs={{0,1},{1,0},{2,3},{3,2},{4,5},{5,4},{6,7},{7,6},{8,9},{9,8},{10,11... | collective-permute-start | bytes 208904 | tf_op jit(solution)/shard_map/ppermute | solution.py:469
  42.5 7.1 %collective-permute-start.10 = (bf16[16,2176]{1,0:T(8,128)(2,1)S(1)}, bf16[16,2176]{1,0:T(8,128)(2,1)S(1)}, u32[]{:S(2)}, u32[]{:S(2)}) collective-permute-start(bf16[16,2176]{1,0:T(8,128)(2,1)S(1)} %pair.1), channel_id=1, source_target_pairs={{0,2},{1,3},{2,0},{3,1},{4,6},{5,7},{6,4},{7,5},{8,10},{9,11},{10,... | collective-permute-start | bytes 208904 | tf_op jit(solution)/shard_map/ppermute | solution.py:469
  44.2 6.1 %collective-permute-start.11 = (bf16[16,2176]{1,0:T(8,128)(2,1)S(1)}, bf16[16,2176]{1,0:T(8,128)(2,1)S(1)}, u32[]{:S(2)}, u32[]{:S(2)}) collective-permute-start(bf16[16,2176]{1,0:T(8,128)(2,1)S(1)} %pair.1), channel_id=1, source_target_pairs={{0,4},{1,5},{2,6},{3,7},{4,0},{5,1},{6,2},{7,3},{8,12},{9,13},{10,... | collective-permute-start | bytes 208904 | tf_op jit(solution)/shard_map/ppermute | solution.py:469
  47.1 5.2 %collective-permute-start.12 = (bf16[16,2176]{1,0:T(8,128)(2,1)S(1)}, bf16[16,2176]{1,0:T(8,128)(2,1)S(1)}, u32[]{:S(2)}, u32[]{:S(2)}) collective-permute-start(bf16[16,2176]{1,0:T(8,128)(2,1)S(1)} %pair.1), channel_id=1, source_target_pairs={{0,6},{1,7},{2,4},{3,5},{4,2},{5,3},{6,0},{7,1},{8,14},{9,15},{10,... | collective-permute-start | bytes 208904 | tf_op jit(solution)/shard_map/ppermute | solution.py:469
  55.1 1.6 %collective-permute-start.13 = (bf16[64,2048]{1,0:T(8,128)(2,1)S(1)}, bf16[64,2048]{1,0:T(8,128)(2,1)S(1)}, u32[]{:S(2)}, u32[]{:S(2)}) collective-permute-start(bf16[64,2048]{1,0:T(8,128)(2,1)S(1)} %get-tuple-element.106.after.refs_0_), channel_id=1, source_target_pairs={{0,1},{1,0},{2,3},{3,2},{4,5},{5,4},{6,7},{7,6},{8,9},{9,8},{10,11... | collective-permute-start | bytes 786440 | tf_op jit(solution)/shard_map/ppermute | solution.py:469
  55.2 9.6 %collective-permute-start.15 = (bf16[64,2048]{1,0:T(8,128)(2,1)S(1)}, bf16[64,2048]{1,0:T(8,128)(2,1)S(1)}, u32[]{:S(2)}, u32[]{:S(2)}) collective-permute-start(bf16[64,2048]{1,0:T(8,128)(2,1)S(1)} %get-tuple-element.109), channel_id=1, source_target_pairs={{0,6},{1,7},{2,4},{3,5},{4,2},{5,3},{6,0},{7,1},{8,14},{9,15},{10,... | collective-permute-start | bytes 786440 | tf_op jit(solution)/shard_map/ppermute | solution.py:469
  64.3 2.6 %collective-permute-start.14 = (bf16[64,2048]{1,0:T(8,128)(2,1)S(1)}, bf16[64,2048]{1,0:T(8,128)(2,1)S(1)}, u32[]{:S(2)}, u32[]{:S(2)}) collective-permute-start(bf16[64,2048]{1,0:T(8,128)(2,1)S(1)} %get-tuple-element.108), channel_id=1, source_target_pairs={{0,1},{1,0},{2,3},{3,2},{4,5},{5,4},{6,7},{7,6},{8,9},{9,8},{10,11... | collective-permute-start | bytes 786440 | tf_op jit(solution)/shard_map/ppermute | solution.py:469
  64.8 2.2 %collective-permute-start.16 = (bf16[64,2048]{1,0:T(8,128)(2,1)S(1)}, bf16[64,2048]{1,0:T(8,128)(2,1)S(1)}, u32[]{:S(2)}, u32[]{:S(2)}) collective-permute-start(bf16[64,2048]{1,0:T(8,128)(2,1)S(1)} %collective-permute-done.15.refs_0_), channel_id=1, source_target_pairs={{0,1},{1,0},{2,3},{3,2},{4,5},{5,4},{6,7},{7,6},{8,9},{9,8},{10,11... | collective-permute-start | bytes 786440 | tf_op jit(solution)/shard_map/ppermute | solution.py:469
  64.9 8.6 %collective-permute-start.18 = (bf16[64,2048]{1,0:T(8,128)(2,1)S(1)}, bf16[64,2048]{1,0:T(8,128)(2,1)S(1)}, u32[]{:S(2)}, u32[]{:S(2)}) collective-permute-start(bf16[64,2048]{1,0:T(8,128)(2,1)S(1)} %get-tuple-element.112), channel_id=1, source_target_pairs={{0,2},{1,3},{2,0},{3,1},{4,6},{5,7},{6,4},{7,5},{8,10},{9,11},{10,... | collective-permute-start | bytes 786440 | tf_op jit(solution)/shard_map/ppermute | solution.py:469
  66.3 8.4 %collective-permute-start.19 = (bf16[64,2048]{1,0:T(8,128)(2,1)S(1)}, bf16[64,2048]{1,0:T(8,128)(2,1)S(1)}, u32[]{:S(2)}, u32[]{:S(2)}) collective-permute-start(bf16[64,2048]{1,0:T(8,128)(2,1)S(1)} %get-tuple-element.113), channel_id=1, source_target_pairs={{0,4},{1,5},{2,6},{3,7},{4,0},{5,1},{6,2},{7,3},{8,12},{9,13},{10,... | collective-permute-start | bytes 786440 | tf_op jit(solution)/shard_map/ppermute | solution.py:469
  71.6 3.2 %collective-permute-start.17 = (bf16[64,2048]{1,0:T(8,128)(2,1)S(1)}, bf16[64,2048]{1,0:T(8,128)(2,1)S(1)}, u32[]{:S(2)}, u32[]{:S(2)}) collective-permute-start(bf16[64,2048]{1,0:T(8,128)(2,1)S(1)} %get-tuple-element.111), channel_id=1, source_target_pairs={{0,1},{1,0},{2,3},{3,2},{4,5},{5,4},{6,7},{7,6},{8,9},{9,8},{10,11... | collective-permute-start | bytes 786440 | tf_op jit(solution)/shard_map/ppermute | solution.py:469
  74.7 3.6 %collective-permute-start.20 = (bf16[128,2048]{1,0:T(8,128)(2,1)S(1)}, bf16[128,2048]{1,0:T(8,128)(2,1)S(1)}, u32[]{:S(2)}, u32[]{:S(2)}) collective-permute-start(bf16[128,2048]{1,0:T(8,128)(2,1)S(1)} %gather.1.refs_0_), channel_id=1, source_target_pairs={{0,1},{1,0},{2,3},{3,2},{4,5},{5,4},{6,7},{7,6},{8,9},{9,8},{10,11... | collective-permute-start | bytes 1572872 | tf_op jit(solution)/shard_map/ppermute | solution.py:469
  74.9 9.7 %collective-permute-start.21 = (bf16[64,2048]{1,0:T(8,128)(2,1)S(1)}, bf16[64,2048]{1,0:T(8,128)(2,1)S(1)}, u32[]{:S(2)}, u32[]{:S(2)}) collective-permute-start(bf16[64,2048]{1,0:T(8,128)(2,1)S(1)} %join.3.after), channel_id=1, source_target_pairs={{0,6},{1,7},{2,4},{3,5},{4,2},{5,3},{6,0},{7,1},{8,14},{9,15},{10,... | collective-permute-start | bytes 786440 | tf_op jit(solution)/shard_map/ppermute | solution.py:469
  87.0 2.0 %collective-permute-start.22 = (bf16[128,2048]{1,0:T(8,128)(2,1)S(1)}, bf16[128,2048]{1,0:T(8,128)(2,1)S(1)}, u32[]{:S(2)}, u32[]{:S(2)}) collective-permute-start(bf16[128,2048]{1,0:T(8,128)(2,1)S(1)} %down.7.after), channel_id=1, source_target_pairs={{0,1},{1,0},{2,3},{3,2},{4,5},{5,4},{6,7},{7,6},{8,9},{9,8},{10,11... | collective-permute-start | bytes 1572872 | tf_op jit(solution)/shard_map/ppermute | solution.py:469
  89.1 6.5 %collective-permute-start.23 = (bf16[64,1152]{1,0:T(8,128)(2,1)S(1)}, bf16[64,1152]{1,0:T(8,128)(2,1)S(1)}, u32[]{:S(2)}, u32[]{:S(2)}) collective-permute-start(bf16[64,1152]{1,0:T(8,128)(2,1)S(1)} %get-tuple-element.114.after), channel_id=1, source_target_pairs={{0,2},{1,3},{2,0},{3,1},{4,6},{5,7},{6,4},{7,5},{8,10},{9,11},{10,... | collective-permute-start | bytes 442376 | tf_op jit(solution)/shard_map/ppermute | solution.py:469
  89.7 6.1 %collective-permute-start.24 = (bf16[64,1152]{1,0:T(8,128)(2,1)S(1)}, bf16[64,1152]{1,0:T(8,128)(2,1)S(1)}, u32[]{:S(2)}, u32[]{:S(2)}) collective-permute-start(bf16[64,1152]{1,0:T(8,128)(2,1)S(1)} %get-tuple-element.115), channel_id=1, source_target_pairs={{0,4},{1,5},{2,6},{3,7},{4,0},{5,1},{6,2},{7,3},{8,12},{9,13},{10,... | collective-permute-start | bytes 442376 | tf_op jit(solution)/shard_map/ppermute | solution.py:469
  92.2 5.6 %collective-permute-start.26 = (bf16[64,896]{1,0:T(8,128)(2,1)S(1)}, bf16[64,896]{1,0:T(8,128)(2,1)S(1)}, u32[]{:S(2)}, u32[]{:S(2)}) collective-permute-start(bf16[64,896]{1,0:T(8,128)(2,1)S(1)} %get-tuple-element.117), channel_id=1, source_target_pairs={{0,2},{1,3},{2,0},{3,1},{4,6},{5,7},{6,4},{7,5},{8,10},{9,11},{10,... | collective-permute-start | bytes 344072 | tf_op jit(solution)/shard_map/ppermute | solution.py:469
  92.9 4.9 %collective-permute-start.27 = (bf16[64,896]{1,0:T(8,128)(2,1)S(1)}, bf16[64,896]{1,0:T(8,128)(2,1)S(1)}, u32[]{:S(2)}, u32[]{:S(2)}) collective-permute-start(bf16[64,896]{1,0:T(8,128)(2,1)S(1)} %get-tuple-element.118), channel_id=1, source_target_pairs={{0,4},{1,5},{2,6},{3,7},{4,0},{5,1},{6,2},{7,3},{8,12},{9,13},{10,... | collective-permute-start | bytes 344072 | tf_op jit(solution)/shard_map/ppermute | solution.py:469
  96.2 14.3 %collective-permute-start.25 = (bf16[128,1152]{1,0:T(8,128)(2,1)S(1)}, bf16[128,1152]{1,0:T(8,128)(2,1)S(1)}, u32[]{:S(2)}, u32[]{:S(2)}) collective-permute-start(bf16[128,1152]{1,0:T(8,128)(2,1)S(1)} %finish.2), channel_id=1, source_target_pairs={{0,8},{8,16},{16,24},{24,0},{1,9},{9,17},{17,25},{25,1},{2,10},{10... | collective-permute-start | bytes 884744 | tf_op jit(solution)/shard_map/ppermute | solution.py:474
  98.1 12.3 %collective-permute-start.28 = (bf16[128,896]{1,0:T(8,128)(2,1)S(1)}, bf16[128,896]{1,0:T(8,128)(2,1)S(1)}, u32[]{:S(2)}, u32[]{:S(2)}) collective-permute-start(bf16[128,896]{1,0:T(8,128)(2,1)S(1)} %finish.3), channel_id=1, source_target_pairs={{0,8},{8,16},{16,24},{24,0},{1,9},{9,17},{17,25},{25,1},{2,10},{10... | collective-permute-start | bytes 688136 | tf_op jit(solution)/shard_map/ppermute | solution.py:474

commit v8 on v6

--- a/solution.py
+++ b/solution.py
@@ -17,6 +17,8 @@
 STRIP = 16
 LANES = 128
 SCALE = HD ** (-0.5) * math.log2(math.e)
+SENT = (3, 1, 2)
+BACK = ((1, 3, 2), (3, 1, 2))
 CHUNKS = 2
 F32 = jnp.float32
 BF16 = jnp.bfloat16
@@ -409,11 +411,11 @@
     )(*[in_hbm(array) for array in arrays], after)
 
 
-def gather_kernel(after, *refs):
+def gather_kernel(order, after, *refs):
     blocks, out = refs[:-1], refs[-1]
     capacity = blocks[0].shape[0]
-    for at, block in enumerate(blocks):
-        out[at * capacity : (at + 1) * capacity, :] = block[...]
+    for slot, block in zip(order, blocks):
+        out[(slot - 1) * capacity : slot * capacity, :] = block[...]
 
 
 def up_kernel(w_up, after, *refs):
@@ -450,13 +452,14 @@
         out[...] = total.astype(BF16)
 
 
-def finish_kernel(start, second, weighting, *refs):
+def finish_kernel(start, order, second, weighting, *refs):
     blocks, parts, out = refs[: EXPERTS - 1], refs[EXPERTS - 1 : -1], refs[-1]
     cols = slice(start, start + out.shape[1])
     total = parts[0][:, cols].astype(F32)
     for part in parts[1:]:
         total = total + part[:, cols].astype(F32)
-    rows = jnp.concatenate([total.astype(BF16)] + [block[...] for block in blocks], 0)
+    blocks = [blocks[order.index(slot)][...] for slot in sorted(order)]
+    rows = jnp.concatenate([total.astype(BF16)] + blocks, 0)
     high, low = split(weighting[...])
     out[...] = (second[:, cols] + (dot(high, rows) + dot(low, rows))).astype(BF16)
 
@@ -724,14 +727,14 @@
     ]
     moved_rows = (EXPERTS - 1) * capacity
     arrived = pl.pallas_call(
-        gather_kernel,
+        functools.partial(gather_kernel, SENT),
         out_shape=shape((moved_rows, width), BF16),
         in_specs=[ANY] + [VMEM] * (EXPERTS - 1),
         out_specs=VMEM,
         compiler_params=params(4),
         cost_estimate=cost(0, 4 * moved_rows * width),
         name="gather",
-    )(stay_sums[-1], *moved)
+    )(stay_sums[-1], *[moved[slot - 1] for slot in SENT])
     hiddens = []
     after = arrived
     for turn in range(parts):
@@ -756,7 +759,7 @@
         after = joined[0]
         returned = between_experts(joined)
         finished = pl.pallas_call(
-            functools.partial(finish_kernel, chunk * half),
+            functools.partial(finish_kernel, chunk * half, BACK[chunk]),
             out_shape=shape((rows, half), BF16),
             in_specs=[VMEM] * (1 + EXPERTS + parts),
             out_specs=VMEM,
@@ -765,7 +768,7 @@
                 4 * rows * EXPERTS * capacity * half, 10 * rows * half
             ),
             name="finish",
-        )(second, weighting, *returned, *stay_sums)
+        )(second, weighting, *[returned[slot - 1] for slot in BACK[chunk]], *stay_sums)
         results.append(shifted(finished, "segment", 1))
     return jnp.concatenate(results, 1)[None]
 

time: 106 us -> 106 us (level)
  transfers between devices with their start and end apart: 28 -> 28, of which waited for: 16 -> 15; matrix products, arithmetic and copies ran while one was open for 0% -> 0% of each run, Pallas kernels for 31% -> 31%
where the time goes in v8:
time: 106 us
  Pallas kernels  47.2 us (45%)
  waiting for transfers between devices  29.7 us (28%)
  starting transfers between devices  28.2 us (27%)
    ppermute x26, starting transfers between devices, exchange(): return lax.ppermute(value, axis, [(at, at ^ mask) for at in range(count)])  24.9 us
    ppermute x26, waiting for transfers between devices, exchange(): return lax.ppermute(value, axis, [(at, at ^ mask) for at in range(count)])  20.8 us
    pallas_call x2, Pallas kernels, fetch(): pl.pallas_call(functools.partial(fetch_kernel, pieces, starts), out_shape...  11.6 us
    ppermute x2, waiting for transfers between devices, shifted(): lax.ppermute(value, axis, [(at, (at + steps) % count) for at in range(cou...  8.89 us
    pallas_call x4, Pallas kernels, lower(): pl.pallas_call(functools.partial(down_kernel, len(weights)), out_shape=(s...  8.5 us
    pallas_call x3, Pallas kernels, lift(): pl.pallas_call(up_kernel, out_shape=shape((count, units), BF16), in_specs...  8.16 us
    pallas_call x1, Pallas kernels, on_device(): pl.pallas_call(prepare_kernel, out_shape=(shape((rows, width), F32), shap...  4.59 us
    ppermute x2, starting transfers between devices, shifted(): lax.ppermute(value, axis, [(at, (at + steps) % count) for at in range(cou...  3.28 us
  transfers between devices with their start and end apart: 28, of which 15 were waited for; matrix products, arithmetic and copies ran while one was open for 0% of the time, Pallas kernels for 31%

profile of v8, /device:TPU:0, one launch (start us, length us, event | category | flops | bytes accessed | tf_op | source)
XLA Modules:
  0.0 106.3 jit_solution(6011841910155651767)
XLA Ops:
  0.0 0.5 collective-permute-start
  0.5 2.5 %collective-permute-start.2 = (bf16[128,2048]{1,0:T(8,128)(2,1)}, bf16[128,2048]{1,0:T(8,128)(2,1)S(1)}, u32[]{:S(2)}, u32[]{:S(2)}) collective-permute-start(bf16[128,2048]{1,0:T(8,128)(2,1)} %bitcast.25), channel_id=1, source_target_pairs={{0,2},{1,3},{2,0},{3,1},{4,6},{5,7},{6,4},{7,5},{8,10},{9,11},{10,... | collective-permute-start | bytes 1572872 | tf_op jit(solution)/shard_map/ppermute | solution.py:469
  2.9 1.5 %collective-permute-start.1 = (bf16[2048,128]{1,0:T(8,128)(2,1)}, bf16[2048,128]{1,0:T(8,128)(2,1)S(1)}, u32[]{:S(2)}, u32[]{:S(2)}) collective-permute-start(bf16[2048,128]{1,0:T(8,128)(2,1)} %bitcast.30), channel_id=1, source_target_pairs={{0,4},{1,5},{2,6},{3,7},{4,0},{5,1},{6,2},{7,3},{8,12},{9,13},{10,... | collective-permute-start | bytes 1572872 | tf_op jit(solution)/shard_map/ppermute | solution.py:469
  4.5 0.1 pad_add_fusion.after.place
  4.5 1.7 %norm.2 = (bf16[128,2048]{1,0:T(8,128)(2,1)S(1)}, bf16[128,2048]{1,0:T(8,128)(2,1)S(1)}) custom-call(f32[3,1,2048]{2,1,0:T(1,128)} %bitcast.33, s32[3]{0:T(128)S(1)} %pad_add_fusion.after.place, bf16[128,2048]{1,0:T(8,128)(2,1)} %bitcast.26, bf16[128,2048]{1,0:T(8,128)(2,1)S(1)} %collective-permute-done.refs_1_), custom_call_target="tpu_custom_call" | custom-call | flops 2097152 | bytes 1048576 | tf_op jit(solution)/shard_map/norm/pallas_call | solution.py:521
  6.3 8.4 %fetch.2 = (bf16[2048,3584]{1,0:T(8,128)(2,1)S(1)}, bf16[3584,1024]{1,0:T(8,128)(2,1)S(1)}, f32[3,1,2048]{2,1,0:T(1,128)S(1)}, bf16[2048,128]{1,0:T(8,128)(2,1)S...) custom-call(bf16[2048,3584]{1,0:T(8,128)(2,1)} %bitcast.23, ...), custom_call_target="tpu_custom_call" | custom-call | bytes 63259648 | tf_op jit(solution)/shard_map/fetch/pallas_call | solution.py:399
  14.7 1.1 %collective-permute-done.2.refs_0_ = bf16[128,2048]{1,0:T(8,128)(2,1)S(1)} collective-permute-done((bf16[128,2048]{1,0:T(8,128)(2,1)}, bf16[128,2048]{1,0:T(8,128)(2,1)S(1)}, u32[]{:S(2)}, u32[]{:S(2)}) %collective-permute-start.2) | collective-permute-done | bytes 524320 | tf_op jit(solution)/shard_map/ppermute | solution.py:469
  15.7 0.3 norm.3.first
  16.1 0.1 collective-permute-start.3
  16.2 1.1 collective-permute-done.1.w_other
  17.2 1.2 %project.1 = (bf16[2,512,128]{2,1,0:T(8,128)(2,1)S(1)}, bf16[2,256,128]{2,1,0:T(8,128)(2,1)S(1)}, bf16[2048,256]{1,0:T(8,128)(2,1)S(1)}) custom-call(s32[3]{0:T(128)S(1)} %pad_add_fusion.after.place, bf16[2048,128]{1,0:T(8,128)(2,1)S(1)} %get-tuple-element.65.w_own, bf16[2048,128]{1,0:T(8,128)(2,1)S(1)} %collective-permute-done.1.w_other, ...), custom_call_target="tpu_custom_call" | custom-call | flops 268435456 | bytes 4194304 | tf_op jit(solution)/shard_map/project/pallas_call | solution.py:544
  18.5 1.6 %collective-permute-start.4 = (bf16[2,256,128]{2,1,0:T(8,128)(2,1)S(1)}, bf16[2,256,128]{2,1,0:T(8,128)(2,1)S(1)}, u32[]{:S(2)}, u32[]{:S(2)}) collective-permute-start(bf16[2,256,128]{2,1,0:T(8,128)(2,1)S(1)} %get-tuple-element.71.refs_2_), channel_id=1, source_target_pairs={{0,4},{1,5},{2,6},{3,7},{4,0},{5,1},{6,2},{7,3},{8,12},{9,13},{10,... | collective-permute-start | bytes 393224 | tf_op jit(solution)/shard_map/ppermute | solution.py:469
  20.0 1.0 project_more.1
  21.0 0.6 collective-permute-start.5
  21.6 2.5 %near.1 = (f32[4,512,128]{2,1,0:T(8,128)S(1)}, f32[4,512,128]{2,1,0:T(8,128)S(1)}, f32[4,512,128]{2,1,0:T(8,128)S(1)}) custom-call(s32[3]{0:T(128)S(1)} %pad_add_fusion.after.place, bf16[2,512,128]{2,1,0:T(8,128)(2,1)S(1)} %get-tuple-element.67.refs_0_, bf16[2,512,128]{2,1,0:T(8,128)(2,1)S(1)} %get-tuple-element.70.refs_1_, ...), custom_call_target="tpu_custom_call" | custom-call | flops 536870912 | bytes 4194304 | tf_op jit(solution)/shard_map/near/pallas_call | solution.py:571
  24.1 2.2 %collective-permute-done.5.refs_6_ = bf16[2,256,128]{2,1,0:T(8,128)(2,1)S(1)} collective-permute-done((bf16[2,256,128]{2,1,0:T(8,128)(2,1)S(1)}, bf16[2,256,128]{2,1,0:T(8,128)(2,1)S(1)}, u32[]{:S(2)}, u32[]{:S(2)}) %collective-permute-start.5) | collective-permute-done | bytes 131104 | tf_op jit(solution)/shard_map/ppermute | solution.py:469
  26.3 0.6 far.3
  26.9 1.7 %collective-permute-start.7 = (bf16[128,512]{1,0:T(8,128)(2,1)S(1)}, bf16[128,512]{1,0:T(8,128)(2,1)S(1)}, u32[]{:S(2)}, u32[]{:S(2)}) collective-permute-start(bf16[128,512]{1,0:T(8,128)(2,1)S(1)} %get-tuple-element.78), channel_id=1, source_target_pairs={{0,2},{1,3},{2,0},{3,1},{4,6},{5,7},{6,4},{7,5},{8,10},{9,11},{10,... | collective-permute-start | bytes 393224 | tf_op jit(solution)/shard_map/ppermute | solution.py:469
  28.6 0.6 far.2
  29.3 0.6 collective-permute-start.6
  29.8 2.7 %collective-permute-done.7.refs_2_ = bf16[128,512]{1,0:T(8,128)(2,1)S(1)} collective-permute-done((bf16[128,512]{1,0:T(8,128)(2,1)S(1)}, bf16[128,512]{1,0:T(8,128)(2,1)S(1)}, u32[]{:S(2)}, u32[]{:S(2)}) %collective-permute-start.7) | collective-permute-done | bytes 131104 | tf_op jit(solution)/shard_map/ppermute | solution.py:469
  32.5 1.9 %collective-permute-done.8.refs_3_ = bf16[128,512]{1,0:T(8,128)(2,1)S(1)} collective-permute-done((bf16[128,512]{1,0:T(8,128)(2,1)S(1)}, bf16[128,512]{1,0:T(8,128)(2,1)S(1)}, u32[]{:S(2)}, u32[]{:S(2)}) %collective-permute-start.8) | collective-permute-done | bytes 131104 | tf_op jit(solution)/shard_map/ppermute | solution.py:469
  34.4 4.6 %prepare.1 = (f32[128,2048]{1,0:T(8,128)S(1)}, f32[128,2048]{1,0:T(8,128)S(1)}, f32[128,2048]{1,0:T(8,128)S(1)}, f32[256,2048]{1,0:T(8,128)S(1)}, f32[16,2048]{1...) custom-call(s32[3]{0:T(128)S(1)} %pad_add_fusion.after.place, ...), custom_call_target="tpu_custom_call" | custom-call | flops 671088640 | bytes 7864320 | tf_op jit(solution)/shard_map/prepare/pallas_call | solution.py:597
  39.0 0.3 collective-permute-start.9
  39.3 0.4 couple.1.coef.after
  39.7 0.6 collective-permute-done.9.other.beside
  40.3 0.6 pair.1
  40.9 3.6 %collective-permute-start.12 = (bf16[16,2176]{1,0:T(8,128)(2,1)S(1)}, bf16[16,2176]{1,0:T(8,128)(2,1)S(1)}, u32[]{:S(2)}, u32[]{:S(2)}) collective-permute-start(bf16[16,2176]{1,0:T(8,128)(2,1)S(1)} %pair.1), channel_id=1, source_target_pairs={{0,6},{1,7},{2,4},{3,5},{4,2},{5,3},{6,0},{7,1},{8,14},{9,15},{10,... | collective-permute-start | bytes 208904 | tf_op jit(solution)/shard_map/ppermute | solution.py:469
  44.5 0.6 collective-permute-start.10
  45.2 1.7 %within.1 = (f32[128,2048]{1,0:T(8,128)S(1)}, f32[128,2048]{1,0:T(8,128)S(1)}) custom-call(f32[128,128]{1,0:T(8,128)S(1)} %couple.1.coef.after, f32[128,2048]{1,0:T(8,128)S(1)} %get-tuple-element.82.base, f32[128,2048]{1,0:T(8,128)S(1)} %get-tuple-element.83.keep, f32[128,2048]{1,0:T(8,128)S(1)} %get-tuple-element.84.drive), custom_call_target="tpu_custom_call" | custom-call | flops 10485760 | bytes 5242880 | tf_op jit(solution)/shard_map/within/pallas_call | solution.py:651
  46.9 0.3 collective-permute-done.12.refs_2_
  47.2 1.6 %collective-permute-done.11.refs_1_ = bf16[16,2176]{1,0:T(8,128)(2,1)S(1)} collective-permute-done((bf16[16,2176]{1,0:T(8,128)(2,1)S(1)}, bf16[16,2176]{1,0:T(8,128)(2,1)S(1)}, u32[]{:S(2)}, u32[]{:S(2)}) %collective-permute-start.11) | collective-permute-done | bytes 69664 | tf_op jit(solution)/shard_map/ppermute | solution.py:469
  48.8 2.8 %route.1 = (f32[128,2048]{1,0:T(8,128)S(1)}, f32[128,256]{1,0:T(8,128)S(1)}, bf16[64,2048]{1,0:T(8,128)(2,1)S(1)}, bf16[64,2048]{1,0:T(8,128)(2,1)S(1)}, bf16[64...) custom-call(s32[3]{0:T(128)S(1)} %pad_add_fusion.after.place, f32[128,2048]{1,0:T(8,128)S(1)} %get-tuple-element.85.before, ...), custom_call_target="tpu_custom_call" | custom-call | flops 671088640 | bytes 7864320 | tf_op jit(solution)/shard_map/route/pallas_call | solution.py:660
  51.7 1.9 %collective-permute-start.15 = (bf16[64,2048]{1,0:T(8,128)(2,1)S(1)}, bf16[64,2048]{1,0:T(8,128)(2,1)S(1)}, u32[]{:S(2)}, u32[]{:S(2)}) collective-permute-start(bf16[64,2048]{1,0:T(8,128)(2,1)S(1)} %get-tuple-element.97), channel_id=1, source_target_pairs={{0,6},{1,7},{2,4},{3,5},{4,2},{5,3},{6,0},{7,1},{8,14},{9,15},{10,... | collective-permute-start | bytes 786440 | tf_op jit(solution)/shard_map/ppermute | solution.py:469
  53.7 1.6 %collective-permute-start.16 = (bf16[64,2048]{1,0:T(8,128)(2,1)S(1)}, bf16[64,2048]{1,0:T(8,128)(2,1)S(1)}, u32[]{:S(2)}, u32[]{:S(2)}) collective-permute-start(bf16[64,2048]{1,0:T(8,128)(2,1)S(1)} %get-tuple-element.98), channel_id=1, source_target_pairs={{0,2},{1,3},{2,0},{3,1},{4,6},{5,7},{6,4},{7,5},{8,10},{9,11},{10,... | collective-permute-start | bytes 786440 | tf_op jit(solution)/shard_map/ppermute | solution.py:469
  55.3 2.1 %up.3.refs_1_.hidden = bf16[128,3584]{1,0:T(8,128)(2,1)S(1)} custom-call(bf16[2048,3584]{1,0:T(8,128)(2,1)S(1)} %get-tuple-element.69.after.w_up, bf16[64,2048]{1,0:T(8,128)(2,1)S(1)} %get-tuple-element.94.after.refs_0_, bf16[64,2048]{1,0:T(8,128)(2,1)S(1)} %get-tuple-element.94.after.refs_0_, bf16[64,2048]{1,0:T(8,128)(2,1)S(1)} %collective-permute-done.13.refs_1_), custom_call_target="tpu_custom_call" | custom-call | flops 1879048192 | bytes 14680064 | tf_op jit(solution)/shard_map/up/pallas_call | solution.py:693
  57.4 3.2 %fetch.3.refs_1_.refs_0_ = bf16[3584,1024]{1,0:T(8,128)(2,1)S(1)} custom-call(bf16[3584,2048]{1,0:T(8,128)(2,1)} %bitcast.22, bf16[128,3584]{1,0:T(8,128)(2,1)S(1)} %up.3.refs_1_.hidden), custom_call_target="tpu_custom_call" | custom-call | tf_op jit(solution)/shard_map/fetch/pallas_call | solution.py:399
  60.6 2.1 %down.4 = (bf16[64,2048]{1,0:T(8,128)(2,1)S(1)}, bf16[64,2048]{1,0:T(8,128)(2,1)S(1)}) custom-call(bf16[128,3584]{1,0:T(8,128)(2,1)S(1)} %up.3.refs_1_.hidden, bf16[64,2048]{1,0:T(8,128)(2,1)S(1)} %get-tuple-element.94.after.refs_0_, bf16[3584,1024]{1,0:T(8,128)(2,1)S(1)} %get-tuple-element.95.refs_0_, bf16[3584,1024]{1,0:T(8,128)(2,1)S(1)} %fetch.3.refs_1_.refs_0_), custom_call_target="tpu_custom_call" | custom-call | flops 1879048192 | bytes 14680064 | tf_op jit(solution)/shard_map/down/pallas_call | solution.py:706
  62.8 4.8 %collective-permute-done.16.refs_1_ = bf16[64,2048]{1,0:T(8,128)(2,1)S(1)} collective-permute-done((bf16[64,2048]{1,0:T(8,128)(2,1)S(1)}, bf16[64,2048]{1,0:T(8,128)(2,1)S(1)}, u32[]{:S(2)}, u32[]{:S(2)}) %collective-permute-start.16) | collective-permute-done | bytes 262176 | tf_op jit(solution)/shard_map/ppermute | solution.py:469
  67.7 3.0 %up.4.after.hidden = bf16[192,3584]{1,0:T(8,128)(2,1)S(1)} custom-call(bf16[2048,3584]{1,0:T(8,128)(2,1)S(1)} %get-tuple-element.69.after.w_up, bf16[192,2048]{1,0:T(8,128)(2,1)S(1)} %gather.1.after.refs_0_, bf16[192,2048]{1,0:T(8,128)(2,1)S(1)} %gather.1.after.refs_0_), custom_call_target="tpu_custom_call" | custom-call | flops 2818572288 | bytes 14680064 | tf_op jit(solution)/shard_map/up/pallas_call | solution.py:693
  70.8 3.0 %up.5.hidden.after = bf16[192,3584]{1,0:T(8,128)(2,1)S(1)} custom-call(bf16[2048,3584]{1,0:T(8,128)(2,1)S(1)} %get-tuple-element.69.after.w_up, bf16[192,3584]{1,0:T(8,128)(2,1)S(1)} %up.4.after.hidden, bf16[192,2048]{1,0:T(8,128)(2,1)S(1)} %collective-permute-done.18.refs_0_), custom_call_target="tpu_custom_call" | custom-call | flops 2818572288 | bytes 14680064 | tf_op jit(solution)/shard_map/up/pallas_call | solution.py:693
  73.8 3.0 %down.5.after = bf16[192,2048]{1,0:T(8,128)(2,1)S(1)} custom-call(bf16[192,3584]{1,0:T(8,128)(2,1)S(1)} %up.5.hidden.after, bf16[192,3584]{1,0:T(8,128)(2,1)S(1)} %up.5.hidden.after, bf16[3584,1024]{1,0:T(8,128)(2,1)S(1)} %get-tuple-element.95.refs_0_, bf16[3584,1024]{1,0:T(8,128)(2,1)S(1)} %fetch.3.refs_1_.refs_0_), custom_call_target="tpu_custom_call" | custom-call | flops 2818572288 | bytes 14680064 | tf_op jit(solution)/shard_map/down/pallas_call | solution.py:706
  76.8 0.6 collective-permute-start.19
  77.4 1.8 %down.6.own = bf16[192,1024]{1,0:T(8,128)(2,1)S(1)} custom-call(bf16[192,3584]{1,0:T(8,128)(2,1)S(1)} %up.4.after.hidden, bf16[192,2048]{1,0:T(8,128)(2,1)S(1)} %down.5.after, bf16[3584,1024]{1,0:T(8,128)(2,1)S(1)} %get-tuple-element.95.refs_0_), custom_call_target="tpu_custom_call" | custom-call | flops 1409286144 | bytes 7340032 | tf_op jit(solution)/shard_map/down/pallas_call | solution.py:706
  79.2 0.1 collective-permute-done.19.refs_0_
  79.3 0.1 join.2
  79.4 1.4 %collective-permute-start.21 = (bf16[64,1024]{1,0:T(8,128)(2,1)S(1)}, bf16[64,1024]{1,0:T(8,128)(2,1)S(1)}, u32[]{:S(2)}, u32[]{:S(2)}) collective-permute-start(bf16[64,1024]{1,0:T(8,128)(2,1)S(1)} %get-tuple-element.101), channel_id=1, source_target_pairs={{0,6},{1,7},{2,4},{3,5},{4,2},{5,3},{6,0},{7,1},{8,14},{9,15},{10,... | collective-permute-start | bytes 393224 | tf_op jit(solution)/shard_map/ppermute | solution.py:469
  80.7 1.2 %collective-permute-start.22 = (bf16[64,1024]{1,0:T(8,128)(2,1)S(1)}, bf16[64,1024]{1,0:T(8,128)(2,1)S(1)}, u32[]{:S(2)}, u32[]{:S(2)}) collective-permute-start(bf16[64,1024]{1,0:T(8,128)(2,1)S(1)} %get-tuple-element.102), channel_id=1, source_target_pairs={{0,4},{1,5},{2,6},{3,7},{4,0},{5,1},{6,2},{7,3},{8,12},{9,13},{10,... | collective-permute-start | bytes 393224 | tf_op jit(solution)/shard_map/ppermute | solution.py:469
  81.9 1.0 collective-permute-start.20
  82.9 1.6 %down.7.own = bf16[192,1024]{1,0:T(8,128)(2,1)S(1)} custom-call(bf16[192,3584]{1,0:T(8,128)(2,1)S(1)} %up.4.after.hidden, bf16[64,1024]{1,0:T(8,128)(2,1)S(1)} %get-tuple-element.100.after, bf16[3584,1024]{1,0:T(8,128)(2,1)S(1)} %fetch.3.refs_1_.refs_0_), custom_call_target="tpu_custom_call" | custom-call | flops 393216 | bytes 2048 | tf_op jit(solution)/shard_map/down/pallas_call | solution.py:706
  84.5 0.1 join.3
  84.7 1.3 %collective-permute-start.24 = (bf16[64,1024]{1,0:T(8,128)(2,1)S(1)}, bf16[64,1024]{1,0:T(8,128)(2,1)S(1)}, u32[]{:S(2)}, u32[]{:S(2)}) collective-permute-start(bf16[64,1024]{1,0:T(8,128)(2,1)S(1)} %get-tuple-element.104), channel_id=1, source_target_pairs={{0,6},{1,7},{2,4},{3,5},{4,2},{5,3},{6,0},{7,1},{8,14},{9,15},{10,... | collective-permute-start | bytes 393224 | tf_op jit(solution)/shard_map/ppermute | solution.py:469
  86.0 1.6 %collective-permute-start.25 = (bf16[64,1024]{1,0:T(8,128)(2,1)S(1)}, bf16[64,1024]{1,0:T(8,128)(2,1)S(1)}, u32[]{:S(2)}, u32[]{:S(2)}) collective-permute-start(bf16[64,1024]{1,0:T(8,128)(2,1)S(1)} %get-tuple-element.105), channel_id=1, source_target_pairs={{0,2},{1,3},{2,0},{3,1},{4,6},{5,7},{6,4},{7,5},{8,10},{9,11},{10,... | collective-permute-start | bytes 393224 | tf_op jit(solution)/shard_map/ppermute | solution.py:469
  87.6 0.6 collective-permute-start.26
  88.2 1.4 %collective-permute-done.22.refs_2_ = bf16[64,1024]{1,0:T(8,128)(2,1)S(1)} collective-permute-done((bf16[64,1024]{1,0:T(8,128)(2,1)S(1)}, bf16[64,1024]{1,0:T(8,128)(2,1)S(1)}, u32[]{:S(2)}, u32[]{:S(2)}) %collective-permute-start.22) | collective-permute-done | bytes 131104 | tf_op jit(solution)/shard_map/ppermute | solution.py:469
  89.6 0.3 finish.2
  89.9 1.6 %collective-permute-start.23 = (bf16[128,1024]{1,0:T(8,128)(2,1)S(1)}, bf16[128,1024]{1,0:T(8,128)(2,1)S(1)}, u32[]{:S(2)}, u32[]{:S(2)}) collective-permute-start(bf16[128,1024]{1,0:T(8,128)(2,1)S(1)} %finish.2), channel_id=1, source_target_pairs={{0,8},{8,16},{16,24},{24,0},{1,9},{9,17},{17,25},{25,1},{2,10},{10... | collective-permute-start | bytes 786440 | tf_op jit(solution)/shard_map/ppermute | solution.py:474
  91.5 0.8 collective-permute-done.24.refs_0_
  92.4 2.2 %collective-permute-done.25.refs_1_ = bf16[64,1024]{1,0:T(8,128)(2,1)S(1)} collective-permute-done((bf16[64,1024]{1,0:T(8,128)(2,1)S(1)}, bf16[64,1024]{1,0:T(8,128)(2,1)S(1)}, u32[]{:S(2)}, u32[]{:S(2)}) %collective-permute-start.25) | collective-permute-done | bytes 131104 | tf_op jit(solution)/shard_map/ppermute | solution.py:469
  94.6 0.3 finish.3
  94.9 1.6 %collective-permute-start.27 = (bf16[128,1024]{1,0:T(8,128)(2,1)S(1)}, bf16[128,1024]{1,0:T(8,128)(2,1)S(1)}, u32[]{:S(2)}, u32[]{:S(2)}) collective-permute-start(bf16[128,1024]{1,0:T(8,128)(2,1)S(1)} %finish.3), channel_id=1, source_target_pairs={{0,8},{8,16},{16,24},{24,0},{1,9},{9,17},{17,25},{25,1},{2,10},{10... | collective-permute-start | bytes 786440 | tf_op jit(solution)/shard_map/ppermute | solution.py:474
  96.6 3.8 %collective-permute-done.23 = bf16[128,1024]{1,0:T(8,128)(2,1)S(1)} collective-permute-done((bf16[128,1024]{1,0:T(8,128)(2,1)S(1)}, bf16[128,1024]{1,0:T(8,128)(2,1)S(1)}, u32[]{:S(2)}, u32[]{:S(2)}) %collective-permute-start.23) | collective-permute-done | bytes 262176 | tf_op jit(solution)/shard_map/ppermute | solution.py:474
  100.3 5.1 %collective-permute-done.27 = bf16[128,1024]{1,0:T(8,128)(2,1)S(1)} collective-permute-done((bf16[128,1024]{1,0:T(8,128)(2,1)S(1)}, bf16[128,1024]{1,0:T(8,128)(2,1)S(1)}, u32[]{:S(2)}, u32[]{:S(2)}) %collective-permute-start.27) | collective-permute-done | bytes 262176 | tf_op jit(solution)/shard_map/ppermute | solution.py:474
  105.5 0.8 maximum_bitcast_fusion
  (20 shorter events, 0.3 us)
Async XLA Ops:
  0.0 4.5 %collective-permute-start = (bf16[128,2048]{1,0:T(8,128)(2,1)}, bf16[128,2048]{1,0:T(8,128)(2,1)S(1)}, u32[]{:S(2)}, u32[]{:S(2)}) collective-permute-start(bf16[128,2048]{1,0:T(8,128)(2,1)} %bitcast.24), channel_id=1, source_target_pairs={{0,1},{1,0},{2,3},{3,2},{4,5},{5,4},{6,7},{7,6},{8,9},{9,8},{10,11... | collective-permute-start | bytes 1572872 | tf_op jit(solution)/shard_map/ppermute | solution.py:469
  0.5 15.3 %collective-permute-start.2 = (bf16[128,2048]{1,0:T(8,128)(2,1)}, bf16[128,2048]{1,0:T(8,128)(2,1)S(1)}, u32[]{:S(2)}, u32[]{:S(2)}) collective-permute-start(bf16[128,2048]{1,0:T(8,128)(2,1)} %bitcast.25), channel_id=1, source_target_pairs={{0,2},{1,3},{2,0},{3,1},{4,6},{5,7},{6,4},{7,5},{8,10},{9,11},{10,... | collective-permute-start | bytes 1572872 | tf_op jit(solution)/shard_map/ppermute | solution.py:469
  2.9 14.3 %collective-permute-start.1 = (bf16[2048,128]{1,0:T(8,128)(2,1)}, bf16[2048,128]{1,0:T(8,128)(2,1)S(1)}, u32[]{:S(2)}, u32[]{:S(2)}) collective-permute-start(bf16[2048,128]{1,0:T(8,128)(2,1)} %bitcast.30), channel_id=1, source_target_pairs={{0,4},{1,5},{2,6},{3,7},{4,0},{5,1},{6,2},{7,3},{8,12},{9,13},{10,... | collective-permute-start | bytes 1572872 | tf_op jit(solution)/shard_map/ppermute | solution.py:469
  16.1 4.0 %collective-permute-start.3 = (bf16[128,2048]{1,0:T(8,128)(2,1)S(1)}, bf16[128,2048]{1,0:T(8,128)(2,1)S(1)}, u32[]{:S(2)}, u32[]{:S(2)}) collective-permute-start(bf16[128,2048]{1,0:T(8,128)(2,1)S(1)} %norm.3.first), channel_id=1, source_target_pairs={{0,1},{1,0},{2,3},{3,2},{4,5},{5,4},{6,7},{7,6},{8,9},{9,8},{10,11... | collective-permute-start | bytes 1572872 | tf_op jit(solution)/shard_map/ppermute | solution.py:469
  18.5 5.6 %collective-permute-start.4 = (bf16[2,256,128]{2,1,0:T(8,128)(2,1)S(1)}, bf16[2,256,128]{2,1,0:T(8,128)(2,1)S(1)}, u32[]{:S(2)}, u32[]{:S(2)}) collective-permute-start(bf16[2,256,128]{2,1,0:T(8,128)(2,1)S(1)} %get-tuple-element.71.refs_2_), channel_id=1, source_target_pairs={{0,4},{1,5},{2,6},{3,7},{4,0},{5,1},{6,2},{7,3},{8,12},{9,13},{10,... | collective-permute-start | bytes 393224 | tf_op jit(solution)/shard_map/ppermute | solution.py:469
  21.0 5.3 %collective-permute-start.5 = (bf16[2,256,128]{2,1,0:T(8,128)(2,1)S(1)}, bf16[2,256,128]{2,1,0:T(8,128)(2,1)S(1)}, u32[]{:S(2)}, u32[]{:S(2)}) collective-permute-start(bf16[2,256,128]{2,1,0:T(8,128)(2,1)S(1)} %get-tuple-element.72.refs_3_), channel_id=1, source_target_pairs={{0,4},{1,5},{2,6},{3,7},{4,0},{5,1},{6,2},{7,3},{8,12},{9,13},{10,... | collective-permute-start | bytes 393224 | tf_op jit(solution)/shard_map/ppermute | solution.py:469
  26.9 5.6 %collective-permute-start.7 = (bf16[128,512]{1,0:T(8,128)(2,1)S(1)}, bf16[128,512]{1,0:T(8,128)(2,1)S(1)}, u32[]{:S(2)}, u32[]{:S(2)}) collective-permute-start(bf16[128,512]{1,0:T(8,128)(2,1)S(1)} %get-tuple-element.78), channel_id=1, source_target_pairs={{0,2},{1,3},{2,0},{3,1},{4,6},{5,7},{6,4},{7,5},{8,10},{9,11},{10,... | collective-permute-start | bytes 393224 | tf_op jit(solution)/shard_map/ppermute | solution.py:469
  28.6 5.8 %collective-permute-start.8 = (bf16[128,512]{1,0:T(8,128)(2,1)S(1)}, bf16[128,512]{1,0:T(8,128)(2,1)S(1)}, u32[]{:S(2)}, u32[]{:S(2)}) collective-permute-start(bf16[128,512]{1,0:T(8,128)(2,1)S(1)} %get-tuple-element.79), channel_id=1, source_target_pairs={{0,3},{1,2},{2,1},{3,0},{4,7},{5,6},{6,5},{7,4},{8,11},{9,10},{10,... | collective-permute-start | bytes 393224 | tf_op jit(solution)/shard_map/ppermute | solution.py:469
  29.3 5.2 %collective-permute-start.6 = (bf16[128,512]{1,0:T(8,128)(2,1)S(1)}, bf16[128,512]{1,0:T(8,128)(2,1)S(1)}, u32[]{:S(2)}, u32[]{:S(2)}) collective-permute-start(bf16[128,512]{1,0:T(8,128)(2,1)S(1)} %get-tuple-element.77), channel_id=1, source_target_pairs={{0,1},{1,0},{2,3},{3,2},{4,5},{5,4},{6,7},{7,6},{8,9},{9,8},{10,11... | collective-permute-start | bytes 393224 | tf_op jit(solution)/shard_map/ppermute | solution.py:469
  39.0 1.3 %collective-permute-start.9 = (bf16[16,2176]{1,0:T(8,128)(2,1)S(1)}, bf16[16,2176]{1,0:T(8,128)(2,1)S(1)}, u32[]{:S(2)}, u32[]{:S(2)}) collective-permute-start(bf16[16,2176]{1,0:T(8,128)(2,1)S(1)} %get-tuple-element.91.own), channel_id=1, source_target_pairs={{0,1},{1,0},{2,3},{3,2},{4,5},{5,4},{6,7},{7,6},{8,9},{9,8},{10,11... | collective-permute-start | bytes 208904 | tf_op jit(solution)/shard_map/ppermute | solution.py:469
  40.9 6.3 %collective-permute-start.12 = (bf16[16,2176]{1,0:T(8,128)(2,1)S(1)}, bf16[16,2176]{1,0:T(8,128)(2,1)S(1)}, u32[]{:S(2)}, u32[]{:S(2)}) collective-permute-start(bf16[16,2176]{1,0:T(8,128)(2,1)S(1)} %pair.1), channel_id=1, source_target_pairs={{0,6},{1,7},{2,4},{3,5},{4,2},{5,3},{6,0},{7,1},{8,14},{9,15},{10,... | collective-permute-start | bytes 208904 | tf_op jit(solution)/shard_map/ppermute | solution.py:469
  44.5 4.3 %collective-permute-start.11 = (bf16[16,2176]{1,0:T(8,128)(2,1)S(1)}, bf16[16,2176]{1,0:T(8,128)(2,1)S(1)}, u32[]{:S(2)}, u32[]{:S(2)}) collective-permute-start(bf16[16,2176]{1,0:T(8,128)(2,1)S(1)} %pair.1), channel_id=1, source_target_pairs={{0,4},{1,5},{2,6},{3,7},{4,0},{5,1},{6,2},{7,3},{8,12},{9,13},{10,... | collective-permute-start | bytes 208904 | tf_op jit(solution)/shard_map/ppermute | solution.py:469
  44.5 4.3 %collective-permute-start.10 = (bf16[16,2176]{1,0:T(8,128)(2,1)S(1)}, bf16[16,2176]{1,0:T(8,128)(2,1)S(1)}, u32[]{:S(2)}, u32[]{:S(2)}) collective-permute-start(bf16[16,2176]{1,0:T(8,128)(2,1)S(1)} %pair.1), channel_id=1, source_target_pairs={{0,2},{1,3},{2,0},{3,1},{4,6},{5,7},{6,4},{7,5},{8,10},{9,11},{10,... | collective-permute-start | bytes 208904 | tf_op jit(solution)/shard_map/ppermute | solution.py:469
  51.6 3.6 %collective-permute-start.13 = (bf16[64,2048]{1,0:T(8,128)(2,1)S(1)}, bf16[64,2048]{1,0:T(8,128)(2,1)S(1)}, u32[]{:S(2)}, u32[]{:S(2)}) collective-permute-start(bf16[64,2048]{1,0:T(8,128)(2,1)S(1)} %get-tuple-element.94.after.refs_0_), channel_id=1, source_target_pairs={{0,1},{1,0},{2,3},{3,2},{4,5},{5,4},{6,7},{7,6},{8,9},{9,8},{10,11... | collective-permute-start | bytes 786440 | tf_op jit(solution)/shard_map/ppermute | solution.py:469
  51.7 11.0 %collective-permute-start.15 = (bf16[64,2048]{1,0:T(8,128)(2,1)S(1)}, bf16[64,2048]{1,0:T(8,128)(2,1)S(1)}, u32[]{:S(2)}, u32[]{:S(2)}) collective-permute-start(bf16[64,2048]{1,0:T(8,128)(2,1)S(1)} %get-tuple-element.97), channel_id=1, source_target_pairs={{0,6},{1,7},{2,4},{3,5},{4,2},{5,3},{6,0},{7,1},{8,14},{9,15},{10,... | collective-permute-start | bytes 786440 | tf_op jit(solution)/shard_map/ppermute | solution.py:469
  53.7 13.9 %collective-permute-start.16 = (bf16[64,2048]{1,0:T(8,128)(2,1)S(1)}, bf16[64,2048]{1,0:T(8,128)(2,1)S(1)}, u32[]{:S(2)}, u32[]{:S(2)}) collective-permute-start(bf16[64,2048]{1,0:T(8,128)(2,1)S(1)} %get-tuple-element.98), channel_id=1, source_target_pairs={{0,2},{1,3},{2,0},{3,1},{4,6},{5,7},{6,4},{7,5},{8,10},{9,11},{10,... | collective-permute-start | bytes 786440 | tf_op jit(solution)/shard_map/ppermute | solution.py:469
  55.3 12.3 %collective-permute-start.17 = (bf16[64,2048]{1,0:T(8,128)(2,1)S(1)}, bf16[64,2048]{1,0:T(8,128)(2,1)S(1)}, u32[]{:S(2)}, u32[]{:S(2)}) collective-permute-start(bf16[64,2048]{1,0:T(8,128)(2,1)S(1)} %get-tuple-element.99), channel_id=1, source_target_pairs={{0,4},{1,5},{2,6},{3,7},{4,0},{5,1},{6,2},{7,3},{8,12},{9,13},{10,... | collective-permute-start | bytes 786440 | tf_op jit(solution)/shard_map/ppermute | solution.py:469
  62.7 4.9 %collective-permute-start.14 = (bf16[64,2048]{1,0:T(8,128)(2,1)S(1)}, bf16[64,2048]{1,0:T(8,128)(2,1)S(1)}, u32[]{:S(2)}, u32[]{:S(2)}) collective-permute-start(bf16[64,2048]{1,0:T(8,128)(2,1)S(1)} %get-tuple-element.96), channel_id=1, source_target_pairs={{0,1},{1,0},{2,3},{3,2},{4,5},{5,4},{6,7},{7,6},{8,9},{9,8},{10,11... | collective-permute-start | bytes 786440 | tf_op jit(solution)/shard_map/ppermute | solution.py:469
  67.6 3.1 %collective-permute-start.18 = (bf16[192,2048]{1,0:T(8,128)(2,1)S(1)}, bf16[192,2048]{1,0:T(8,128)(2,1)S(1)}, u32[]{:S(2)}, u32[]{:S(2)}) collective-permute-start(bf16[192,2048]{1,0:T(8,128)(2,1)S(1)} %gather.1.after.refs_0_), channel_id=1, source_target_pairs={{0,1},{1,0},{2,3},{3,2},{4,5},{5,4},{6,7},{7,6},{8,9},{9,8},{10,11... | collective-permute-start | bytes 2359304 | tf_op jit(solution)/shard_map/ppermute | solution.py:469
  76.8 2.5 %collective-permute-start.19 = (bf16[192,2048]{1,0:T(8,128)(2,1)S(1)}, bf16[192,2048]{1,0:T(8,128)(2,1)S(1)}, u32[]{:S(2)}, u32[]{:S(2)}) collective-permute-start(bf16[192,2048]{1,0:T(8,128)(2,1)S(1)} %down.5.after), channel_id=1, source_target_pairs={{0,1},{1,0},{2,3},{3,2},{4,5},{5,4},{6,7},{7,6},{8,9},{9,8},{10,11... | collective-permute-start | bytes 2359304 | tf_op jit(solution)/shard_map/ppermute | solution.py:469
  79.4 8.2 %collective-permute-start.21 = (bf16[64,1024]{1,0:T(8,128)(2,1)S(1)}, bf16[64,1024]{1,0:T(8,128)(2,1)S(1)}, u32[]{:S(2)}, u32[]{:S(2)}) collective-permute-start(bf16[64,1024]{1,0:T(8,128)(2,1)S(1)} %get-tuple-element.101), channel_id=1, source_target_pairs={{0,6},{1,7},{2,4},{3,5},{4,2},{5,3},{6,0},{7,1},{8,14},{9,15},{10,... | collective-permute-start | bytes 393224 | tf_op jit(solution)/shard_map/ppermute | solution.py:469
  80.7 8.8 %collective-permute-start.22 = (bf16[64,1024]{1,0:T(8,128)(2,1)S(1)}, bf16[64,1024]{1,0:T(8,128)(2,1)S(1)}, u32[]{:S(2)}, u32[]{:S(2)}) collective-permute-start(bf16[64,1024]{1,0:T(8,128)(2,1)S(1)} %get-tuple-element.102), channel_id=1, source_target_pairs={{0,4},{1,5},{2,6},{3,7},{4,0},{5,1},{6,2},{7,3},{8,12},{9,13},{10,... | collective-permute-start | bytes 393224 | tf_op jit(solution)/shard_map/ppermute | solution.py:469
  81.9 7.6 %collective-permute-start.20 = (bf16[64,1024]{1,0:T(8,128)(2,1)S(1)}, bf16[64,1024]{1,0:T(8,128)(2,1)S(1)}, u32[]{:S(2)}, u32[]{:S(2)}) collective-permute-start(bf16[64,1024]{1,0:T(8,128)(2,1)S(1)} %get-tuple-element.100.after), channel_id=1, source_target_pairs={{0,2},{1,3},{2,0},{3,1},{4,6},{5,7},{6,4},{7,5},{8,10},{9,11},{10,... | collective-permute-start | bytes 393224 | tf_op jit(solution)/shard_map/ppermute | solution.py:469
  84.7 7.7 %collective-permute-start.24 = (bf16[64,1024]{1,0:T(8,128)(2,1)S(1)}, bf16[64,1024]{1,0:T(8,128)(2,1)S(1)}, u32[]{:S(2)}, u32[]{:S(2)}) collective-permute-start(bf16[64,1024]{1,0:T(8,128)(2,1)S(1)} %get-tuple-element.104), channel_id=1, source_target_pairs={{0,6},{1,7},{2,4},{3,5},{4,2},{5,3},{6,0},{7,1},{8,14},{9,15},{10,... | collective-permute-start | bytes 393224 | tf_op jit(solution)/shard_map/ppermute | solution.py:469
  86.0 8.6 %collective-permute-start.25 = (bf16[64,1024]{1,0:T(8,128)(2,1)S(1)}, bf16[64,1024]{1,0:T(8,128)(2,1)S(1)}, u32[]{:S(2)}, u32[]{:S(2)}) collective-permute-start(bf16[64,1024]{1,0:T(8,128)(2,1)S(1)} %get-tuple-element.105), channel_id=1, source_target_pairs={{0,2},{1,3},{2,0},{3,1},{4,6},{5,7},{6,4},{7,5},{8,10},{9,11},{10,... | collective-permute-start | bytes 393224 | tf_op jit(solution)/shard_map/ppermute | solution.py:469
  87.6 7.0 %collective-permute-start.26 = (bf16[64,1024]{1,0:T(8,128)(2,1)S(1)}, bf16[64,1024]{1,0:T(8,128)(2,1)S(1)}, u32[]{:S(2)}, u32[]{:S(2)}) collective-permute-start(bf16[64,1024]{1,0:T(8,128)(2,1)S(1)} %get-tuple-element.106), channel_id=1, source_target_pairs={{0,4},{1,5},{2,6},{3,7},{4,0},{5,1},{6,2},{7,3},{8,12},{9,13},{10,... | collective-permute-start | bytes 393224 | tf_op jit(solution)/shard_map/ppermute | solution.py:469
  89.9 10.4 %collective-permute-start.23 = (bf16[128,1024]{1,0:T(8,128)(2,1)S(1)}, bf16[128,1024]{1,0:T(8,128)(2,1)S(1)}, u32[]{:S(2)}, u32[]{:S(2)}) collective-permute-start(bf16[128,1024]{1,0:T(8,128)(2,1)S(1)} %finish.2), channel_id=1, source_target_pairs={{0,8},{8,16},{16,24},{24,0},{1,9},{9,17},{17,25},{25,1},{2,10},{10... | collective-permute-start | bytes 786440 | tf_op jit(solution)/shard_map/ppermute | solution.py:474
  94.9 10.5 %collective-permute-start.27 = (bf16[128,1024]{1,0:T(8,128)(2,1)S(1)}, bf16[128,1024]{1,0:T(8,128)(2,1)S(1)}, u32[]{:S(2)}, u32[]{:S(2)}) collective-permute-start(bf16[128,1024]{1,0:T(8,128)(2,1)S(1)} %finish.3), channel_id=1, source_target_pairs={{0,8},{8,16},{16,24},{24,0},{1,9},{9,17},{17,25},{25,1},{2,10},{10... | collective-permute-start | bytes 786440 | tf_op jit(solution)/shard_map/ppermute | solution.py:474
